TPU v7x, 256 devices: a whole 4x4x8 slice. The times are simulated.
256 devices in a mesh: clu: 64 (over y, z, core), rk: 4 (over x).
Axes of the slice: x: 4, y: 4, z: 8, core: 2. Of those that a mesh axis runs over, the one named last changes fastest.
Arguments:
- bases: float32 [64, 32, 256, 64], P('clu', None, None, 'rk'), may hold values from -0.4 to 0.4
- leaf_transfer: float32 [64, 32, 64, 64], P('clu')
- node_transfer: float32 [64, 64, 64], P('clu'), as said below
- pair_transfer: float32 [64, 64, 64], P('clu'), as said below
- quad_transfer: float32 [64, 64, 64], P('clu'), as said below
- coupling: float32 [64, 32, 32, 64, 64], P('clu', None, None, 'rk'), may hold values from -1.2 to 1.2
- row_device: int32 [64, 32, 32, 1], P('clu'), may hold values from 0 to 63; in each aligned block of 1024 rows (0 to 1023, 1024 to 2047, ..., all dimensions but the last counted through in order) at most 24 rows name the same one
- row_slot: int32 [64, 32, 32], P('clu'), may hold values from 0 to 31
- block_count: int32 [64, 32], P('clu'), may hold values from 16 to 32
Outputs:
- leaf_weights: float32 [64, 32, 64, 64], P('clu', None, None, 'rk')
- node_weights: float32 [4, 64, 64, 64], P(None, 'clu', None, 'rk')
- coupled: float32 [64, 32, 64, 64], P('clu', None, None, 'rk')
Inputs may be any that keep to these rules, and one draw needn't show every extreme that they name: node_transfer[c] is drawn anew for every clu index. pair_transfer[c] equals pair_transfer[c xor 1]: one matrix for each node over two clu indices. quad_transfer[c] is the same for the four clu indices c of one node (equal c // 4). Among the 1024 listed blocks of one clu index, at most 24 name the same row_device.
All inputs are finite; a program needn't handle non-finite values.
Results may differ from a plain program's by a relative error of at most 0.00014.
Values sent between devices are 32-bit elements; how exact they have to be, the bound alone decides.
No kernel may reach another device: no remote copies, remote signals or barrier semaphores. Data moves between devices by JAX's collectives and lax.ppermute only.
A program may use at most 128 MiB of HBM per device.

v0:
```python
import jax
import jax.numpy as jnp
from jax import lax
from jax.sharding import PartitionSpec as P


def from_partner(value, axis, bit):
    mask = 2**bit
    pairs = [(source, source ^ mask) for source in range(lax.axis_size(axis))]
    return lax.ppermute(value, axis, pairs)


def upper_factor(gram):
    return jnp.swapaxes(jnp.linalg.cholesky(gram), -1, -2)


def shards(
    bases,
    leaf_transfer,
    node_transfer,
    pair_transfer,
    quad_transfer,
    coupling,
    row_device,
    row_slot,
    block_count,
):
    highest = lax.Precision.HIGHEST
    n_rank = lax.axis_size("rk")
    rank_index = lax.axis_index("rk")
    local = bases[0]
    leaves = local.shape[0]
    width = local.shape[2]
    full_rank = width * n_rank
    whole = lax.all_gather(local, "rk", axis=2, tiled=True)
    gram = jnp.einsum("jpa,jpb->jab", whole, whole, precision=highest)
    leaf_moves = leaf_transfer[0]
    moved = jnp.einsum("jab,jbe->jae", gram, leaf_moves, precision=highest)
    term = jnp.einsum("jaf,jae->jfe", leaf_moves, moved, precision=highest)
    level = jnp.sum(term, axis=0)
    grams = [level]
    for bit, transfer in enumerate((node_transfer[0], pair_transfer[0], quad_transfer[0])):
        moved = jnp.dot(level, transfer, precision=highest)
        term = jnp.dot(transfer.T, moved, precision=highest)
        level = term + from_partner(term, "clu", bit)
        grams.append(level)
    factor_all = upper_factor(jnp.concatenate([gram, jnp.stack(grams)], axis=0))
    leaf_factor = factor_all[:leaves]
    node_factors = factor_all[leaves:]
    node_weights = lax.dynamic_slice_in_dim(node_factors, rank_index * width, width, 2)
    leaf_weights = lax.dynamic_slice_in_dim(leaf_factor, rank_index * width, width, 2)
    blocks = coupling[0]
    listed = blocks.shape[1]
    prod = jnp.einsum("jkab,jcb->jkac", blocks, leaf_factor, precision=highest)
    count = leaves * listed
    feature = width * full_rank
    flat = prod.reshape(count, feature)
    dest = row_device[0, :, :, 0].reshape(count)
    slot = row_slot[0].reshape(count)
    valid = (jnp.arange(listed, dtype=jnp.int32)[None, :] < block_count[0][:, None]).reshape(count)
    n_clu = lax.axis_size("clu")
    capacity = 3 * count // (2 * n_clu)
    owners_table = jnp.arange(n_clu, dtype=jnp.int32)[None, :]
    onehot = ((dest[:, None] == owners_table) & valid[:, None]).astype(jnp.int32)
    before = jnp.cumsum(onehot, axis=0) - onehot
    place = jnp.sum(before * onehot, axis=1)
    target = jnp.where(valid, dest * capacity + place, n_clu * capacity)
    buffer = jnp.zeros((n_clu * capacity + 1, feature), jnp.float32).at[target].set(flat)
    buffer = buffer[:-1].reshape(n_clu, capacity, feature)
    labels = jnp.full((n_clu * capacity + 1,), float(leaves), jnp.float32)
    labels = labels.at[target].set(jnp.where(valid, slot, leaves).astype(jnp.float32))
    labels = labels[:-1].reshape(n_clu, capacity)
    arrived, owners = (
        lax.all_to_all(buffer, "clu", split_axis=0, concat_axis=0, tiled=True),
        lax.all_to_all(labels, "clu", split_axis=0, concat_axis=0, tiled=True),
    )
    owner_ids = owners.reshape(-1).astype(jnp.int32)
    summed = jax.ops.segment_sum(arrived.reshape(-1, feature), owner_ids, num_segments=leaves + 1)[
        :leaves
    ]
    gathered = summed.reshape(leaves, width, full_rank)
    partial_sum = jnp.einsum("jab,jbe->jae", leaf_weights, gathered, precision=highest)
    coupled = lax.psum_scatter(partial_sum, "rk", scatter_dimension=2, tiled=True)
    return (leaf_weights[None], node_weights[:, None], coupled[None])


def solution(mesh):
    placed = (
        P("clu", None, None, "rk"),
        P("clu", None, None, None),
        P("clu", None, None),
        P("clu", None, None),
        P("clu", None, None),
        P("clu", None, None, "rk", None),
        P("clu", None, None, None),
        P("clu", None, None),
        P("clu", None),
    )
    return jax.shard_map(
        shards,
        mesh=mesh,
        in_specs=placed,
        out_specs=(
            P("clu", None, None, "rk"),
            P(None, "clu", None, "rk"),
            P("clu", None, None, "rk"),
        ),
        check_vma=False,
    )
```

profile of v0, /device:TPU:32, one launch (start us, length us, event | category | flops | bytes accessed | tf_op | source)
XLA Modules:
  0.0 532.6 jit_solution(13422580980584530736)
XLA Ops:
  7.2 0.7 all-gather.3.cloned.1.call-update
  7.9 0.7 iota_compare_fusion.4
  8.8 0.5 broadcast.117
  9.4 1.3 reduce.23
  11.0 0.8 eq.29
  11.8 18.0 %reduce-window.6 = s32[64,8,128]{2,1,0:T(8,128)S(1)} reduce-window(s32[64,8,128]{2,1,0:T(8,128)S(1)} %fusion.20, s32[]{:T(128)} %constant.58.clone.1), window={size=1x1x128 pad=0_0x0_0x127_0}, to_apply=%region_2.3 | reduce-window | flops 8323072 | bytes 524292 | tf_op jit(solution)/shard_map/reduce-window
  30.0 0.1 copy.35
  30.3 0.7 fusion.41
  31.2 0.1 broadcast_add_fusion
  31.5 4.3 scatter_custom_fusion
  35.8 0.7 all_to_all.9
  36.5 11.8 %all-to-all-start = ((f32[64,1,24]{2,1,0:T(1,128)}), f32[64,1,24]{2,1,0:T(1,128)S(1)}, u32[]{:S(2)}, u32[]{:S(2)}) async-start(f32[64,1,24]{2,1,0:T(1,128)} %bitcast.23), calls=%async_computation | async-start | bytes 65536 | tf_op jit(solution)/shard_map/all_to_all | solution.py:75
  48.3 4.3 fusion.7
  52.6 1.3 copy.33
  53.9 1.3 constant_dynamic-update-slice_fusion
  55.2 1.9 fusion.13
  57.1 1.1 bitcast_dynamic-update-slice_fusion
  58.2 0.2 fusion.32
  58.5 0.2 convolution_bitcast_fusion.2
  58.7 0.2 collective-permute-start
  59.0 1.0 collective-permute-done
  60.0 0.2 fusion.29
  60.3 0.2 convolution_bitcast_fusion.1
  60.5 0.5 collective-permute-start.1
  61.1 3.5 collective-permute-done.1
  64.5 0.2 fusion.26
  64.8 0.2 convolution_bitcast_fusion
  65.0 2.9 collective-permute-start.2
  67.9 2.4 collective-permute-done.2
  70.4 0.4 copy.34
  70.7 1.2 fusion.9
  71.9 211.7 %custom-call.4 = f32[36,64,64]{2,1,0:T(8,128)S(1)} custom-call(f32[36,64,64]{2,1,0:T(8,128)} %fusion.9), custom_call_target="Cholesky" | custom-call | tf_op jit(solution)/shard_map/jit(cholesky)/cholesky | solution.py:14
  283.6 0.2 select_reduce_fusion
  283.9 0.2 select_bitcast_fusion
  284.1 13.7 %fusion.2 = f32[32,32,16,64]{3,1,2,0:T(8,128)S(1)} fusion(f32[32,32,16,64]{3,2,1,0:T(8,128)} %bitcast.100, f32[36,64,64]{1,2,0:T(8,128)S(1)} %select_bitcast_fusion), kind=kOutput, calls=%fused_computation.5 | convolution fusion | flops 805306368 | bytes 9437184 | tf_op jit(solution)/shard_map/jkab,jcb->jkac/dot_general | solution.py:54
  297.7 10.8 %copy.40 = f32[32,32,16,64]{3,2,1,0:T(8,128)} copy(f32[32,32,16,64]{3,1,2,0:T(8,128)S(1)} %fusion.2) | data formatting | bytes 8388608 | tf_op jit(solution)/shard_map/jkab,jcb->jkac/dot_general | solution.py:54
  308.5 7.6 %reshape.148 = f32[1024,1024]{1,0:T(8,128)} reshape(f32[32,32,16,64]{3,2,1,0:T(8,128)} %copy.40) | data formatting | bytes 8388608 | tf_op jit(solution)/shard_map/reshape | solution.py:57
  316.1 9.0 %scatter_custom_fusion.1 = f32[1537,1024]{1,0:T(8,128)} fusion(s32[1024]{0:T(1024)S(1)} %bitcast.107, f32[1024,1024]{1,0:T(8,128)} %reshape.148, f32[]{:T(128)} %constant.55.clone.1), kind=kCustom, calls=%fused_computation.6 | custom fusion | bytes 6296064 | tf_op jit(solution)/shard_map/scatter | solution.py:68
  325.2 6.6 %slice.39 = f32[1536,1024]{1,0:T(8,128)} slice(f32[1537,1024]{1,0:T(8,128)} %scatter_custom_fusion.1), slice={[0:1536], [0:1024]} | slice | bytes 12582912 | tf_op jit(solution)/shard_map/slice | solution.py:69
  331.8 10.8 %all-to-all-start.1 = ((f32[64,24,1024]{2,1,0:T(8,128)}), f32[64,24,1024]{2,1,0:T(8,128)}, u32[]{:S(2)}, u32[]{:S(2)}) async-start(f32[64,24,1024]{2,1,0:T(8,128)} %bitcast.99), calls=%async_computation.1 | async-start | bytes 12582912 | tf_op jit(solution)/shard_map/all_to_all | solution.py:74
  343.0 138.7 %all-to-all-done.1 = f32[64,24,1024]{2,1,0:T(8,128)} async-done(((f32[64,24,1024]{2,1,0:T(8,128)}), f32[64,24,1024]{2,1,0:T(8,128)}, u32[]{:S(2)}, u32[]{:S(2)}) %all-to-all-start.1) | async-done | bytes 6291488 | tf_op jit(solution)/shard_map/all_to_all | solution.py:74
  481.6 14.7 %scatter_custom_fusion.2 = f32[33,1024]{1,0:T(8,128)S(1)} fusion(s32[1536]{0:T(1024)S(1)} %reshape.154, f32[1536,1024]{1,0:T(8,128)} %bitcast.28, f32[]{:T(128)} %constant.55.clone.1), kind=kCustom, calls=%fused_computation.35 | custom fusion | flops 1572864 | bytes 135680 | tf_op jit(solution)/shard_map/scatter-add | solution.py:78
  496.3 0.7 slice.40
  497.0 1.0 reshape.135
  498.0 2.8 fusion.21
  500.9 0.6 dynamic-slice_bitcast_fusion.1
  501.5 0.7 dynamic-slice_bitcast_fusion
  502.2 23.4 %reduce-scatter.2.cloned.1.call-done = f32[32,64,16]{1,2,0:T(8,128)} async-done(((f32[32,64,64]{1,2,0:T(8,128)}), f32[32,64,16]{1,2,0:T(8,128)}) %reduce-scatter.2.cloned.1.call-update) | async-done | bytes 131088 | tf_op jit(solution)/shard_map/reduce_scatter | solution.py:83
  (46 shorter events, 1.7 us)
Async XLA Ops:
  7.2 48.1 %copy-start = (f32[1,32,64,64]{3,2,1,0:T(8,128)S(1)}, f32[1,32,64,64]{3,2,1,0:T(8,128)}, u32[]{:S(2)}) copy-start(f32[1,32,64,64]{3,2,1,0:T(8,128)} %param.10) | copy-start | bytes 1572868
  7.2 23.1 %copy-start.4 = (s32[1,32,32,1]{2,3,1,0:T(1,128)S(1)}, s32[1,32,32,1]{2,3,1,0:T(1,128)}, u32[]{:S(2)}) copy-start(s32[1,32,32,1]{2,3,1,0:T(1,128)} %param.15) | copy-start | bytes 12292
  7.2 24.0 %copy-start.5 = (s32[1,32,32]{2,1,0:T(8,128)S(1)}, s32[1,32,32]{2,1,0:T(8,128)}, u32[]{:S(2)}) copy-start(s32[1,32,32]{2,1,0:T(8,128)} %param.16) | copy-start | bytes 12292
  7.2 41.1 %all-gather.3.cloned.1.call-start = ((), (), s32[]{:S(2)}) async-start(), calls=%async_computation.4 | async-start | bytes 2621440 | tf_op jit(solution)/shard_map/all_gather | solution.py:35
  36.5 295.2 %all-to-all-start = ((f32[64,1,24]{2,1,0:T(1,128)}), f32[64,1,24]{2,1,0:T(1,128)S(1)}, u32[]{:S(2)}, u32[]{:S(2)}) async-start(f32[64,1,24]{2,1,0:T(1,128)} %bitcast.23), calls=%async_computation | async-start | bytes 65536 | tf_op jit(solution)/shard_map/all_to_all | solution.py:75
  57.1 1.1 copy-start.1
  57.1 2.9 copy-start.2
  57.1 7.4 %copy-start.3 = (f32[1,64,64]{2,1,0:T(8,128)S(1)}, f32[1,64,64]{2,1,0:T(8,128)}, u32[]{:S(2)}) copy-start(f32[1,64,64]{2,1,0:T(8,128)} %param.13) | copy-start | bytes 49156
  58.7 1.3 collective-permute-start
  60.5 4.0 collective-permute-start.1
  65.0 5.4 %collective-permute-start.2 = (f32[64,64]{0,1:T(8,128)S(1)}, f32[64,64]{0,1:T(8,128)S(1)}, u32[]{:S(2)}, u32[]{:S(2)}) collective-permute-start(f32[64,64]{0,1:T(8,128)S(1)} %convolution_bitcast_fusion), channel_id=1, source_target_pairs={{0,16},{4,20},{8,24},{12,28},{16,0},{20,4},{24,8},{28,12},{32,48},... | collective-permute-start | bytes 49160 | tf_op jit(solution)/shard_map/ppermute | solution.py:10
  331.8 149.9 %all-to-all-start.1 = ((f32[64,24,1024]{2,1,0:T(8,128)}), f32[64,24,1024]{2,1,0:T(8,128)}, u32[]{:S(2)}, u32[]{:S(2)}) async-start(f32[64,24,1024]{2,1,0:T(8,128)} %bitcast.99), calls=%async_computation.1 | async-start | bytes 12582912 | tf_op jit(solution)/shard_map/all_to_all | solution.py:74
  342.6 183.0 %reduce-scatter.2.cloned.1.call-start = ((), (), s32[]{:S(2)}) async-start(), calls=%async_computation.3 | async-start | bytes 1310720 | tf_op jit(solution)/shard_map/reduce_scatter | solution.py:83
Sparse Core Ops, SparseCore 0:
  9.8 35.9 all-gather.2
  501.0 24.5 reduce-scatter.1
where the time goes:
time: 541 us; the launch traced here: 533 us
  other arithmetic  249 us (46%)
  waiting for transfers between devices  170 us (31%)
  local copies, waits for them, and re-layouts  47.6 us (9%)
  starting transfers between devices  26.4 us (5%)
  matrix products  25.1 us (5%)
  between operations  14.6 us (3%)
    another operation x4, other arithmetic, upper_factor(): return jnp.swapaxes(jnp.linalg.cholesky(gram), -1, -2)  212 us
    all_to_all x1, waiting for transfers between devices, shards(): lax.all_to_all(buffer, 'clu', split_axis=0, concat_axis=0, tiled=True)  139 us
    reduce_scatter x1, waiting for transfers between devices, shards(): lax.psum_scatter(partial_sum, 'rk', scatter_dimension=2, tiled=True)  23.4 us
    another operation x3, other arithmetic  18.2 us
    scatter-add x1, other arithmetic, shards(): jax.ops.segment_sum(arrived.reshape(-1, feature), owner_ids, num_segments...  14.7 us
    dot_general x1, matrix products, shards(): prod = jnp.einsum('jkab,jcb->jkac', blocks, leaf_factor, precision=highest)  13.7 us
    all_to_all x1, starting transfers between devices, shards(): lax.all_to_all(labels, 'clu', split_axis=0, concat_axis=0, tiled=True)  11.8 us
    all_to_all x1, starting transfers between devices, shards(): lax.all_to_all(buffer, 'clu', split_axis=0, concat_axis=0, tiled=True)  10.8 us
  transfers between devices with their start and end apart: 7, of which 5 were waited for; matrix products, arithmetic and copies ran while one was open for 57% of the time, Pallas kernels for 0%

commit v1 on v0

v1 whole, which is shorter than its diff:
```python
import functools

import jax
import jax.numpy as jnp
from jax import lax
from jax.experimental import pallas as pl
from jax.experimental.pallas import tpu as pltpu
from jax.sharding import Mesh
from jax.sharding import PartitionSpec as P

HIGHEST = lax.Precision.HIGHEST
RANK = 64
TILE = 8
TILES = RANK // TILE


def shift(value, axis, step):
    size = lax.axis_size(axis)
    return lax.ppermute(value, axis, [(i, (i + step) % size) for i in range(size)])


def swap(value, axis, mask):
    return lax.ppermute(value, axis, [(i, i ^ mask) for i in range(lax.axis_size(axis))])


def factor_in_place(s_ref):
    batch = s_ref.shape[2]
    sub = lax.broadcasted_iota(jnp.int32, (TILE, batch), 0)
    for jb in range(TILES):
        count = TILES - jb
        base = jb * TILE
        rows = [
            [s_ref[base + k, pl.ds((jb + t) * TILE, TILE), :] for t in range(count)]
            for k in range(TILE)
        ]
        for k in range(TILE):
            scale = lax.rsqrt(rows[k][0][k : k + 1, :])
            row = [v * scale for v in rows[k]]
            row[0] = jnp.where(sub >= k, row[0], 0.0)
            rows[k] = row
            for t in range(count):
                s_ref[base + k, pl.ds((jb + t) * TILE, TILE), :] = row[t]
            for t in range(jb):
                s_ref[base + k, pl.ds(t * TILE, TILE), :] = jnp.zeros((TILE, batch), jnp.float32)
            for k2 in range(k + 1, TILE):
                s = row[0][k2 : k2 + 1, :]
                rows[k2] = [v - s * u for v, u in zip(rows[k2], row)]
        for rb in range(jb + 1, TILES):
            for r in range(rb * TILE, (rb + 1) * TILE):
                heads = [s_ref[base + k, pl.ds(r, 1), :] for k in range(TILE)]
                for ct in range(rb, TILES):
                    total = s_ref[r, pl.ds(ct * TILE, TILE), :]
                    for k in range(TILE):
                        total = total - heads[k] * rows[k][ct - jb]
                    s_ref[r, pl.ds(ct * TILE, TILE), :] = total


def to_lanes(g_ref, s_ref):
    for a in range(RANK):
        s_ref[a] = g_ref[:, a, :].T


def column_of(s_ref, c):
    return s_ref[:, c, :].T


def leaf_kernel(x_ref, gram_ref, packed_ref, s_ref):
    sources, leaves = x_ref.shape[0], x_ref.shape[1]
    for m in range(leaves):
        x = jnp.concatenate([x_ref[s, m] for s in range(sources)], axis=0)
        gram_ref[m] = lax.dot_general(
            x, x, (((1,), (1,)), ((), ())), precision=HIGHEST, preferred_element_type=jnp.float32
        )
    to_lanes(gram_ref, s_ref)
    factor_in_place(s_ref)
    half = RANK // 2
    for c in range(half):
        packed_ref[:, c, :] = jnp.concatenate(
            [column_of(s_ref, c), column_of(s_ref, c + half)], axis=1
        )


def leaf_factors(x):
    leaves = x.shape[1]
    return pl.pallas_call(
        leaf_kernel,
        out_shape=(
            jax.ShapeDtypeStruct((leaves, RANK, RANK), jnp.float32),
            jax.ShapeDtypeStruct((leaves, RANK // 2, 2 * RANK), jnp.float32),
        ),
        in_specs=[pl.BlockSpec(memory_space=pltpu.VMEM)],
        out_specs=(pl.BlockSpec(memory_space=pltpu.VMEM),) * 2,
        scratch_shapes=[pltpu.VMEM((RANK, RANK, leaves), jnp.float32)],
        compiler_params=pltpu.CompilerParams(vmem_limit_bytes=32 * 2**20),
        name="leaf_factors",
    )(x)


def node_kernel(g_ref, out_ref, s_ref):
    to_lanes(g_ref, s_ref)
    factor_in_place(s_ref)
    for c in range(RANK):
        out_ref[:, c, :] = column_of(s_ref, c)


def node_lower(grams):
    return pl.pallas_call(
        node_kernel,
        out_shape=jax.ShapeDtypeStruct(grams.shape, jnp.float32),
        in_specs=[pl.BlockSpec(memory_space=pltpu.VMEM)],
        out_specs=pl.BlockSpec(memory_space=pltpu.VMEM),
        scratch_shapes=[pltpu.VMEM((RANK, RANK, grams.shape[0]), jnp.float32)],
        compiler_params=pltpu.CompilerParams(vmem_limit_bytes=32 * 2**20),
        name="node_factors",
    )(grams)


def split(value):
    high = value.astype(jnp.bfloat16)
    return high, (value - high.astype(jnp.float32)).astype(jnp.bfloat16)


def product_kernel(half, place_ref, c_ref, l_ref, away_ref, keep_ref, acc_ref, sems):
    step = pl.program_id(0)
    per_step, listed, width, rank = c_ref.shape
    top = width // 2

    @pl.when(step == 0)
    def _():
        acc_ref[...] = jnp.zeros_like(acc_ref)

    zero = jnp.zeros((rank, rank), jnp.float32)
    for jj in range(per_step):
        packed = l_ref[jj]
        lower = jnp.concatenate([packed[:, :rank], packed[:, rank:]], axis=0)
        blocks = c_ref[jj]
        total = None
        for part, weight in (
            (blocks[:, :top, :], jnp.concatenate([lower, zero], axis=1)),
            (blocks[:, top:, :], jnp.concatenate([zero, lower], axis=1)),
        ):
            a_high, a_low = split(part.reshape(listed * top, rank))
            w_high, w_low = split(weight)
            for a, w in ((a_high, w_high), (a_low, w_high), (a_high, w_low)):
                term = jnp.dot(a, w, preferred_element_type=jnp.float32)
                total = term if total is None else total + term
        for k in range(listed):
            place = place_ref[(step * per_step + jj) * listed + k]
            acc_ref[place] = acc_ref[place] + total[k * top : (k + 1) * top, :]

    @pl.when(step == pl.num_programs(0) - 1)
    def _():
        first = pltpu.make_async_copy(acc_ref.at[pl.ds(0, half)], away_ref, sems.at[0])
        second = pltpu.make_async_copy(acc_ref.at[pl.ds(half, half)], keep_ref, sems.at[1])
        first.start()
        second.start()
        first.wait()
        second.wait()


def weighted_sums(place, blocks, packed, half):
    leaves, listed, width, rank = blocks.shape
    per_step = 4
    top = width // 2
    out = jax.ShapeDtypeStruct((half, top, 2 * rank), jnp.float32)
    return pl.pallas_call(
        functools.partial(product_kernel, half),
        grid_spec=pltpu.PrefetchScalarGridSpec(
            num_scalar_prefetch=1,
            grid=(leaves // per_step,),
            in_specs=[
                pl.BlockSpec((per_step, listed, width, rank), lambda i, p: (i, 0, 0, 0)),
                pl.BlockSpec((per_step, rank // 2, 2 * rank), lambda i, p: (i, 0, 0)),
            ],
            out_specs=(pl.BlockSpec(memory_space=pl.ANY),) * 2,
            scratch_shapes=[
                pltpu.VMEM((2 * half + TILE, top, 2 * rank), jnp.float32),
                pltpu.SemaphoreType.DMA((2,)),
            ],
        ),
        out_shape=(out, out),
        compiler_params=pltpu.CompilerParams(vmem_limit_bytes=48 * 2**20),
        name="weighted_sums",
    )(place, blocks, packed)


def shards(
    bases,
    leaf_transfer,
    node_transfer,
    pair_transfer,
    quad_transfer,
    coupling,
    row_device,
    row_slot,
    block_count,
):
    n_rank = lax.axis_size("rk")
    rank_index = lax.axis_index("rk")
    n_z = lax.axis_size("z")
    n_core = lax.axis_size("core")
    core = lax.axis_index("core")
    n_clu = lax.axis_size("y") * n_z * n_core
    local = jnp.swapaxes(bases[0], 1, 2)
    leaves, width, points = local.shape
    full_rank = width * n_rank
    share = leaves // n_rank

    blocks = coupling[0]
    listed = blocks.shape[1]
    half = (n_clu // n_core) * leaves
    dest = row_device[0, :, :, 0]
    valid = jnp.arange(listed, dtype=jnp.int32)[None, :] < block_count[0][:, None]
    own = (dest % n_core) == core
    place = jnp.where(own, half, 0) + (dest // n_core) * leaves + row_slot[0]
    place = jnp.where(valid, place, n_core * half).reshape(-1).astype(jnp.int32)

    pieces = lax.all_to_all(local, "rk", split_axis=0, concat_axis=0, tiled=True)
    gram, mine = leaf_factors(pieces.reshape(n_rank, share, width, points))
    packed = lax.all_gather(mine, "rk", axis=0, tiled=True)

    away, keep = weighted_sums(place, blocks, packed, half)
    dense = keep + swap(away, "core", 1)
    dense = lax.psum_scatter(dense, "y", scatter_dimension=0, tiled=True)
    gathered = lax.psum_scatter(dense, "z", scatter_dimension=0, tiled=True)

    lower = jnp.concatenate([packed[:, :, :full_rank], packed[:, :, full_rank:]], axis=1)
    gathered = gathered.reshape(leaves, width // 2, 2, full_rank)
    gathered = jnp.transpose(gathered, (0, 2, 1, 3)).reshape(leaves, width, full_rank)
    wide = lax.all_to_all(gathered, "rk", split_axis=2, concat_axis=1, tiled=True)
    coupled = jnp.einsum("jbe,jba->jea", wide, lower, precision=HIGHEST)

    moves = lax.dynamic_slice_in_dim(leaf_transfer[0], rank_index * share, share, 0)
    moved = jnp.einsum("jab,jbe->jae", gram, moves, precision=HIGHEST)
    level = jnp.einsum("jaf,jae->fe", moves, moved, precision=HIGHEST)
    level = level + swap(level, "rk", 1)
    level = level + swap(level, "rk", 2)
    grams = [level]
    partners = (("core", 1), ("z", 1), ("z", 2))
    for (axis, mask), transfer in zip(
        partners, (node_transfer[0], pair_transfer[0], quad_transfer[0])
    ):
        moved = jnp.dot(level, transfer, precision=HIGHEST)
        term = jnp.dot(transfer.T, moved, precision=HIGHEST)
        level = term + swap(term, axis, mask)
        grams.append(level)
    nodes = node_lower(jnp.stack(grams))

    node_weights = lax.dynamic_slice_in_dim(nodes, rank_index * width, width, 1)
    leaf_weights = lax.dynamic_slice_in_dim(lower, rank_index * width, width, 1)
    return (
        jnp.swapaxes(leaf_weights, 1, 2)[None],
        jnp.swapaxes(node_weights, 1, 2)[:, None],
        jnp.swapaxes(coupled, 1, 2)[None],
    )


def solution(mesh):
    devices = mesh.devices
    fine = Mesh(devices.reshape(4, 8, 2, devices.shape[1]), ("y", "z", "core", "rk"))
    clu = ("y", "z", "core")
    placed = (
        P(clu, None, None, "rk"),
        P(clu, None, None, None),
        P(clu, None, None),
        P(clu, None, None),
        P(clu, None, None),
        P(clu, None, None, "rk", None),
        P(clu, None, None, None),
        P(clu, None, None),
        P(clu, None),
    )
    return jax.shard_map(
        shards,
        mesh=fine,
        in_specs=placed,
        out_specs=(
            P(clu, None, None, "rk"),
            P(None, clu, None, "rk"),
            P(clu, None, None, "rk"),
        ),
        check_vma=False,
    )
```

time: 541 us -> 180 us (0.33); the launches traced: 533 us -> 179 us
  other arithmetic: 249 us -> 8.5 us
  waiting for transfers between devices: 170 us -> 96.6 us
  local copies, waits for them, and re-layouts: 47.6 us -> 5.82 us
  Pallas kernels: 0 us -> 22.3 us
  matrix products: 25.1 us -> 4.15 us
  blocking collectives: 0 us -> 12.9 us
  starting transfers between devices: 26.4 us -> 14.3 us
    another operation x7 -> x5, other arithmetic: 230 us -> 0.03 us  [shards(): nodes = node_lower(jnp.stack(grams))]
    all_to_all x2, waiting for transfers between devices: 139 us -> 11.2 us  [the longest x1 5.85 us: shards(): lax.all_to_all(local, 'rk', split_axis=0, concat_axis=0, tiled=True)]
    reduce_scatter x1 -> x2, waiting for transfers between devices: 23.4 us -> 64.9 us  [the longest x1 40 us: shards(): dense = lax.psum_scatter(dense, 'y', scatter_dimension=0, tiled=True)]
    pallas_call x0 -> x3, Pallas kernels: none -> 22.3 us  [the longest x1 13.3 us: weighted_sums(): pl.pallas_call(functools.partial(product_kernel, half), grid_spec=pltpu.P...]
    dot_general x11 -> x9, matrix products: 25.1 us -> 4.15 us  [the longest x1 1.76 us: shards(): coupled = jnp.einsum('jbe,jba->jea', wide, lower, precision=HIGHEST)]
    scatter-add x1 -> x0, other arithmetic: 14.7 us -> none  [shards(): jax.ops.segment_sum(arrived.reshape(-1, feature), owner_ids, num_segments...]
    all_to_all x2, starting transfers between devices: 22.6 us -> 8.68 us  [the longest x1 4.44 us: shards(): lax.all_to_all(local, 'rk', split_axis=0, concat_axis=0, tiled=True)]
    ppermute x3 -> x6, waiting for transfers between devices: 6.95 us -> 20.5 us  [swap(): lax.ppermute(value, axis, [(i, i ^ mask) for i in range(lax.axis_size(axi...]
  transfers between devices with their start and end apart: 7 -> 10, of which waited for: 5 -> 10; matrix products, arithmetic and copies ran while one was open for 57% -> 4% of each run, Pallas kernels for 0% -> 2%
where the time goes in v1:
time: 180 us; the launch traced here: 179 us
  waiting for transfers between devices  96.6 us (54%)
  Pallas kernels  22.3 us (12%)
  starting transfers between devices  14.3 us (8%)
  between operations  14.2 us (8%)
  blocking collectives  12.9 us (7%)
  other arithmetic  8.5 us (5%)
  local copies, waits for them, and re-layouts  5.82 us (3%)
  matrix products  4.15 us (2%)
    reduce_scatter x1, waiting for transfers between devices, shards(): dense = lax.psum_scatter(dense, 'y', scatter_dimension=0, tiled=True)  40 us
    reduce_scatter x1, waiting for transfers between devices, shards(): gathered = lax.psum_scatter(dense, 'z', scatter_dimension=0, tiled=True)  24.9 us
    ppermute x6, waiting for transfers between devices, swap(): lax.ppermute(value, axis, [(i, i ^ mask) for i in range(lax.axis_size(axi...  20.5 us
    pallas_call x1, Pallas kernels, weighted_sums(): pl.pallas_call(functools.partial(product_kernel, half), grid_spec=pltpu.P...  13.3 us
    all_gather x1, blocking collectives, shards(): packed = lax.all_gather(mine, 'rk', axis=0, tiled=True)  12.9 us
    all_to_all x1, waiting for transfers between devices, shards(): lax.all_to_all(local, 'rk', split_axis=0, concat_axis=0, tiled=True)  5.85 us
    ppermute x6, starting transfers between devices, swap(): lax.ppermute(value, axis, [(i, i ^ mask) for i in range(lax.axis_size(axi...  5.53 us
    all_to_all x1, waiting for transfers between devices, shards(): lax.all_to_all(gathered, 'rk', split_axis=2, concat_axis=1, tiled=True)  5.36 us
  transfers between devices with their start and end apart: 10, of which 10 were waited for; matrix products, arithmetic and copies ran while one was open for 4% of the time, Pallas kernels for 2%

profile of v1, /device:TPU:32, one launch (start us, length us, event | category | flops | bytes accessed | tf_op | source)
XLA Modules:
  0.0 178.8 jit_solution(11118958953322968540)
XLA Ops:
  7.2 4.4 %all-to-all-start = ((f32[32,16,256]{2,1,0:T(8,128)}), f32[32,16,256]{2,1,0:T(8,128)S(1)}, u32[]{:S(2)}, u32[]{:S(2)}) async-start(f32[32,16,256]{2,1,0:T(8,128)} %bitcast.80), calls=%async_computation | async-start | bytes 1048576 | tf_op jit(solution)/shard_map/all_to_all | solution.py:218
  11.6 0.7 iota_compare_fusion
  12.3 0.1 lt.38
  12.4 0.8 squeeze.27
  13.2 0.5 broadcast.34
  13.7 1.4 reduce.3
  15.2 5.9 %all-to-all-done = f32[32,16,256]{2,1,0:T(8,128)S(1)} async-done(((f32[32,16,256]{2,1,0:T(8,128)}), f32[32,16,256]{2,1,0:T(8,128)S(1)}, u32[]{:S(2)}, u32[]{:S(2)}) %all-to-all-start) | async-done | bytes 524320 | tf_op jit(solution)/shard_map/all_to_all | solution.py:218
  21.1 4.9 %leaf_factors.1 = (f32[8,64,64]{2,1,0:T(8,128)S(1)}, f32[8,32,128]{2,1,0:T(8,128)S(1)}) custom-call(f32[4,8,16,256]{3,2,1,0:T(8,128)S(1)} %bitcast.76), custom_call_target="tpu_custom_call" | custom-call | tf_op jit(solution)/shard_map/leaf_factors/pallas_call | solution.py:85
  26.0 12.9 %all_gather.3.l_ref = f32[32,32,128]{2,1,0:T(8,128)S(1)} all-gather(f32[8,32,128]{2,1,0:T(8,128)S(1)} %get-tuple-element.7), channel_id=1, replica_groups=mesh['y'=4,'z'=8,'core'=2,'rk'=4] {'rk'}, dimensions={0}, use_global_device_ids=true | all-gather | bytes 655360 | tf_op jit(solution)/shard_map/all_gather | solution.py:220
  38.9 13.3 %weighted_sums.1 = (f32[1024,8,128]{2,1,0:T(8,128)S(1)}, f32[1024,8,128]{2,1,0:T(8,128)}) custom-call(s32[1024]{0:T(1024)S(1)} %fusion.22.place_ref, f32[32,32,16,64]{3,2,1,0:T(8,128)} %bitcast.77, f32[32,32,128]{2,1,0:T(8,128)S(1)} %all_gather.3.l_ref), custom_call_target="tpu_custom_call" | custom-call | tf_op jit(solution)/shard_map/weighted_sums/pallas_call | solution.py:166
  52.2 0.1 collective-permute-start.5
  52.3 7.1 %collective-permute-done.5 = f32[1024,8,128]{2,1,0:T(8,128)S(1)} collective-permute-done((f32[1024,8,128]{2,1,0:T(8,128)S(1)}, f32[1024,8,128]{2,1,0:T(8,128)S(1)}, u32[]{:S(2)}, u32[]{:S(2)}) %collective-permute-start.5) | collective-permute-done | bytes 4194336 | tf_op jit(solution)/shard_map/ppermute | solution.py:23
  59.5 4.6 %add.56 = f32[1024,8,128]{2,1,0:T(8,128)} add(f32[1024,8,128]{2,1,0:T(8,128)} %get-tuple-element.9, f32[1024,8,128]{2,1,0:T(8,128)S(1)} %collective-permute-done.5) | non-fusion elementwise | flops 1048576 | bytes 12582912 | tf_op jit(solution)/shard_map/add | solution.py:223
  64.1 0.6 convolution_bitcast_fusion
  64.7 0.6 convolution_bitcast_fusion.5
  65.3 0.5 collective-permute-start
  65.9 0.2 fusion.28
  66.1 3.2 %collective-permute-done = f32[64,64]{1,0:T(8,128)S(1)} collective-permute-done((f32[64,64]{1,0:T(8,128)S(1)}, f32[64,64]{1,0:T(8,128)S(1)}, u32[]{:S(2)}, u32[]{:S(2)}) %collective-permute-start) | collective-permute-done | bytes 16416 | tf_op jit(solution)/shard_map/ppermute | solution.py:23
  69.3 1.5 collective-permute-start.1
  70.8 0.8 fusion.1
  71.6 3.2 %collective-permute-done.1 = f32[64,64]{1,0:T(8,128)S(1)} collective-permute-done((f32[64,64]{1,0:T(8,128)S(1)}, f32[64,64]{1,0:T(8,128)S(1)}, u32[]{:S(2)}, u32[]{:S(2)}) %collective-permute-start.1) | collective-permute-done | bytes 16416 | tf_op jit(solution)/shard_map/ppermute | solution.py:23
  74.8 0.2 fusion.13
  74.9 40.0 %reduce-scatter.3.cloned.1.call-done = f32[256,8,128]{2,1,0:T(8,128)} async-done(((f32[1024,8,128]{2,1,0:T(8,128)}), f32[256,8,128]{2,1,0:T(8,128)}) %reduce-scatter.3.cloned.1.call-update) | async-done | bytes 1048592 | tf_op jit(solution)/shard_map/reduce_scatter | solution.py:224
  114.9 0.2 convolution_bitcast_fusion.4
  115.2 0.1 collective-permute-start.2
  115.3 1.2 collective-permute-done.2
  116.5 0.2 fusion.10
  116.6 0.2 convolution_bitcast_fusion.3
  116.9 0.5 collective-permute-start.3
  117.4 3.5 %collective-permute-done.3 = f32[64,64]{1,0:T(8,128)S(1)} collective-permute-done((f32[64,64]{1,0:T(8,128)S(1)}, f32[64,64]{1,0:T(8,128)S(1)}, u32[]{:S(2)}, u32[]{:S(2)}) %collective-permute-start.3) | collective-permute-done | bytes 16416 | tf_op jit(solution)/shard_map/ppermute | solution.py:23
  120.9 0.2 fusion.7
  121.1 0.2 convolution_bitcast_fusion.2
  121.3 2.8 %collective-permute-start.4 = (f32[64,64]{1,0:T(8,128)S(1)}, f32[64,64]{1,0:T(8,128)S(1)}, u32[]{:S(2)}, u32[]{:S(2)}) collective-permute-start(f32[64,64]{1,0:T(8,128)S(1)} %convolution_bitcast_fusion.2), channel_id=1, source_target_pairs={{0,16},{8,24},{16,0},{24,8},{32,48},{40,56},{48,32},{56,40},{1,17}... | collective-permute-start | bytes 49160 | tf_op jit(solution)/shard_map/ppermute | solution.py:23
  124.1 2.3 %collective-permute-done.4 = f32[64,64]{1,0:T(8,128)S(1)} collective-permute-done((f32[64,64]{1,0:T(8,128)S(1)}, f32[64,64]{1,0:T(8,128)S(1)}, u32[]{:S(2)}, u32[]{:S(2)}) %collective-permute-start.4) | collective-permute-done | bytes 16416 | tf_op jit(solution)/shard_map/ppermute | solution.py:23
  126.4 4.1 %node_factors.1 = f32[4,64,64]{2,1,0:T(8,128)S(1)} custom-call(f32[4,64,64]{2,1,0:T(8,128)S(1)} %pad_maximum_fusion.2.g_ref), custom_call_target="tpu_custom_call" | custom-call | tf_op jit(solution)/shard_map/node_factors/pallas_call | solution.py:107
  130.5 24.9 %reduce-scatter.5.cloned.1.call-done = f32[32,8,128]{2,1,0:T(8,128)} async-done(((f32[256,8,128]{2,1,0:T(8,128)}), f32[32,8,128]{2,1,0:T(8,128)}) %reduce-scatter.5.cloned.1.call-update) | async-done | bytes 131088 | tf_op jit(solution)/shard_map/reduce_scatter | solution.py:225
  155.4 1.1 reshape.24
  156.5 0.3 copy.52
  156.9 0.9 reshape.36
  157.8 4.2 %all-to-all-start.1 = ((f32[4,1,8192]{2,1,0:T(1,128)}), f32[4,1,8192]{2,1,0:T(1,128)S(1)}, u32[]{:S(2)}, u32[]{:S(2)}) async-start(f32[4,1,8192]{2,1,0:T(1,128)} %reshape.36), calls=%async_computation.3 | async-start | bytes 262144 | tf_op jit(solution)/shard_map/all_to_all | solution.py:230
  162.0 0.6 dynamic-slice_bitcast_fusion
  162.7 5.4 %all-to-all-done.1 = f32[4,1,8192]{2,1,0:T(1,128)S(1)} async-done(((f32[4,1,8192]{2,1,0:T(1,128)}), f32[4,1,8192]{2,1,0:T(1,128)S(1)}, u32[]{:S(2)}, u32[]{:S(2)}) %all-to-all-start.1) | async-done | bytes 131104 | tf_op jit(solution)/shard_map/all_to_all | solution.py:230
  168.0 0.5 broadcast.35
  168.5 1.0 reduce.4
  169.5 0.2 reshape.37
  169.7 0.2 copy.45
  169.9 0.3 copy.46
  170.2 1.8 convolution_bitcast_fusion.1
  (21 shorter events, 0.3 us)
Async XLA Ops:
  7.2 57.0 %copy-start = (f32[1,32,64,64]{3,2,1,0:T(8,128)S(1)}, f32[1,32,64,64]{3,2,1,0:T(8,128)}, u32[]{:S(2)}) copy-start(f32[1,32,64,64]{3,2,1,0:T(8,128)} %param.10) | copy-start | bytes 1572868
  7.2 13.9 %all-to-all-start = ((f32[32,16,256]{2,1,0:T(8,128)}), f32[32,16,256]{2,1,0:T(8,128)S(1)}, u32[]{:S(2)}, u32[]{:S(2)}) async-start(f32[32,16,256]{2,1,0:T(8,128)} %bitcast.80), calls=%async_computation | async-start | bytes 1048576 | tf_op jit(solution)/shard_map/all_to_all | solution.py:218
  11.6 103.3 %reduce-scatter.3.cloned.1.call-start = ((), (), s32[]{:S(2)}) async-start(), calls=%async_computation.4 | async-start | bytes 5242880 | tf_op jit(solution)/shard_map/reduce_scatter | solution.py:224
  52.2 7.2 %collective-permute-start.5 = (f32[1024,8,128]{2,1,0:T(8,128)S(1)}, f32[1024,8,128]{2,1,0:T(8,128)S(1)}, u32[]{:S(2)}, u32[]{:S(2)}) collective-permute-start(f32[1024,8,128]{2,1,0:T(8,128)S(1)} %get-tuple-element.10), channel_id=1, source_target_pairs={{0,4},{4,0},{1,5},{5,1},{2,6},{6,2},{3,7},{7,3},{8,12},{12,8},{9,1... | collective-permute-start | bytes 12582920 | tf_op jit(solution)/shard_map/ppermute | solution.py:23
  64.0 10.7 %copy-start.1 = (f32[1,64,64]{2,1,0:T(8,128)S(1)}, f32[1,64,64]{2,1,0:T(8,128)}, u32[]{:S(2)}) copy-start(f32[1,64,64]{2,1,0:T(8,128)} %param.11) | copy-start | bytes 49156
  64.0 52.4 %copy-start.2 = (f32[1,64,64]{2,1,0:T(8,128)S(1)}, f32[1,64,64]{2,1,0:T(8,128)}, u32[]{:S(2)}) copy-start(f32[1,64,64]{2,1,0:T(8,128)} %param.12) | copy-start | bytes 49156
  64.1 56.8 %copy-start.3 = (f32[1,64,64]{2,1,0:T(8,128)S(1)}, f32[1,64,64]{2,1,0:T(8,128)}, u32[]{:S(2)}) copy-start(f32[1,64,64]{2,1,0:T(8,128)} %param.13) | copy-start | bytes 49156
  64.1 91.4 %reduce-scatter.5.cloned.1.call-start = ((), (), s32[]{:S(2)}) async-start(), calls=%async_computation.5 | async-start | bytes 1179648 | tf_op jit(solution)/shard_map/reduce_scatter | solution.py:225
  65.3 4.0 %collective-permute-start = (f32[64,64]{1,0:T(8,128)S(1)}, f32[64,64]{1,0:T(8,128)S(1)}, u32[]{:S(2)}, u32[]{:S(2)}) collective-permute-start(f32[64,64]{1,0:T(8,128)S(1)} %convolution_bitcast_fusion.5), channel_id=1, source_target_pairs={{0,1},{1,0},{2,3},{3,2},{4,5},{5,4},{6,7},{7,6},{8,9},{9,8},{10,11... | collective-permute-start | bytes 49160 | tf_op jit(solution)/shard_map/ppermute | solution.py:23
  69.3 5.4 %collective-permute-start.1 = (f32[64,64]{1,0:T(8,128)S(1)}, f32[64,64]{1,0:T(8,128)S(1)}, u32[]{:S(2)}, u32[]{:S(2)}) collective-permute-start(f32[64,64]{1,0:T(8,128)S(1)} %add.48), channel_id=1, source_target_pairs={{0,2},{1,3},{2,0},{3,1},{4,6},{5,7},{6,4},{7,5},{8,10},{9,11},{10,... | collective-permute-start | bytes 49160 | tf_op jit(solution)/shard_map/ppermute | solution.py:23
  115.2 1.3 collective-permute-start.2
  116.9 4.0 %collective-permute-start.3 = (f32[64,64]{1,0:T(8,128)S(1)}, f32[64,64]{1,0:T(8,128)S(1)}, u32[]{:S(2)}, u32[]{:S(2)}) collective-permute-start(f32[64,64]{1,0:T(8,128)S(1)} %convolution_bitcast_fusion.3), channel_id=1, source_target_pairs={{0,8},{8,0},{16,24},{24,16},{32,40},{40,32},{48,56},{56,48},{1,9},... | collective-permute-start | bytes 49160 | tf_op jit(solution)/shard_map/ppermute | solution.py:23
  121.3 5.1 %collective-permute-start.4 = (f32[64,64]{1,0:T(8,128)S(1)}, f32[64,64]{1,0:T(8,128)S(1)}, u32[]{:S(2)}, u32[]{:S(2)}) collective-permute-start(f32[64,64]{1,0:T(8,128)S(1)} %convolution_bitcast_fusion.2), channel_id=1, source_target_pairs={{0,16},{8,24},{16,0},{24,8},{32,48},{40,56},{48,32},{56,40},{1,17}... | collective-permute-start | bytes 49160 | tf_op jit(solution)/shard_map/ppermute | solution.py:23
  157.8 10.2 %all-to-all-start.1 = ((f32[4,1,8192]{2,1,0:T(1,128)}), f32[4,1,8192]{2,1,0:T(1,128)S(1)}, u32[]{:S(2)}, u32[]{:S(2)}) async-start(f32[4,1,8192]{2,1,0:T(1,128)} %reshape.36), calls=%async_computation.3 | async-start | bytes 262144 | tf_op jit(solution)/shard_map/all_to_all | solution.py:230
Sparse Core Ops, SparseCore 0:
  64.2 50.6 reduce-scatter.2
  117.6 37.7 reduce-scatter.4

commit v2 on v1

--- a/solution.py
+++ b/solution.py
@@ -120,68 +120,132 @@
     return high, (value - high.astype(jnp.float32)).astype(jnp.bfloat16)
 
 
-def product_kernel(half, place_ref, c_ref, l_ref, away_ref, keep_ref, acc_ref, sems):
-    step = pl.program_id(0)
-    per_step, listed, width, rank = c_ref.shape
+def product_kernel(near, away, place_ref, c_ref, l_ref, first_ref, second_ref, keep_ref, acc_ref):
+    leaves, listed, width, rank = c_ref.shape
     top = width // 2
-
-    @pl.when(step == 0)
-    def _():
-        acc_ref[...] = jnp.zeros_like(acc_ref)
-
-    zero = jnp.zeros((rank, rank), jnp.float32)
-    for jj in range(per_step):
-        packed = l_ref[jj]
-        lower = jnp.concatenate([packed[:, :rank], packed[:, rank:]], axis=0)
-        blocks = c_ref[jj]
-        total = None
-        for part, weight in (
-            (blocks[:, :top, :], jnp.concatenate([lower, zero], axis=1)),
-            (blocks[:, top:, :], jnp.concatenate([zero, lower], axis=1)),
-        ):
-            a_high, a_low = split(part.reshape(listed * top, rank))
-            w_high, w_low = split(weight)
-            for a, w in ((a_high, w_high), (a_low, w_high), (a_high, w_low)):
-                term = jnp.dot(a, w, preferred_element_type=jnp.float32)
-                total = term if total is None else total + term
+    zero = jnp.zeros((rank, rank), jnp.bfloat16)
+    acc_ref[...] = jnp.zeros_like(acc_ref)
+
+    def leaf(j, carry):
+        packed = l_ref[j]
+        high, low = split(jnp.concatenate([packed[:, :rank], packed[:, rank:]], axis=0))
+        blocks = c_ref[j]
+        wide = jnp.concatenate(
+            [
+                blocks[:, :top, :].reshape(listed * top, rank),
+                blocks[:, top:, :].reshape(listed * top, rank),
+            ],
+            axis=1,
+        )
+        w_high = jnp.concatenate(
+            [jnp.concatenate([high, zero], axis=1), jnp.concatenate([zero, high], axis=1)], axis=0
+        )
+        w_low = jnp.concatenate(
+            [jnp.concatenate([low, zero], axis=1), jnp.concatenate([zero, low], axis=1)], axis=0
+        )
+        c_high, c_low = split(wide)
+        total = jnp.dot(
+            jnp.concatenate([c_high, c_low], axis=1),
+            jnp.concatenate([w_high, w_high], axis=0),
+            preferred_element_type=jnp.float32,
+        )
+        total = total + jnp.dot(c_high, w_low, preferred_element_type=jnp.float32)
         for k in range(listed):
-            place = place_ref[(step * per_step + jj) * listed + k]
+            place = place_ref[j * listed + k]
             acc_ref[place] = acc_ref[place] + total[k * top : (k + 1) * top, :]
-
-    @pl.when(step == pl.num_programs(0) - 1)
-    def _():
-        first = pltpu.make_async_copy(acc_ref.at[pl.ds(0, half)], away_ref, sems.at[0])
-        second = pltpu.make_async_copy(acc_ref.at[pl.ds(half, half)], keep_ref, sems.at[1])
-        first.start()
-        second.start()
-        first.wait()
-        second.wait()
-
-
-def weighted_sums(place, blocks, packed, half):
+        return carry
+
+    lax.fori_loop(0, leaves, leaf, 0)
+    first_ref[...] = acc_ref[:near]
+    second_ref[...] = acc_ref[near:away]
+    keep_ref[...] = acc_ref[away : 2 * away]
+
+
+def weighted_sums(place, blocks, packed, near, away):
     leaves, listed, width, rank = blocks.shape
-    per_step = 4
     top = width // 2
-    out = jax.ShapeDtypeStruct((half, top, 2 * rank), jnp.float32)
+    vmem = pl.BlockSpec(memory_space=pltpu.VMEM)
+
+    def out(rows):
+        return jax.ShapeDtypeStruct((rows, top, 2 * rank), jnp.float32)
+
     return pl.pallas_call(
-        functools.partial(product_kernel, half),
-        grid_spec=pltpu.PrefetchScalarGridSpec(
-            num_scalar_prefetch=1,
-            grid=(leaves // per_step,),
-            in_specs=[
-                pl.BlockSpec((per_step, listed, width, rank), lambda i, p: (i, 0, 0, 0)),
-                pl.BlockSpec((per_step, rank // 2, 2 * rank), lambda i, p: (i, 0, 0)),
-            ],
-            out_specs=(pl.BlockSpec(memory_space=pl.ANY),) * 2,
-            scratch_shapes=[
-                pltpu.VMEM((2 * half + TILE, top, 2 * rank), jnp.float32),
-                pltpu.SemaphoreType.DMA((2,)),
-            ],
-        ),
-        out_shape=(out, out),
-        compiler_params=pltpu.CompilerParams(vmem_limit_bytes=48 * 2**20),
+        functools.partial(product_kernel, near, away),
+        in_specs=[pl.BlockSpec(memory_space=pltpu.SMEM), vmem, vmem],
+        out_specs=(vmem, vmem, vmem),
+        scratch_shapes=[pltpu.VMEM((2 * away + TILE, top, 2 * rank), jnp.float32)],
+        out_shape=(out(near), out(away - near), out(away)),
+        compiler_params=pltpu.CompilerParams(vmem_limit_bytes=32 * 2**20),
         name="weighted_sums",
     )(place, blocks, packed)
+
+
+class Plan:
+    def __init__(self, n_y, n_z, slots):
+        self.cut = slots // 2
+        self.rest = slots - self.cut
+        self.order = (3, 1, 5, 7, 4, 2, 6, 0)
+        self.spot = tuple(self.order.index(r) for r in range(n_z))
+        self.y_rows = n_z * self.cut
+        self.z_rows = n_y * self.rest
+        self.base = {}
+        at = 0
+        for group in ("y2", "z4", "y1", "y3", "z3", "z1", "z5", "z7", "z2", "z6", "y0", "z0"):
+            if group == "y1":
+                self.near = at
+            self.base[group] = at
+            at += self.y_rows if group[0] == "y" else self.z_rows
+        self.total = at
+        self.n_y, self.n_z = n_y, n_z
+
+    def rows(self, rel_y, rel_z, slot):
+        base_y = sum(jnp.where(rel_y == r, self.base["y%d" % r], 0) for r in range(self.n_y))
+        base_z = sum(jnp.where(rel_z == r, self.base["z%d" % r], 0) for r in range(self.n_z))
+        spot = sum(jnp.where(rel_z == r, self.spot[r], 0) for r in range(self.n_z))
+        by_y = base_y + spot * self.cut + slot
+        by_z = base_z + rel_y * self.rest + slot - self.cut
+        return jnp.where(slot < self.cut, by_y, by_z)
+
+
+def sum_over_grid(plan, keep, first, second):
+    near = plan.near
+
+    def part(group, count=1, skip=0, rows=None):
+        size = (plan.y_rows if group[0] == "y" else plan.z_rows) * count if rows is None else rows
+        at = plan.base[group] + skip
+        other = first[at : at + size] if at < near else second[at - near : at - near + size]
+        return keep[at : at + size] + other
+
+    half = plan.z_rows // 2
+    y_far = shift(part("y2"), "y", 2)
+    z_up2 = shift(part("z4", rows=half), "z", 2)
+    z_down2 = shift(part("z4", skip=half, rows=half), "z", -2)
+    y_up = shift(part("y1"), "y", 1)
+    y_down = shift(part("y3"), "y", -1)
+    z_up = shift(part("z3", 2), "z", 1)
+    z_down = shift(part("z5", 2), "z", -1)
+    rows = plan.z_rows
+    pad = ((0, half), (0, 0), (0, 0))
+    pad_low = ((half, 0), (0, 0), (0, 0))
+    z_two = shift(part("z2") + z_up[:rows] + jnp.pad(z_up2, pad), "z", 2)
+    z_six = shift(part("z6") + z_down[:rows] + jnp.pad(z_down2, pad_low), "z", -2)
+
+    by_y = part("y0") + y_far + y_up + y_down
+    cut = plan.cut
+    up = shift(by_y[: 2 * cut], "z", 1)
+    down = shift(by_y[2 * cut : 4 * cut], "z", -1)
+    far = shift(by_y[4 * cut : 5 * cut], "z", 4)
+    two = shift(by_y[5 * cut : 6 * cut] + up[:cut], "z", 2)
+    six = shift(by_y[6 * cut : 7 * cut] + down[:cut], "z", -2)
+    out_y = by_y[7 * cut :] + up[cut:] + down[cut:] + far + two + six
+
+    by_z = part("z0") + z_up[rows:] + z_down[rows:] + z_two + z_six
+    rest = plan.rest
+    r1 = shift(by_z[rest : 2 * rest], "y", 1)
+    r2 = shift(by_z[2 * rest : 3 * rest], "y", 2)
+    r3 = shift(by_z[3 * rest :], "y", -1)
+    out_z = by_z[:rest] + r1 + r2 + r3
+    return jnp.concatenate([out_y, out_z], axis=0)
 
 
 def shards(
@@ -197,10 +261,8 @@
 ):
     n_rank = lax.axis_size("rk")
     rank_index = lax.axis_index("rk")
-    n_z = lax.axis_size("z")
-    n_core = lax.axis_size("core")
+    n_y, n_z, n_core = (lax.axis_size(axis) for axis in ("y", "z", "core"))
     core = lax.axis_index("core")
-    n_clu = lax.axis_size("y") * n_z * n_core
     local = jnp.swapaxes(bases[0], 1, 2)
     leaves, width, points = local.shape
     full_rank = width * n_rank
@@ -208,21 +270,23 @@
 
     blocks = coupling[0]
     listed = blocks.shape[1]
-    half = (n_clu // n_core) * leaves
+    plan = Plan(n_y, n_z, leaves)
     dest = row_device[0, :, :, 0]
     valid = jnp.arange(listed, dtype=jnp.int32)[None, :] < block_count[0][:, None]
-    own = (dest % n_core) == core
-    place = jnp.where(own, half, 0) + (dest // n_core) * leaves + row_slot[0]
-    place = jnp.where(valid, place, n_core * half).reshape(-1).astype(jnp.int32)
+    rel_z = (dest // n_core - lax.axis_index("z")) % n_z
+    rel_y = (dest // (n_core * n_z) - lax.axis_index("y")) % n_y
+    place = plan.rows(rel_y, rel_z, row_slot[0])
+    place = place + jnp.where(dest % n_core == core, plan.total, 0)
+    place = jnp.where(valid, place, 2 * plan.total).reshape(-1).astype(jnp.int32)
 
     pieces = lax.all_to_all(local, "rk", split_axis=0, concat_axis=0, tiled=True)
     gram, mine = leaf_factors(pieces.reshape(n_rank, share, width, points))
     packed = lax.all_gather(mine, "rk", axis=0, tiled=True)
 
-    away, keep = weighted_sums(place, blocks, packed, half)
-    dense = keep + swap(away, "core", 1)
-    dense = lax.psum_scatter(dense, "y", scatter_dimension=0, tiled=True)
-    gathered = lax.psum_scatter(dense, "z", scatter_dimension=0, tiled=True)
+    first, second, keep = weighted_sums(place, blocks, packed, plan.near, plan.total)
+    first = swap(first, "core", 1)
+    second = swap(second, "core", 1)
+    gathered = sum_over_grid(plan, keep, first, second)
 
     lower = jnp.concatenate([packed[:, :, :full_rank], packed[:, :, full_rank:]], axis=1)
     gathered = gathered.reshape(leaves, width // 2, 2, full_rank)

time: 180 us -> 169 us (0.939)
  waiting for transfers between devices: 96.6 us -> 53.2 us
  starting transfers between devices: 14.3 us -> 51.2 us
  between operations: 14.2 us -> 0.96 us
  local copies, waits for them, and re-layouts: 5.82 us -> 10.3 us
  Pallas kernels: 22.3 us -> 26.2 us
    reduce_scatter x2 -> x0, waiting for transfers between devices: 64.9 us -> none  [the longest x1 40 us: shards(): dense = lax.psum_scatter(dense, 'y', scatter_dimension=0, tiled=True)]
    ppermute x0 -> x17, starting transfers between devices: none -> 37.8 us  [shift(): lax.ppermute(value, axis, [(i, (i + step) % size) for i in range(size)])]
    ppermute x0 -> x17, waiting for transfers between devices: none -> 34.8 us  [shift(): lax.ppermute(value, axis, [(i, (i + step) % size) for i in range(size)])]
    ppermute x6 -> x7, waiting for transfers between devices: 20.5 us -> 7.31 us  [swap(): lax.ppermute(value, axis, [(i, i ^ mask) for i in range(lax.axis_size(axi...]
    unnamed x13 -> x23, local copies, waits for them, and re-layouts: 2.28 us -> 7.65 us
    pallas_call x1, Pallas kernels: 13.3 us -> 17.2 us  [weighted_sums(): pl.pallas_call(functools.partial(product_kernel, near, away), in_specs=[p...]
    add x1 -> x7, other arithmetic: 4.56 us -> 5.31 us  [the longest x1 1.67 us: sum_over_grid(): by_y = part('y0') + y_far + y_up + y_down]
    ppermute x6 -> x7, starting transfers between devices: 5.53 us -> 5.63 us  [swap(): lax.ppermute(value, axis, [(i, i ^ mask) for i in range(lax.axis_size(axi...]
  transfers between devices with their start and end apart: 10 -> 26, of which waited for: 10 -> 12; matrix products, arithmetic and copies ran while one was open for 4% -> 8% of each run, Pallas kernels for 2% -> 2%
where the time goes in v2:
time: 169 us; the launch traced here: 168 us
  waiting for transfers between devices  53.2 us (31%)
  starting transfers between devices  51.2 us (30%)
  Pallas kernels  26.2 us (16%)
  blocking collectives  12.9 us (8%)
  local copies, waits for them, and re-layouts  10.3 us (6%)
  other arithmetic  9.3 us (6%)
  matrix products  4.15 us (2%)
    ppermute x17, starting transfers between devices, shift(): lax.ppermute(value, axis, [(i, (i + step) % size) for i in range(size)])  37.8 us
    ppermute x17, waiting for transfers between devices, shift(): lax.ppermute(value, axis, [(i, (i + step) % size) for i in range(size)])  34.8 us
    pallas_call x1, Pallas kernels, weighted_sums(): pl.pallas_call(functools.partial(product_kernel, near, away), in_specs=[p...  17.2 us
    all_gather x1, blocking collectives, shards(): packed = lax.all_gather(mine, 'rk', axis=0, tiled=True)  12.9 us
    unnamed x23, local copies, waits for them, and re-layouts  7.65 us
    ppermute x7, waiting for transfers between devices, swap(): lax.ppermute(value, axis, [(i, i ^ mask) for i in range(lax.axis_size(axi...  7.31 us
    all_to_all x1, waiting for transfers between devices, shards(): lax.all_to_all(local, 'rk', split_axis=0, concat_axis=0, tiled=True)  5.84 us
    ppermute x7, starting transfers between devices, swap(): lax.ppermute(value, axis, [(i, i ^ mask) for i in range(lax.axis_size(axi...  5.63 us
  transfers between devices with their start and end apart: 26, of which 12 were waited for; matrix products, arithmetic and copies ran while one was open for 8% of the time, Pallas kernels for 2%

profile of v2, /device:TPU:32, one launch (start us, length us, event | category | flops | bytes accessed | tf_op | source)
XLA Modules:
  0.0 168.2 jit_solution(16956336417486849137)
XLA Ops:
  0.6 4.4 %all-to-all-start = ((f32[32,16,256]{2,1,0:T(8,128)}), f32[32,16,256]{2,1,0:T(8,128)S(1)}, u32[]{:S(2)}, u32[]{:S(2)}) async-start(f32[32,16,256]{2,1,0:T(8,128)} %bitcast.80), calls=%async_computation | async-start | bytes 1048576 | tf_op jit(solution)/shard_map/all_to_all | solution.py:282
  5.6 1.4 reduce.3
  7.1 0.7 iota_compare_fusion
  7.9 0.8 squeeze.26
  8.7 5.8 %all-to-all-done = f32[32,16,256]{2,1,0:T(8,128)S(1)} async-done(((f32[32,16,256]{2,1,0:T(8,128)}), f32[32,16,256]{2,1,0:T(8,128)S(1)}, u32[]{:S(2)}, u32[]{:S(2)}) %all-to-all-start) | async-done | bytes 524320 | tf_op jit(solution)/shard_map/all_to_all | solution.py:282
  14.6 4.9 %leaf_factors.1 = (f32[8,64,64]{2,1,0:T(8,128)S(1)}, f32[8,32,128]{2,1,0:T(8,128)S(1)}) custom-call(f32[4,8,16,256]{3,2,1,0:T(8,128)S(1)} %bitcast.77), custom_call_target="tpu_custom_call" | custom-call | tf_op jit(solution)/shard_map/leaf_factors/pallas_call | solution.py:85
  19.5 12.9 %all_gather.3.l_ref = f32[32,32,128]{2,1,0:T(8,128)S(1)} all-gather(f32[8,32,128]{2,1,0:T(8,128)S(1)} %get-tuple-element.8), channel_id=1, replica_groups=mesh['y'=4,'z'=8,'core'=2,'rk'=4] {'rk'}, dimensions={0}, use_global_device_ids=true | all-gather | bytes 655360 | tf_op jit(solution)/shard_map/all_gather | solution.py:284
  32.4 3.4 %copy-done.1 = f32[1,32,32,16,64]{4,3,2,1,0:T(8,128)S(1)} copy-done((f32[1,32,32,16,64]{4,3,2,1,0:T(8,128)S(1)}, f32[1,32,32,16,64]{4,3,2,1,0:T(8,128)}, u32[]{:S(2)}) %copy-start.1) | copy-done | bytes 4194328
  35.7 17.2 %weighted_sums.1 = (f32[192,8,128]{2,1,0:T(8,128)S(1)}, f32[832,8,128]{2,1,0:T(8,128)}, f32[1024,8,128]{2,1,0:T(8,128)S(1)}) custom-call(s32[1024]{0:T(1024)S(1)} %add_select_fusion.5.place_ref, f32[32,32,16,64]{3,2,1,0:T(8,128)S(1)} %bitcast.76, f32[32,32,128]{2,1,0:T(8,128)S(1)} %all_gather.3.l_ref), custom_call_target="tpu_custom_call" | custom-call | tf_op jit(solution)/shard_map/weighted_sums/pallas_call | solution.py:172
  52.9 2.0 %copy-done.2 = f32[1024,8,128]{2,1,0:T(8,128)} copy-done((f32[1024,8,128]{2,1,0:T(8,128)}, f32[1024,8,128]{2,1,0:T(8,128)S(1)}, u32[]{:S(2)}) %copy-start.2) | copy-done | bytes 4194328
  54.9 0.6 convolution_bitcast_fusion
  55.5 0.6 convolution_bitcast_fusion.5
  56.1 0.5 collective-permute-start
  57.2 2.9 %collective-permute-done = f32[64,64]{1,0:T(8,128)S(1)} collective-permute-done((f32[64,64]{1,0:T(8,128)S(1)}, f32[64,64]{1,0:T(8,128)S(1)}, u32[]{:S(2)}, u32[]{:S(2)}) %collective-permute-start) | collective-permute-done | bytes 16416 | tf_op jit(solution)/shard_map/ppermute | solution.py:23
  60.1 1.5 collective-permute-start.1
  61.6 0.8 fusion.4
  62.4 3.2 %collective-permute-done.1 = f32[64,64]{1,0:T(8,128)S(1)} collective-permute-done((f32[64,64]{1,0:T(8,128)S(1)}, f32[64,64]{1,0:T(8,128)S(1)}, u32[]{:S(2)}, u32[]{:S(2)}) %collective-permute-start.1) | collective-permute-done | bytes 16416 | tf_op jit(solution)/shard_map/ppermute | solution.py:23
  66.1 1.2 collective-permute-done.2
  67.8 1.4 slice_add_fusion.3
  69.3 3.5 %collective-permute-start.7 = (f32[128,8,128]{2,1,0:T(8,128)S(1)}, f32[128,8,128]{2,1,0:T(8,128)S(1)}, u32[]{:S(2)}, u32[]{:S(2)}) collective-permute-start(f32[128,8,128]{2,1,0:T(8,128)S(1)} %get-tuple-element.34), channel_id=1, source_target_pairs={{0,128},{64,192},{128,0},{192,64},{1,129},{65,193},{129,1},{193,65... | collective-permute-start | bytes 1572872 | tf_op jit(solution)/shard_map/ppermute | solution.py:19
  73.3 2.7 %collective-permute-start.9 = (f32[128,8,128]{2,1,0:T(8,128)S(1)}, f32[128,8,128]{2,1,0:T(8,128)S(1)}, u32[]{:S(2)}, u32[]{:S(2)}) collective-permute-start(f32[128,8,128]{2,1,0:T(8,128)S(1)} %get-tuple-element.29), channel_id=1, source_target_pairs={{0,192},{64,0},{128,64},{192,128},{1,193},{65,1},{129,65},{193,129... | collective-permute-start | bytes 1572872 | tf_op jit(solution)/shard_map/ppermute | solution.py:19
  76.5 3.1 %collective-permute-start.4 = (f32[64,64]{1,0:T(8,128)S(1)}, f32[64,64]{1,0:T(8,128)S(1)}, u32[]{:S(2)}, u32[]{:S(2)}) collective-permute-start(f32[64,64]{1,0:T(8,128)S(1)} %convolution_bitcast_fusion.2), channel_id=1, source_target_pairs={{0,16},{8,24},{16,0},{24,8},{32,48},{40,56},{48,32},{56,40},{1,17}... | collective-permute-start | bytes 49160 | tf_op jit(solution)/shard_map/ppermute | solution.py:23
  79.6 6.1 %collective-permute-done.7 = f32[128,8,128]{2,1,0:T(8,128)S(1)} collective-permute-done((f32[128,8,128]{2,1,0:T(8,128)S(1)}, f32[128,8,128]{2,1,0:T(8,128)S(1)}, u32[]{:S(2)}, u32[]{:S(2)}) %collective-permute-start.7) | collective-permute-done | bytes 524320 | tf_op jit(solution)/shard_map/ppermute | solution.py:19
  85.7 10.4 %collective-permute-done.8 = f32[128,8,128]{2,1,0:T(8,128)S(1)} collective-permute-done((f32[128,8,128]{2,1,0:T(8,128)S(1)}, f32[128,8,128]{2,1,0:T(8,128)S(1)}, u32[]{:S(2)}, u32[]{:S(2)}) %collective-permute-start.8) | collective-permute-done | bytes 524320 | tf_op jit(solution)/shard_map/ppermute | solution.py:19
  96.5 1.7 fusion.2
  98.2 3.5 %collective-permute-start.15 = (f32[128,8,128]{2,1,0:T(8,128)S(1)}, f32[128,8,128]{2,1,0:T(8,128)S(1)}, u32[]{:S(2)}, u32[]{:S(2)}) collective-permute-start(f32[128,8,128]{2,1,0:T(8,128)S(1)} %get-tuple-element.27), channel_id=1, source_target_pairs={{0,8},{8,16},{16,24},{24,32},{32,40},{40,48},{48,56},{56,0},{1,9},... | collective-permute-start | bytes 1572872 | tf_op jit(solution)/shard_map/ppermute | solution.py:19
  101.8 3.6 %collective-permute-start.17 = (f32[32,8,128]{2,1,0:T(8,128)S(1)}, f32[32,8,128]{2,1,0:T(8,128)S(1)}, u32[]{:S(2)}, u32[]{:S(2)}) collective-permute-start(f32[32,8,128]{2,1,0:T(8,128)S(1)} %get-tuple-element.32), channel_id=1, source_target_pairs={{0,16},{8,24},{16,32},{24,40},{32,48},{40,56},{48,0},{56,8},{1,17}... | collective-permute-start | bytes 393224 | tf_op jit(solution)/shard_map/ppermute | solution.py:19
  105.4 1.4 collective-permute-start.19
  106.8 1.9 %collective-permute-start.10 = (f32[32,8,128]{2,1,0:T(8,128)S(1)}, f32[32,8,128]{2,1,0:T(8,128)S(1)}, u32[]{:S(2)}, u32[]{:S(2)}) collective-permute-start(f32[32,8,128]{2,1,0:T(8,128)S(1)} %get-tuple-element.38), channel_id=1, source_target_pairs={{0,8},{8,16},{16,24},{24,32},{32,40},{40,48},{48,56},{56,0},{1,9},... | collective-permute-start | bytes 393224 | tf_op jit(solution)/shard_map/ppermute | solution.py:19
  108.7 13.9 %collective-permute-done.17 = f32[32,8,128]{2,1,0:T(8,128)S(1)} collective-permute-done((f32[32,8,128]{2,1,0:T(8,128)S(1)}, f32[32,8,128]{2,1,0:T(8,128)S(1)}, u32[]{:S(2)}, u32[]{:S(2)}) %collective-permute-start.17) | collective-permute-done | bytes 131104 | tf_op jit(solution)/shard_map/ppermute | solution.py:19
  122.6 1.7 %collective-permute-start.11 = (f32[32,8,128]{2,1,0:T(8,128)S(1)}, f32[32,8,128]{2,1,0:T(8,128)S(1)}, u32[]{:S(2)}, u32[]{:S(2)}) collective-permute-start(f32[32,8,128]{2,1,0:T(8,128)S(1)} %get-tuple-element.39), channel_id=1, source_target_pairs={{0,56},{8,0},{16,8},{24,16},{32,24},{40,32},{48,40},{56,48},{1,57}... | collective-permute-start | bytes 393224 | tf_op jit(solution)/shard_map/ppermute | solution.py:19
  124.3 1.1 fusion.6
  125.5 4.1 %collective-permute-start.20 = (f32[64,8,128]{2,1,0:T(8,128)S(1)}, f32[64,8,128]{2,1,0:T(8,128)S(1)}, u32[]{:S(2)}, u32[]{:S(2)}) collective-permute-start(f32[64,8,128]{2,1,0:T(8,128)S(1)} %get-tuple-element.31), channel_id=1, source_target_pairs={{0,48},{8,56},{16,0},{24,8},{32,16},{40,24},{48,32},{56,40},{1,49}... | collective-permute-start | bytes 786440 | tf_op jit(solution)/shard_map/ppermute | solution.py:19
  129.6 4.1 %node_factors.1 = f32[4,64,64]{2,1,0:T(8,128)S(1)} custom-call(f32[4,64,64]{2,1,0:T(8,128)S(1)} %pad_maximum_fusion.2.g_ref), custom_call_target="tpu_custom_call" | custom-call | tf_op jit(solution)/shard_map/node_factors/pallas_call | solution.py:107
  133.8 5.8 %collective-permute-start.12 = (f32[16,8,128]{2,1,0:T(8,128)S(1)}, f32[16,8,128]{2,1,0:T(8,128)S(1)}, u32[]{:S(2)}, u32[]{:S(2)}) collective-permute-start(f32[16,8,128]{2,1,0:T(8,128)S(1)} %get-tuple-element.35), channel_id=1, source_target_pairs={{0,32},{8,40},{16,48},{24,56},{32,0},{40,8},{48,16},{56,24},{1,33}... | collective-permute-start | bytes 196616 | tf_op jit(solution)/shard_map/ppermute | solution.py:19
  139.6 4.1 %collective-permute-start.14 = (f32[16,8,128]{2,1,0:T(8,128)S(1)}, f32[16,8,128]{2,1,0:T(8,128)S(1)}, u32[]{:S(2)}, u32[]{:S(2)}) collective-permute-start(f32[16,8,128]{2,1,0:T(8,128)S(1)} %get-tuple-element.36), channel_id=1, source_target_pairs={{0,48},{8,56},{16,0},{24,8},{32,16},{40,24},{48,32},{56,40},{1,49}... | collective-permute-start | bytes 196616 | tf_op jit(solution)/shard_map/ppermute | solution.py:19
  143.7 1.0 fusion.8
  144.8 1.5 collective-permute-start.21
  146.3 2.9 %collective-permute-start.22 = (f32[16,8,128]{2,1,0:T(8,128)S(1)}, f32[16,8,128]{2,1,0:T(8,128)S(1)}, u32[]{:S(2)}, u32[]{:S(2)}) collective-permute-start(f32[16,8,128]{2,1,0:T(8,128)S(1)} %get-tuple-element.44), channel_id=1, source_target_pairs={{0,128},{64,192},{128,0},{192,64},{1,129},{65,193},{129,1},{193,65... | collective-permute-start | bytes 196616 | tf_op jit(solution)/shard_map/ppermute | solution.py:19
  149.6 0.8 collective-permute-done.21
  150.3 1.8 %collective-permute-done.22 = f32[16,8,128]{2,1,0:T(8,128)S(1)} collective-permute-done((f32[16,8,128]{2,1,0:T(8,128)S(1)}, f32[16,8,128]{2,1,0:T(8,128)S(1)}, u32[]{:S(2)}, u32[]{:S(2)}) %collective-permute-start.22) | collective-permute-done | bytes 65568 | tf_op jit(solution)/shard_map/ppermute | solution.py:19
  152.1 1.3 collective-permute-done.23
  154.1 0.9 reshape.36
  155.0 3.3 %all-to-all-start.1 = ((f32[4,1,8192]{2,1,0:T(1,128)}), f32[4,1,8192]{2,1,0:T(1,128)S(1)}, u32[]{:S(2)}, u32[]{:S(2)}) async-start(f32[4,1,8192]{2,1,0:T(1,128)} %reshape.36), calls=%async_computation.1 | async-start | bytes 262144 | tf_op jit(solution)/shard_map/all_to_all | solution.py:294
  158.3 0.6 dynamic-slice_bitcast_fusion
  158.9 5.3 %all-to-all-done.1 = f32[4,1,8192]{2,1,0:T(1,128)S(1)} async-done(((f32[4,1,8192]{2,1,0:T(1,128)}), f32[4,1,8192]{2,1,0:T(1,128)S(1)}, u32[]{:S(2)}, u32[]{:S(2)}) %all-to-all-start.1) | async-done | bytes 131104 | tf_op jit(solution)/shard_map/all_to_all | solution.py:294
  164.8 1.0 reduce.4
  166.4 1.8 %convolution_bitcast_fusion.1 = f32[1,32,64,16]{2,3,1,0:T(8,128)} fusion(f32[32,64,16]{1,2,0:T(8,128)S(1)} %copy.46, f32[32,32,64]{2,1,0:T(8,128)S(1)} %get-tuple-element.40, f32[32,32,64]{2,1,0:T(8,128)S(1)} %copy-done.5), kind=kOutput, calls=%fused_computation.4 | convolution fusion | flops 25296896 | bytes 786432 | tf_op jit(solution)/shard_map/jbe,jba->jea/dot_general | solution.py:295
  (71 shorter events, 5.9 us)
Async XLA Ops:
  0.6 54.3 %copy-start = (f32[1,32,64,64]{3,2,1,0:T(8,128)S(1)}, f32[1,32,64,64]{3,2,1,0:T(8,128)}, u32[]{:S(2)}) copy-start(f32[1,32,64,64]{3,2,1,0:T(8,128)} %param.10) | copy-start | bytes 1572868
  0.6 13.9 %all-to-all-start = ((f32[32,16,256]{2,1,0:T(8,128)}), f32[32,16,256]{2,1,0:T(8,128)S(1)}, u32[]{:S(2)}, u32[]{:S(2)}) async-start(f32[32,16,256]{2,1,0:T(8,128)} %bitcast.80), calls=%async_computation | async-start | bytes 1048576 | tf_op jit(solution)/shard_map/all_to_all | solution.py:282
  32.4 3.4 %copy-start.1 = (f32[1,32,32,16,64]{4,3,2,1,0:T(8,128)S(1)}, f32[1,32,32,16,64]{4,3,2,1,0:T(8,128)}, u32[]{:S(2)}) copy-start(f32[1,32,32,16,64]{4,3,2,1,0:T(8,128)} %param.14) | copy-start | bytes 12582916
  52.9 2.0 %copy-start.2 = (f32[1024,8,128]{2,1,0:T(8,128)}, f32[1024,8,128]{2,1,0:T(8,128)S(1)}, u32[]{:S(2)}) copy-start(f32[1024,8,128]{2,1,0:T(8,128)S(1)} %get-tuple-element.10) | copy-start | bytes 12582916
  54.9 10.7 %copy-start.6 = (f32[1,64,64]{2,1,0:T(8,128)S(1)}, f32[1,64,64]{2,1,0:T(8,128)}, u32[]{:S(2)}) copy-start(f32[1,64,64]{2,1,0:T(8,128)} %param.11) | copy-start | bytes 49156
  54.9 12.4 %copy-start.7 = (f32[1,64,64]{2,1,0:T(8,128)S(1)}, f32[1,64,64]{2,1,0:T(8,128)}, u32[]{:S(2)}) copy-start(f32[1,64,64]{2,1,0:T(8,128)} %param.12) | copy-start | bytes 49156
  54.9 12.9 %collective-permute-start.5 = (f32[832,8,128]{2,1,0:T(8,128)}, f32[832,8,128]{2,1,0:T(8,128)}, u32[]{:S(2)}, u32[]{:S(2)}) collective-permute-start(f32[832,8,128]{2,1,0:T(8,128)} %get-tuple-element.11), channel_id=1, source_target_pairs={{0,4},{4,0},{1,5},{5,1},{2,6},{6,2},{3,7},{7,3},{8,12},{12,8},{9,1... | collective-permute-start | bytes 10223624 | tf_op jit(solution)/shard_map/ppermute | solution.py:23
  54.9 12.9 %copy-start.3 = (f32[1024,8,128]{2,1,0:T(8,128)S(1)}, f32[1024,8,128]{2,1,0:T(8,128)}, u32[]{:S(2)}) copy-start(f32[1024,8,128]{2,1,0:T(8,128)} %copy-done.2) | copy-start | bytes 12582916
  56.1 19.9 %copy-start.8 = (f32[1,64,64]{2,1,0:T(8,128)S(1)}, f32[1,64,64]{2,1,0:T(8,128)}, u32[]{:S(2)}) copy-start(f32[1,64,64]{2,1,0:T(8,128)} %param.13) | copy-start | bytes 49156
  56.1 4.0 %collective-permute-start = (f32[64,64]{1,0:T(8,128)S(1)}, f32[64,64]{1,0:T(8,128)S(1)}, u32[]{:S(2)}, u32[]{:S(2)}) collective-permute-start(f32[64,64]{1,0:T(8,128)S(1)} %convolution_bitcast_fusion.5), channel_id=1, source_target_pairs={{0,1},{1,0},{2,3},{3,2},{4,5},{5,4},{6,7},{7,6},{8,9},{9,8},{10,11... | collective-permute-start | bytes 49160 | tf_op jit(solution)/shard_map/ppermute | solution.py:23
  56.9 10.9 %copy-start.4 = (f32[32,32,64]{2,1,0:T(8,128)}, f32[32,32,64]{2,1,0:T(8,128)S(1)}, u32[]{:S(2)}) copy-start(f32[32,32,64]{2,1,0:T(8,128)S(1)} %get-tuple-element.41) | copy-start | bytes 786436
  56.9 10.9 %collective-permute-start.6 = (f32[192,8,128]{2,1,0:T(8,128)S(1)}, f32[192,8,128]{2,1,0:T(8,128)S(1)}, u32[]{:S(2)}, u32[]{:S(2)}) collective-permute-start(f32[192,8,128]{2,1,0:T(8,128)S(1)} %get-tuple-element.12), channel_id=1, source_target_pairs={{0,4},{4,0},{1,5},{5,1},{2,6},{6,2},{3,7},{7,3},{8,12},{12,8},{9,1... | collective-permute-start | bytes 2359304 | tf_op jit(solution)/shard_map/ppermute | solution.py:23
  60.1 5.4 %collective-permute-start.1 = (f32[64,64]{1,0:T(8,128)S(1)}, f32[64,64]{1,0:T(8,128)S(1)}, u32[]{:S(2)}, u32[]{:S(2)}) collective-permute-start(f32[64,64]{1,0:T(8,128)S(1)} %add.229), channel_id=1, source_target_pairs={{0,2},{1,3},{2,0},{3,1},{4,6},{5,7},{6,4},{7,5},{8,10},{9,11},{10,... | collective-permute-start | bytes 49160 | tf_op jit(solution)/shard_map/ppermute | solution.py:23
  66.0 1.3 collective-permute-start.2
  67.7 8.4 %collective-permute-start.3 = (f32[64,64]{1,0:T(8,128)S(1)}, f32[64,64]{1,0:T(8,128)S(1)}, u32[]{:S(2)}, u32[]{:S(2)}) collective-permute-start(f32[64,64]{1,0:T(8,128)S(1)} %convolution_bitcast_fusion.3), channel_id=1, source_target_pairs={{0,8},{8,0},{16,24},{24,16},{32,40},{40,32},{48,56},{56,48},{1,9},... | collective-permute-start | bytes 49160 | tf_op jit(solution)/shard_map/ppermute | solution.py:23
  69.3 16.4 %collective-permute-start.7 = (f32[128,8,128]{2,1,0:T(8,128)S(1)}, f32[128,8,128]{2,1,0:T(8,128)S(1)}, u32[]{:S(2)}, u32[]{:S(2)}) collective-permute-start(f32[128,8,128]{2,1,0:T(8,128)S(1)} %get-tuple-element.34), channel_id=1, source_target_pairs={{0,128},{64,192},{128,0},{192,64},{1,129},{65,193},{129,1},{193,65... | collective-permute-start | bytes 1572872 | tf_op jit(solution)/shard_map/ppermute | solution.py:19
  72.8 23.3 %collective-permute-start.8 = (f32[128,8,128]{2,1,0:T(8,128)S(1)}, f32[128,8,128]{2,1,0:T(8,128)S(1)}, u32[]{:S(2)}, u32[]{:S(2)}) collective-permute-start(f32[128,8,128]{2,1,0:T(8,128)S(1)} %get-tuple-element.28), channel_id=1, source_target_pairs={{0,64},{64,128},{128,192},{192,0},{1,65},{65,129},{129,193},{193,1... | collective-permute-start | bytes 1572872 | tf_op jit(solution)/shard_map/ppermute | solution.py:19
  73.3 23.2 %collective-permute-start.9 = (f32[128,8,128]{2,1,0:T(8,128)S(1)}, f32[128,8,128]{2,1,0:T(8,128)S(1)}, u32[]{:S(2)}, u32[]{:S(2)}) collective-permute-start(f32[128,8,128]{2,1,0:T(8,128)S(1)} %get-tuple-element.29), channel_id=1, source_target_pairs={{0,192},{64,0},{128,64},{192,128},{1,193},{65,1},{129,65},{193,129... | collective-permute-start | bytes 1572872 | tf_op jit(solution)/shard_map/ppermute | solution.py:19
  76.5 25.3 %collective-permute-start.4 = (f32[64,64]{1,0:T(8,128)S(1)}, f32[64,64]{1,0:T(8,128)S(1)}, u32[]{:S(2)}, u32[]{:S(2)}) collective-permute-start(f32[64,64]{1,0:T(8,128)S(1)} %convolution_bitcast_fusion.2), channel_id=1, source_target_pairs={{0,16},{8,24},{16,0},{24,8},{32,48},{40,56},{48,32},{56,40},{1,17}... | collective-permute-start | bytes 49160 | tf_op jit(solution)/shard_map/ppermute | solution.py:23
  98.2 26.1 %collective-permute-start.15 = (f32[128,8,128]{2,1,0:T(8,128)S(1)}, f32[128,8,128]{2,1,0:T(8,128)S(1)}, u32[]{:S(2)}, u32[]{:S(2)}) collective-permute-start(f32[128,8,128]{2,1,0:T(8,128)S(1)} %get-tuple-element.27), channel_id=1, source_target_pairs={{0,8},{8,16},{16,24},{24,32},{32,40},{40,48},{48,56},{56,0},{1,9},... | collective-permute-start | bytes 1572872 | tf_op jit(solution)/shard_map/ppermute | solution.py:19
  101.7 22.6 %collective-permute-start.16 = (f32[128,8,128]{2,1,0:T(8,128)S(1)}, f32[128,8,128]{2,1,0:T(8,128)S(1)}, u32[]{:S(2)}, u32[]{:S(2)}) collective-permute-start(f32[128,8,128]{2,1,0:T(8,128)S(1)} %get-tuple-element.26), channel_id=1, source_target_pairs={{0,56},{8,0},{16,8},{24,16},{32,24},{40,32},{48,40},{56,48},{1,57}... | collective-permute-start | bytes 1572872 | tf_op jit(solution)/shard_map/ppermute | solution.py:19
  101.8 20.8 %collective-permute-start.17 = (f32[32,8,128]{2,1,0:T(8,128)S(1)}, f32[32,8,128]{2,1,0:T(8,128)S(1)}, u32[]{:S(2)}, u32[]{:S(2)}) collective-permute-start(f32[32,8,128]{2,1,0:T(8,128)S(1)} %get-tuple-element.32), channel_id=1, source_target_pairs={{0,16},{8,24},{16,32},{24,40},{32,48},{40,56},{48,0},{56,8},{1,17}... | collective-permute-start | bytes 393224 | tf_op jit(solution)/shard_map/ppermute | solution.py:19
  105.4 18.9 %collective-permute-start.19 = (f32[32,8,128]{2,1,0:T(8,128)S(1)}, f32[32,8,128]{2,1,0:T(8,128)S(1)}, u32[]{:S(2)}, u32[]{:S(2)}) collective-permute-start(f32[32,8,128]{2,1,0:T(8,128)S(1)} %get-tuple-element.33), channel_id=1, source_target_pairs={{0,48},{8,56},{16,0},{24,8},{32,16},{40,24},{48,32},{56,40},{1,49}... | collective-permute-start | bytes 393224 | tf_op jit(solution)/shard_map/ppermute | solution.py:19
  106.8 26.9 %collective-permute-start.10 = (f32[32,8,128]{2,1,0:T(8,128)S(1)}, f32[32,8,128]{2,1,0:T(8,128)S(1)}, u32[]{:S(2)}, u32[]{:S(2)}) collective-permute-start(f32[32,8,128]{2,1,0:T(8,128)S(1)} %get-tuple-element.38), channel_id=1, source_target_pairs={{0,8},{8,16},{16,24},{24,32},{32,40},{40,48},{48,56},{56,0},{1,9},... | collective-permute-start | bytes 393224 | tf_op jit(solution)/shard_map/ppermute | solution.py:19
  122.6 11.2 %collective-permute-start.11 = (f32[32,8,128]{2,1,0:T(8,128)S(1)}, f32[32,8,128]{2,1,0:T(8,128)S(1)}, u32[]{:S(2)}, u32[]{:S(2)}) collective-permute-start(f32[32,8,128]{2,1,0:T(8,128)S(1)} %get-tuple-element.39), channel_id=1, source_target_pairs={{0,56},{8,0},{16,8},{24,16},{32,24},{40,32},{48,40},{56,48},{1,57}... | collective-permute-start | bytes 393224 | tf_op jit(solution)/shard_map/ppermute | solution.py:19
  125.4 18.3 %collective-permute-start.18 = (f32[64,8,128]{2,1,0:T(8,128)S(1)}, f32[64,8,128]{2,1,0:T(8,128)S(1)}, u32[]{:S(2)}, u32[]{:S(2)}) collective-permute-start(f32[64,8,128]{2,1,0:T(8,128)S(1)} %get-tuple-element.30), channel_id=1, source_target_pairs={{0,16},{8,24},{16,32},{24,40},{32,48},{40,56},{48,0},{56,8},{1,17}... | collective-permute-start | bytes 786440 | tf_op jit(solution)/shard_map/ppermute | solution.py:19
  125.5 18.2 %collective-permute-start.20 = (f32[64,8,128]{2,1,0:T(8,128)S(1)}, f32[64,8,128]{2,1,0:T(8,128)S(1)}, u32[]{:S(2)}, u32[]{:S(2)}) collective-permute-start(f32[64,8,128]{2,1,0:T(8,128)S(1)} %get-tuple-element.31), channel_id=1, source_target_pairs={{0,48},{8,56},{16,0},{24,8},{32,16},{40,24},{48,32},{56,40},{1,49}... | collective-permute-start | bytes 786440 | tf_op jit(solution)/shard_map/ppermute | solution.py:19
  133.8 15.4 %collective-permute-start.12 = (f32[16,8,128]{2,1,0:T(8,128)S(1)}, f32[16,8,128]{2,1,0:T(8,128)S(1)}, u32[]{:S(2)}, u32[]{:S(2)}) collective-permute-start(f32[16,8,128]{2,1,0:T(8,128)S(1)} %get-tuple-element.35), channel_id=1, source_target_pairs={{0,32},{8,40},{16,48},{24,56},{32,0},{40,8},{48,16},{56,24},{1,33}... | collective-permute-start | bytes 196616 | tf_op jit(solution)/shard_map/ppermute | solution.py:19
  139.6 10.0 %collective-permute-start.13 = (f32[16,8,128]{2,1,0:T(8,128)S(1)}, f32[16,8,128]{2,1,0:T(8,128)S(1)}, u32[]{:S(2)}, u32[]{:S(2)}) collective-permute-start(f32[16,8,128]{2,1,0:T(8,128)S(1)} %get-tuple-element.37), channel_id=1, source_target_pairs={{0,16},{8,24},{16,32},{24,40},{32,48},{40,56},{48,0},{56,8},{1,17}... | collective-permute-start | bytes 196616 | tf_op jit(solution)/shard_map/ppermute | solution.py:19
  139.6 26.9 %copy-start.5 = (f32[32,32,64]{2,1,0:T(8,128)S(1)}, f32[32,32,64]{2,1,0:T(8,128)}, u32[]{:S(2)}) copy-start(f32[32,32,64]{2,1,0:T(8,128)} %copy-done.4) | copy-start | bytes 786436
  139.6 10.0 %collective-permute-start.14 = (f32[16,8,128]{2,1,0:T(8,128)S(1)}, f32[16,8,128]{2,1,0:T(8,128)S(1)}, u32[]{:S(2)}, u32[]{:S(2)}) collective-permute-start(f32[16,8,128]{2,1,0:T(8,128)S(1)} %get-tuple-element.36), channel_id=1, source_target_pairs={{0,48},{8,56},{16,0},{24,8},{32,16},{40,24},{48,32},{56,40},{1,49}... | collective-permute-start | bytes 196616 | tf_op jit(solution)/shard_map/ppermute | solution.py:19
  144.8 5.6 %collective-permute-start.21 = (f32[16,8,128]{2,1,0:T(8,128)S(1)}, f32[16,8,128]{2,1,0:T(8,128)S(1)}, u32[]{:S(2)}, u32[]{:S(2)}) collective-permute-start(f32[16,8,128]{2,1,0:T(8,128)S(1)} %get-tuple-element.42), channel_id=1, source_target_pairs={{0,64},{64,128},{128,192},{192,0},{1,65},{65,129},{129,193},{193,1... | collective-permute-start | bytes 196616 | tf_op jit(solution)/shard_map/ppermute | solution.py:19
  146.3 5.9 %collective-permute-start.22 = (f32[16,8,128]{2,1,0:T(8,128)S(1)}, f32[16,8,128]{2,1,0:T(8,128)S(1)}, u32[]{:S(2)}, u32[]{:S(2)}) collective-permute-start(f32[16,8,128]{2,1,0:T(8,128)S(1)} %get-tuple-element.44), channel_id=1, source_target_pairs={{0,128},{64,192},{128,0},{192,64},{1,129},{65,193},{129,1},{193,65... | collective-permute-start | bytes 196616 | tf_op jit(solution)/shard_map/ppermute | solution.py:19
  149.2 4.3 %collective-permute-start.23 = (f32[16,8,128]{2,1,0:T(8,128)S(1)}, f32[16,8,128]{2,1,0:T(8,128)S(1)}, u32[]{:S(2)}, u32[]{:S(2)}) collective-permute-start(f32[16,8,128]{2,1,0:T(8,128)S(1)} %get-tuple-element.43), channel_id=1, source_target_pairs={{0,192},{64,0},{128,64},{192,128},{1,193},{65,1},{129,65},{193,129... | collective-permute-start | bytes 196616 | tf_op jit(solution)/shard_map/ppermute | solution.py:19
  155.0 9.3 %all-to-all-start.1 = ((f32[4,1,8192]{2,1,0:T(1,128)}), f32[4,1,8192]{2,1,0:T(1,128)S(1)}, u32[]{:S(2)}, u32[]{:S(2)}) async-start(f32[4,1,8192]{2,1,0:T(1,128)} %reshape.36), calls=%async_computation.1 | async-start | bytes 262144 | tf_op jit(solution)/shard_map/all_to_all | solution.py:294

commit v3 on v2

v3 whole, which is shorter than its diff:
```python
import functools

import jax
import jax.numpy as jnp
from jax import lax
from jax.experimental import pallas as pl
from jax.experimental.pallas import tpu as pltpu
from jax.sharding import Mesh
from jax.sharding import PartitionSpec as P

HIGHEST = lax.Precision.HIGHEST
RANK = 64
TILE = 8
TILES = RANK // TILE


def shift(value, axis, step):
    size = lax.axis_size(axis)
    return lax.ppermute(value, axis, [(i, (i + step) % size) for i in range(size)])


def swap(value, axis, mask):
    return lax.ppermute(value, axis, [(i, i ^ mask) for i in range(lax.axis_size(axis))])


def factor_in_place(s_ref):
    batch = s_ref.shape[2]
    sub = lax.broadcasted_iota(jnp.int32, (TILE, batch), 0)
    for jb in range(TILES):
        count = TILES - jb
        base = jb * TILE
        rows = [
            [s_ref[base + k, pl.ds((jb + t) * TILE, TILE), :] for t in range(count)]
            for k in range(TILE)
        ]
        for k in range(TILE):
            scale = lax.rsqrt(rows[k][0][k : k + 1, :])
            row = [v * scale for v in rows[k]]
            row[0] = jnp.where(sub >= k, row[0], 0.0)
            rows[k] = row
            for t in range(count):
                s_ref[base + k, pl.ds((jb + t) * TILE, TILE), :] = row[t]
            for t in range(jb):
                s_ref[base + k, pl.ds(t * TILE, TILE), :] = jnp.zeros((TILE, batch), jnp.float32)
            for k2 in range(k + 1, TILE):
                s = row[0][k2 : k2 + 1, :]
                rows[k2] = [v - s * u for v, u in zip(rows[k2], row)]
        for rb in range(jb + 1, TILES):
            for r in range(rb * TILE, (rb + 1) * TILE):
                heads = [s_ref[base + k, pl.ds(r, 1), :] for k in range(TILE)]
                for ct in range(rb, TILES):
                    total = s_ref[r, pl.ds(ct * TILE, TILE), :]
                    for k in range(TILE):
                        total = total - heads[k] * rows[k][ct - jb]
                    s_ref[r, pl.ds(ct * TILE, TILE), :] = total


def to_lanes(g_ref, s_ref):
    for a in range(RANK):
        s_ref[a] = g_ref[:, a, :].T


def column_of(s_ref, c):
    return s_ref[:, c, :].T


def packed_rows(matrix):
    half = matrix.shape[0] // 2
    return jnp.concatenate([matrix[:half], matrix[half:]], axis=1)


def unpacked(rows):
    half = rows.shape[-1] // 2
    return jnp.concatenate([rows[..., :half], rows[..., half:]], axis=-2)


def leaf_kernel(x_ref, move_ref, packed_ref, gram_ref, s_ref):
    sources, leaves = x_ref.shape[0], x_ref.shape[1]
    term = None
    for m in range(leaves):
        x = jnp.concatenate([x_ref[s, m] for s in range(sources)], axis=0)
        gram_ref[m] = lax.dot_general(
            x, x, (((1,), (1,)), ((), ())), precision=HIGHEST, preferred_element_type=jnp.float32
        )
    to_lanes(gram_ref, s_ref)
    for m in range(leaves):
        move = move_ref[m]
        moved = jnp.dot(gram_ref[m], move, precision=HIGHEST, preferred_element_type=jnp.float32)
        last = jnp.dot(move.T, moved, precision=HIGHEST, preferred_element_type=jnp.float32)
        term = last if term is None else term + last
    packed_ref[leaves] = packed_rows(term)
    factor_in_place(s_ref)
    half = RANK // 2
    for c in range(half):
        packed_ref[:leaves, c, :] = jnp.concatenate(
            [column_of(s_ref, c), column_of(s_ref, c + half)], axis=1
        )


def leaf_factors(x, moves):
    leaves = x.shape[1]
    vmem = pl.BlockSpec(memory_space=pltpu.VMEM)
    return pl.pallas_call(
        leaf_kernel,
        out_shape=jax.ShapeDtypeStruct((leaves + 1, RANK // 2, 2 * RANK), jnp.float32),
        in_specs=[vmem, vmem],
        out_specs=vmem,
        scratch_shapes=[
            pltpu.VMEM((leaves, RANK, RANK), jnp.float32),
            pltpu.VMEM((RANK, RANK, leaves), jnp.float32),
        ],
        compiler_params=pltpu.CompilerParams(vmem_limit_bytes=32 * 2**20),
        name="leaf_factors",
    )(x, moves)


def node_kernel(g_ref, out_ref, s_ref):
    to_lanes(g_ref, s_ref)
    factor_in_place(s_ref)
    for c in range(RANK):
        out_ref[:, c, :] = column_of(s_ref, c)


def node_lower(grams):
    return pl.pallas_call(
        node_kernel,
        out_shape=jax.ShapeDtypeStruct(grams.shape, jnp.float32),
        in_specs=[pl.BlockSpec(memory_space=pltpu.VMEM)],
        out_specs=pl.BlockSpec(memory_space=pltpu.VMEM),
        scratch_shapes=[pltpu.VMEM((RANK, RANK, grams.shape[0]), jnp.float32)],
        compiler_params=pltpu.CompilerParams(vmem_limit_bytes=32 * 2**20),
        name="node_factors",
    )(grams)


def split(value):
    high = value.astype(jnp.bfloat16)
    return high, (value - high.astype(jnp.float32)).astype(jnp.bfloat16)


def block_products(blocks, packed):
    listed, width, rank = blocks.shape
    top = width // 2
    zero = jnp.zeros((rank, rank), jnp.bfloat16)
    high, low = split(unpacked(packed))
    wide = jnp.concatenate(
        [
            blocks[:, :top, :].reshape(listed * top, rank),
            blocks[:, top:, :].reshape(listed * top, rank),
        ],
        axis=1,
    )
    w_high = jnp.concatenate(
        [jnp.concatenate([high, zero], axis=1), jnp.concatenate([zero, high], axis=1)], axis=0
    )
    w_low = jnp.concatenate(
        [jnp.concatenate([low, zero], axis=1), jnp.concatenate([zero, low], axis=1)], axis=0
    )
    c_high, c_low = split(wide)
    total = jnp.dot(
        jnp.concatenate([c_high, c_low], axis=1),
        jnp.concatenate([w_high, w_high], axis=0),
        preferred_element_type=jnp.float32,
    )
    return total + jnp.dot(c_high, w_low, preferred_element_type=jnp.float32)


def product_kernel(
    near, away, place_ref, c_hbm, l_ref, first_ref, second_ref, keep_ref, acc_ref, c_ref, sems
):
    leaves, listed, width, _ = c_hbm.shape
    slots, group = c_ref.shape[0], c_ref.shape[1]
    steps = leaves // group
    top = width // 2
    share = l_ref.shape[1] - 1

    def fetch(step, slot):
        return pltpu.make_async_copy(
            c_hbm.at[pl.ds(step * group, group)], c_ref.at[slot], sems.at[slot]
        )

    for step in range(slots - 1):
        fetch(step, step).start()
    acc_ref[...] = jnp.zeros_like(acc_ref)

    def body(step, carry):
        slot = lax.rem(step, slots)
        ahead = step + slots - 1

        @pl.when(ahead < steps)
        def _():
            fetch(ahead, lax.rem(ahead, slots)).start()

        fetch(step, slot).wait()
        source = lax.div(step * group, share)
        first_leaf = step * group - source * share
        totals = [
            block_products(c_ref[slot, u], l_ref[source, first_leaf + u]) for u in range(group)
        ]
        for u in range(group):
            for k in range(listed):
                place = place_ref[(step * group + u) * listed + k]
                acc_ref[place] = acc_ref[place] + totals[u][k * top : (k + 1) * top, :]
        return carry

    lax.fori_loop(0, steps, body, 0)
    first_ref[...] = acc_ref[:near]
    second_ref[...] = acc_ref[near:away]
    keep_ref[...] = acc_ref[away : 2 * away]


def weighted_sums(place, blocks, packed, near, away):
    leaves, listed, width, rank = blocks.shape
    top = width // 2
    group, slots = 4, 4
    vmem = pl.BlockSpec(memory_space=pltpu.VMEM)

    def out(rows):
        return jax.ShapeDtypeStruct((rows, top, 2 * rank), jnp.float32)

    return pl.pallas_call(
        functools.partial(product_kernel, near, away),
        in_specs=[
            pl.BlockSpec(memory_space=pltpu.SMEM),
            pl.BlockSpec(memory_space=pl.ANY),
            vmem,
        ],
        out_specs=(vmem, vmem, vmem),
        scratch_shapes=[
            pltpu.VMEM((2 * away + TILE, top, 2 * rank), jnp.float32),
            pltpu.VMEM((slots, group, listed, width, rank), jnp.float32),
            pltpu.SemaphoreType.DMA((slots,)),
        ],
        out_shape=(out(near), out(away - near), out(away)),
        compiler_params=pltpu.CompilerParams(vmem_limit_bytes=32 * 2**20),
        name="weighted_sums",
    )(place, blocks, packed)


def pack_kernel(
    cut, me_ref, y_ref, up_ref, down_ref, far_ref, two_ref, six_ref,
    z_ref, r1_ref, r2_ref, r3_ref, o0_ref, o1_ref, o2_ref, o3_ref, g_ref, m_ref,
):
    slots = g_ref.shape[0]
    rest = slots - cut
    g_ref[:cut] = (
        y_ref[7 * cut :] + up_ref[cut:] + down_ref[cut:] + far_ref[...] + two_ref[...] + six_ref[...]
    )
    g_ref[cut:] = z_ref[:rest] + r1_ref[...] + r2_ref[...] + r3_ref[...]
    chunks = m_ref.shape[0]
    piece = RANK // chunks
    batch = 2 * RANK // piece
    for g in range(slots // batch):
        rows = [g_ref[g * batch + q] for q in range(batch)]
        for c in range(chunks):
            for h in range(2):
                at = h * RANK + c * piece
                m_ref[c, 2 * g + h] = jnp.concatenate([r[:, at : at + piece] for r in rows], axis=1)
    for step, o_ref in enumerate((o0_ref, o1_ref, o2_ref, o3_ref)):
        o_ref[...] = m_ref[lax.rem(me_ref[0] + step, chunks)]


def pack(me, cut, slots, arrays):
    vmem = pl.BlockSpec(memory_space=pltpu.VMEM)
    top, lanes = arrays[0].shape[1:]
    tiles = slots * RANK // 4 * top * 2 // (top * lanes)
    message = jax.ShapeDtypeStruct((tiles, top, lanes), jnp.float32)
    return pl.pallas_call(
        functools.partial(pack_kernel, cut),
        in_specs=[pl.BlockSpec(memory_space=pltpu.SMEM)] + [vmem] * len(arrays),
        out_specs=(vmem,) * 4,
        out_shape=(message,) * 4,
        scratch_shapes=[
            pltpu.VMEM((slots, top, lanes), jnp.float32),
            pltpu.VMEM((4, tiles, top, lanes), jnp.float32),
        ],
        compiler_params=pltpu.CompilerParams(vmem_limit_bytes=16 * 2**20),
        name="pack",
    )(me, *arrays)


def final_kernel(me_ref, l_ref, m0_ref, m1_ref, m2_ref, m3_ref, out_ref, m_ref):
    chunks, tiles = m_ref.shape[0], m_ref.shape[1]
    for step, ref in enumerate((m0_ref, m1_ref, m2_ref, m3_ref)):
        m_ref[lax.rem(me_ref[0] + chunks - step, chunks)] = ref[...]
    share = l_ref.shape[1] - 1
    piece = RANK // chunks
    batch = 2 * RANK // piece
    for g in range(tiles // 2):
        rows = [m_ref[c, 2 * g + h] for c in range(chunks) for h in range(2)]
        turned = jnp.concatenate(rows, axis=0).T
        for q in range(batch):
            j = g * batch + q
            out_ref[j] = jnp.dot(
                turned[q * piece : (q + 1) * piece, :],
                unpacked(l_ref[j // share, j % share]),
                precision=HIGHEST,
                preferred_element_type=jnp.float32,
            )


def final(me, packed, messages, slots):
    vmem = pl.BlockSpec(memory_space=pltpu.VMEM)
    return pl.pallas_call(
        final_kernel,
        in_specs=[pl.BlockSpec(memory_space=pltpu.SMEM)] + [vmem] * 5,
        out_specs=vmem,
        out_shape=jax.ShapeDtypeStruct((slots, RANK // 4, RANK), jnp.float32),
        scratch_shapes=[pltpu.VMEM((4,) + messages[0].shape, jnp.float32)],
        compiler_params=pltpu.CompilerParams(vmem_limit_bytes=16 * 2**20),
        name="left_factor",
    )(me, packed, *messages)


class Plan:
    def __init__(self, n_y, n_z, slots):
        self.cut = 9 * slots // 16
        self.rest = slots - self.cut
        self.order = (3, 1, 5, 7, 4, 2, 6, 0)
        self.spot = tuple(self.order.index(r) for r in range(n_z))
        self.y_rows = n_z * self.cut
        self.z_rows = n_y * self.rest
        self.base = {}
        at = 0
        for group in ("y2", "z4", "y1", "y3", "z3", "z1", "z5", "z7", "z2", "z6", "y0", "z0"):
            if group == "y1":
                self.near = at
            self.base[group] = at
            at += self.y_rows if group[0] == "y" else self.z_rows
        self.total = at
        self.n_y, self.n_z = n_y, n_z

    def rows(self, rel_y, rel_z, slot):
        base_y = sum(jnp.where(rel_y == r, self.base["y%d" % r], 0) for r in range(self.n_y))
        base_z = sum(jnp.where(rel_z == r, self.base["z%d" % r], 0) for r in range(self.n_z))
        spot = sum(jnp.where(rel_z == r, self.spot[r], 0) for r in range(self.n_z))
        by_y = base_y + spot * self.cut + slot
        by_z = base_z + rel_y * self.rest + slot - self.cut
        return jnp.where(slot < self.cut, by_y, by_z)


def tie(*values):
    return lax.optimization_barrier(values)


def shards(
    bases,
    leaf_transfer,
    node_transfer,
    pair_transfer,
    quad_transfer,
    coupling,
    row_device,
    row_slot,
    block_count,
):
    n_rank = lax.axis_size("rk")
    rank_index = lax.axis_index("rk")
    me = rank_index.astype(jnp.int32).reshape(1)
    n_y, n_z, n_core = (lax.axis_size(axis) for axis in ("y", "z", "core"))
    core = lax.axis_index("core")
    local = jnp.swapaxes(bases[0], 1, 2)
    leaves, width, points = local.shape
    share = leaves // n_rank

    blocks = coupling[0]
    listed = blocks.shape[1]
    plan = Plan(n_y, n_z, leaves)
    dest = row_device[0, :, :, 0]
    valid = jnp.arange(listed, dtype=jnp.int32)[None, :] < block_count[0][:, None]
    rel_z = (dest // n_core - lax.axis_index("z")) % n_z
    rel_y = (dest // (n_core * n_z) - lax.axis_index("y")) % n_y
    place = plan.rows(rel_y, rel_z, row_slot[0])
    place = place + jnp.where(dest % n_core == core, plan.total, 0)
    place = jnp.where(valid, place, 2 * plan.total).reshape(-1).astype(jnp.int32)

    pieces = lax.all_to_all(local, "rk", split_axis=0, concat_axis=0, tiled=True)
    moves = lax.dynamic_slice_in_dim(leaf_transfer[0], rank_index * share, share, 0)
    mine = leaf_factors(pieces.reshape(n_rank, share, width, points), moves)
    packed = lax.all_gather(mine, "rk", axis=0, tiled=False)

    first, second, keep = weighted_sums(place, blocks, packed, plan.near, plan.total)
    first = swap(first, "core", 1)
    second = swap(second, "core", 1)
    near = plan.near

    def part(group, count=1, skip=0, rows=None):
        size = (plan.y_rows if group[0] == "y" else plan.z_rows) * count if rows is None else rows
        at = plan.base[group] + skip
        other = first[at : at + size] if at < near else second[at - near : at - near + size]
        return keep[at : at + size] + other

    def level_term(level, transfer):
        moved = jnp.dot(level, transfer, precision=HIGHEST)
        return jnp.dot(transfer.T, moved, precision=HIGHEST)

    rows = plan.z_rows
    half = rows // 2
    y_far, z_up2, z_down2, z_up, z_down, y_up, y_down, terms = tie(
        part("y2"),
        part("z4", rows=half),
        part("z4", skip=half, rows=half),
        part("z3", 2),
        part("z5", 2),
        part("y1"),
        part("y3"),
        packed[:, share],
    )
    y_far = shift(y_far, "y", 2)
    z_up2 = shift(z_up2, "z", 2)
    z_down2 = shift(z_down2, "z", -2)
    z_up = shift(z_up, "z", 1)
    z_down = shift(z_down, "z", -1)
    grams = [unpacked(jnp.sum(terms, axis=0))]
    term = level_term(grams[0], node_transfer[0])
    other = swap(term, "core", 1)

    y_far, z_up2, z_down2, z_up, z_down, y_up, y_down, other = tie(
        y_far, z_up2, z_down2, z_up, z_down, y_up, y_down, other
    )
    z_two = part("z2") + z_up[:rows] + jnp.pad(z_up2, ((0, half), (0, 0), (0, 0)))
    z_six = part("z6") + z_down[:rows] + jnp.pad(z_down2, ((half, 0), (0, 0), (0, 0)))
    y_up, y_down, z_two, z_six, other = tie(y_up, y_down, z_two, z_six, other)
    y_up = shift(y_up, "y", 1)
    y_down = shift(y_down, "y", -1)
    z_two = shift(z_two, "z", 2)
    z_six = shift(z_six, "z", -2)
    grams.append(term + other)
    term = level_term(grams[1], pair_transfer[0])
    other = swap(term, "z", 1)

    y_up, y_down, z_two, z_six, other = tie(y_up, y_down, z_two, z_six, other)
    by_y = part("y0") + y_far + y_up + y_down
    by_z = part("z0") + z_up[rows:] + z_down[rows:] + z_two + z_six
    cut, rest = plan.cut, plan.rest
    by_y, by_z, other = tie(by_y, by_z, other)
    up = shift(by_y[: 2 * cut], "z", 1)
    down = shift(by_y[2 * cut : 4 * cut], "z", -1)
    far = shift(by_y[4 * cut : 5 * cut], "z", 4)
    r1 = shift(by_z[rest : 2 * rest], "y", 1)
    r2 = shift(by_z[2 * rest : 3 * rest], "y", 2)
    r3 = shift(by_z[3 * rest :], "y", -1)
    grams.append(term + other)
    term = level_term(grams[2], quad_transfer[0])
    other = swap(term, "z", 2)

    up, down, other = tie(up, down, other)
    two = shift(by_y[5 * cut : 6 * cut] + up[:cut], "z", 2)
    six = shift(by_y[6 * cut : 7 * cut] + down[:cut], "z", -2)
    grams.append(term + other)
    nodes = node_lower(jnp.stack(grams))

    messages = pack(
        me, cut, leaves, (by_y, up, down, far, two, six, by_z, r1, r2, r3)
    )
    arrived = [messages[0]] + [shift(messages[s], "rk", s) for s in range(1, n_rank)]
    coupled = final(me, packed, arrived, leaves)

    lower = unpacked(packed[:, :share]).reshape(leaves, RANK, RANK)
    node_weights = lax.dynamic_slice_in_dim(nodes, rank_index * width, width, 1)
    leaf_weights = lax.dynamic_slice_in_dim(lower, rank_index * width, width, 1)
    return (
        jnp.swapaxes(leaf_weights, 1, 2)[None],
        jnp.swapaxes(node_weights, 1, 2)[:, None],
        jnp.swapaxes(coupled, 1, 2)[None],
    )


def solution(mesh):
    devices = mesh.devices
    fine = Mesh(devices.reshape(4, 8, 2, devices.shape[1]), ("y", "z", "core", "rk"))
    clu = ("y", "z", "core")
    placed = (
        P(clu, None, None, "rk"),
        P(clu, None, None, None),
        P(clu, None, None),
        P(clu, None, None),
        P(clu, None, None),
        P(clu, None, None, "rk", None),
        P(clu, None, None, None),
        P(clu, None, None),
        P(clu, None),
    )
    return jax.shard_map(
        shards,
        mesh=fine,
        in_specs=placed,
        out_specs=(
            P(clu, None, None, "rk"),
            P(None, clu, None, "rk"),
            P(clu, None, None, "rk"),
        ),
        check_vma=False,
    )
```

time: 169 us -> 144 us (0.85); the launches traced: 168 us -> 141 us
  waiting for transfers between devices: 53.2 us -> 35.2 us
  starting transfers between devices: 51.2 us -> 44.8 us
  other arithmetic: 9.3 us -> 14.1 us
  Pallas kernels: 26.2 us -> 23 us
  matrix products: 4.15 us -> 1.19 us
    ppermute x17 -> x20, waiting for transfers between devices: 34.8 us -> 13.7 us  [shift(): lax.ppermute(value, axis, [(i, (i + step) % size) for i in range(size)])]
    ppermute x7 -> x5, waiting for transfers between devices: 7.31 us -> 15.7 us  [swap(): lax.ppermute(value, axis, [(i, i ^ mask) for i in range(lax.axis_size(axi...]
    add x2 -> x3, other arithmetic: 1.46 us -> 7.59 us  [part(): return keep[at:at + size] + other]
    pallas_call x1, Pallas kernels: 17.2 us -> 11.6 us  [weighted_sums(): pl.pallas_call(functools.partial(product_kernel, near, away), in_specs=[p...]
    all_to_all x1 -> x0, waiting for transfers between devices: 5.31 us -> none  [shards(): lax.all_to_all(gathered, 'rk', split_axis=2, concat_axis=1, tiled=True)]
    all_to_all x1 -> x0, starting transfers between devices: 3.33 us -> none  [shards(): lax.all_to_all(gathered, 'rk', split_axis=2, concat_axis=1, tiled=True)]
    dot_general x9 -> x6, matrix products: 4.15 us -> 1.19 us  [the longest x3 0.71 us: level_term(): return jnp.dot(transfer.T, moved, precision=HIGHEST)]
    ppermute x17 -> x20, starting transfers between devices: 37.8 us -> 35.2 us  [shift(): lax.ppermute(value, axis, [(i, (i + step) % size) for i in range(size)])]
  transfers between devices with their start and end apart: 26 -> 26, of which waited for: 12 -> 8; matrix products, arithmetic and copies ran while one was open for 8% -> 6% of each run, Pallas kernels for 2% -> 3%
where the time goes in v3:
time: 144 us; the launch traced here: 141 us
  starting transfers between devices  44.8 us (31%)
  waiting for transfers between devices  35.2 us (24%)
  Pallas kernels  23 us (16%)
  other arithmetic  14.1 us (10%)
  blocking collectives  13.1 us (9%)
  local copies, waits for them, and re-layouts  9.14 us (6%)
    ppermute x20, starting transfers between devices, shift(): lax.ppermute(value, axis, [(i, (i + step) % size) for i in range(size)])  35.2 us
    ppermute x5, waiting for transfers between devices, swap(): lax.ppermute(value, axis, [(i, i ^ mask) for i in range(lax.axis_size(axi...  15.7 us
    ppermute x20, waiting for transfers between devices, shift(): lax.ppermute(value, axis, [(i, (i + step) % size) for i in range(size)])  13.7 us
    all_gather x1, blocking collectives, shards(): packed = lax.all_gather(mine, 'rk', axis=0, tiled=False)  13.1 us
    pallas_call x1, Pallas kernels, weighted_sums(): pl.pallas_call(functools.partial(product_kernel, near, away), in_specs=[p...  11.6 us
    add x3, other arithmetic, part(): return keep[at:at + size] + other  7.59 us
    unnamed x20, local copies, waits for them, and re-layouts  6.51 us
    all_to_all x1, waiting for transfers between devices, shards(): lax.all_to_all(local, 'rk', split_axis=0, concat_axis=0, tiled=True)  5.81 us
  transfers between devices with their start and end apart: 26, of which 8 were waited for; matrix products, arithmetic and copies ran while one was open for 6% of the time, Pallas kernels for 3%

profile of v3, /device:TPU:32, one launch (start us, length us, event | category | flops | bytes accessed | tf_op | source)
XLA Modules:
  0.0 141.4 jit_solution(9388753979443484828)
XLA Ops:
  0.6 4.4 %all-to-all-start = ((f32[32,16,256]{2,1,0:T(8,128)}), f32[32,16,256]{2,1,0:T(8,128)S(1)}, u32[]{:S(2)}, u32[]{:S(2)}) async-start(f32[32,16,256]{2,1,0:T(8,128)} %bitcast.66), calls=%async_computation | async-start | bytes 1048576 | tf_op jit(solution)/shard_map/all_to_all | solution.py:377
  5.1 0.7 iota_compare_fusion
  5.8 0.5 broadcast.146
  6.3 1.4 reduce.3
  7.9 0.8 squeeze.26
  8.7 5.8 %all-to-all-done = f32[32,16,256]{2,1,0:T(8,128)S(1)} async-done(((f32[32,16,256]{2,1,0:T(8,128)}), f32[32,16,256]{2,1,0:T(8,128)S(1)}, u32[]{:S(2)}, u32[]{:S(2)}) %all-to-all-start) | async-done | bytes 524320 | tf_op jit(solution)/shard_map/all_to_all | solution.py:377
  14.6 5.2 %leaf_factors.1 = f32[9,32,128]{2,1,0:T(8,128)S(1)} custom-call(f32[4,8,16,256]{3,2,1,0:T(8,128)S(1)} %bitcast.64, f32[8,64,64]{2,1,0:T(8,128)S(1)} %dynamic-slice_bitcast_fusion.1.move_ref), custom_call_target="tpu_custom_call" | custom-call | tf_op jit(solution)/shard_map/leaf_factors/pallas_call | solution.py:103
  19.7 13.1 %all-gather = f32[36,32,128]{2,1,0:T(8,128)S(1)} all-gather(f32[9,32,128]{2,1,0:T(8,128)S(1)} %leaf_factors.1), channel_id=2, replica_groups=mesh['y'=4,'z'=8,'core'=2,'rk'=4] {'rk'}, dimensions={0}, use_global_device_ids=true | all-gather | bytes 737280 | tf_op jit(solution)/shard_map/all_gather | solution.py:380
  32.9 3.4 %copy-done.1 = f32[1,32,32,16,64]{4,3,2,1,0:T(8,128)S(1)} copy-done((f32[1,32,32,16,64]{4,3,2,1,0:T(8,128)S(1)}, f32[1,32,32,16,64]{4,3,2,1,0:T(8,128)}, u32[]{:S(2)}) %copy-start.1) | copy-done | bytes 4194328
  36.2 11.6 %weighted_sums.1 = (f32[200,8,128]{2,1,0:T(8,128)S(1)}, f32[824,8,128]{2,1,0:T(8,128)}, f32[1024,8,128]{2,1,0:T(8,128)S(1)}) custom-call(s32[1024]{0:T(1024)S(1)} %add_select_fusion.5.place_ref, f32[32,32,16,64]{3,2,1,0:T(8,128)S(1)} %bitcast.63, f32[4,9,32,128]{3,2,1,0:T(8,128)S(1)} %bitcast.59), custom_call_target="tpu_custom_call" | custom-call | tf_op jit(solution)/shard_map/weighted_sums/pallas_call | solution.py:221
  47.9 2.0 %copy-done.2 = f32[1024,8,128]{2,1,0:T(8,128)} copy-done((f32[1024,8,128]{2,1,0:T(8,128)}, f32[1024,8,128]{2,1,0:T(8,128)S(1)}, u32[]{:S(2)}) %copy-start.2) | copy-done | bytes 4194328
  50.3 0.6 slice_bitcast_fusion
  51.2 5.6 %collective-permute-done = f32[200,8,128]{2,1,0:T(8,128)} collective-permute-done((f32[200,8,128]{2,1,0:T(8,128)S(1)}, f32[200,8,128]{2,1,0:T(8,128)}, u32[]{:S(2)}, u32[]{:S(2)}) %collective-permute-start) | collective-permute-done | bytes 819232 | tf_op jit(solution)/shard_map/ppermute | solution.py:23
  56.7 1.8 %slice_add_fusion.9 = (f32[28,8,128]{2,1,0:T(8,128)}, f32[28,8,128]{2,1,0:T(8,128)}) fusion(f32[200,8,128]{2,1,0:T(8,128)} %collective-permute-done, f32[1024,8,128]{2,1,0:T(8,128)} %copy-done.2), kind=kLoop, calls=%fused_computation.27 | loop fusion | flops 57344 | bytes 688128 | tf_op jit(solution)/shard_map/add | solution.py:391
  58.6 3.3 %slice_add_fusion.1 = (f32[144,8,128]{2,1,0:T(8,128)}, f32[144,8,128]{2,1,0:T(8,128)}, f32[144,8,128]{2,1,0:T(8,128)}) fusion(f32[824,8,128]{2,1,0:T(8,128)} %collective-permute-done.1, f32[1024,8,128]{2,1,0:T(8,128)} %copy-done.2, f32[200,8,128]{2,1,0:T(8,128)} %collective-permute-done), kind=kLoop, calls=%fused_computation.8 | loop fusion | flops 442368 | bytes 5308416 | tf_op jit(solution)/shard_map/add | solution.py:391
  61.9 2.5 %slice_add_fusion.4 = (f32[112,8,128]{2,1,0:T(8,128)}, f32[112,8,128]{2,1,0:T(8,128)}) fusion(f32[824,8,128]{2,1,0:T(8,128)} %collective-permute-done.1, f32[1024,8,128]{2,1,0:T(8,128)} %copy-done.2), kind=kLoop, calls=%fused_computation.11 | loop fusion | flops 229376 | bytes 2752512 | tf_op jit(solution)/shard_map/add | solution.py:391
  64.4 3.0 %collective-permute-start.2 = (f32[144,8,128]{2,1,0:T(8,128)}, f32[144,8,128]{2,1,0:T(8,128)S(1)}, u32[]{:S(2)}, u32[]{:S(2)}) collective-permute-start(f32[144,8,128]{2,1,0:T(8,128)} %get-tuple-element.46), channel_id=1, source_target_pairs={{0,128},{64,192},{128,0},{192,64},{1,129},{65,193},{129,1},{193,65... | collective-permute-start | bytes 1769480 | tf_op jit(solution)/shard_map/ppermute | solution.py:19
  67.4 1.8 %collective-permute-start.5 = (f32[112,8,128]{2,1,0:T(8,128)}, f32[112,8,128]{2,1,0:T(8,128)}, u32[]{:S(2)}, u32[]{:S(2)}) collective-permute-start(f32[112,8,128]{2,1,0:T(8,128)} %get-tuple-element.49), channel_id=1, source_target_pairs={{0,8},{8,16},{16,24},{24,32},{32,40},{40,48},{48,56},{56,0},{1,9},... | collective-permute-start | bytes 1376264 | tf_op jit(solution)/shard_map/ppermute | solution.py:19
  70.1 4.7 %collective-permute-start.3 = (f32[28,8,128]{2,1,0:T(8,128)}, f32[28,8,128]{2,1,0:T(8,128)S(1)}, u32[]{:S(2)}, u32[]{:S(2)}) collective-permute-start(f32[28,8,128]{2,1,0:T(8,128)} %get-tuple-element.47), channel_id=1, source_target_pairs={{0,16},{8,24},{16,32},{24,40},{32,48},{40,56},{48,0},{56,8},{1,17}... | collective-permute-start | bytes 344072 | tf_op jit(solution)/shard_map/ppermute | solution.py:19
  74.9 1.9 %collective-permute-start.4 = (f32[28,8,128]{2,1,0:T(8,128)}, f32[28,8,128]{2,1,0:T(8,128)S(1)}, u32[]{:S(2)}, u32[]{:S(2)}) collective-permute-start(f32[28,8,128]{2,1,0:T(8,128)} %get-tuple-element.48), channel_id=1, source_target_pairs={{0,48},{8,56},{16,0},{24,8},{32,16},{40,24},{48,32},{56,40},{1,49}... | collective-permute-start | bytes 344072 | tf_op jit(solution)/shard_map/ppermute | solution.py:19
  76.7 0.7 dynamic-slice_bitcast_fusion
  77.5 11.3 %collective-permute-done.3 = f32[28,8,128]{2,1,0:T(8,128)S(1)} collective-permute-done((f32[28,8,128]{2,1,0:T(8,128)}, f32[28,8,128]{2,1,0:T(8,128)S(1)}, u32[]{:S(2)}, u32[]{:S(2)}) %collective-permute-start.3) | collective-permute-done | bytes 114720 | tf_op jit(solution)/shard_map/ppermute | solution.py:19
  88.8 1.5 %fusion.8 = (f32[56,8,128]{2,1,0:T(8,128)S(1)}, f32[56,8,128]{2,1,0:T(8,128)S(1)}) fusion(f32[824,8,128]{2,1,0:T(8,128)} %collective-permute-done.1, f32[28,8,128]{2,1,0:T(8,128)S(1)} %collective-permute-done.4, f32[112,8,128]{2,1,0:T(8,128)} %collective-permute-done.6, f32[1024,8,128]{2,1,0:T(8,128)} %copy-done.2, ...), kind=kLoop, calls=%fused_computation.22 | loop fusion | flops 344064 | bytes 2064384 | tf_op jit(solution)/shard_map/add | solution.py:422
  90.3 0.9 collective-permute-start.8
  91.2 2.5 %collective-permute-start.9 = (f32[144,8,128]{2,1,0:T(8,128)S(1)}, f32[144,8,128]{2,1,0:T(8,128)S(1)}, u32[]{:S(2)}, u32[]{:S(2)}) collective-permute-start(f32[144,8,128]{2,1,0:T(8,128)S(1)} %copy-done.3), channel_id=1, source_target_pairs={{0,192},{64,0},{128,64},{192,128},{1,193},{65,1},{129,65},{193,129... | collective-permute-start | bytes 1769480 | tf_op jit(solution)/shard_map/ppermute | solution.py:19
  93.6 2.5 %collective-permute-start.10 = (f32[56,8,128]{2,1,0:T(8,128)S(1)}, f32[56,8,128]{2,1,0:T(8,128)S(1)}, u32[]{:S(2)}, u32[]{:S(2)}) collective-permute-start(f32[56,8,128]{2,1,0:T(8,128)S(1)} %get-tuple-element.64), channel_id=1, source_target_pairs={{0,16},{8,24},{16,32},{24,40},{32,48},{40,56},{48,0},{56,8},{1,17}... | collective-permute-start | bytes 688136 | tf_op jit(solution)/shard_map/ppermute | solution.py:19
  96.1 1.6 %collective-permute-start.11 = (f32[56,8,128]{2,1,0:T(8,128)S(1)}, f32[56,8,128]{2,1,0:T(8,128)S(1)}, u32[]{:S(2)}, u32[]{:S(2)}) collective-permute-start(f32[56,8,128]{2,1,0:T(8,128)S(1)} %get-tuple-element.65), channel_id=1, source_target_pairs={{0,48},{8,56},{16,0},{24,8},{32,16},{40,24},{48,32},{56,40},{1,49}... | collective-permute-start | bytes 688136 | tf_op jit(solution)/shard_map/ppermute | solution.py:19
  98.2 1.1 collective-permute-start.12
  99.3 9.0 %collective-permute-done.12 = f32[64,64]{1,0:T(8,128)S(1)} collective-permute-done((f32[64,64]{1,0:T(8,128)S(1)}, f32[64,64]{1,0:T(8,128)S(1)}, u32[]{:S(2)}, u32[]{:S(2)}) %collective-permute-start.12) | collective-permute-done | bytes 16416 | tf_op jit(solution)/shard_map/ppermute | solution.py:23
  108.3 1.3 fusion.6.z_ref
  109.6 1.4 fusion.2.y_ref
  111.0 1.2 collective-permute-start.13
  112.2 0.9 collective-permute-start.14
  113.6 3.5 %collective-permute-start.15 = (f32[64,64]{1,0:T(8,128)S(1)}, f32[64,64]{1,0:T(8,128)S(1)}, u32[]{:S(2)}, u32[]{:S(2)}) collective-permute-start(f32[64,64]{1,0:T(8,128)S(1)} %convolution_bitcast_fusion), channel_id=1, source_target_pairs={{0,16},{8,24},{16,0},{24,8},{32,48},{40,56},{48,32},{56,40},{1,17}... | collective-permute-start | bytes 49160 | tf_op jit(solution)/shard_map/ppermute | solution.py:23
  117.2 1.7 %collective-permute-start.20 = (f32[14,8,128]{2,1,0:T(8,128)S(1)}, f32[14,8,128]{2,1,0:T(8,128)S(1)}, u32[]{:S(2)}, u32[]{:S(2)}) collective-permute-start(f32[14,8,128]{2,1,0:T(8,128)S(1)} %get-tuple-element.104), channel_id=1, source_target_pairs={{0,128},{64,192},{128,0},{192,64},{1,129},{65,193},{129,1},{193,65... | collective-permute-start | bytes 172040 | tf_op jit(solution)/shard_map/ppermute | solution.py:19
  118.9 1.1 collective-permute-done.15
  120.0 0.6 collective-permute-start.21
  120.7 3.0 %collective-permute-start.16 = (f32[18,8,128]{2,1,0:T(8,128)S(1)}, f32[18,8,128]{2,1,0:T(8,128)S(1)}, u32[]{:S(2)}, u32[]{:S(2)}) collective-permute-start(f32[18,8,128]{2,1,0:T(8,128)S(1)} %get-tuple-element.98), channel_id=1, source_target_pairs={{0,32},{8,40},{16,48},{24,56},{32,0},{40,8},{48,16},{56,24},{1,33}... | collective-permute-start | bytes 221192 | tf_op jit(solution)/shard_map/ppermute | solution.py:19
  123.6 0.7 collective-permute-start.17
  124.4 3.7 %collective-permute-start.18 = (f32[18,8,128]{2,1,0:T(8,128)S(1)}, f32[18,8,128]{2,1,0:T(8,128)S(1)}, u32[]{:S(2)}, u32[]{:S(2)}) collective-permute-start(f32[18,8,128]{2,1,0:T(8,128)S(1)} %get-tuple-element.96), channel_id=1, source_target_pairs={{0,48},{8,56},{16,0},{24,8},{32,16},{40,24},{48,32},{56,40},{1,49}... | collective-permute-start | bytes 221192 | tf_op jit(solution)/shard_map/ppermute | solution.py:19
  128.1 4.1 %node_factors.1 = f32[4,64,64]{2,1,0:T(8,128)S(1)} custom-call(f32[4,64,64]{2,1,0:T(8,128)S(1)} %pad_maximum_fusion.1.g_ref), custom_call_target="tpu_custom_call" | custom-call | tf_op jit(solution)/shard_map/node_factors/pallas_call | solution.py:125
  132.6 0.6 collective-permute-start.22
  133.1 2.7 %collective-permute-start.23 = (f32[8,8,128]{2,1,0:T(8,128)S(1)}, f32[8,8,128]{2,1,0:T(8,128)S(1)}, u32[]{:S(2)}, u32[]{:S(2)}) collective-permute-start(f32[8,8,128]{2,1,0:T(8,128)S(1)} %get-tuple-element.79), channel_id=1, source_target_pairs={{0,2},{1,3},{2,0},{3,1},{4,6},{5,7},{6,4},{7,5},{8,10},{9,11},{10,... | collective-permute-start | bytes 98312 | tf_op jit(solution)/shard_map/ppermute | solution.py:19
  135.8 0.9 collective-permute-start.24
  136.7 0.6 dynamic-slice_bitcast_fusion.2
  137.8 0.8 collective-permute-done.23.m2_ref
  138.6 1.2 collective-permute-done.24.m3_ref
  139.7 1.7 %left_factor.1 = f32[32,16,64]{2,1,0:T(8,128)} custom-call(s32[1]{0:T(128)} %bitcast.24.me_ref, f32[4,9,32,128]{3,2,1,0:T(8,128)S(1)} %bitcast.62, f32[8,8,128]{2,1,0:T(8,128)S(1)} %get-tuple-element.77.m0_ref, f32[8,8,128]{2,1,0:T(8,128)S(1)} %collective-permute-done.22.m1_ref, f32[8,8,128]{2,1,0:T(8,128)S(1)} %collective-permute-done.23.m2_ref, ...), custom_call_target="tpu_custom_call" | custom-call | tf_op jit(solution)/shard_map/left_factor/pallas_call | solution.py:304
  (63 shorter events, 3.6 us)
Async XLA Ops:
  0.6 8.1 %copy-start = (f32[1,32,64,64]{3,2,1,0:T(8,128)S(1)}, f32[1,32,64,64]{3,2,1,0:T(8,128)}, u32[]{:S(2)}) copy-start(f32[1,32,64,64]{3,2,1,0:T(8,128)} %param.10) | copy-start | bytes 1572868
  0.6 13.9 %all-to-all-start = ((f32[32,16,256]{2,1,0:T(8,128)}), f32[32,16,256]{2,1,0:T(8,128)S(1)}, u32[]{:S(2)}, u32[]{:S(2)}) async-start(f32[32,16,256]{2,1,0:T(8,128)} %bitcast.66), calls=%async_computation | async-start | bytes 1048576 | tf_op jit(solution)/shard_map/all_to_all | solution.py:377
  32.9 3.4 %copy-start.1 = (f32[1,32,32,16,64]{4,3,2,1,0:T(8,128)S(1)}, f32[1,32,32,16,64]{4,3,2,1,0:T(8,128)}, u32[]{:S(2)}) copy-start(f32[1,32,32,16,64]{4,3,2,1,0:T(8,128)} %param.14) | copy-start | bytes 12582916
  47.9 2.0 %copy-start.2 = (f32[1024,8,128]{2,1,0:T(8,128)}, f32[1024,8,128]{2,1,0:T(8,128)S(1)}, u32[]{:S(2)}) copy-start(f32[1024,8,128]{2,1,0:T(8,128)S(1)} %get-tuple-element.42) | copy-start | bytes 12582916
  49.8 8.7 %collective-permute-start.1 = (f32[824,8,128]{2,1,0:T(8,128)}, f32[824,8,128]{2,1,0:T(8,128)}, u32[]{:S(2)}, u32[]{:S(2)}) collective-permute-start(f32[824,8,128]{2,1,0:T(8,128)} %get-tuple-element.44), channel_id=1, source_target_pairs={{0,4},{4,0},{1,5},{5,1},{2,6},{6,2},{3,7},{7,3},{8,12},{12,8},{9,1... | collective-permute-start | bytes 10125320 | tf_op jit(solution)/shard_map/ppermute | solution.py:23
  49.8 6.9 %collective-permute-start = (f32[200,8,128]{2,1,0:T(8,128)S(1)}, f32[200,8,128]{2,1,0:T(8,128)}, u32[]{:S(2)}, u32[]{:S(2)}) collective-permute-start(f32[200,8,128]{2,1,0:T(8,128)S(1)} %get-tuple-element.43), channel_id=1, source_target_pairs={{0,4},{4,0},{1,5},{5,1},{2,6},{6,2},{3,7},{7,3},{8,12},{12,8},{9,1... | collective-permute-start | bytes 2457608 | tf_op jit(solution)/shard_map/ppermute | solution.py:23
  58.5 10.9 %copy-start.5 = (f32[4,32,128]{2,1,0:T(8,128)S(1)}, f32[4,32,128]{2,1,0:T(8,128)}, u32[]{:S(2)}) copy-start(f32[4,32,128]{2,1,0:T(8,128)} %slice_bitcast_fusion) | copy-start | bytes 196612
  58.5 11.0 %copy-start.6 = (f32[1,64,64]{2,1,0:T(8,128)S(1)}, f32[1,64,64]{2,1,0:T(8,128)}, u32[]{:S(2)}) copy-start(f32[1,64,64]{2,1,0:T(8,128)} %param.11) | copy-start | bytes 49156
  61.9 35.9 %copy-start.7 = (f32[1,64,64]{2,1,0:T(8,128)S(1)}, f32[1,64,64]{2,1,0:T(8,128)}, u32[]{:S(2)}) copy-start(f32[1,64,64]{2,1,0:T(8,128)} %param.12) | copy-start | bytes 49156
  64.4 24.4 %collective-permute-start.2 = (f32[144,8,128]{2,1,0:T(8,128)}, f32[144,8,128]{2,1,0:T(8,128)S(1)}, u32[]{:S(2)}, u32[]{:S(2)}) collective-permute-start(f32[144,8,128]{2,1,0:T(8,128)} %get-tuple-element.46), channel_id=1, source_target_pairs={{0,128},{64,192},{128,0},{192,64},{1,129},{65,193},{129,1},{193,65... | collective-permute-start | bytes 1769480 | tf_op jit(solution)/shard_map/ppermute | solution.py:19
  67.4 21.4 %collective-permute-start.5 = (f32[112,8,128]{2,1,0:T(8,128)}, f32[112,8,128]{2,1,0:T(8,128)}, u32[]{:S(2)}, u32[]{:S(2)}) collective-permute-start(f32[112,8,128]{2,1,0:T(8,128)} %get-tuple-element.49), channel_id=1, source_target_pairs={{0,8},{8,16},{16,24},{24,32},{32,40},{40,48},{48,56},{56,0},{1,9},... | collective-permute-start | bytes 1376264 | tf_op jit(solution)/shard_map/ppermute | solution.py:19
  69.2 19.5 %collective-permute-start.6 = (f32[112,8,128]{2,1,0:T(8,128)}, f32[112,8,128]{2,1,0:T(8,128)}, u32[]{:S(2)}, u32[]{:S(2)}) collective-permute-start(f32[112,8,128]{2,1,0:T(8,128)} %get-tuple-element.50), channel_id=1, source_target_pairs={{0,56},{8,0},{16,8},{24,16},{32,24},{40,32},{48,40},{56,48},{1,57}... | collective-permute-start | bytes 1376264 | tf_op jit(solution)/shard_map/ppermute | solution.py:19
  69.4 20.9 %copy-start.4 = (f32[144,8,128]{2,1,0:T(8,128)S(1)}, f32[144,8,128]{2,1,0:T(8,128)}, u32[]{:S(2)}) copy-start(f32[144,8,128]{2,1,0:T(8,128)} %get-tuple-element.62) | copy-start | bytes 1769476
  69.4 21.7 %copy-start.3 = (f32[144,8,128]{2,1,0:T(8,128)S(1)}, f32[144,8,128]{2,1,0:T(8,128)}, u32[]{:S(2)}) copy-start(f32[144,8,128]{2,1,0:T(8,128)} %get-tuple-element.63) | copy-start | bytes 1769476
  69.9 4.9 %collective-permute-start.7 = (f32[64,64]{1,0:T(8,128)S(1)}, f32[64,64]{1,0:T(8,128)S(1)}, u32[]{:S(2)}, u32[]{:S(2)}) collective-permute-start(f32[64,64]{1,0:T(8,128)S(1)} %convolution_bitcast_fusion.2), channel_id=1, source_target_pairs={{0,4},{4,0},{1,5},{5,1},{2,6},{6,2},{3,7},{7,3},{8,12},{12,8},{9,1... | collective-permute-start | bytes 49160 | tf_op jit(solution)/shard_map/ppermute | solution.py:23
  70.1 18.6 %collective-permute-start.3 = (f32[28,8,128]{2,1,0:T(8,128)}, f32[28,8,128]{2,1,0:T(8,128)S(1)}, u32[]{:S(2)}, u32[]{:S(2)}) collective-permute-start(f32[28,8,128]{2,1,0:T(8,128)} %get-tuple-element.47), channel_id=1, source_target_pairs={{0,16},{8,24},{16,32},{24,40},{32,48},{40,56},{48,0},{56,8},{1,17}... | collective-permute-start | bytes 344072 | tf_op jit(solution)/shard_map/ppermute | solution.py:19
  74.9 13.9 %collective-permute-start.4 = (f32[28,8,128]{2,1,0:T(8,128)}, f32[28,8,128]{2,1,0:T(8,128)S(1)}, u32[]{:S(2)}, u32[]{:S(2)}) collective-permute-start(f32[28,8,128]{2,1,0:T(8,128)} %get-tuple-element.48), channel_id=1, source_target_pairs={{0,48},{8,56},{16,0},{24,8},{32,16},{40,24},{48,32},{56,40},{1,49}... | collective-permute-start | bytes 344072 | tf_op jit(solution)/shard_map/ppermute | solution.py:19
  77.4 35.7 %copy-start.8 = (f32[1,64,64]{2,1,0:T(8,128)S(1)}, f32[1,64,64]{2,1,0:T(8,128)}, u32[]{:S(2)}) copy-start(f32[1,64,64]{2,1,0:T(8,128)} %param.13) | copy-start | bytes 49156
  90.3 18.0 %collective-permute-start.8 = (f32[144,8,128]{2,1,0:T(8,128)S(1)}, f32[144,8,128]{2,1,0:T(8,128)S(1)}, u32[]{:S(2)}, u32[]{:S(2)}) collective-permute-start(f32[144,8,128]{2,1,0:T(8,128)S(1)} %copy-done.4), channel_id=1, source_target_pairs={{0,64},{64,128},{128,192},{192,0},{1,65},{65,129},{129,193},{193,1... | collective-permute-start | bytes 1769480 | tf_op jit(solution)/shard_map/ppermute | solution.py:19
  91.2 17.1 %collective-permute-start.9 = (f32[144,8,128]{2,1,0:T(8,128)S(1)}, f32[144,8,128]{2,1,0:T(8,128)S(1)}, u32[]{:S(2)}, u32[]{:S(2)}) collective-permute-start(f32[144,8,128]{2,1,0:T(8,128)S(1)} %copy-done.3), channel_id=1, source_target_pairs={{0,192},{64,0},{128,64},{192,128},{1,193},{65,1},{129,65},{193,129... | collective-permute-start | bytes 1769480 | tf_op jit(solution)/shard_map/ppermute | solution.py:19
  93.6 14.6 %collective-permute-start.10 = (f32[56,8,128]{2,1,0:T(8,128)S(1)}, f32[56,8,128]{2,1,0:T(8,128)S(1)}, u32[]{:S(2)}, u32[]{:S(2)}) collective-permute-start(f32[56,8,128]{2,1,0:T(8,128)S(1)} %get-tuple-element.64), channel_id=1, source_target_pairs={{0,16},{8,24},{16,32},{24,40},{32,48},{40,56},{48,0},{56,8},{1,17}... | collective-permute-start | bytes 688136 | tf_op jit(solution)/shard_map/ppermute | solution.py:19
  96.1 12.2 %collective-permute-start.11 = (f32[56,8,128]{2,1,0:T(8,128)S(1)}, f32[56,8,128]{2,1,0:T(8,128)S(1)}, u32[]{:S(2)}, u32[]{:S(2)}) collective-permute-start(f32[56,8,128]{2,1,0:T(8,128)S(1)} %get-tuple-element.65), channel_id=1, source_target_pairs={{0,48},{8,56},{16,0},{24,8},{32,16},{40,24},{48,32},{56,40},{1,49}... | collective-permute-start | bytes 688136 | tf_op jit(solution)/shard_map/ppermute | solution.py:19
  98.2 10.1 %collective-permute-start.12 = (f32[64,64]{1,0:T(8,128)S(1)}, f32[64,64]{1,0:T(8,128)S(1)}, u32[]{:S(2)}, u32[]{:S(2)}) collective-permute-start(f32[64,64]{1,0:T(8,128)S(1)} %convolution_bitcast_fusion.1), channel_id=1, source_target_pairs={{0,8},{8,0},{16,24},{24,16},{32,40},{40,32},{48,56},{56,48},{1,9},... | collective-permute-start | bytes 49160 | tf_op jit(solution)/shard_map/ppermute | solution.py:23
  111.0 9.6 %collective-permute-start.13 = (f32[36,8,128]{2,1,0:T(8,128)S(1)}, f32[36,8,128]{2,1,0:T(8,128)S(1)}, u32[]{:S(2)}, u32[]{:S(2)}) collective-permute-start(f32[36,8,128]{2,1,0:T(8,128)S(1)} %get-tuple-element.100), channel_id=1, source_target_pairs={{0,8},{8,16},{16,24},{24,32},{32,40},{40,48},{48,56},{56,0},{1,9},... | collective-permute-start | bytes 442376 | tf_op jit(solution)/shard_map/ppermute | solution.py:19
  112.2 8.4 %collective-permute-start.14 = (f32[36,8,128]{2,1,0:T(8,128)S(1)}, f32[36,8,128]{2,1,0:T(8,128)S(1)}, u32[]{:S(2)}, u32[]{:S(2)}) collective-permute-start(f32[36,8,128]{2,1,0:T(8,128)S(1)} %get-tuple-element.99), channel_id=1, source_target_pairs={{0,56},{8,0},{16,8},{24,16},{32,24},{40,32},{48,40},{56,48},{1,57}... | collective-permute-start | bytes 442376 | tf_op jit(solution)/shard_map/ppermute | solution.py:19
  113.6 6.5 %collective-permute-start.15 = (f32[64,64]{1,0:T(8,128)S(1)}, f32[64,64]{1,0:T(8,128)S(1)}, u32[]{:S(2)}, u32[]{:S(2)}) collective-permute-start(f32[64,64]{1,0:T(8,128)S(1)} %convolution_bitcast_fusion), channel_id=1, source_target_pairs={{0,16},{8,24},{16,0},{24,8},{32,48},{40,56},{48,32},{56,40},{1,17}... | collective-permute-start | bytes 49160 | tf_op jit(solution)/shard_map/ppermute | solution.py:23
  117.1 7.3 %collective-permute-start.19 = (f32[14,8,128]{2,1,0:T(8,128)S(1)}, f32[14,8,128]{2,1,0:T(8,128)S(1)}, u32[]{:S(2)}, u32[]{:S(2)}) collective-permute-start(f32[14,8,128]{2,1,0:T(8,128)S(1)} %get-tuple-element.105), channel_id=1, source_target_pairs={{0,64},{64,128},{128,192},{192,0},{1,65},{65,129},{129,193},{193,1... | collective-permute-start | bytes 172040 | tf_op jit(solution)/shard_map/ppermute | solution.py:19
  117.2 15.0 %collective-permute-start.20 = (f32[14,8,128]{2,1,0:T(8,128)S(1)}, f32[14,8,128]{2,1,0:T(8,128)S(1)}, u32[]{:S(2)}, u32[]{:S(2)}) collective-permute-start(f32[14,8,128]{2,1,0:T(8,128)S(1)} %get-tuple-element.104), channel_id=1, source_target_pairs={{0,128},{64,192},{128,0},{192,64},{1,129},{65,193},{129,1},{193,65... | collective-permute-start | bytes 172040 | tf_op jit(solution)/shard_map/ppermute | solution.py:19
  120.0 12.2 %collective-permute-start.21 = (f32[14,8,128]{2,1,0:T(8,128)S(1)}, f32[14,8,128]{2,1,0:T(8,128)S(1)}, u32[]{:S(2)}, u32[]{:S(2)}) collective-permute-start(f32[14,8,128]{2,1,0:T(8,128)S(1)} %get-tuple-element.103), channel_id=1, source_target_pairs={{0,192},{64,0},{128,64},{192,128},{1,193},{65,1},{129,65},{193,129... | collective-permute-start | bytes 172040 | tf_op jit(solution)/shard_map/ppermute | solution.py:19
  120.7 11.6 %collective-permute-start.16 = (f32[18,8,128]{2,1,0:T(8,128)S(1)}, f32[18,8,128]{2,1,0:T(8,128)S(1)}, u32[]{:S(2)}, u32[]{:S(2)}) collective-permute-start(f32[18,8,128]{2,1,0:T(8,128)S(1)} %get-tuple-element.98), channel_id=1, source_target_pairs={{0,32},{8,40},{16,48},{24,56},{32,0},{40,8},{48,16},{56,24},{1,33}... | collective-permute-start | bytes 221192 | tf_op jit(solution)/shard_map/ppermute | solution.py:19
  123.6 8.6 %collective-permute-start.17 = (f32[18,8,128]{2,1,0:T(8,128)S(1)}, f32[18,8,128]{2,1,0:T(8,128)S(1)}, u32[]{:S(2)}, u32[]{:S(2)}) collective-permute-start(f32[18,8,128]{2,1,0:T(8,128)S(1)} %get-tuple-element.97), channel_id=1, source_target_pairs={{0,16},{8,24},{16,32},{24,40},{32,48},{40,56},{48,0},{56,8},{1,17}... | collective-permute-start | bytes 221192 | tf_op jit(solution)/shard_map/ppermute | solution.py:19
  124.4 7.9 %collective-permute-start.18 = (f32[18,8,128]{2,1,0:T(8,128)S(1)}, f32[18,8,128]{2,1,0:T(8,128)S(1)}, u32[]{:S(2)}, u32[]{:S(2)}) collective-permute-start(f32[18,8,128]{2,1,0:T(8,128)S(1)} %get-tuple-element.96), channel_id=1, source_target_pairs={{0,48},{8,56},{16,0},{24,8},{32,16},{40,24},{48,32},{56,40},{1,49}... | collective-permute-start | bytes 221192 | tf_op jit(solution)/shard_map/ppermute | solution.py:19
  132.6 5.2 %collective-permute-start.22 = (f32[8,8,128]{2,1,0:T(8,128)S(1)}, f32[8,8,128]{2,1,0:T(8,128)S(1)}, u32[]{:S(2)}, u32[]{:S(2)}) collective-permute-start(f32[8,8,128]{2,1,0:T(8,128)S(1)} %get-tuple-element.78), channel_id=1, source_target_pairs={{0,1},{1,2},{2,3},{3,0},{4,5},{5,6},{6,7},{7,4},{8,9},{9,10},{10,1... | collective-permute-start | bytes 98312 | tf_op jit(solution)/shard_map/ppermute | solution.py:19
  133.1 5.4 %collective-permute-start.23 = (f32[8,8,128]{2,1,0:T(8,128)S(1)}, f32[8,8,128]{2,1,0:T(8,128)S(1)}, u32[]{:S(2)}, u32[]{:S(2)}) collective-permute-start(f32[8,8,128]{2,1,0:T(8,128)S(1)} %get-tuple-element.79), channel_id=1, source_target_pairs={{0,2},{1,3},{2,0},{3,1},{4,6},{5,7},{6,4},{7,5},{8,10},{9,11},{10,... | collective-permute-start | bytes 98312 | tf_op jit(solution)/shard_map/ppermute | solution.py:19
  135.8 3.9 %collective-permute-start.24 = (f32[8,8,128]{2,1,0:T(8,128)S(1)}, f32[8,8,128]{2,1,0:T(8,128)S(1)}, u32[]{:S(2)}, u32[]{:S(2)}) collective-permute-start(f32[8,8,128]{2,1,0:T(8,128)S(1)} %get-tuple-element.80), channel_id=1, source_target_pairs={{0,3},{1,0},{2,1},{3,2},{4,7},{5,4},{6,5},{7,6},{8,11},{9,8},{10,9... | collective-permute-start | bytes 98312 | tf_op jit(solution)/shard_map/ppermute | solution.py:19

commit v4 on v3

--- a/solution.py
+++ b/solution.py
@@ -165,9 +165,7 @@
     return total + jnp.dot(c_high, w_low, preferred_element_type=jnp.float32)
 
 
-def product_kernel(
-    near, away, place_ref, c_hbm, l_ref, first_ref, second_ref, keep_ref, acc_ref, c_ref, sems
-):
+def product_kernel(place_ref, c_hbm, l_ref, o0_ref, o1_ref, o2_ref, o3_ref, acc_ref, c_ref, sems):
     leaves, listed, width, _ = c_hbm.shape
     slots, group = c_ref.shape[0], c_ref.shape[1]
     steps = leaves // group
@@ -204,12 +202,13 @@
         return carry
 
     lax.fori_loop(0, steps, body, 0)
-    first_ref[...] = acc_ref[:near]
-    second_ref[...] = acc_ref[near:away]
-    keep_ref[...] = acc_ref[away : 2 * away]
-
-
-def weighted_sums(place, blocks, packed, near, away):
+    at = 0
+    for ref in (o0_ref, o1_ref, o2_ref, o3_ref):
+        ref[...] = acc_ref[at : at + ref.shape[0]]
+        at += ref.shape[0]
+
+
+def weighted_sums(place, blocks, packed, parts):
     leaves, listed, width, rank = blocks.shape
     top = width // 2
     group, slots = 4, 4
@@ -219,34 +218,29 @@
         return jax.ShapeDtypeStruct((rows, top, 2 * rank), jnp.float32)
 
     return pl.pallas_call(
-        functools.partial(product_kernel, near, away),
+        product_kernel,
         in_specs=[
             pl.BlockSpec(memory_space=pltpu.SMEM),
-            pl.BlockSpec(memory_space=pl.ANY),
+            pl.BlockSpec(memory_space=pltpu.HBM),
             vmem,
         ],
-        out_specs=(vmem, vmem, vmem),
+        out_specs=(vmem,) * len(parts),
         scratch_shapes=[
-            pltpu.VMEM((2 * away + TILE, top, 2 * rank), jnp.float32),
+            pltpu.VMEM((sum(parts) + TILE, top, 2 * rank), jnp.float32),
             pltpu.VMEM((slots, group, listed, width, rank), jnp.float32),
             pltpu.SemaphoreType.DMA((slots,)),
         ],
-        out_shape=(out(near), out(away - near), out(away)),
-        compiler_params=pltpu.CompilerParams(vmem_limit_bytes=32 * 2**20),
+        out_shape=tuple(out(rows) for rows in parts),
+        compiler_params=pltpu.CompilerParams(vmem_limit_bytes=24 * 2**20),
         name="weighted_sums",
     )(place, blocks, packed)
 
 
-def pack_kernel(
-    cut, me_ref, y_ref, up_ref, down_ref, far_ref, two_ref, six_ref,
-    z_ref, r1_ref, r2_ref, r3_ref, o0_ref, o1_ref, o2_ref, o3_ref, g_ref, m_ref,
-):
+def pack_kernel(me_ref, y_ref, z_ref, o0_ref, o1_ref, o2_ref, o3_ref, g_ref, m_ref):
     slots = g_ref.shape[0]
-    rest = slots - cut
-    g_ref[:cut] = (
-        y_ref[7 * cut :] + up_ref[cut:] + down_ref[cut:] + far_ref[...] + two_ref[...] + six_ref[...]
-    )
-    g_ref[cut:] = z_ref[:rest] + r1_ref[...] + r2_ref[...] + r3_ref[...]
+    cut = y_ref.shape[1]
+    g_ref[:cut] = jnp.sum(y_ref[...], axis=0)
+    g_ref[cut:] = jnp.sum(z_ref[...], axis=0)
     chunks = m_ref.shape[0]
     piece = RANK // chunks
     batch = 2 * RANK // piece
@@ -260,13 +254,14 @@
         o_ref[...] = m_ref[lax.rem(me_ref[0] + step, chunks)]
 
 
-def pack(me, cut, slots, arrays):
+def pack(me, *arrays):
     vmem = pl.BlockSpec(memory_space=pltpu.VMEM)
-    top, lanes = arrays[0].shape[1:]
+    slots = sum(array.shape[1] for array in arrays)
+    top, lanes = arrays[0].shape[2:]
     tiles = slots * RANK // 4 * top * 2 // (top * lanes)
     message = jax.ShapeDtypeStruct((tiles, top, lanes), jnp.float32)
     return pl.pallas_call(
-        functools.partial(pack_kernel, cut),
+        pack_kernel,
         in_specs=[pl.BlockSpec(memory_space=pltpu.SMEM)] + [vmem] * len(arrays),
         out_specs=(vmem,) * 4,
         out_shape=(message,) * 4,
@@ -310,33 +305,6 @@
         compiler_params=pltpu.CompilerParams(vmem_limit_bytes=16 * 2**20),
         name="left_factor",
     )(me, packed, *messages)
-
-
-class Plan:
-    def __init__(self, n_y, n_z, slots):
-        self.cut = 9 * slots // 16
-        self.rest = slots - self.cut
-        self.order = (3, 1, 5, 7, 4, 2, 6, 0)
-        self.spot = tuple(self.order.index(r) for r in range(n_z))
-        self.y_rows = n_z * self.cut
-        self.z_rows = n_y * self.rest
-        self.base = {}
-        at = 0
-        for group in ("y2", "z4", "y1", "y3", "z3", "z1", "z5", "z7", "z2", "z6", "y0", "z0"):
-            if group == "y1":
-                self.near = at
-            self.base[group] = at
-            at += self.y_rows if group[0] == "y" else self.z_rows
-        self.total = at
-        self.n_y, self.n_z = n_y, n_z
-
-    def rows(self, rel_y, rel_z, slot):
-        base_y = sum(jnp.where(rel_y == r, self.base["y%d" % r], 0) for r in range(self.n_y))
-        base_z = sum(jnp.where(rel_z == r, self.base["z%d" % r], 0) for r in range(self.n_z))
-        spot = sum(jnp.where(rel_z == r, self.spot[r], 0) for r in range(self.n_z))
-        by_y = base_y + spot * self.cut + slot
-        by_z = base_z + rel_y * self.rest + slot - self.cut
-        return jnp.where(slot < self.cut, by_y, by_z)
 
 
 def tie(*values):
@@ -365,94 +333,59 @@
 
     blocks = coupling[0]
     listed = blocks.shape[1]
-    plan = Plan(n_y, n_z, leaves)
+    cut = 21 * leaves // 32
+    rest = leaves - cut
+    cells = n_y * n_z
     dest = row_device[0, :, :, 0]
     valid = jnp.arange(listed, dtype=jnp.int32)[None, :] < block_count[0][:, None]
-    rel_z = (dest // n_core - lax.axis_index("z")) % n_z
-    rel_y = (dest // (n_core * n_z) - lax.axis_index("y")) % n_y
-    place = plan.rows(rel_y, rel_z, row_slot[0])
-    place = place + jnp.where(dest % n_core == core, plan.total, 0)
-    place = jnp.where(valid, place, 2 * plan.total).reshape(-1).astype(jnp.int32)
+    to_core = dest % n_core
+    to_z = (dest // n_core) % n_z
+    to_y = dest // (n_core * n_z)
+    slot = row_slot[0]
+    by_z = (to_z * n_y + to_y) * rest + slot - cut
+    by_y = cells * rest + (to_y * n_z + to_z) * cut + slot
+    place = jnp.where(slot < cut, by_y, by_z)
+    place = place + jnp.where(to_core == core, cells * leaves, 0)
+    place = jnp.where(valid, place, n_core * cells * leaves).reshape(-1).astype(jnp.int32)
 
     pieces = lax.all_to_all(local, "rk", split_axis=0, concat_axis=0, tiled=True)
     moves = lax.dynamic_slice_in_dim(leaf_transfer[0], rank_index * share, share, 0)
     mine = leaf_factors(pieces.reshape(n_rank, share, width, points), moves)
     packed = lax.all_gather(mine, "rk", axis=0, tiled=False)
 
-    first, second, keep = weighted_sums(place, blocks, packed, plan.near, plan.total)
-    first = swap(first, "core", 1)
-    second = swap(second, "core", 1)
-    near = plan.near
-
-    def part(group, count=1, skip=0, rows=None):
-        size = (plan.y_rows if group[0] == "y" else plan.z_rows) * count if rows is None else rows
-        at = plan.base[group] + skip
-        other = first[at : at + size] if at < near else second[at - near : at - near + size]
-        return keep[at : at + size] + other
+    away_z, away_y, keep_z, keep_y = weighted_sums(
+        place, blocks, packed, (cells * rest, cells * cut) * 2
+    )
+    away_z = swap(away_z, "core", 1)
+    away_y = swap(away_y, "core", 1)
+
+    def exchange(value, axis):
+        return lax.all_to_all(value, axis, split_axis=0, concat_axis=0, tiled=True)
 
     def level_term(level, transfer):
         moved = jnp.dot(level, transfer, precision=HIGHEST)
         return jnp.dot(transfer.T, moved, precision=HIGHEST)
 
-    rows = plan.z_rows
-    half = rows // 2
-    y_far, z_up2, z_down2, z_up, z_down, y_up, y_down, terms = tie(
-        part("y2"),
-        part("z4", rows=half),
-        part("z4", skip=half, rows=half),
-        part("z3", 2),
-        part("z5", 2),
-        part("y1"),
-        part("y3"),
-        packed[:, share],
-    )
-    y_far = shift(y_far, "y", 2)
-    z_up2 = shift(z_up2, "z", 2)
-    z_down2 = shift(z_down2, "z", -2)
-    z_up = shift(z_up, "z", 1)
-    z_down = shift(z_down, "z", -1)
+    tail = away_z.shape[1:]
+    by_z = (keep_z + away_z).reshape((n_z, n_y, rest) + tail)
+    by_y = (keep_y + away_y).reshape((n_y, n_z, cut) + tail)
+    by_z, by_y, terms = tie(by_z, by_y, packed[:, share])
+    by_z = exchange(by_z, "z")
+    by_y = exchange(by_y, "y")
     grams = [unpacked(jnp.sum(terms, axis=0))]
-    term = level_term(grams[0], node_transfer[0])
-    other = swap(term, "core", 1)
-
-    y_far, z_up2, z_down2, z_up, z_down, y_up, y_down, other = tie(
-        y_far, z_up2, z_down2, z_up, z_down, y_up, y_down, other
-    )
-    z_two = part("z2") + z_up[:rows] + jnp.pad(z_up2, ((0, half), (0, 0), (0, 0)))
-    z_six = part("z6") + z_down[:rows] + jnp.pad(z_down2, ((half, 0), (0, 0), (0, 0)))
-    y_up, y_down, z_two, z_six, other = tie(y_up, y_down, z_two, z_six, other)
-    y_up = shift(y_up, "y", 1)
-    y_down = shift(y_down, "y", -1)
-    z_two = shift(z_two, "z", 2)
-    z_six = shift(z_six, "z", -2)
-    grams.append(term + other)
-    term = level_term(grams[1], pair_transfer[0])
-    other = swap(term, "z", 1)
-
-    y_up, y_down, z_two, z_six, other = tie(y_up, y_down, z_two, z_six, other)
-    by_y = part("y0") + y_far + y_up + y_down
-    by_z = part("z0") + z_up[rows:] + z_down[rows:] + z_two + z_six
-    cut, rest = plan.cut, plan.rest
-    by_y, by_z, other = tie(by_y, by_z, other)
-    up = shift(by_y[: 2 * cut], "z", 1)
-    down = shift(by_y[2 * cut : 4 * cut], "z", -1)
-    far = shift(by_y[4 * cut : 5 * cut], "z", 4)
-    r1 = shift(by_z[rest : 2 * rest], "y", 1)
-    r2 = shift(by_z[2 * rest : 3 * rest], "y", 2)
-    r3 = shift(by_z[3 * rest :], "y", -1)
-    grams.append(term + other)
-    term = level_term(grams[2], quad_transfer[0])
-    other = swap(term, "z", 2)
-
-    up, down, other = tie(up, down, other)
-    two = shift(by_y[5 * cut : 6 * cut] + up[:cut], "z", 2)
-    six = shift(by_y[6 * cut : 7 * cut] + down[:cut], "z", -2)
-    grams.append(term + other)
-    nodes = node_lower(jnp.stack(grams))
-
-    messages = pack(
-        me, cut, leaves, (by_y, up, down, far, two, six, by_z, r1, r2, r3)
-    )
+    for (axis, mask), transfer in zip(
+        (("core", 1), ("z", 1), ("z", 2)), (node_transfer[0], pair_transfer[0], quad_transfer[0])
+    ):
+        term = level_term(grams[-1], transfer)
+        grams.append(term + swap(term, axis, mask))
+
+    by_z, by_y, grams = tie(by_z, by_y, jnp.stack(grams))
+    by_z = exchange(jnp.sum(by_z, axis=0), "y")
+    by_y = exchange(jnp.sum(by_y, axis=0), "z")
+    nodes = node_lower(grams)
+    by_z, by_y = tie(by_z, by_y)
+
+    messages = pack(me, by_y, by_z)
     arrived = [messages[0]] + [shift(messages[s], "rk", s) for s in range(1, n_rank)]
     coupled = final(me, packed, arrived, leaves)
 

time: 144 us -> 184 us (1.28)
  blocking collectives: 13.1 us -> 51.2 us
  waiting for transfers between devices: 35.2 us -> 61.3 us
  starting transfers between devices: 44.8 us -> 32.8 us
  other arithmetic: 14.1 us -> 7.43 us
  local copies, waits for them, and re-layouts: 9.14 us -> 6.51 us
    all_to_all x0 -> x1, blocking collectives: none -> 38.1 us  [exchange(): return lax.all_to_all(value, axis, split_axis=0, concat_axis=0, tiled=True)]
    ppermute x20 -> x3, starting transfers between devices: 35.2 us -> 4.17 us  [shift(): lax.ppermute(value, axis, [(i, (i + step) % size) for i in range(size)])]
    ppermute x5, waiting for transfers between devices: 15.7 us -> 37.8 us  [swap(): lax.ppermute(value, axis, [(i, i ^ mask) for i in range(lax.axis_size(axi...]
    all_to_all x0 -> x3, starting transfers between devices: none -> 20.3 us  [exchange(): return lax.all_to_all(value, axis, split_axis=0, concat_axis=0, tiled=True)]
    all_to_all x0 -> x3, waiting for transfers between devices: none -> 15.4 us  [exchange(): return lax.all_to_all(value, axis, split_axis=0, concat_axis=0, tiled=True)]
    ppermute x20 -> x3, waiting for transfers between devices: 13.7 us -> 2.35 us  [shift(): lax.ppermute(value, axis, [(i, (i + step) % size) for i in range(size)])]
    add x7 -> x2, other arithmetic: 11.8 us -> 1.54 us  [the longest x1 1.26 us: shards(): by_z = (keep_z + away_z).reshape((n_z, n_y, rest) + tail)]
    reduce_sum x0 -> x2, other arithmetic: none -> 3.6 us  [the longest x1 2.84 us: shards(): by_y = exchange(jnp.sum(by_y, axis=0), 'z')]
  transfers between devices with their start and end apart: 26 -> 12, of which waited for: 8 -> 10; matrix products, arithmetic and copies ran while one was open for 6% -> 6% of each run, Pallas kernels for 3% -> 2%
where the time goes in v4:
time: 184 us; the launch traced here: 183 us
  waiting for transfers between devices  61.3 us (33%)
  blocking collectives  51.2 us (28%)
  starting transfers between devices  32.8 us (18%)
  Pallas kernels  21.4 us (12%)
  other arithmetic  7.43 us (4%)
  local copies, waits for them, and re-layouts  6.51 us (4%)
    all_to_all x1, blocking collectives, exchange(): return lax.all_to_all(value, axis, split_axis=0, concat_axis=0, tiled=True)  38.1 us
    ppermute x5, waiting for transfers between devices, swap(): lax.ppermute(value, axis, [(i, i ^ mask) for i in range(lax.axis_size(axi...  37.8 us
    all_to_all x3, starting transfers between devices, exchange(): return lax.all_to_all(value, axis, split_axis=0, concat_axis=0, tiled=True)  20.3 us
    all_to_all x3, waiting for transfers between devices, exchange(): return lax.all_to_all(value, axis, split_axis=0, concat_axis=0, tiled=True)  15.4 us
    all_gather x1, blocking collectives, shards(): packed = lax.all_gather(mine, 'rk', axis=0, tiled=False)  13.1 us
    pallas_call x1, Pallas kernels, weighted_sums(): pl.pallas_call(product_kernel, in_specs=[pl.BlockSpec(memory_space=pltpu....  10 us
    all_to_all x1, waiting for transfers between devices, shards(): lax.all_to_all(local, 'rk', split_axis=0, concat_axis=0, tiled=True)  5.82 us
    pallas_call x1, Pallas kernels, leaf_factors(): pl.pallas_call(leaf_kernel, out_shape=jax.ShapeDtypeStruct((leaves + 1, R...  5.19 us
  transfers between devices with their start and end apart: 12, of which 10 were waited for; matrix products, arithmetic and copies ran while one was open for 6% of the time, Pallas kernels for 2%

profile of v4, /device:TPU:32, one launch (start us, length us, event | category | flops | bytes accessed | tf_op | source)
XLA Modules:
  0.0 182.7 jit_solution(12181008097376556469)
XLA Ops:
  0.6 4.4 %all-to-all-start = ((f32[32,16,256]{2,1,0:T(8,128)}), f32[32,16,256]{2,1,0:T(8,128)S(1)}, u32[]{:S(2)}, u32[]{:S(2)}) async-start(f32[32,16,256]{2,1,0:T(8,128)} %bitcast.69), calls=%async_computation | async-start | bytes 1048576 | tf_op jit(solution)/shard_map/all_to_all | solution.py:351
  5.1 0.7 iota_compare_fusion
  5.9 0.8 squeeze.26
  6.7 0.5 broadcast.69
  7.2 1.4 reduce.3
  8.7 5.8 %all-to-all-done = f32[32,16,256]{2,1,0:T(8,128)S(1)} async-done(((f32[32,16,256]{2,1,0:T(8,128)}), f32[32,16,256]{2,1,0:T(8,128)S(1)}, u32[]{:S(2)}, u32[]{:S(2)}) %all-to-all-start) | async-done | bytes 524320 | tf_op jit(solution)/shard_map/all_to_all | solution.py:351
  14.6 5.2 %leaf_factors.1 = f32[9,32,128]{2,1,0:T(8,128)S(1)} custom-call(f32[4,8,16,256]{3,2,1,0:T(8,128)S(1)} %bitcast.66, f32[8,64,64]{2,1,0:T(8,128)S(1)} %dynamic-slice_bitcast_fusion.1.move_ref), custom_call_target="tpu_custom_call" | custom-call | tf_op jit(solution)/shard_map/leaf_factors/pallas_call | solution.py:103
  19.8 13.1 %all-gather = f32[36,32,128]{2,1,0:T(8,128)S(1)} all-gather(f32[9,32,128]{2,1,0:T(8,128)S(1)} %leaf_factors.1), channel_id=2, replica_groups=mesh['y'=4,'z'=8,'core'=2,'rk'=4] {'rk'}, dimensions={0}, use_global_device_ids=true | all-gather | bytes 737280 | tf_op jit(solution)/shard_map/all_gather | solution.py:354
  32.9 3.4 %copy-done.1 = f32[1,32,32,16,64]{4,3,2,1,0:T(8,128)S(1)} copy-done((f32[1,32,32,16,64]{4,3,2,1,0:T(8,128)S(1)}, f32[1,32,32,16,64]{4,3,2,1,0:T(8,128)}, u32[]{:S(2)}) %copy-start.1) | copy-done | bytes 4194328
  36.2 10.0 %weighted_sums.1 = (f32[352,8,128]{2,1,0:T(8,128)S(1)}, f32[672,8,128]{2,1,0:T(8,128)S(1)}, f32[352,8,128]{2,1,0:T(8,128)S(1)}, f32[672,8,128]{2,1,0:T(8,128)S(1)}) custom-call(s32[1024]{0:T(1024)S(1)} %add_select_fusion.4.place_ref, f32[32,32,16,64]{3,2,1,0:T(8,128)S(1)} %bitcast.65, f32[4,9,32,128]{3,2,1,0:T(8,128)S(1)} %bitcast.61), custom_call_target="tpu_custom_call" | custom-call | tf_op jit(solution)/shard_map/weighted_sums/pallas_call | solution.py:220
  46.3 0.1 collective-permute-start.1
  46.4 0.5 collective-permute-start
  46.9 6.6 %collective-permute-done = f32[352,8,128]{2,1,0:T(8,128)S(1)} collective-permute-done((f32[352,8,128]{2,1,0:T(8,128)S(1)}, f32[352,8,128]{2,1,0:T(8,128)S(1)}, u32[]{:S(2)}, u32[]{:S(2)}) %collective-permute-start) | collective-permute-done | bytes 1441824 | tf_op jit(solution)/shard_map/ppermute | solution.py:23
  53.5 1.3 add.78
  54.8 0.3 add.79
  55.1 38.1 %all_to_all.25 = f32[4,8,21,8,128]{4,3,2,1,0:T(8,128)} all-to-all(f32[4,8,21,8,128]{4,3,2,1,0:T(8,128)S(1)} %bitcast.67), channel_id=1, replica_groups=mesh['y'=4,'z'=8,'core'=2,'rk'=4] {'y'}, dimensions={0} | all-to-all | bytes 5505024 | tf_op jit(solution)/shard_map/all_to_all | solution.py:363
  93.2 8.6 %all-to-all-start.1 = ((f32[8,4,11,8,128]{4,3,2,1,0:T(8,128)}), f32[8,4,11,8,128]{4,3,2,1,0:T(8,128)S(1)}, u32[]{:S(2)}, u32[]{:S(2)}) async-start(f32[8,4,11,8,128]{4,3,2,1,0:T(8,128)} %bitcast.10), calls=%async_computation.1 | async-start | bytes 2883584 | tf_op jit(solution)/shard_map/all_to_all | solution.py:363
  101.9 0.2 fusion.7
  102.1 0.2 convolution_bitcast_fusion.2
  102.3 0.1 collective-permute-start.2
  102.4 1.2 collective-permute-done.2
  103.6 0.2 fusion.4
  103.8 0.2 convolution_bitcast_fusion.1
  104.0 0.1 collective-permute-start.3
  104.1 28.0 %collective-permute-done.3 = f32[64,64]{1,0:T(8,128)S(1)} collective-permute-done((f32[64,64]{1,0:T(8,128)S(1)}, f32[64,64]{1,0:T(8,128)S(1)}, u32[]{:S(2)}, u32[]{:S(2)}) %collective-permute-start.3) | collective-permute-done | bytes 16416 | tf_op jit(solution)/shard_map/ppermute | solution.py:23
  132.2 0.2 fusion.1
  132.4 0.2 convolution_bitcast_fusion
  132.6 3.2 %collective-permute-start.4 = (f32[64,64]{1,0:T(8,128)S(1)}, f32[64,64]{1,0:T(8,128)S(1)}, u32[]{:S(2)}, u32[]{:S(2)}) collective-permute-start(f32[64,64]{1,0:T(8,128)S(1)} %convolution_bitcast_fusion), channel_id=1, source_target_pairs={{0,16},{8,24},{16,0},{24,8},{32,48},{40,56},{48,32},{56,40},{1,17}... | collective-permute-start | bytes 49160 | tf_op jit(solution)/shard_map/ppermute | solution.py:23
  135.8 1.9 %collective-permute-done.4 = f32[64,64]{1,0:T(8,128)S(1)} collective-permute-done((f32[64,64]{1,0:T(8,128)S(1)}, f32[64,64]{1,0:T(8,128)S(1)}, u32[]{:S(2)}, u32[]{:S(2)}) %collective-permute-start.4) | collective-permute-done | bytes 16416 | tf_op jit(solution)/shard_map/ppermute | solution.py:23
  137.7 0.8 reduce_sum.28
  138.4 3.4 %all-to-all-start.3 = ((f32[4,11,8,128]{3,2,1,0:T(8,128)}), f32[4,11,8,128]{3,2,1,0:T(8,128)S(1)}, u32[]{:S(2)}, u32[]{:S(2)}) async-start(f32[4,11,8,128]{3,2,1,0:T(8,128)} %reduce_sum.28), calls=%async_computation.3 | async-start | bytes 360448 | tf_op jit(solution)/shard_map/all_to_all | solution.py:363
  141.8 2.8 %reduce_sum.29 = f32[8,21,8,128]{3,2,1,0:T(8,128)} reduce(f32[4,8,21,8,128]{4,3,2,1,0:T(8,128)} %all_to_all.25, f32[]{:T(128)} %constant.79.clone.1), dimensions={0}, to_apply=%region_2.3 | reduce | flops 516096 | bytes 3440644 | tf_op jit(solution)/shard_map/reduce_sum | solution.py:384
  144.6 3.4 %all-to-all-done.3.z_ref = f32[4,11,8,128]{3,2,1,0:T(8,128)S(1)} async-done(((f32[4,11,8,128]{3,2,1,0:T(8,128)}), f32[4,11,8,128]{3,2,1,0:T(8,128)S(1)}, u32[]{:S(2)}, u32[]{:S(2)}) %all-to-all-start.3) | async-done | bytes 180256 | tf_op jit(solution)/shard_map/all_to_all | solution.py:363
  148.0 8.3 %all-to-all-start.4 = ((f32[8,21,8,128]{3,2,1,0:T(8,128)}), f32[8,21,8,128]{3,2,1,0:T(8,128)S(1)}, u32[]{:S(2)}, u32[]{:S(2)}) async-start(f32[8,21,8,128]{3,2,1,0:T(8,128)} %reduce_sum.29), calls=%async_computation.4 | async-start | bytes 1376256 | tf_op jit(solution)/shard_map/all_to_all | solution.py:363
  156.3 0.2 fusion.18
  156.6 0.1 pad_maximum_fusion
  156.7 0.7 dynamic-slice_bitcast_fusion
  157.4 4.1 %node_factors.1 = f32[4,64,64]{2,1,0:T(8,128)S(1)} custom-call(f32[4,64,64]{2,1,0:T(8,128)S(1)} %pad_maximum_fusion.1.g_ref), custom_call_target="tpu_custom_call" | custom-call | tf_op jit(solution)/shard_map/node_factors/pallas_call | solution.py:125
  161.5 12.0 %all-to-all-done.4.y_ref = f32[8,21,8,128]{3,2,1,0:T(8,128)S(1)} async-done(((f32[8,21,8,128]{3,2,1,0:T(8,128)}), f32[8,21,8,128]{3,2,1,0:T(8,128)S(1)}, u32[]{:S(2)}, u32[]{:S(2)}) %all-to-all-start.4) | async-done | bytes 688160 | tf_op jit(solution)/shard_map/all_to_all | solution.py:363
  173.5 0.3 pack.1
  173.8 0.5 collective-permute-start.5
  174.4 2.7 %collective-permute-start.6 = (f32[8,8,128]{2,1,0:T(8,128)S(1)}, f32[8,8,128]{2,1,0:T(8,128)S(1)}, u32[]{:S(2)}, u32[]{:S(2)}) collective-permute-start(f32[8,8,128]{2,1,0:T(8,128)S(1)} %get-tuple-element.33), channel_id=1, source_target_pairs={{0,2},{1,3},{2,0},{3,1},{4,6},{5,7},{6,4},{7,5},{8,10},{9,11},{10,... | collective-permute-start | bytes 98312 | tf_op jit(solution)/shard_map/ppermute | solution.py:19
  177.1 0.9 collective-permute-start.7
  178.0 0.6 dynamic-slice_bitcast_fusion.2
  178.6 0.4 collective-permute-done.5.m1_ref
  179.0 0.8 collective-permute-done.6.m2_ref
  179.8 1.2 collective-permute-done.7.m3_ref
  181.0 1.7 left_factor.1
  (23 shorter events, 0.4 us)
Async XLA Ops:
  0.6 8.1 %copy-start = (f32[1,32,64,64]{3,2,1,0:T(8,128)S(1)}, f32[1,32,64,64]{3,2,1,0:T(8,128)}, u32[]{:S(2)}) copy-start(f32[1,32,64,64]{3,2,1,0:T(8,128)} %param.10) | copy-start | bytes 1572868
  0.6 13.9 %all-to-all-start = ((f32[32,16,256]{2,1,0:T(8,128)}), f32[32,16,256]{2,1,0:T(8,128)S(1)}, u32[]{:S(2)}, u32[]{:S(2)}) async-start(f32[32,16,256]{2,1,0:T(8,128)} %bitcast.69), calls=%async_computation | async-start | bytes 1048576 | tf_op jit(solution)/shard_map/all_to_all | solution.py:351
  32.9 3.4 %copy-start.1 = (f32[1,32,32,16,64]{4,3,2,1,0:T(8,128)S(1)}, f32[1,32,32,16,64]{4,3,2,1,0:T(8,128)}, u32[]{:S(2)}) copy-start(f32[1,32,32,16,64]{4,3,2,1,0:T(8,128)} %param.14) | copy-start | bytes 12582916
  46.3 8.5 %collective-permute-start.1 = (f32[672,8,128]{2,1,0:T(8,128)S(1)}, f32[672,8,128]{2,1,0:T(8,128)S(1)}, u32[]{:S(2)}, u32[]{:S(2)}) collective-permute-start(f32[672,8,128]{2,1,0:T(8,128)S(1)} %get-tuple-element.22), channel_id=1, source_target_pairs={{0,4},{4,0},{1,5},{5,1},{2,6},{6,2},{3,7},{7,3},{8,12},{12,8},{9,1... | collective-permute-start | bytes 8257544 | tf_op jit(solution)/shard_map/ppermute | solution.py:23
  46.4 7.1 %collective-permute-start = (f32[352,8,128]{2,1,0:T(8,128)S(1)}, f32[352,8,128]{2,1,0:T(8,128)S(1)}, u32[]{:S(2)}, u32[]{:S(2)}) collective-permute-start(f32[352,8,128]{2,1,0:T(8,128)S(1)} %get-tuple-element.20), channel_id=1, source_target_pairs={{0,4},{4,0},{1,5},{5,1},{2,6},{6,2},{3,7},{7,3},{8,12},{12,8},{9,1... | collective-permute-start | bytes 4325384 | tf_op jit(solution)/shard_map/ppermute | solution.py:23
  93.2 8.7 %copy-start.2 = (f32[1,64,64]{2,1,0:T(8,128)S(1)}, f32[1,64,64]{2,1,0:T(8,128)}, u32[]{:S(2)}) copy-start(f32[1,64,64]{2,1,0:T(8,128)} %param.11) | copy-start | bytes 49156
  93.2 10.4 %copy-start.3 = (f32[1,64,64]{2,1,0:T(8,128)S(1)}, f32[1,64,64]{2,1,0:T(8,128)}, u32[]{:S(2)}) copy-start(f32[1,64,64]{2,1,0:T(8,128)} %param.12) | copy-start | bytes 49156
  93.2 39.0 %copy-start.4 = (f32[1,64,64]{2,1,0:T(8,128)S(1)}, f32[1,64,64]{2,1,0:T(8,128)}, u32[]{:S(2)}) copy-start(f32[1,64,64]{2,1,0:T(8,128)} %param.13) | copy-start | bytes 49156
  93.2 44.5 %all-to-all-start.1 = ((f32[8,4,11,8,128]{4,3,2,1,0:T(8,128)}), f32[8,4,11,8,128]{4,3,2,1,0:T(8,128)S(1)}, u32[]{:S(2)}, u32[]{:S(2)}) async-start(f32[8,4,11,8,128]{4,3,2,1,0:T(8,128)} %bitcast.10), calls=%async_computation.1 | async-start | bytes 2883584 | tf_op jit(solution)/shard_map/all_to_all | solution.py:363
  102.3 1.3 collective-permute-start.2
  104.0 28.2 %collective-permute-start.3 = (f32[64,64]{1,0:T(8,128)S(1)}, f32[64,64]{1,0:T(8,128)S(1)}, u32[]{:S(2)}, u32[]{:S(2)}) collective-permute-start(f32[64,64]{1,0:T(8,128)S(1)} %convolution_bitcast_fusion.1), channel_id=1, source_target_pairs={{0,8},{8,0},{16,24},{24,16},{32,40},{40,32},{48,56},{56,48},{1,9},... | collective-permute-start | bytes 49160 | tf_op jit(solution)/shard_map/ppermute | solution.py:23
  132.6 5.1 %collective-permute-start.4 = (f32[64,64]{1,0:T(8,128)S(1)}, f32[64,64]{1,0:T(8,128)S(1)}, u32[]{:S(2)}, u32[]{:S(2)}) collective-permute-start(f32[64,64]{1,0:T(8,128)S(1)} %convolution_bitcast_fusion), channel_id=1, source_target_pairs={{0,16},{8,24},{16,0},{24,8},{32,48},{40,56},{48,32},{56,40},{1,17}... | collective-permute-start | bytes 49160 | tf_op jit(solution)/shard_map/ppermute | solution.py:23
  138.4 9.6 %all-to-all-start.3 = ((f32[4,11,8,128]{3,2,1,0:T(8,128)}), f32[4,11,8,128]{3,2,1,0:T(8,128)S(1)}, u32[]{:S(2)}, u32[]{:S(2)}) async-start(f32[4,11,8,128]{3,2,1,0:T(8,128)} %reduce_sum.28), calls=%async_computation.3 | async-start | bytes 360448 | tf_op jit(solution)/shard_map/all_to_all | solution.py:363
  148.0 25.5 %all-to-all-start.4 = ((f32[8,21,8,128]{3,2,1,0:T(8,128)}), f32[8,21,8,128]{3,2,1,0:T(8,128)S(1)}, u32[]{:S(2)}, u32[]{:S(2)}) async-start(f32[8,21,8,128]{3,2,1,0:T(8,128)} %reduce_sum.29), calls=%async_computation.4 | async-start | bytes 1376256 | tf_op jit(solution)/shard_map/all_to_all | solution.py:363
  173.8 5.2 %collective-permute-start.5 = (f32[8,8,128]{2,1,0:T(8,128)S(1)}, f32[8,8,128]{2,1,0:T(8,128)S(1)}, u32[]{:S(2)}, u32[]{:S(2)}) collective-permute-start(f32[8,8,128]{2,1,0:T(8,128)S(1)} %get-tuple-element.32), channel_id=1, source_target_pairs={{0,1},{1,2},{2,3},{3,0},{4,5},{5,6},{6,7},{7,4},{8,9},{9,10},{10,1... | collective-permute-start | bytes 98312 | tf_op jit(solution)/shard_map/ppermute | solution.py:19
  174.4 5.4 %collective-permute-start.6 = (f32[8,8,128]{2,1,0:T(8,128)S(1)}, f32[8,8,128]{2,1,0:T(8,128)S(1)}, u32[]{:S(2)}, u32[]{:S(2)}) collective-permute-start(f32[8,8,128]{2,1,0:T(8,128)S(1)} %get-tuple-element.33), channel_id=1, source_target_pairs={{0,2},{1,3},{2,0},{3,1},{4,6},{5,7},{6,4},{7,5},{8,10},{9,11},{10,... | collective-permute-start | bytes 98312 | tf_op jit(solution)/shard_map/ppermute | solution.py:19
  177.1 3.9 %collective-permute-start.7 = (f32[8,8,128]{2,1,0:T(8,128)S(1)}, f32[8,8,128]{2,1,0:T(8,128)S(1)}, u32[]{:S(2)}, u32[]{:S(2)}) collective-permute-start(f32[8,8,128]{2,1,0:T(8,128)S(1)} %get-tuple-element.34), channel_id=1, source_target_pairs={{0,3},{1,0},{2,1},{3,2},{4,7},{5,4},{6,5},{7,6},{8,11},{9,8},{10,9... | collective-permute-start | bytes 98312 | tf_op jit(solution)/shard_map/ppermute | solution.py:19

commit v5 on v4

--- a/solution.py
+++ b/solution.py
@@ -233,14 +233,123 @@
         out_shape=tuple(out(rows) for rows in parts),
         compiler_params=pltpu.CompilerParams(vmem_limit_bytes=24 * 2**20),
         name="weighted_sums",
-    )(place, blocks, packed)
-
-
-def pack_kernel(me_ref, y_ref, z_ref, o0_ref, o1_ref, o2_ref, o3_ref, g_ref, m_ref):
+    )(place, pltpu.with_memory_space_constraint(blocks, pltpu.HBM), packed)
+
+
+class Plan:
+    def __init__(self, n_y, n_z, slots):
+        self.n_y, self.n_z = n_y, n_z
+        self.cut = 3 * slots // 8
+        self.rest = slots - self.cut
+        self.rows = {"y": n_z * self.cut, "z": n_y * self.rest}
+        self.base = {}
+        at = 0
+        for group in (
+            ("y", 2), ("z", 4), ("y", 1), ("y", 3), ("z", 3), ("z", 5), ("y", 0), ("z", 2),
+            ("z", 6), ("z", 1), ("z", 7), ("z", 0),
+        ):
+            if group == ("y", 1):
+                self.near = at
+            self.base[group] = at
+            at += self.rows[group[0]]
+        self.total = at
+
+    def places(self, rel_y, rel_z, slot):
+        base_y = sum(jnp.where(rel_y == r, self.base["y", r], 0) for r in range(self.n_y))
+        base_z = sum(jnp.where(rel_z == r, self.base["z", r], 0) for r in range(self.n_z))
+        by_y = base_y + rel_z * self.cut + slot
+        by_z = base_z + rel_y * self.rest + slot - self.cut
+        return jnp.where(slot < self.cut, by_y, by_z)
+
+    def part(self, ref, group):
+        at = self.base[group] - (0 if self.base[group] < self.near else self.near)
+        return ref[at : at + self.rows[group[0]]]
+
+
+def low_add(whole, extra):
+    rows = extra.shape[0]
+    return jnp.concatenate([whole[:rows] + extra, whole[rows:]], axis=0)
+
+
+def high_add(whole, extra):
+    rows = whole.shape[0] - extra.shape[0]
+    return jnp.concatenate([whole[:rows], whole[rows:] + extra], axis=0)
+
+
+def round1_kernel(plan, keep, swapped, y_up, y_down, z_up, z_down):
+    y = plan.part(keep, ("y", 2)) + plan.part(swapped, ("y", 2))
+    z = plan.part(keep, ("z", 4)) + plan.part(swapped, ("z", 4))
+    half = y.shape[0] // 2
+    y_up[...] = y[:half]
+    y_down[...] = y[half:]
+    half = z.shape[0] // 2
+    z_up[...] = z[:half]
+    z_down[...] = z[half:]
+
+
+def round2_kernel(plan, d, ry_up, ry_down, rz_up, rz_down, y_up, y_down, z_up, z_down):
+    y_up[...] = low_add(plan.part(d, ("y", 1)), ry_up[...])
+    y_down[...] = high_add(plan.part(d, ("y", 3)), ry_down[...])
+    z_up[...] = low_add(plan.part(d, ("z", 3)), rz_up[...])
+    z_down[...] = high_add(plan.part(d, ("z", 5)), rz_down[...])
+
+
+def round3_kernel(plan, d, ry_up, ry_down, rz_up, rz_down, ey, z_up, z_down):
+    ey[...] = plan.part(d, ("y", 0)) + ry_up[...] + ry_down[...]
+    rows, cut = plan.rows["z"], plan.cut
+    half = cut // 2
+    z_up[:rows] = plan.part(d, ("z", 2)) + rz_up[...]
+    z_up[rows:] = ey[4 * cut : 4 * cut + half]
+    z_down[:rows] = plan.part(d, ("z", 6)) + rz_down[...]
+    z_down[rows:] = ey[4 * cut + half : 5 * cut]
+
+
+def round4_kernel(plan, d, ey, rz_up, rz_down, z_up, z_down):
+    rows, cut = plan.rows["z"], plan.cut
+    z_up[:rows] = plan.part(d, ("z", 1)) + rz_up[:rows]
+    z_up[rows:] = low_add(ey[3 * cut : 4 * cut], rz_up[rows:])
+    z_down[:rows] = plan.part(d, ("z", 7)) + rz_down[:rows]
+    z_down[rows:] = high_add(ey[5 * cut : 6 * cut], rz_down[rows:])
+
+
+def round5_kernel(plan, d, ey, rz_up, rz_down, ez, y_up, y_down, z_up, z_down):
+    rows, cut, rest = plan.rows["z"], plan.cut, plan.rest
+    half = rest // 2
+    ez[...] = plan.part(d, ("z", 0)) + rz_up[:rows] + rz_down[:rows]
+    y_up[...] = ez[2 * rest : 2 * rest + half]
+    y_down[...] = ez[2 * rest + half : 3 * rest]
+    z_up[...] = ey[2 * cut : 3 * cut] + rz_up[rows:]
+    z_down[...] = ey[6 * cut : 7 * cut] + rz_down[rows:]
+
+
+def round6_kernel(plan, ey, ez, ry_up, ry_down, rz_up, rz_down, y_up, y_down, z_up, z_down):
+    cut, rest = plan.cut, plan.rest
+    y_up[...] = low_add(ez[rest : 2 * rest], ry_up[...])
+    y_down[...] = high_add(ez[3 * rest :], ry_down[...])
+    z_up[...] = ey[cut : 2 * cut] + rz_up[...]
+    z_down[...] = ey[7 * cut :] + rz_down[...]
+
+
+def run_round(kernel, plan, rows, *arrays):
+    vmem = pl.BlockSpec(memory_space=pltpu.VMEM)
+    tail = arrays[0].shape[1:]
+    return pl.pallas_call(
+        functools.partial(kernel, plan),
+        in_specs=[vmem] * len(arrays),
+        out_specs=(vmem,) * len(rows),
+        out_shape=tuple(jax.ShapeDtypeStruct((r,) + tail, jnp.float32) for r in rows),
+        compiler_params=pltpu.CompilerParams(vmem_limit_bytes=12 * 2**20),
+        name=kernel.__name__,
+    )(*arrays)
+
+
+def pack_kernel(
+    me_ref, ey, ez, ry_up, ry_down, rz_up, rz_down, o0_ref, o1_ref, o2_ref, o3_ref, g_ref, m_ref
+):
     slots = g_ref.shape[0]
-    cut = y_ref.shape[1]
-    g_ref[:cut] = jnp.sum(y_ref[...], axis=0)
-    g_ref[cut:] = jnp.sum(z_ref[...], axis=0)
+    cut = rz_up.shape[0]
+    g_ref[:cut] = ey[:cut] + rz_up[...] + rz_down[...]
+    g_ref[cut:] = ez[: slots - cut] + ry_up[...] + ry_down[...]
     chunks = m_ref.shape[0]
     piece = RANK // chunks
     batch = 2 * RANK // piece
@@ -256,8 +365,8 @@
 
 def pack(me, *arrays):
     vmem = pl.BlockSpec(memory_space=pltpu.VMEM)
-    slots = sum(array.shape[1] for array in arrays)
-    top, lanes = arrays[0].shape[2:]
+    slots = arrays[2].shape[0] + arrays[4].shape[0]
+    top, lanes = arrays[0].shape[1:]
     tiles = slots * RANK // 4 * top * 2 // (top * lanes)
     message = jax.ShapeDtypeStruct((tiles, top, lanes), jnp.float32)
     return pl.pallas_call(
@@ -333,65 +442,94 @@
 
     blocks = coupling[0]
     listed = blocks.shape[1]
-    cut = 21 * leaves // 32
-    rest = leaves - cut
-    cells = n_y * n_z
+    plan = Plan(n_y, n_z, leaves)
     dest = row_device[0, :, :, 0]
     valid = jnp.arange(listed, dtype=jnp.int32)[None, :] < block_count[0][:, None]
-    to_core = dest % n_core
-    to_z = (dest // n_core) % n_z
-    to_y = dest // (n_core * n_z)
-    slot = row_slot[0]
-    by_z = (to_z * n_y + to_y) * rest + slot - cut
-    by_y = cells * rest + (to_y * n_z + to_z) * cut + slot
-    place = jnp.where(slot < cut, by_y, by_z)
-    place = place + jnp.where(to_core == core, cells * leaves, 0)
-    place = jnp.where(valid, place, n_core * cells * leaves).reshape(-1).astype(jnp.int32)
+    rel_z = (dest // n_core - lax.axis_index("z")) % n_z
+    rel_y = (dest // (n_core * n_z) - lax.axis_index("y")) % n_y
+    place = plan.places(rel_y, rel_z, row_slot[0])
+    place = place + jnp.where(dest % n_core == core, plan.total, 0)
+    place = jnp.where(valid, place, n_core * plan.total).reshape(-1).astype(jnp.int32)
 
     pieces = lax.all_to_all(local, "rk", split_axis=0, concat_axis=0, tiled=True)
     moves = lax.dynamic_slice_in_dim(leaf_transfer[0], rank_index * share, share, 0)
     mine = leaf_factors(pieces.reshape(n_rank, share, width, points), moves)
     packed = lax.all_gather(mine, "rk", axis=0, tiled=False)
 
-    away_z, away_y, keep_z, keep_y = weighted_sums(
-        place, blocks, packed, (cells * rest, cells * cut) * 2
-    )
-    away_z = swap(away_z, "core", 1)
-    away_y = swap(away_y, "core", 1)
-
-    def exchange(value, axis):
-        return lax.all_to_all(value, axis, split_axis=0, concat_axis=0, tiled=True)
+    near, far = plan.near, plan.total - plan.near
+    away_near, away_far, keep_near, keep_far = weighted_sums(
+        place, blocks, packed, (near, far, near, far)
+    )
+    got_near = swap(away_near, "core", 1)
+    got_far = swap(away_far, "core", 1)
 
     def level_term(level, transfer):
         moved = jnp.dot(level, transfer, precision=HIGHEST)
         return jnp.dot(transfer.T, moved, precision=HIGHEST)
 
-    tail = away_z.shape[1:]
-    by_z = (keep_z + away_z).reshape((n_z, n_y, rest) + tail)
-    by_y = (keep_y + away_y).reshape((n_y, n_z, cut) + tail)
-    by_z, by_y, terms = tie(by_z, by_y, packed[:, share])
-    by_z = exchange(by_z, "z")
-    by_y = exchange(by_y, "y")
+    def along(axis, up, down):
+        return shift(up, axis, 1), shift(down, axis, -1)
+
+    def send(messages):
+        y_up, y_down, z_up, z_down = messages
+        return along("z", z_up, z_down) + along("y", y_up, y_down)
+
+    y_rows, z_rows, cut, rest = plan.rows["y"], plan.rows["z"], plan.cut, plan.rest
+    sent = run_round(
+        round1_kernel, plan, (y_rows // 2,) * 2 + (z_rows // 2,) * 2, keep_near, got_near
+    )
+    sent, terms = tie(sent, packed[:, share])
+    rz_up, rz_down, ry_up, ry_down = send(sent)
     grams = [unpacked(jnp.sum(terms, axis=0))]
-    for (axis, mask), transfer in zip(
-        (("core", 1), ("z", 1), ("z", 2)), (node_transfer[0], pair_transfer[0], quad_transfer[0])
-    ):
-        term = level_term(grams[-1], transfer)
-        grams.append(term + swap(term, axis, mask))
-
-    by_z, by_y, grams = tie(by_z, by_y, jnp.stack(grams))
-    by_z = exchange(jnp.sum(by_z, axis=0), "y")
-    by_y = exchange(jnp.sum(by_y, axis=0), "z")
-    nodes = node_lower(grams)
-    by_z, by_y = tie(by_z, by_y)
-
-    messages = pack(me, by_y, by_z)
+    term = level_term(grams[0], node_transfer[0])
+    other = swap(term, "core", 1)
+    d = keep_far + got_far
+    ry_up, ry_down, rz_up, rz_down, d, other = tie(ry_up, ry_down, rz_up, rz_down, d, other)
+
+    sent = run_round(
+        round2_kernel, plan, (y_rows,) * 2 + (z_rows,) * 2, d, ry_up, ry_down, rz_up, rz_down
+    )
+    sent, other = tie(sent, other)
+    rz_up, rz_down, ry_up, ry_down = send(sent)
+    grams.append(term + other)
+    term = level_term(grams[1], pair_transfer[0])
+    other = swap(term, "z", 1)
+    ry_up, ry_down, rz_up, rz_down, other = tie(ry_up, ry_down, rz_up, rz_down, other)
+
+    both = z_rows + cut // 2
+    ey, up, down = run_round(
+        round3_kernel, plan, (y_rows, both, both), d, ry_up, ry_down, rz_up, rz_down
+    )
+    up, down, other, lower = tie(up, down, other, packed[:, :share])
+    rz_up, rz_down = along("z", up, down)
+    grams.append(term + other)
+    term = level_term(grams[2], quad_transfer[0])
+    other = swap(term, "z", 2)
+    lower = unpacked(lower).reshape(leaves, RANK, RANK)
+    leaf_weights = lax.dynamic_slice_in_dim(lower, rank_index * width, width, 1)
+    rz_up, rz_down, other, leaf_weights = tie(rz_up, rz_down, other, leaf_weights)
+
+    both = z_rows + cut
+    up, down = run_round(round4_kernel, plan, (both, both), d, ey, rz_up, rz_down)
+    up, down, other = tie(up, down, other)
+    rz_up, rz_down = along("z", up, down)
+    grams.append(term + other)
+    nodes = node_lower(jnp.stack(grams))
+    node_weights = lax.dynamic_slice_in_dim(nodes, rank_index * width, width, 1)
+    rz_up, rz_down, node_weights = tie(rz_up, rz_down, node_weights)
+
+    ez, *sent = run_round(
+        round5_kernel, plan, (z_rows, rest // 2, rest // 2, cut, cut), d, ey, rz_up, rz_down
+    )
+    rz_up, rz_down, ry_up, ry_down = send(sent)
+    sent = run_round(
+        round6_kernel, plan, (rest, rest, cut, cut), ey, ez, ry_up, ry_down, rz_up, rz_down
+    )
+    rz_up, rz_down, ry_up, ry_down = send(sent)
+    messages = pack(me, ey, ez, ry_up, ry_down, rz_up, rz_down)
     arrived = [messages[0]] + [shift(messages[s], "rk", s) for s in range(1, n_rank)]
     coupled = final(me, packed, arrived, leaves)
 
-    lower = unpacked(packed[:, :share]).reshape(leaves, RANK, RANK)
-    node_weights = lax.dynamic_slice_in_dim(nodes, rank_index * width, width, 1)
-    leaf_weights = lax.dynamic_slice_in_dim(lower, rank_index * width, width, 1)
     return (
         jnp.swapaxes(leaf_weights, 1, 2)[None],
         jnp.swapaxes(node_weights, 1, 2)[:, None],

time: 184 us -> 133 us (0.72)
  blocking collectives: 51.2 us -> 13.1 us
  waiting for transfers between devices: 61.3 us -> 32 us
  starting transfers between devices: 32.8 us -> 46.4 us
  Pallas kernels: 21.4 us -> 24.5 us
    all_to_all x1 -> x0, blocking collectives: 38.1 us -> none  [exchange(): return lax.all_to_all(value, axis, split_axis=0, concat_axis=0, tiled=True)]
    ppermute x3 -> x23, starting transfers between devices: 4.17 us -> 34.1 us  [shift(): lax.ppermute(value, axis, [(i, (i + step) % size) for i in range(size)])]
    ppermute x5, waiting for transfers between devices: 37.8 us -> 16.1 us  [swap(): lax.ppermute(value, axis, [(i, i ^ mask) for i in range(lax.axis_size(axi...]
    all_to_all x3 -> x0, starting transfers between devices: 20.3 us -> none  [exchange(): return lax.all_to_all(value, axis, split_axis=0, concat_axis=0, tiled=True)]
    all_to_all x3 -> x0, waiting for transfers between devices: 15.4 us -> none  [exchange(): return lax.all_to_all(value, axis, split_axis=0, concat_axis=0, tiled=True)]
    ppermute x3 -> x23, waiting for transfers between devices: 2.35 us -> 10 us  [shift(): lax.ppermute(value, axis, [(i, (i + step) % size) for i in range(size)])]
    ppermute x5, starting transfers between devices: 3.93 us -> 7.88 us  [swap(): lax.ppermute(value, axis, [(i, i ^ mask) for i in range(lax.axis_size(axi...]
    reduce_sum x2 -> x0, other arithmetic: 3.6 us -> none  [the longest x1 2.84 us: shards(): by_y = exchange(jnp.sum(by_y, axis=0), 'z')]
  transfers between devices with their start and end apart: 12 -> 29, of which waited for: 10 -> 12; matrix products, arithmetic and copies ran while one was open for 6% -> 9% of each run, Pallas kernels for 2% -> 4%
where the time goes in v5:
time: 133 us; the launch traced here: 131 us
  starting transfers between devices  46.4 us (35%)
  waiting for transfers between devices  32 us (24%)
  Pallas kernels  24.5 us (18%)
  blocking collectives  13.1 us (10%)
  local copies, waits for them, and re-layouts  5.77 us (4%)
  other arithmetic  5.7 us (4%)
  matrix products  2.71 us (2%)
    ppermute x23, starting transfers between devices, shift(): lax.ppermute(value, axis, [(i, (i + step) % size) for i in range(size)])  34.1 us
    ppermute x5, waiting for transfers between devices, swap(): lax.ppermute(value, axis, [(i, i ^ mask) for i in range(lax.axis_size(axi...  16.1 us
    all_gather x1, blocking collectives, shards(): packed = lax.all_gather(mine, 'rk', axis=0, tiled=False)  13.1 us
    pallas_call x1, Pallas kernels, weighted_sums(): pl.pallas_call(product_kernel, in_specs=[pl.BlockSpec(memory_space=pltpu....  11.8 us
    ppermute x23, waiting for transfers between devices, shift(): lax.ppermute(value, axis, [(i, (i + step) % size) for i in range(size)])  10 us
    ppermute x5, starting transfers between devices, swap(): lax.ppermute(value, axis, [(i, i ^ mask) for i in range(lax.axis_size(axi...  7.88 us
    all_to_all x1, waiting for transfers between devices, shards(): lax.all_to_all(local, 'rk', split_axis=0, concat_axis=0, tiled=True)  5.82 us
    pallas_call x1, Pallas kernels, leaf_factors(): pl.pallas_call(leaf_kernel, out_shape=jax.ShapeDtypeStruct((leaves + 1, R...  5.19 us
  transfers between devices with their start and end apart: 29, of which 12 were waited for; matrix products, arithmetic and copies ran while one was open for 9% of the time, Pallas kernels for 4%

profile of v5, /device:TPU:32, one launch (start us, length us, event | category | flops | bytes accessed | tf_op | source)
XLA Modules:
  0.0 131.0 jit_solution(1756846107426283525)
XLA Ops:
  0.6 4.4 %all-to-all-start = ((f32[32,16,256]{2,1,0:T(8,128)}), f32[32,16,256]{2,1,0:T(8,128)S(1)}, u32[]{:S(2)}, u32[]{:S(2)}) async-start(f32[32,16,256]{2,1,0:T(8,128)} %bitcast.64), calls=%async_computation | async-start | bytes 1048576 | tf_op jit(solution)/shard_map/all_to_all | solution.py:454
  5.1 0.7 iota_compare_fusion
  5.9 0.8 squeeze.25
  6.7 0.5 broadcast.120
  7.2 1.4 %reduce.3 = s32[32,32]{1,0:T(8,128)S(1)} reduce(s32[1,32,32,1]{2,3,1,0:T(1,128)} %param.15, s32[]{:T(128)} %broadcast.120), dimensions={0,3}, to_apply=%param.15.reduce_sub_computation.3 | reduce | bytes 8196 | tf_op args[6]
  8.7 5.8 %all-to-all-done = f32[32,16,256]{2,1,0:T(8,128)S(1)} async-done(((f32[32,16,256]{2,1,0:T(8,128)}), f32[32,16,256]{2,1,0:T(8,128)S(1)}, u32[]{:S(2)}, u32[]{:S(2)}) %all-to-all-start) | async-done | bytes 524320 | tf_op jit(solution)/shard_map/all_to_all | solution.py:454
  14.6 5.2 %leaf_factors.1 = f32[9,32,128]{2,1,0:T(8,128)S(1)} custom-call(f32[4,8,16,256]{3,2,1,0:T(8,128)S(1)} %bitcast.61, f32[8,64,64]{2,1,0:T(8,128)S(1)} %dynamic-slice_bitcast_fusion.move_ref), custom_call_target="tpu_custom_call" | custom-call | tf_op jit(solution)/shard_map/leaf_factors/pallas_call | solution.py:103
  19.8 13.1 %all-gather = f32[36,32,128]{2,1,0:T(8,128)S(1)} all-gather(f32[9,32,128]{2,1,0:T(8,128)S(1)} %leaf_factors.1), channel_id=2, replica_groups=mesh['y'=4,'z'=8,'core'=2,'rk'=4] {'rk'}, dimensions={0}, use_global_device_ids=true | all-gather | bytes 737280 | tf_op jit(solution)/shard_map/all_gather | solution.py:457
  32.9 11.8 %weighted_sums.1 = (f32[176,8,128]{2,1,0:T(8,128)}, f32[848,8,128]{2,1,0:T(8,128)}, f32[176,8,128]{2,1,0:T(8,128)S(1)}, f32[848,8,128]{2,1,0:T(8,128)S(1)}) custom-call(s32[1024]{0:T(1024)S(1)} %add_select_fusion.5.place_ref, f32[32,32,16,64]{3,2,1,0:T(8,128)} %bitcast.62, f32[4,9,32,128]{3,2,1,0:T(8,128)S(1)} %bitcast.57), custom_call_target="tpu_custom_call" | custom-call | tf_op jit(solution)/shard_map/weighted_sums/pallas_call | solution.py:220
  44.7 1.8 %copy-done.1 = f32[848,8,128]{2,1,0:T(8,128)} copy-done((f32[848,8,128]{2,1,0:T(8,128)}, f32[848,8,128]{2,1,0:T(8,128)S(1)}, u32[]{:S(2)}) %copy-start.1) | copy-done | bytes 3473432
  47.0 0.8 slice.27
  47.9 5.6 %collective-permute-done.swapped = f32[176,8,128]{2,1,0:T(8,128)S(1)} collective-permute-done((f32[176,8,128]{2,1,0:T(8,128)}, f32[176,8,128]{2,1,0:T(8,128)S(1)}, u32[]{:S(2)}, u32[]{:S(2)}) %collective-permute-start) | collective-permute-done | bytes 720928 | tf_op jit(solution)/shard_map/ppermute | solution.py:23
  53.5 0.8 round1_kernel.1
  54.3 1.5 %collective-permute-start.1 = (f32[48,8,128]{2,1,0:T(8,128)S(1)}, f32[48,8,128]{2,1,0:T(8,128)S(1)}, u32[]{:S(2)}, u32[]{:S(2)}) collective-permute-start(f32[48,8,128]{2,1,0:T(8,128)S(1)} %get-tuple-element.74), channel_id=1, source_target_pairs={{0,64},{64,128},{128,192},{192,0},{1,65},{65,129},{129,193},{193,1... | collective-permute-start | bytes 589832 | tf_op jit(solution)/shard_map/ppermute | solution.py:19
  55.8 1.7 %collective-permute-start.2 = (f32[48,8,128]{2,1,0:T(8,128)S(1)}, f32[48,8,128]{2,1,0:T(8,128)S(1)}, u32[]{:S(2)}, u32[]{:S(2)}) collective-permute-start(f32[48,8,128]{2,1,0:T(8,128)S(1)} %get-tuple-element.75), channel_id=1, source_target_pairs={{0,192},{64,0},{128,64},{192,128},{1,193},{65,1},{129,65},{193,129... | collective-permute-start | bytes 589832 | tf_op jit(solution)/shard_map/ppermute | solution.py:19
  57.5 2.0 %collective-permute-start.3 = (f32[40,8,128]{2,1,0:T(8,128)}, f32[40,8,128]{2,1,0:T(8,128)S(1)}, u32[]{:S(2)}, u32[]{:S(2)}) collective-permute-start(f32[40,8,128]{2,1,0:T(8,128)} %get-tuple-element.76), channel_id=1, source_target_pairs={{0,8},{8,16},{16,24},{24,32},{32,40},{40,48},{48,56},{56,0},{1,9},... | collective-permute-start | bytes 491528 | tf_op jit(solution)/shard_map/ppermute | solution.py:19
  59.6 0.9 fusion.7
  60.6 1.0 convolution_bitcast_fusion.2
  61.9 3.4 %add.117.d = f32[848,8,128]{2,1,0:T(8,128)S(1)} add(f32[848,8,128]{2,1,0:T(8,128)} %copy-done.1, f32[848,8,128]{2,1,0:T(8,128)} %collective-permute-done.5) | non-fusion elementwise | flops 868352 | bytes 10420224 | tf_op jit(solution)/shard_map/add | solution.py:486
  65.9 3.0 %collective-permute-start.8 = (f32[96,8,128]{2,1,0:T(8,128)S(1)}, f32[96,8,128]{2,1,0:T(8,128)S(1)}, u32[]{:S(2)}, u32[]{:S(2)}) collective-permute-start(f32[96,8,128]{2,1,0:T(8,128)S(1)} %get-tuple-element.92), channel_id=1, source_target_pairs={{0,192},{64,0},{128,64},{192,128},{1,193},{65,1},{129,65},{193,129... | collective-permute-start | bytes 1179656 | tf_op jit(solution)/shard_map/ppermute | solution.py:19
  69.0 3.1 %collective-permute-start.9 = (f32[80,8,128]{2,1,0:T(8,128)S(1)}, f32[80,8,128]{2,1,0:T(8,128)S(1)}, u32[]{:S(2)}, u32[]{:S(2)}) collective-permute-start(f32[80,8,128]{2,1,0:T(8,128)S(1)} %get-tuple-element.93), channel_id=1, source_target_pairs={{0,8},{8,16},{16,24},{24,32},{32,40},{40,48},{48,56},{56,0},{1,9},... | collective-permute-start | bytes 983048 | tf_op jit(solution)/shard_map/ppermute | solution.py:19
  72.0 0.7 collective-permute-start.10
  73.1 3.3 %collective-permute-start.11 = (f32[64,64]{1,0:T(8,128)S(1)}, f32[64,64]{1,0:T(8,128)S(1)}, u32[]{:S(2)}, u32[]{:S(2)}) collective-permute-start(f32[64,64]{1,0:T(8,128)S(1)} %convolution_bitcast_fusion.1), channel_id=1, source_target_pairs={{0,8},{8,0},{16,24},{24,16},{32,40},{40,32},{48,56},{56,48},{1,9},... | collective-permute-start | bytes 49160 | tf_op jit(solution)/shard_map/ppermute | solution.py:23
  76.4 4.8 %collective-permute-done.11 = f32[64,64]{1,0:T(8,128)S(1)} collective-permute-done((f32[64,64]{1,0:T(8,128)S(1)}, f32[64,64]{1,0:T(8,128)S(1)}, u32[]{:S(2)}, u32[]{:S(2)}) %collective-permute-start.11) | collective-permute-done | bytes 16416 | tf_op jit(solution)/shard_map/ppermute | solution.py:23
  81.4 4.0 %collective-permute-start.12 = (f32[86,8,128]{2,1,0:T(8,128)S(1)}, f32[86,8,128]{2,1,0:T(8,128)S(1)}, u32[]{:S(2)}, u32[]{:S(2)}) collective-permute-start(f32[86,8,128]{2,1,0:T(8,128)S(1)} %get-tuple-element.103), channel_id=1, source_target_pairs={{0,8},{8,16},{16,24},{24,32},{32,40},{40,48},{48,56},{56,0},{1,9},... | collective-permute-start | bytes 1056776 | tf_op jit(solution)/shard_map/ppermute | solution.py:19
  85.9 3.8 %collective-permute-start.14 = (f32[64,64]{1,0:T(8,128)S(1)}, f32[64,64]{1,0:T(8,128)S(1)}, u32[]{:S(2)}, u32[]{:S(2)}) collective-permute-start(f32[64,64]{1,0:T(8,128)S(1)} %convolution_bitcast_fusion), channel_id=1, source_target_pairs={{0,16},{8,24},{16,0},{24,8},{32,48},{40,56},{48,32},{56,40},{1,17}... | collective-permute-start | bytes 49160 | tf_op jit(solution)/shard_map/ppermute | solution.py:23
  90.0 0.7 constant_dynamic-slice_fusion.1
  90.7 5.7 %collective-permute-done.14 = f32[64,64]{1,0:T(8,128)S(1)} collective-permute-done((f32[64,64]{1,0:T(8,128)S(1)}, f32[64,64]{1,0:T(8,128)S(1)}, u32[]{:S(2)}, u32[]{:S(2)}) %collective-permute-start.14) | collective-permute-done | bytes 16416 | tf_op jit(solution)/shard_map/ppermute | solution.py:23
  96.8 1.8 %collective-permute-start.16 = (f32[92,8,128]{2,1,0:T(8,128)S(1)}, f32[92,8,128]{2,1,0:T(8,128)S(1)}, u32[]{:S(2)}, u32[]{:S(2)}) collective-permute-start(f32[92,8,128]{2,1,0:T(8,128)S(1)} %get-tuple-element.115), channel_id=1, source_target_pairs={{0,56},{8,0},{16,8},{24,16},{32,24},{40,32},{48,40},{56,48},{1,57}... | collective-permute-start | bytes 1130504 | tf_op jit(solution)/shard_map/ppermute | solution.py:19
  98.7 4.1 %node_factors.1 = f32[4,64,64]{2,1,0:T(8,128)S(1)} custom-call(f32[4,64,64]{2,1,0:T(8,128)S(1)} %pad_maximum_fusion.1.g_ref), custom_call_target="tpu_custom_call" | custom-call | tf_op jit(solution)/shard_map/node_factors/pallas_call | solution.py:125
  102.8 0.6 constant_dynamic-slice_fusion
  103.4 1.6 %collective-permute-done.15.rz_up = f32[92,8,128]{2,1,0:T(8,128)S(1)} collective-permute-done((f32[92,8,128]{2,1,0:T(8,128)S(1)}, f32[92,8,128]{2,1,0:T(8,128)S(1)}, u32[]{:S(2)}, u32[]{:S(2)}) %collective-permute-start.15) | collective-permute-done | bytes 376864 | tf_op jit(solution)/shard_map/ppermute | solution.py:19
  105.1 1.5 %collective-permute-start.19 = (f32[12,8,128]{2,1,0:T(8,128)S(1)}, f32[12,8,128]{2,1,0:T(8,128)S(1)}, u32[]{:S(2)}, u32[]{:S(2)}) collective-permute-start(f32[12,8,128]{2,1,0:T(8,128)S(1)} %get-tuple-element.123), channel_id=1, source_target_pairs={{0,8},{8,16},{16,24},{24,32},{32,40},{40,48},{48,56},{56,0},{1,9},... | collective-permute-start | bytes 147464 | tf_op jit(solution)/shard_map/ppermute | solution.py:19
  106.7 0.6 collective-permute-start.20
  107.2 3.2 %collective-permute-start.18 = (f32[10,8,128]{2,1,0:T(8,128)S(1)}, f32[10,8,128]{2,1,0:T(8,128)S(1)}, u32[]{:S(2)}, u32[]{:S(2)}) collective-permute-start(f32[10,8,128]{2,1,0:T(8,128)S(1)} %get-tuple-element.122), channel_id=1, source_target_pairs={{0,192},{64,0},{128,64},{192,128},{1,193},{65,1},{129,65},{193,129... | collective-permute-start | bytes 122888 | tf_op jit(solution)/shard_map/ppermute | solution.py:19
  110.5 2.0 %collective-permute-done.17.ry_up = f32[10,8,128]{2,1,0:T(8,128)S(1)} collective-permute-done((f32[10,8,128]{2,1,0:T(8,128)S(1)}, f32[10,8,128]{2,1,0:T(8,128)S(1)}, u32[]{:S(2)}, u32[]{:S(2)}) %collective-permute-start.17) | collective-permute-done | bytes 40992 | tf_op jit(solution)/shard_map/ppermute | solution.py:19
  112.9 3.0 %collective-permute-start.22 = (f32[20,8,128]{2,1,0:T(8,128)S(1)}, f32[20,8,128]{2,1,0:T(8,128)S(1)}, u32[]{:S(2)}, u32[]{:S(2)}) collective-permute-start(f32[20,8,128]{2,1,0:T(8,128)S(1)} %get-tuple-element.126), channel_id=1, source_target_pairs={{0,192},{64,0},{128,64},{192,128},{1,193},{65,1},{129,65},{193,129... | collective-permute-start | bytes 245768 | tf_op jit(solution)/shard_map/ppermute | solution.py:19
  115.9 1.8 %collective-permute-start.23 = (f32[12,8,128]{2,1,0:T(8,128)S(1)}, f32[12,8,128]{2,1,0:T(8,128)S(1)}, u32[]{:S(2)}, u32[]{:S(2)}) collective-permute-start(f32[12,8,128]{2,1,0:T(8,128)S(1)} %get-tuple-element.127), channel_id=1, source_target_pairs={{0,8},{8,16},{16,24},{24,32},{32,40},{40,48},{48,56},{56,0},{1,9},... | collective-permute-start | bytes 147464 | tf_op jit(solution)/shard_map/ppermute | solution.py:19
  117.7 0.9 collective-permute-start.24
  118.6 2.1 %collective-permute-done.23.rz_up = f32[12,8,128]{2,1,0:T(8,128)S(1)} collective-permute-done((f32[12,8,128]{2,1,0:T(8,128)S(1)}, f32[12,8,128]{2,1,0:T(8,128)S(1)}, u32[]{:S(2)}, u32[]{:S(2)}) %collective-permute-start.23) | collective-permute-done | bytes 49184 | tf_op jit(solution)/shard_map/ppermute | solution.py:19
  120.7 1.1 collective-permute-done.24.rz_down
  122.1 0.6 collective-permute-start.25
  122.7 2.7 %collective-permute-start.26 = (f32[8,8,128]{2,1,0:T(8,128)S(1)}, f32[8,8,128]{2,1,0:T(8,128)S(1)}, u32[]{:S(2)}, u32[]{:S(2)}) collective-permute-start(f32[8,8,128]{2,1,0:T(8,128)S(1)} %get-tuple-element.131), channel_id=1, source_target_pairs={{0,2},{1,3},{2,0},{3,1},{4,6},{5,7},{6,4},{7,5},{8,10},{9,11},{10,... | collective-permute-start | bytes 98312 | tf_op jit(solution)/shard_map/ppermute | solution.py:19
  125.4 0.9 collective-permute-start.27
  126.3 1.0 collective-permute-done.25.m1_ref
  127.3 0.8 collective-permute-done.26.m2_ref
  128.1 1.2 collective-permute-done.27.m3_ref
  129.3 1.7 %left_factor.1 = f32[32,16,64]{2,1,0:T(8,128)} custom-call(s32[1]{0:T(128)} %bitcast.24.me_ref, f32[4,9,32,128]{3,2,1,0:T(8,128)S(1)} %bitcast.60, f32[8,8,128]{2,1,0:T(8,128)S(1)} %get-tuple-element.129.m0_ref, f32[8,8,128]{2,1,0:T(8,128)S(1)} %collective-permute-done.25.m1_ref, f32[8,8,128]{2,1,0:T(8,128)S(1)} %collective-permute-done.26.m2_ref, ...), custom_call_target="tpu_custom_call" | custom-call | tf_op jit(solution)/shard_map/left_factor/pallas_call | solution.py:408
  (60 shorter events, 4.3 us)
Async XLA Ops:
  0.6 8.1 %copy-start = (f32[1,32,64,64]{3,2,1,0:T(8,128)S(1)}, f32[1,32,64,64]{3,2,1,0:T(8,128)}, u32[]{:S(2)}) copy-start(f32[1,32,64,64]{3,2,1,0:T(8,128)} %param.10) | copy-start | bytes 1572868
  0.6 13.9 %all-to-all-start = ((f32[32,16,256]{2,1,0:T(8,128)}), f32[32,16,256]{2,1,0:T(8,128)S(1)}, u32[]{:S(2)}, u32[]{:S(2)}) async-start(f32[32,16,256]{2,1,0:T(8,128)} %bitcast.64), calls=%async_computation | async-start | bytes 1048576 | tf_op jit(solution)/shard_map/all_to_all | solution.py:454
  44.7 1.8 %copy-start.1 = (f32[848,8,128]{2,1,0:T(8,128)}, f32[848,8,128]{2,1,0:T(8,128)S(1)}, u32[]{:S(2)}) copy-start(f32[848,8,128]{2,1,0:T(8,128)S(1)} %get-tuple-element.78) | copy-start | bytes 10420228
  46.5 15.1 %collective-permute-start.5 = (f32[848,8,128]{2,1,0:T(8,128)}, f32[848,8,128]{2,1,0:T(8,128)}, u32[]{:S(2)}, u32[]{:S(2)}) collective-permute-start(f32[848,8,128]{2,1,0:T(8,128)} %get-tuple-element.79), channel_id=1, source_target_pairs={{0,4},{4,0},{1,5},{5,1},{2,6},{6,2},{3,7},{7,3},{8,12},{12,8},{9,1... | collective-permute-start | bytes 10420232 | tf_op jit(solution)/shard_map/ppermute | solution.py:23
  46.5 7.0 %collective-permute-start = (f32[176,8,128]{2,1,0:T(8,128)}, f32[176,8,128]{2,1,0:T(8,128)S(1)}, u32[]{:S(2)}, u32[]{:S(2)}) collective-permute-start(f32[176,8,128]{2,1,0:T(8,128)} %get-tuple-element.69), channel_id=1, source_target_pairs={{0,4},{4,0},{1,5},{5,1},{2,6},{6,2},{3,7},{7,3},{8,12},{12,8},{9,1... | collective-permute-start | bytes 2162696 | tf_op jit(solution)/shard_map/ppermute | solution.py:23
  54.3 11.2 %collective-permute-start.1 = (f32[48,8,128]{2,1,0:T(8,128)S(1)}, f32[48,8,128]{2,1,0:T(8,128)S(1)}, u32[]{:S(2)}, u32[]{:S(2)}) collective-permute-start(f32[48,8,128]{2,1,0:T(8,128)S(1)} %get-tuple-element.74), channel_id=1, source_target_pairs={{0,64},{64,128},{128,192},{192,0},{1,65},{65,129},{129,193},{193,1... | collective-permute-start | bytes 589832 | tf_op jit(solution)/shard_map/ppermute | solution.py:19
  55.8 9.7 %collective-permute-start.2 = (f32[48,8,128]{2,1,0:T(8,128)S(1)}, f32[48,8,128]{2,1,0:T(8,128)S(1)}, u32[]{:S(2)}, u32[]{:S(2)}) collective-permute-start(f32[48,8,128]{2,1,0:T(8,128)S(1)} %get-tuple-element.75), channel_id=1, source_target_pairs={{0,192},{64,0},{128,64},{192,128},{1,193},{65,1},{129,65},{193,129... | collective-permute-start | bytes 589832 | tf_op jit(solution)/shard_map/ppermute | solution.py:19
  57.5 7.8 %collective-permute-start.3 = (f32[40,8,128]{2,1,0:T(8,128)}, f32[40,8,128]{2,1,0:T(8,128)S(1)}, u32[]{:S(2)}, u32[]{:S(2)}) collective-permute-start(f32[40,8,128]{2,1,0:T(8,128)} %get-tuple-element.76), channel_id=1, source_target_pairs={{0,8},{8,16},{16,24},{24,32},{32,40},{40,48},{48,56},{56,0},{1,9},... | collective-permute-start | bytes 491528 | tf_op jit(solution)/shard_map/ppermute | solution.py:19
  59.5 6.0 %collective-permute-start.4 = (f32[40,8,128]{2,1,0:T(8,128)}, f32[40,8,128]{2,1,0:T(8,128)S(1)}, u32[]{:S(2)}, u32[]{:S(2)}) collective-permute-start(f32[40,8,128]{2,1,0:T(8,128)} %get-tuple-element.77), channel_id=1, source_target_pairs={{0,56},{8,0},{16,8},{24,16},{32,24},{40,32},{48,40},{56,48},{1,57}... | collective-permute-start | bytes 491528 | tf_op jit(solution)/shard_map/ppermute | solution.py:19
  61.6 3.7 %collective-permute-start.6 = (f32[64,64]{1,0:T(8,128)S(1)}, f32[64,64]{1,0:T(8,128)S(1)}, u32[]{:S(2)}, u32[]{:S(2)}) collective-permute-start(f32[64,64]{1,0:T(8,128)S(1)} %convolution_bitcast_fusion.2), channel_id=1, source_target_pairs={{0,4},{4,0},{1,5},{5,1},{2,6},{6,2},{3,7},{7,3},{8,12},{12,8},{9,1... | collective-permute-start | bytes 49160 | tf_op jit(solution)/shard_map/ppermute | solution.py:23
  65.3 7.4 %copy-start.3 = (f32[1,64,64]{2,1,0:T(8,128)S(1)}, f32[1,64,64]{2,1,0:T(8,128)}, u32[]{:S(2)}) copy-start(f32[1,64,64]{2,1,0:T(8,128)} %param.12) | copy-start | bytes 49156
  65.6 19.8 %copy-start.4 = (f32[1,64,64]{2,1,0:T(8,128)S(1)}, f32[1,64,64]{2,1,0:T(8,128)}, u32[]{:S(2)}) copy-start(f32[1,64,64]{2,1,0:T(8,128)} %param.13) | copy-start | bytes 49156
  65.6 24.0 %copy-start.2 = (f32[4,8,32,128]{3,2,1,0:T(8,128)S(1)}, f32[4,8,32,128]{3,2,1,0:T(8,128)}, u32[]{:S(2)}) copy-start(f32[4,8,32,128]{3,2,1,0:T(8,128)} %slice.27) | copy-start | bytes 1572868
  65.6 15.6 %collective-permute-start.7 = (f32[96,8,128]{2,1,0:T(8,128)S(1)}, f32[96,8,128]{2,1,0:T(8,128)S(1)}, u32[]{:S(2)}, u32[]{:S(2)}) collective-permute-start(f32[96,8,128]{2,1,0:T(8,128)S(1)} %get-tuple-element.91), channel_id=1, source_target_pairs={{0,64},{64,128},{128,192},{192,0},{1,65},{65,129},{129,193},{193,1... | collective-permute-start | bytes 1179656 | tf_op jit(solution)/shard_map/ppermute | solution.py:19
  65.9 15.3 %collective-permute-start.8 = (f32[96,8,128]{2,1,0:T(8,128)S(1)}, f32[96,8,128]{2,1,0:T(8,128)S(1)}, u32[]{:S(2)}, u32[]{:S(2)}) collective-permute-start(f32[96,8,128]{2,1,0:T(8,128)S(1)} %get-tuple-element.92), channel_id=1, source_target_pairs={{0,192},{64,0},{128,64},{192,128},{1,193},{65,1},{129,65},{193,129... | collective-permute-start | bytes 1179656 | tf_op jit(solution)/shard_map/ppermute | solution.py:19
  69.0 12.3 %collective-permute-start.9 = (f32[80,8,128]{2,1,0:T(8,128)S(1)}, f32[80,8,128]{2,1,0:T(8,128)S(1)}, u32[]{:S(2)}, u32[]{:S(2)}) collective-permute-start(f32[80,8,128]{2,1,0:T(8,128)S(1)} %get-tuple-element.93), channel_id=1, source_target_pairs={{0,8},{8,16},{16,24},{24,32},{32,40},{40,48},{48,56},{56,0},{1,9},... | collective-permute-start | bytes 983048 | tf_op jit(solution)/shard_map/ppermute | solution.py:19
  72.0 9.2 %collective-permute-start.10 = (f32[80,8,128]{2,1,0:T(8,128)S(1)}, f32[80,8,128]{2,1,0:T(8,128)S(1)}, u32[]{:S(2)}, u32[]{:S(2)}) collective-permute-start(f32[80,8,128]{2,1,0:T(8,128)S(1)} %get-tuple-element.94), channel_id=1, source_target_pairs={{0,56},{8,0},{16,8},{24,16},{32,24},{40,32},{48,40},{56,48},{1,57}... | collective-permute-start | bytes 983048 | tf_op jit(solution)/shard_map/ppermute | solution.py:19
  73.1 8.1 %collective-permute-start.11 = (f32[64,64]{1,0:T(8,128)S(1)}, f32[64,64]{1,0:T(8,128)S(1)}, u32[]{:S(2)}, u32[]{:S(2)}) collective-permute-start(f32[64,64]{1,0:T(8,128)S(1)} %convolution_bitcast_fusion.1), channel_id=1, source_target_pairs={{0,8},{8,0},{16,24},{24,16},{32,40},{40,32},{48,56},{56,48},{1,9},... | collective-permute-start | bytes 49160 | tf_op jit(solution)/shard_map/ppermute | solution.py:23
  81.4 15.0 %collective-permute-start.12 = (f32[86,8,128]{2,1,0:T(8,128)S(1)}, f32[86,8,128]{2,1,0:T(8,128)S(1)}, u32[]{:S(2)}, u32[]{:S(2)}) collective-permute-start(f32[86,8,128]{2,1,0:T(8,128)S(1)} %get-tuple-element.103), channel_id=1, source_target_pairs={{0,8},{8,16},{16,24},{24,32},{32,40},{40,48},{48,56},{56,0},{1,9},... | collective-permute-start | bytes 1056776 | tf_op jit(solution)/shard_map/ppermute | solution.py:19
  85.4 11.0 %collective-permute-start.13 = (f32[86,8,128]{2,1,0:T(8,128)S(1)}, f32[86,8,128]{2,1,0:T(8,128)S(1)}, u32[]{:S(2)}, u32[]{:S(2)}) collective-permute-start(f32[86,8,128]{2,1,0:T(8,128)S(1)} %get-tuple-element.104), channel_id=1, source_target_pairs={{0,56},{8,0},{16,8},{24,16},{32,24},{40,32},{48,40},{56,48},{1,57}... | collective-permute-start | bytes 1056776 | tf_op jit(solution)/shard_map/ppermute | solution.py:19
  85.9 10.6 %collective-permute-start.14 = (f32[64,64]{1,0:T(8,128)S(1)}, f32[64,64]{1,0:T(8,128)S(1)}, u32[]{:S(2)}, u32[]{:S(2)}) collective-permute-start(f32[64,64]{1,0:T(8,128)S(1)} %convolution_bitcast_fusion), channel_id=1, source_target_pairs={{0,16},{8,24},{16,0},{24,8},{32,48},{40,56},{48,32},{56,40},{1,17}... | collective-permute-start | bytes 49160 | tf_op jit(solution)/shard_map/ppermute | solution.py:23
  96.5 8.5 %collective-permute-start.15 = (f32[92,8,128]{2,1,0:T(8,128)S(1)}, f32[92,8,128]{2,1,0:T(8,128)S(1)}, u32[]{:S(2)}, u32[]{:S(2)}) collective-permute-start(f32[92,8,128]{2,1,0:T(8,128)S(1)} %get-tuple-element.114), channel_id=1, source_target_pairs={{0,8},{8,16},{16,24},{24,32},{32,40},{40,48},{48,56},{56,0},{1,9},... | collective-permute-start | bytes 1130504 | tf_op jit(solution)/shard_map/ppermute | solution.py:19
  96.8 8.2 %collective-permute-start.16 = (f32[92,8,128]{2,1,0:T(8,128)S(1)}, f32[92,8,128]{2,1,0:T(8,128)S(1)}, u32[]{:S(2)}, u32[]{:S(2)}) collective-permute-start(f32[92,8,128]{2,1,0:T(8,128)S(1)} %get-tuple-element.115), channel_id=1, source_target_pairs={{0,56},{8,0},{16,8},{24,16},{32,24},{40,32},{48,40},{56,48},{1,57}... | collective-permute-start | bytes 1130504 | tf_op jit(solution)/shard_map/ppermute | solution.py:19
  105.1 7.3 %collective-permute-start.19 = (f32[12,8,128]{2,1,0:T(8,128)S(1)}, f32[12,8,128]{2,1,0:T(8,128)S(1)}, u32[]{:S(2)}, u32[]{:S(2)}) collective-permute-start(f32[12,8,128]{2,1,0:T(8,128)S(1)} %get-tuple-element.123), channel_id=1, source_target_pairs={{0,8},{8,16},{16,24},{24,32},{32,40},{40,48},{48,56},{56,0},{1,9},... | collective-permute-start | bytes 147464 | tf_op jit(solution)/shard_map/ppermute | solution.py:19
  106.7 5.8 %collective-permute-start.20 = (f32[12,8,128]{2,1,0:T(8,128)S(1)}, f32[12,8,128]{2,1,0:T(8,128)S(1)}, u32[]{:S(2)}, u32[]{:S(2)}) collective-permute-start(f32[12,8,128]{2,1,0:T(8,128)S(1)} %get-tuple-element.124), channel_id=1, source_target_pairs={{0,56},{8,0},{16,8},{24,16},{32,24},{40,32},{48,40},{56,48},{1,57}... | collective-permute-start | bytes 147464 | tf_op jit(solution)/shard_map/ppermute | solution.py:19
  107.2 5.2 %collective-permute-start.17 = (f32[10,8,128]{2,1,0:T(8,128)S(1)}, f32[10,8,128]{2,1,0:T(8,128)S(1)}, u32[]{:S(2)}, u32[]{:S(2)}) collective-permute-start(f32[10,8,128]{2,1,0:T(8,128)S(1)} %get-tuple-element.121), channel_id=1, source_target_pairs={{0,64},{64,128},{128,192},{192,0},{1,65},{65,129},{129,193},{193,1... | collective-permute-start | bytes 122888 | tf_op jit(solution)/shard_map/ppermute | solution.py:19
  107.2 5.2 %collective-permute-start.18 = (f32[10,8,128]{2,1,0:T(8,128)S(1)}, f32[10,8,128]{2,1,0:T(8,128)S(1)}, u32[]{:S(2)}, u32[]{:S(2)}) collective-permute-start(f32[10,8,128]{2,1,0:T(8,128)S(1)} %get-tuple-element.122), channel_id=1, source_target_pairs={{0,192},{64,0},{128,64},{192,128},{1,193},{65,1},{129,65},{193,129... | collective-permute-start | bytes 122888 | tf_op jit(solution)/shard_map/ppermute | solution.py:19
  112.5 9.3 %collective-permute-start.21 = (f32[20,8,128]{2,1,0:T(8,128)S(1)}, f32[20,8,128]{2,1,0:T(8,128)S(1)}, u32[]{:S(2)}, u32[]{:S(2)}) collective-permute-start(f32[20,8,128]{2,1,0:T(8,128)S(1)} %get-tuple-element.125), channel_id=1, source_target_pairs={{0,64},{64,128},{128,192},{192,0},{1,65},{65,129},{129,193},{193,1... | collective-permute-start | bytes 245768 | tf_op jit(solution)/shard_map/ppermute | solution.py:19
  112.9 8.9 %collective-permute-start.22 = (f32[20,8,128]{2,1,0:T(8,128)S(1)}, f32[20,8,128]{2,1,0:T(8,128)S(1)}, u32[]{:S(2)}, u32[]{:S(2)}) collective-permute-start(f32[20,8,128]{2,1,0:T(8,128)S(1)} %get-tuple-element.126), channel_id=1, source_target_pairs={{0,192},{64,0},{128,64},{192,128},{1,193},{65,1},{129,65},{193,129... | collective-permute-start | bytes 245768 | tf_op jit(solution)/shard_map/ppermute | solution.py:19
  115.9 4.8 %collective-permute-start.23 = (f32[12,8,128]{2,1,0:T(8,128)S(1)}, f32[12,8,128]{2,1,0:T(8,128)S(1)}, u32[]{:S(2)}, u32[]{:S(2)}) collective-permute-start(f32[12,8,128]{2,1,0:T(8,128)S(1)} %get-tuple-element.127), channel_id=1, source_target_pairs={{0,8},{8,16},{16,24},{24,32},{32,40},{40,48},{48,56},{56,0},{1,9},... | collective-permute-start | bytes 147464 | tf_op jit(solution)/shard_map/ppermute | solution.py:19
  117.7 4.1 %collective-permute-start.24 = (f32[12,8,128]{2,1,0:T(8,128)S(1)}, f32[12,8,128]{2,1,0:T(8,128)S(1)}, u32[]{:S(2)}, u32[]{:S(2)}) collective-permute-start(f32[12,8,128]{2,1,0:T(8,128)S(1)} %get-tuple-element.128), channel_id=1, source_target_pairs={{0,56},{8,0},{16,8},{24,16},{32,24},{40,32},{48,40},{56,48},{1,57}... | collective-permute-start | bytes 147464 | tf_op jit(solution)/shard_map/ppermute | solution.py:19
  122.1 5.2 %collective-permute-start.25 = (f32[8,8,128]{2,1,0:T(8,128)S(1)}, f32[8,8,128]{2,1,0:T(8,128)S(1)}, u32[]{:S(2)}, u32[]{:S(2)}) collective-permute-start(f32[8,8,128]{2,1,0:T(8,128)S(1)} %get-tuple-element.130), channel_id=1, source_target_pairs={{0,1},{1,2},{2,3},{3,0},{4,5},{5,6},{6,7},{7,4},{8,9},{9,10},{10,1... | collective-permute-start | bytes 98312 | tf_op jit(solution)/shard_map/ppermute | solution.py:19
  122.7 5.4 %collective-permute-start.26 = (f32[8,8,128]{2,1,0:T(8,128)S(1)}, f32[8,8,128]{2,1,0:T(8,128)S(1)}, u32[]{:S(2)}, u32[]{:S(2)}) collective-permute-start(f32[8,8,128]{2,1,0:T(8,128)S(1)} %get-tuple-element.131), channel_id=1, source_target_pairs={{0,2},{1,3},{2,0},{3,1},{4,6},{5,7},{6,4},{7,5},{8,10},{9,11},{10,... | collective-permute-start | bytes 98312 | tf_op jit(solution)/shard_map/ppermute | solution.py:19
  125.4 3.9 %collective-permute-start.27 = (f32[8,8,128]{2,1,0:T(8,128)S(1)}, f32[8,8,128]{2,1,0:T(8,128)S(1)}, u32[]{:S(2)}, u32[]{:S(2)}) collective-permute-start(f32[8,8,128]{2,1,0:T(8,128)S(1)} %get-tuple-element.132), channel_id=1, source_target_pairs={{0,3},{1,0},{2,1},{3,2},{4,7},{5,4},{6,5},{7,6},{8,11},{9,8},{10,9... | collective-permute-start | bytes 98312 | tf_op jit(solution)/shard_map/ppermute | solution.py:19

commit v6 on v5

--- a/solution.py
+++ b/solution.py
@@ -109,28 +109,34 @@
             pltpu.VMEM((leaves, RANK, RANK), jnp.float32),
             pltpu.VMEM((RANK, RANK, leaves), jnp.float32),
         ],
-        compiler_params=pltpu.CompilerParams(vmem_limit_bytes=32 * 2**20),
+        compiler_params=pltpu.CompilerParams(vmem_limit_bytes=10 * 2**20),
         name="leaf_factors",
     )(x, moves)
 
 
-def node_kernel(g_ref, out_ref, s_ref):
+def node_kernel(me_ref, g_ref, out_ref, s_ref, l_ref):
     to_lanes(g_ref, s_ref)
     factor_in_place(s_ref)
     for c in range(RANK):
-        out_ref[:, c, :] = column_of(s_ref, c)
-
-
-def node_lower(grams):
+        l_ref[:, c, :] = column_of(s_ref, c)
+    width = out_ref.shape[1]
+    out_ref[...] = l_ref[:, pl.ds(pl.multiple_of(me_ref[0] * width, width), width), :]
+
+
+def node_lower(me, grams, width):
+    vmem = pl.BlockSpec(memory_space=pltpu.VMEM)
     return pl.pallas_call(
         node_kernel,
-        out_shape=jax.ShapeDtypeStruct(grams.shape, jnp.float32),
-        in_specs=[pl.BlockSpec(memory_space=pltpu.VMEM)],
-        out_specs=pl.BlockSpec(memory_space=pltpu.VMEM),
-        scratch_shapes=[pltpu.VMEM((RANK, RANK, grams.shape[0]), jnp.float32)],
-        compiler_params=pltpu.CompilerParams(vmem_limit_bytes=32 * 2**20),
+        out_shape=jax.ShapeDtypeStruct((grams.shape[0], width, RANK), jnp.float32),
+        in_specs=[pl.BlockSpec(memory_space=pltpu.SMEM), vmem],
+        out_specs=vmem,
+        scratch_shapes=[
+            pltpu.VMEM((RANK, RANK, grams.shape[0]), jnp.float32),
+            pltpu.VMEM(grams.shape, jnp.float32),
+        ],
+        compiler_params=pltpu.CompilerParams(vmem_limit_bytes=10 * 2**20),
         name="node_factors",
-    )(grams)
+    )(me, grams)
 
 
 def split(value):
@@ -165,7 +171,10 @@
     return total + jnp.dot(c_high, w_low, preferred_element_type=jnp.float32)
 
 
-def product_kernel(place_ref, c_hbm, l_ref, o0_ref, o1_ref, o2_ref, o3_ref, acc_ref, c_ref, sems):
+def product_kernel(
+    me_ref, place_ref, c_hbm, l_ref, o0_ref, o1_ref, o2_ref, o3_ref, rows_ref,
+    acc_ref, c_ref, sems, out_sems,
+):
     leaves, listed, width, _ = c_hbm.shape
     slots, group = c_ref.shape[0], c_ref.shape[1]
     steps = leaves // group
@@ -180,6 +189,12 @@
     for step in range(slots - 1):
         fetch(step, step).start()
     acc_ref[...] = jnp.zeros_like(acc_ref)
+
+    me = me_ref[0]
+    at = pl.multiple_of(lax.rem(me, 2) * width, width)
+    for j in range(leaves):
+        rows = l_ref[j // share, j % share, pl.ds(at, width), :]
+        rows_ref[j] = jnp.where(me < 2, rows[:, :RANK], rows[:, RANK:])
 
     def body(step, carry):
         slot = lax.rem(step, slots)
@@ -202,17 +217,26 @@
         return carry
 
     lax.fori_loop(0, steps, body, 0)
-    at = 0
-    for ref in (o0_ref, o1_ref, o2_ref, o3_ref):
-        ref[...] = acc_ref[at : at + ref.shape[0]]
-        at += ref.shape[0]
-
-
-def weighted_sums(place, blocks, packed, parts):
+    near, far = o0_ref.shape[0], o1_ref.shape[0]
+    total = near + far
+    copies = [
+        pltpu.make_async_copy(acc_ref.at[pl.ds(at, far)], ref, sem)
+        for at, ref, sem in ((near, o1_ref, out_sems.at[0]), (total + near, o3_ref, out_sems.at[1]))
+    ]
+    for copy in copies:
+        copy.start()
+    o0_ref[...] = acc_ref[:near]
+    o2_ref[...] = acc_ref[total : total + near]
+    for copy in copies:
+        copy.wait()
+
+
+def weighted_sums(me, place, blocks, packed, parts):
     leaves, listed, width, rank = blocks.shape
     top = width // 2
     group, slots = 4, 4
     vmem = pl.BlockSpec(memory_space=pltpu.VMEM)
+    hbm = pl.BlockSpec(memory_space=pltpu.HBM)
 
     def out(rows):
         return jax.ShapeDtypeStruct((rows, top, 2 * rank), jnp.float32)
@@ -221,19 +245,22 @@
         product_kernel,
         in_specs=[
             pl.BlockSpec(memory_space=pltpu.SMEM),
-            pl.BlockSpec(memory_space=pltpu.HBM),
+            pl.BlockSpec(memory_space=pltpu.SMEM),
+            hbm,
             vmem,
         ],
-        out_specs=(vmem,) * len(parts),
+        out_specs=(vmem, hbm, vmem, hbm, vmem),
         scratch_shapes=[
             pltpu.VMEM((sum(parts) + TILE, top, 2 * rank), jnp.float32),
             pltpu.VMEM((slots, group, listed, width, rank), jnp.float32),
             pltpu.SemaphoreType.DMA((slots,)),
+            pltpu.SemaphoreType.DMA((2,)),
         ],
-        out_shape=tuple(out(rows) for rows in parts),
-        compiler_params=pltpu.CompilerParams(vmem_limit_bytes=24 * 2**20),
+        out_shape=tuple(out(rows) for rows in parts)
+        + (jax.ShapeDtypeStruct((leaves, width, rank), jnp.float32),),
+        compiler_params=pltpu.CompilerParams(vmem_limit_bytes=16 * 2**20),
         name="weighted_sums",
-    )(place, pltpu.with_memory_space_constraint(blocks, pltpu.HBM), packed)
+    )(me, place, pltpu.with_memory_space_constraint(blocks, pltpu.HBM), packed)
 
 
 class Plan:
@@ -265,6 +292,9 @@
         at = self.base[group] - (0 if self.base[group] < self.near else self.near)
         return ref[at : at + self.rows[group[0]]]
 
+    def both(self, keep, got, group):
+        return self.part(keep, group) + self.part(got, group)
+
 
 def low_add(whole, extra):
     rows = extra.shape[0]
@@ -276,9 +306,9 @@
     return jnp.concatenate([whole[:rows], whole[rows:] + extra], axis=0)
 
 
-def round1_kernel(plan, keep, swapped, y_up, y_down, z_up, z_down):
-    y = plan.part(keep, ("y", 2)) + plan.part(swapped, ("y", 2))
-    z = plan.part(keep, ("z", 4)) + plan.part(swapped, ("z", 4))
+def round1_kernel(plan, keep, got, y_up, y_down, z_up, z_down):
+    y = plan.both(keep, got, ("y", 2))
+    z = plan.both(keep, got, ("z", 4))
     half = y.shape[0] // 2
     y_up[...] = y[:half]
     y_down[...] = y[half:]
@@ -287,47 +317,41 @@
     z_down[...] = z[half:]
 
 
-def round2_kernel(plan, d, ry_up, ry_down, rz_up, rz_down, y_up, y_down, z_up, z_down):
-    y_up[...] = low_add(plan.part(d, ("y", 1)), ry_up[...])
-    y_down[...] = high_add(plan.part(d, ("y", 3)), ry_down[...])
-    z_up[...] = low_add(plan.part(d, ("z", 3)), rz_up[...])
-    z_down[...] = high_add(plan.part(d, ("z", 5)), rz_down[...])
-
-
-def round3_kernel(plan, d, ry_up, ry_down, rz_up, rz_down, ey, z_up, z_down):
-    ey[...] = plan.part(d, ("y", 0)) + ry_up[...] + ry_down[...]
+def round2_kernel(plan, keep, got, ry_up, ry_down, rz_up, rz_down, y_up, y_down, z_up, z_down):
+    y_up[...] = low_add(plan.both(keep, got, ("y", 1)), ry_up[...])
+    y_down[...] = high_add(plan.both(keep, got, ("y", 3)), ry_down[...])
+    z_up[...] = low_add(plan.both(keep, got, ("z", 3)), rz_up[...])
+    z_down[...] = high_add(plan.both(keep, got, ("z", 5)), rz_down[...])
+
+
+def round3_kernel(plan, keep, got, ry_up, ry_down, rz_up, rz_down, ey, z_up, z_down):
+    ey[...] = plan.both(keep, got, ("y", 0)) + ry_up[...] + ry_down[...]
     rows, cut = plan.rows["z"], plan.cut
     half = cut // 2
-    z_up[:rows] = plan.part(d, ("z", 2)) + rz_up[...]
-    z_up[rows:] = ey[4 * cut : 4 * cut + half]
-    z_down[:rows] = plan.part(d, ("z", 6)) + rz_down[...]
-    z_down[rows:] = ey[4 * cut + half : 5 * cut]
-
-
-def round4_kernel(plan, d, ey, rz_up, rz_down, z_up, z_down):
+    z_up[:rows] = plan.both(keep, got, ("z", 2)) + rz_up[...]
+    z_up[rows : rows + half] = ey[4 * cut : 4 * cut + half]
+    z_up[rows + half :] = ey[cut : 2 * cut]
+    z_down[:rows] = plan.both(keep, got, ("z", 6)) + rz_down[...]
+    z_down[rows : rows + half] = ey[4 * cut + half : 5 * cut]
+    z_down[rows + half :] = ey[7 * cut :]
+
+
+def round4_kernel(plan, keep, got, ey, rz_up, rz_down, z_up, z_down):
     rows, cut = plan.rows["z"], plan.cut
-    z_up[:rows] = plan.part(d, ("z", 1)) + rz_up[:rows]
-    z_up[rows:] = low_add(ey[3 * cut : 4 * cut], rz_up[rows:])
-    z_down[:rows] = plan.part(d, ("z", 7)) + rz_down[:rows]
-    z_down[rows:] = high_add(ey[5 * cut : 6 * cut], rz_down[rows:])
-
-
-def round5_kernel(plan, d, ey, rz_up, rz_down, ez, y_up, y_down, z_up, z_down):
+    half = cut // 2
+    z_up[:rows] = plan.both(keep, got, ("z", 1)) + rz_up[:rows]
+    z_up[rows:] = low_add(ey[3 * cut : 4 * cut], rz_up[rows : rows + half])
+    z_down[:rows] = plan.both(keep, got, ("z", 7)) + rz_down[:rows]
+    z_down[rows:] = high_add(ey[5 * cut : 6 * cut], rz_down[rows : rows + half])
+
+
+def round5_kernel(plan, keep, got, ey, rz_up, rz_down, own, y_one, y_two, y_three, z_two, z_six):
     rows, cut, rest = plan.rows["z"], plan.cut, plan.rest
-    half = rest // 2
-    ez[...] = plan.part(d, ("z", 0)) + rz_up[:rows] + rz_down[:rows]
-    y_up[...] = ez[2 * rest : 2 * rest + half]
-    y_down[...] = ez[2 * rest + half : 3 * rest]
-    z_up[...] = ey[2 * cut : 3 * cut] + rz_up[rows:]
-    z_down[...] = ey[6 * cut : 7 * cut] + rz_down[rows:]
-
-
-def round6_kernel(plan, ey, ez, ry_up, ry_down, rz_up, rz_down, y_up, y_down, z_up, z_down):
-    cut, rest = plan.cut, plan.rest
-    y_up[...] = low_add(ez[rest : 2 * rest], ry_up[...])
-    y_down[...] = high_add(ez[3 * rest :], ry_down[...])
-    z_up[...] = ey[cut : 2 * cut] + rz_up[...]
-    z_down[...] = ey[7 * cut :] + rz_down[...]
+    ez = plan.both(keep, got, ("z", 0)) + rz_up[:rows] + rz_down[:rows]
+    for r, ref in enumerate((own, y_one, y_two, y_three)):
+        ref[...] = ez[r * rest : (r + 1) * rest]
+    z_two[...] = ey[2 * cut : 3 * cut] + rz_up[rows:]
+    z_six[...] = ey[6 * cut : 7 * cut] + rz_down[rows:]
 
 
 def run_round(kernel, plan, rows, *arrays):
@@ -344,12 +368,14 @@
 
 
 def pack_kernel(
-    me_ref, ey, ez, ry_up, ry_down, rz_up, rz_down, o0_ref, o1_ref, o2_ref, o3_ref, g_ref, m_ref
+    me_ref, ey, z_up, z_down, z_two, z_six, ez, y_one, y_two, y_three,
+    o0_ref, o1_ref, o2_ref, o3_ref, g_ref, m_ref,
 ):
     slots = g_ref.shape[0]
-    cut = rz_up.shape[0]
-    g_ref[:cut] = ey[:cut] + rz_up[...] + rz_down[...]
-    g_ref[cut:] = ez[: slots - cut] + ry_up[...] + ry_down[...]
+    cut = z_two.shape[0]
+    skip = z_up.shape[0] - cut
+    g_ref[:cut] = ey[:cut] + z_up[skip:] + z_down[skip:] + z_two[...] + z_six[...]
+    g_ref[cut:] = ez[...] + y_one[...] + y_two[...] + y_three[...]
     chunks = m_ref.shape[0]
     piece = RANK // chunks
     batch = 2 * RANK // piece
@@ -365,7 +391,7 @@
 
 def pack(me, *arrays):
     vmem = pl.BlockSpec(memory_space=pltpu.VMEM)
-    slots = arrays[2].shape[0] + arrays[4].shape[0]
+    slots = arrays[4].shape[0] + arrays[5].shape[0]
     top, lanes = arrays[0].shape[1:]
     tiles = slots * RANK // 4 * top * 2 // (top * lanes)
     message = jax.ShapeDtypeStruct((tiles, top, lanes), jnp.float32)
@@ -378,7 +404,7 @@
             pltpu.VMEM((slots, top, lanes), jnp.float32),
             pltpu.VMEM((4, tiles, top, lanes), jnp.float32),
         ],
-        compiler_params=pltpu.CompilerParams(vmem_limit_bytes=16 * 2**20),
+        compiler_params=pltpu.CompilerParams(vmem_limit_bytes=8 * 2**20),
         name="pack",
     )(me, *arrays)
 
@@ -411,7 +437,7 @@
         out_specs=vmem,
         out_shape=jax.ShapeDtypeStruct((slots, RANK // 4, RANK), jnp.float32),
         scratch_shapes=[pltpu.VMEM((4,) + messages[0].shape, jnp.float32)],
-        compiler_params=pltpu.CompilerParams(vmem_limit_bytes=16 * 2**20),
+        compiler_params=pltpu.CompilerParams(vmem_limit_bytes=8 * 2**20),
         name="left_factor",
     )(me, packed, *messages)
 
@@ -457,10 +483,11 @@
     packed = lax.all_gather(mine, "rk", axis=0, tiled=False)
 
     near, far = plan.near, plan.total - plan.near
-    away_near, away_far, keep_near, keep_far = weighted_sums(
-        place, blocks, packed, (near, far, near, far)
+    away_near, away_far, keep_near, keep_far, leaf_weights = weighted_sums(
+        me, place, blocks, packed, (near, far, near, far)
     )
     got_near = swap(away_near, "core", 1)
+    got_near, away_far = tie(got_near, away_far)
     got_far = swap(away_far, "core", 1)
 
     def level_term(level, transfer):
@@ -483,50 +510,48 @@
     grams = [unpacked(jnp.sum(terms, axis=0))]
     term = level_term(grams[0], node_transfer[0])
     other = swap(term, "core", 1)
-    d = keep_far + got_far
-    ry_up, ry_down, rz_up, rz_down, d, other = tie(ry_up, ry_down, rz_up, rz_down, d, other)
+    ry_up, ry_down, rz_up, rz_down, got_far, term = tie(
+        ry_up, ry_down, rz_up, rz_down, got_far, term
+    )
+    sums = (keep_far, got_far)
 
     sent = run_round(
-        round2_kernel, plan, (y_rows,) * 2 + (z_rows,) * 2, d, ry_up, ry_down, rz_up, rz_down
-    )
-    sent, other = tie(sent, other)
+        round2_kernel, plan, (y_rows,) * 2 + (z_rows,) * 2, *sums, ry_up, ry_down, rz_up, rz_down
+    )
+    sent, term = tie(sent, term)
     rz_up, rz_down, ry_up, ry_down = send(sent)
     grams.append(term + other)
     term = level_term(grams[1], pair_transfer[0])
     other = swap(term, "z", 1)
-    ry_up, ry_down, rz_up, rz_down, other = tie(ry_up, ry_down, rz_up, rz_down, other)
-
-    both = z_rows + cut // 2
+    ry_up, ry_down, rz_up, rz_down, term = tie(ry_up, ry_down, rz_up, rz_down, term)
+
+    ride = z_rows + cut // 2 + cut
     ey, up, down = run_round(
-        round3_kernel, plan, (y_rows, both, both), d, ry_up, ry_down, rz_up, rz_down
-    )
-    up, down, other, lower = tie(up, down, other, packed[:, :share])
-    rz_up, rz_down = along("z", up, down)
+        round3_kernel, plan, (y_rows, ride, ride), *sums, ry_up, ry_down, rz_up, rz_down
+    )
+    up, down, term = tie(up, down, term)
+    ride_up, ride_down = along("z", up, down)
     grams.append(term + other)
     term = level_term(grams[2], quad_transfer[0])
     other = swap(term, "z", 2)
-    lower = unpacked(lower).reshape(leaves, RANK, RANK)
-    leaf_weights = lax.dynamic_slice_in_dim(lower, rank_index * width, width, 1)
-    rz_up, rz_down, other, leaf_weights = tie(rz_up, rz_down, other, leaf_weights)
+    ride_up, ride_down, term = tie(ride_up, ride_down, term)
 
     both = z_rows + cut
-    up, down = run_round(round4_kernel, plan, (both, both), d, ey, rz_up, rz_down)
-    up, down, other = tie(up, down, other)
+    up, down = run_round(round4_kernel, plan, (both, both), *sums, ey, ride_up, ride_down)
+    up, down, term = tie(up, down, term)
     rz_up, rz_down = along("z", up, down)
     grams.append(term + other)
-    nodes = node_lower(jnp.stack(grams))
-    node_weights = lax.dynamic_slice_in_dim(nodes, rank_index * width, width, 1)
+    node_weights = node_lower(me, jnp.stack(grams), width)
     rz_up, rz_down, node_weights = tie(rz_up, rz_down, node_weights)
 
-    ez, *sent = run_round(
-        round5_kernel, plan, (z_rows, rest // 2, rest // 2, cut, cut), d, ey, rz_up, rz_down
-    )
-    rz_up, rz_down, ry_up, ry_down = send(sent)
-    sent = run_round(
-        round6_kernel, plan, (rest, rest, cut, cut), ey, ez, ry_up, ry_down, rz_up, rz_down
-    )
-    rz_up, rz_down, ry_up, ry_down = send(sent)
-    messages = pack(me, ey, ez, ry_up, ry_down, rz_up, rz_down)
+    ez, y_one, y_two, y_three, z_two, z_six = run_round(
+        round5_kernel, plan, (rest,) * 4 + (cut,) * 2, *sums, ey, rz_up, rz_down
+    )
+    z_two = shift(z_two, "z", 2)
+    z_six = shift(z_six, "z", -2)
+    y_one, y_three = along("y", y_one, y_three)
+    y_two = shift(y_two, "y", 2)
+    messages = pack(me, ey, ride_up, ride_down, z_two, z_six, ez, y_one, y_two, y_three)
     arrived = [messages[0]] + [shift(messages[s], "rk", s) for s in range(1, n_rank)]
     coupled = final(me, packed, arrived, leaves)
 

time: 133 us -> 131 us (0.985)
  Pallas kernels: 24.5 us -> 32.3 us
  starting transfers between devices: 46.4 us -> 40.2 us
  other arithmetic: 5.7 us -> 2.22 us
  waiting for transfers between devices: 32 us -> 35 us
  matrix products: 2.71 us -> 1.19 us
    ppermute x23 -> x20, waiting for transfers between devices: 10 us -> 27 us  [shift(): lax.ppermute(value, axis, [(i, (i + step) % size) for i in range(size)])]
    ppermute x5, waiting for transfers between devices: 16.1 us -> 2.2 us  [swap(): lax.ppermute(value, axis, [(i, i ^ mask) for i in range(lax.axis_size(axi...]
    pallas_call x6 -> x5, Pallas kernels: 1.27 us -> 8.6 us  [run_round(): pl.pallas_call(functools.partial(kernel, plan), in_specs=[vmem] * len(arr...]
    ppermute x23 -> x20, starting transfers between devices: 34.1 us -> 28.8 us  [shift(): lax.ppermute(value, axis, [(i, (i + step) % size) for i in range(size)])]
    add x1 -> x0, other arithmetic: 3.39 us -> none  [shards(): d = keep_far + got_far]
    unnamed x11 -> x13, local copies, waits for them, and re-layouts: 2.32 us -> 4.27 us
    dynamic_slice x2 -> x0, local copies, waits for them, and re-layouts: 1.36 us -> none  [the longest x1 0.73 us: shards(): leaf_weights = lax.dynamic_slice_in_dim(lower, rank_index * width, width, 1)]
  transfers between devices with their start and end apart: 29 -> 26, of which waited for: 12 -> 15; matrix products, arithmetic and copies ran while one was open for 9% -> 4% of each run, Pallas kernels for 4% -> 9%
where the time goes in v6:
time: 131 us; the launch traced here: 130 us
  starting transfers between devices  40.2 us (31%)
  waiting for transfers between devices  35 us (27%)
  Pallas kernels  32.3 us (25%)
  blocking collectives  13.1 us (10%)
  local copies, waits for them, and re-layouts  5.31 us (4%)
  other arithmetic  2.22 us (2%)
    ppermute x20, starting transfers between devices, shift(): lax.ppermute(value, axis, [(i, (i + step) % size) for i in range(size)])  28.8 us
    ppermute x20, waiting for transfers between devices, shift(): lax.ppermute(value, axis, [(i, (i + step) % size) for i in range(size)])  27 us
    all_gather x1, blocking collectives, shards(): packed = lax.all_gather(mine, 'rk', axis=0, tiled=False)  13.1 us
    pallas_call x1, Pallas kernels, weighted_sums(): pl.pallas_call(product_kernel, in_specs=[pl.BlockSpec(memory_space=pltpu....  11.7 us
    pallas_call x5, Pallas kernels, run_round(): pl.pallas_call(functools.partial(kernel, plan), in_specs=[vmem] * len(arr...  8.6 us
    ppermute x5, starting transfers between devices, swap(): lax.ppermute(value, axis, [(i, i ^ mask) for i in range(lax.axis_size(axi...  6.95 us
    all_to_all x1, waiting for transfers between devices, shards(): lax.all_to_all(local, 'rk', split_axis=0, concat_axis=0, tiled=True)  5.81 us
    pallas_call x1, Pallas kernels, leaf_factors(): pl.pallas_call(leaf_kernel, out_shape=jax.ShapeDtypeStruct((leaves + 1, R...  5.19 us
  transfers between devices with their start and end apart: 26, of which 15 were waited for; matrix products, arithmetic and copies ran while one was open for 4% of the time, Pallas kernels for 9%

profile of v6, /device:TPU:32, one launch (start us, length us, event | category | flops | bytes accessed | tf_op | source)
XLA Modules:
  0.0 130.1 jit_solution(7012055270169409256)
XLA Ops:
  0.6 4.4 %all-to-all-start = ((f32[32,16,256]{2,1,0:T(8,128)}), f32[32,16,256]{2,1,0:T(8,128)S(1)}, u32[]{:S(2)}, u32[]{:S(2)}) async-start(f32[32,16,256]{2,1,0:T(8,128)} %bitcast.61), calls=%async_computation | async-start | bytes 1048576 | tf_op jit(solution)/shard_map/all_to_all | solution.py:480
  5.1 0.7 iota_compare_fusion
  5.8 0.5 broadcast.120
  6.3 1.4 %reduce.3 = s32[32,32]{1,0:T(8,128)S(1)} reduce(s32[1,32,32,1]{2,3,1,0:T(1,128)} %param.15, s32[]{:T(128)} %broadcast.120), dimensions={0,3}, to_apply=%param.15.reduce_sub_computation.3 | reduce | bytes 8196 | tf_op args[6]
  7.9 0.8 squeeze.25
  8.7 5.8 %all-to-all-done = f32[32,16,256]{2,1,0:T(8,128)S(1)} async-done(((f32[32,16,256]{2,1,0:T(8,128)}), f32[32,16,256]{2,1,0:T(8,128)S(1)}, u32[]{:S(2)}, u32[]{:S(2)}) %all-to-all-start) | async-done | bytes 524320 | tf_op jit(solution)/shard_map/all_to_all | solution.py:480
  14.6 5.2 %leaf_factors.1 = f32[9,32,128]{2,1,0:T(8,128)S(1)} custom-call(f32[4,8,16,256]{3,2,1,0:T(8,128)S(1)} %bitcast.59, f32[8,64,64]{2,1,0:T(8,128)S(1)} %dynamic-slice_bitcast_fusion.move_ref), custom_call_target="tpu_custom_call" | custom-call | tf_op jit(solution)/shard_map/leaf_factors/pallas_call | solution.py:103
  19.8 13.1 %all-gather = f32[36,32,128]{2,1,0:T(8,128)S(1)} all-gather(f32[9,32,128]{2,1,0:T(8,128)S(1)} %leaf_factors.1), channel_id=2, replica_groups=mesh['y'=4,'z'=8,'core'=2,'rk'=4] {'rk'}, dimensions={0}, use_global_device_ids=true | all-gather | bytes 737280 | tf_op jit(solution)/shard_map/all_gather | solution.py:483
  32.9 11.7 %weighted_sums.1 = (f32[176,8,128]{2,1,0:T(8,128)S(1)}, f32[848,8,128]{2,1,0:T(8,128)}, f32[176,8,128]{2,1,0:T(8,128)S(1)}, f32[848,8,128]{2,1,0:T(8,128)S(1)}, f32[32,16,64]{2,1,0:T(8,128)}) custom-call(s32[1]{0:T(128)} %bitcast.me_ref, s32[1024]{0:T(1024)S(1)} %add_select_fusion.5.place_ref, f32[32,32,16,64]{3,2,1,0:T(8,128)} %bitcast.60, ...), custom_call_target="tpu_custom_call" | custom-call | tf_op jit(solution)/shard_map/weighted_sums/pallas_call | solution.py:244
  44.6 1.8 %copy-done.1 = f32[848,8,128]{2,1,0:T(8,128)} copy-done((f32[848,8,128]{2,1,0:T(8,128)}, f32[848,8,128]{2,1,0:T(8,128)S(1)}, u32[]{:S(2)}) %copy-start.1) | copy-done | bytes 3473432
  46.3 2.2 %collective-permute-done.got = f32[176,8,128]{2,1,0:T(8,128)S(1)} collective-permute-done((f32[176,8,128]{2,1,0:T(8,128)S(1)}, f32[176,8,128]{2,1,0:T(8,128)S(1)}, u32[]{:S(2)}, u32[]{:S(2)}) %collective-permute-start) | collective-permute-done | bytes 720928 | tf_op jit(solution)/shard_map/ppermute | solution.py:23
  48.7 1.7 %collective-permute-start.1 = (f32[48,8,128]{2,1,0:T(8,128)S(1)}, f32[48,8,128]{2,1,0:T(8,128)S(1)}, u32[]{:S(2)}, u32[]{:S(2)}) collective-permute-start(f32[48,8,128]{2,1,0:T(8,128)S(1)} %get-tuple-element.76), channel_id=1, source_target_pairs={{0,64},{64,128},{128,192},{192,0},{1,65},{65,129},{129,193},{193,1... | collective-permute-start | bytes 589832 | tf_op jit(solution)/shard_map/ppermute | solution.py:19
  50.5 1.6 %collective-permute-start.2 = (f32[48,8,128]{2,1,0:T(8,128)S(1)}, f32[48,8,128]{2,1,0:T(8,128)S(1)}, u32[]{:S(2)}, u32[]{:S(2)}) collective-permute-start(f32[48,8,128]{2,1,0:T(8,128)S(1)} %get-tuple-element.77), channel_id=1, source_target_pairs={{0,192},{64,0},{128,64},{192,128},{1,193},{65,1},{129,65},{193,129... | collective-permute-start | bytes 589832 | tf_op jit(solution)/shard_map/ppermute | solution.py:19
  52.1 2.1 %collective-permute-start.3 = (f32[40,8,128]{2,1,0:T(8,128)S(1)}, f32[40,8,128]{2,1,0:T(8,128)S(1)}, u32[]{:S(2)}, u32[]{:S(2)}) collective-permute-start(f32[40,8,128]{2,1,0:T(8,128)S(1)} %get-tuple-element.78), channel_id=1, source_target_pairs={{0,8},{8,16},{16,24},{24,32},{32,40},{40,48},{48,56},{56,0},{1,9},... | collective-permute-start | bytes 491528 | tf_op jit(solution)/shard_map/ppermute | solution.py:19
  54.7 3.5 %collective-permute-done.3.rz_up = f32[40,8,128]{2,1,0:T(8,128)S(1)} collective-permute-done((f32[40,8,128]{2,1,0:T(8,128)S(1)}, f32[40,8,128]{2,1,0:T(8,128)S(1)}, u32[]{:S(2)}, u32[]{:S(2)}) %collective-permute-start.3) | collective-permute-done | bytes 163872 | tf_op jit(solution)/shard_map/ppermute | solution.py:19
  58.2 1.8 %collective-permute-done.4.rz_down = f32[40,8,128]{2,1,0:T(8,128)S(1)} collective-permute-done((f32[40,8,128]{2,1,0:T(8,128)S(1)}, f32[40,8,128]{2,1,0:T(8,128)S(1)}, u32[]{:S(2)}, u32[]{:S(2)}) %collective-permute-start.4) | collective-permute-done | bytes 163872 | tf_op jit(solution)/shard_map/ppermute | solution.py:19
  60.1 2.0 %copy-done.2 = f32[848,8,128]{2,1,0:T(8,128)S(1)} copy-done((f32[848,8,128]{2,1,0:T(8,128)S(1)}, f32[848,8,128]{2,1,0:T(8,128)}, u32[]{:S(2)}) %copy-start.2) | copy-done | bytes 3473432
  62.0 2.2 %round2_kernel.1 = (f32[96,8,128]{2,1,0:T(8,128)S(1)}, f32[96,8,128]{2,1,0:T(8,128)S(1)}, f32[80,8,128]{2,1,0:T(8,128)S(1)}, f32[80,8,128]{2,1,0:T(8,128)S(1)}) custom-call(f32[848,8,128]{2,1,0:T(8,128)S(1)} %copy-done.2, f32[848,8,128]{2,1,0:T(8,128)} %collective-permute-done.5.got, f32[48,8,128]{2,1,0:T(8,128)S(1)} %collective-permute-done.1.ry_up, ...), custom_call_target="tpu_custom_call" | custom-call | tf_op jit(solution)/shard_map/round2_kernel/pallas_call | solution.py:360
  64.2 0.4 collective-permute-start.6
  64.6 3.1 %collective-permute-start.7 = (f32[96,8,128]{2,1,0:T(8,128)S(1)}, f32[96,8,128]{2,1,0:T(8,128)S(1)}, u32[]{:S(2)}, u32[]{:S(2)}) collective-permute-start(f32[96,8,128]{2,1,0:T(8,128)S(1)} %get-tuple-element.93), channel_id=1, source_target_pairs={{0,192},{64,0},{128,64},{192,128},{1,193},{65,1},{129,65},{193,129... | collective-permute-start | bytes 1179656 | tf_op jit(solution)/shard_map/ppermute | solution.py:19
  67.7 3.0 %collective-permute-start.8 = (f32[80,8,128]{2,1,0:T(8,128)S(1)}, f32[80,8,128]{2,1,0:T(8,128)S(1)}, u32[]{:S(2)}, u32[]{:S(2)}) collective-permute-start(f32[80,8,128]{2,1,0:T(8,128)S(1)} %get-tuple-element.94), channel_id=1, source_target_pairs={{0,8},{8,16},{16,24},{24,32},{32,40},{40,48},{48,56},{56,0},{1,9},... | collective-permute-start | bytes 983048 | tf_op jit(solution)/shard_map/ppermute | solution.py:19
  71.2 2.7 %collective-permute-start.13 = (f32[64,64]{1,0:T(8,128)S(1)}, f32[64,64]{1,0:T(8,128)S(1)}, u32[]{:S(2)}, u32[]{:S(2)}) collective-permute-start(f32[64,64]{1,0:T(8,128)S(1)} %convolution_bitcast_fusion.1), channel_id=1, source_target_pairs={{0,8},{8,0},{16,24},{24,16},{32,40},{40,32},{48,56},{56,48},{1,9},... | collective-permute-start | bytes 49160 | tf_op jit(solution)/shard_map/ppermute | solution.py:23
  73.8 4.4 %collective-permute-done.8.rz_up = f32[80,8,128]{2,1,0:T(8,128)S(1)} collective-permute-done((f32[80,8,128]{2,1,0:T(8,128)S(1)}, f32[80,8,128]{2,1,0:T(8,128)S(1)}, u32[]{:S(2)}, u32[]{:S(2)}) %collective-permute-start.8) | collective-permute-done | bytes 327712 | tf_op jit(solution)/shard_map/ppermute | solution.py:19
  78.2 1.2 collective-permute-done.9.rz_down
  79.4 2.2 %round3_kernel.1 = (f32[96,8,128]{2,1,0:T(8,128)S(1)}, f32[98,8,128]{2,1,0:T(8,128)S(1)}, f32[98,8,128]{2,1,0:T(8,128)S(1)}) custom-call(f32[848,8,128]{2,1,0:T(8,128)S(1)} %copy-done.2, f32[848,8,128]{2,1,0:T(8,128)} %collective-permute-done.5.got, f32[96,8,128]{2,1,0:T(8,128)S(1)} %collective-permute-done.6.ry_up, ...), custom_call_target="tpu_custom_call" | custom-call | tf_op jit(solution)/shard_map/round3_kernel/pallas_call | solution.py:360
  81.6 2.6 %collective-permute-start.11 = (f32[98,8,128]{2,1,0:T(8,128)S(1)}, f32[98,8,128]{2,1,0:T(8,128)S(1)}, u32[]{:S(2)}, u32[]{:S(2)}) collective-permute-start(f32[98,8,128]{2,1,0:T(8,128)S(1)} %get-tuple-element.105), channel_id=1, source_target_pairs={{0,8},{8,16},{16,24},{24,32},{32,40},{40,48},{48,56},{56,0},{1,9},... | collective-permute-start | bytes 1204232 | tf_op jit(solution)/shard_map/ppermute | solution.py:19
  84.6 4.1 %collective-permute-start.16 = (f32[64,64]{1,0:T(8,128)S(1)}, f32[64,64]{1,0:T(8,128)S(1)}, u32[]{:S(2)}, u32[]{:S(2)}) collective-permute-start(f32[64,64]{1,0:T(8,128)S(1)} %convolution_bitcast_fusion), channel_id=1, source_target_pairs={{0,16},{8,24},{16,0},{24,8},{32,48},{40,56},{48,32},{56,40},{1,17}... | collective-permute-start | bytes 49160 | tf_op jit(solution)/shard_map/ppermute | solution.py:23
  88.8 3.3 %collective-permute-done.11.rz_up.z_up = f32[98,8,128]{2,1,0:T(8,128)S(1)} collective-permute-done((f32[98,8,128]{2,1,0:T(8,128)S(1)}, f32[98,8,128]{2,1,0:T(8,128)S(1)}, u32[]{:S(2)}, u32[]{:S(2)}) %collective-permute-start.11) | collective-permute-done | bytes 401440 | tf_op jit(solution)/shard_map/ppermute | solution.py:19
  92.0 3.4 %collective-permute-done.12.rz_down.z_down = f32[98,8,128]{2,1,0:T(8,128)S(1)} collective-permute-done((f32[98,8,128]{2,1,0:T(8,128)S(1)}, f32[98,8,128]{2,1,0:T(8,128)S(1)}, u32[]{:S(2)}, u32[]{:S(2)}) %collective-permute-start.12) | collective-permute-done | bytes 401440 | tf_op jit(solution)/shard_map/ppermute | solution.py:19
  95.4 2.1 %round4_kernel.1 = (f32[92,8,128]{2,1,0:T(8,128)S(1)}, f32[92,8,128]{2,1,0:T(8,128)S(1)}) custom-call(f32[848,8,128]{2,1,0:T(8,128)S(1)} %copy-done.2, f32[848,8,128]{2,1,0:T(8,128)} %collective-permute-done.5.got, f32[96,8,128]{2,1,0:T(8,128)S(1)} %get-tuple-element.101.ey, f32[98,8,128]{2,1,0:T(8,128)S(1)} %collective-permute-done.11.rz_up.z_up, ...), custom_call_target="tpu_custom_call" | custom-call | tf_op jit(solution)/shard_map/round4_kernel/pallas_call | solution.py:360
  97.5 1.5 %collective-permute-start.14 = (f32[92,8,128]{2,1,0:T(8,128)S(1)}, f32[92,8,128]{2,1,0:T(8,128)S(1)}, u32[]{:S(2)}, u32[]{:S(2)}) collective-permute-start(f32[92,8,128]{2,1,0:T(8,128)S(1)} %get-tuple-element.113), channel_id=1, source_target_pairs={{0,8},{8,16},{16,24},{24,32},{32,40},{40,48},{48,56},{56,0},{1,9},... | collective-permute-start | bytes 1130504 | tf_op jit(solution)/shard_map/ppermute | solution.py:19
  99.0 0.6 collective-permute-start.15
  99.7 4.7 %node_factors.1 = f32[4,16,64]{2,1,0:T(8,128)} custom-call(s32[1]{0:T(128)} %bitcast.me_ref, f32[4,64,64]{2,1,0:T(8,128)S(1)} %pad_maximum_fusion.g_ref), custom_call_target="tpu_custom_call" | custom-call | tf_op jit(solution)/shard_map/node_factors/pallas_call | solution.py:128
  104.4 1.0 collective-permute-done.14.rz_up
  105.4 1.6 %collective-permute-done.15.rz_down = f32[92,8,128]{2,1,0:T(8,128)S(1)} collective-permute-done((f32[92,8,128]{2,1,0:T(8,128)S(1)}, f32[92,8,128]{2,1,0:T(8,128)S(1)}, u32[]{:S(2)}, u32[]{:S(2)}) %collective-permute-start.15) | collective-permute-done | bytes 376864 | tf_op jit(solution)/shard_map/ppermute | solution.py:19
  107.0 2.1 %round5_kernel.1 = (f32[20,8,128]{2,1,0:T(8,128)S(1)}, f32[20,8,128]{2,1,0:T(8,128)S(1)}, f32[20,8,128]{2,1,0:T(8,128)S(1)}, f32[20,8,128]{2,1,0:T(8,128)S(1)}, ...) custom-call(f32[848,8,128]{2,1,0:T(8,128)S(1)} %copy-done.2, f32[848,8,128]{2,1,0:T(8,128)} %collective-permute-done.5.got, ...), custom_call_target="tpu_custom_call" | custom-call | tf_op jit(solution)/shard_map/round5_kernel/pallas_call | solution.py:360
  109.1 3.8 %collective-permute-start.20 = (f32[20,8,128]{2,1,0:T(8,128)S(1)}, f32[20,8,128]{2,1,0:T(8,128)S(1)}, u32[]{:S(2)}, u32[]{:S(2)}) collective-permute-start(f32[20,8,128]{2,1,0:T(8,128)S(1)} %get-tuple-element.123), channel_id=1, source_target_pairs={{0,128},{64,192},{128,0},{192,64},{1,129},{65,193},{129,1},{193,65... | collective-permute-start | bytes 245768 | tf_op jit(solution)/shard_map/ppermute | solution.py:19
  112.9 3.0 %collective-permute-start.17 = (f32[12,8,128]{2,1,0:T(8,128)S(1)}, f32[12,8,128]{2,1,0:T(8,128)S(1)}, u32[]{:S(2)}, u32[]{:S(2)}) collective-permute-start(f32[12,8,128]{2,1,0:T(8,128)S(1)} %get-tuple-element.119), channel_id=1, source_target_pairs={{0,16},{8,24},{16,32},{24,40},{32,48},{40,56},{48,0},{56,8},{1,17}... | collective-permute-start | bytes 147464 | tf_op jit(solution)/shard_map/ppermute | solution.py:19
  115.9 1.2 collective-permute-start.18
  117.0 2.1 %collective-permute-done.17.z_two = f32[12,8,128]{2,1,0:T(8,128)S(1)} collective-permute-done((f32[12,8,128]{2,1,0:T(8,128)S(1)}, f32[12,8,128]{2,1,0:T(8,128)S(1)}, u32[]{:S(2)}, u32[]{:S(2)}) %collective-permute-start.17) | collective-permute-done | bytes 49184 | tf_op jit(solution)/shard_map/ppermute | solution.py:19
  119.1 1.7 %collective-permute-done.18.z_six = f32[12,8,128]{2,1,0:T(8,128)S(1)} collective-permute-done((f32[12,8,128]{2,1,0:T(8,128)S(1)}, f32[12,8,128]{2,1,0:T(8,128)S(1)}, u32[]{:S(2)}, u32[]{:S(2)}) %collective-permute-start.18) | collective-permute-done | bytes 49184 | tf_op jit(solution)/shard_map/ppermute | solution.py:19
  121.2 0.6 collective-permute-start.22
  121.7 2.7 %collective-permute-start.23 = (f32[8,8,128]{2,1,0:T(8,128)S(1)}, f32[8,8,128]{2,1,0:T(8,128)S(1)}, u32[]{:S(2)}, u32[]{:S(2)}) collective-permute-start(f32[8,8,128]{2,1,0:T(8,128)S(1)} %get-tuple-element.127), channel_id=1, source_target_pairs={{0,2},{1,3},{2,0},{3,1},{4,6},{5,7},{6,4},{7,5},{8,10},{9,11},{10,... | collective-permute-start | bytes 98312 | tf_op jit(solution)/shard_map/ppermute | solution.py:19
  124.4 0.9 collective-permute-start.24
  125.4 1.0 collective-permute-done.22.m1_ref
  126.4 0.8 collective-permute-done.23.m2_ref
  127.2 1.2 collective-permute-done.24.m3_ref
  128.3 1.7 %left_factor.1 = f32[32,16,64]{2,1,0:T(8,128)} custom-call(s32[1]{0:T(128)} %bitcast.me_ref, f32[4,9,32,128]{3,2,1,0:T(8,128)S(1)} %bitcast.58, f32[8,8,128]{2,1,0:T(8,128)S(1)} %get-tuple-element.125.m0_ref, f32[8,8,128]{2,1,0:T(8,128)S(1)} %collective-permute-done.22.m1_ref, f32[8,8,128]{2,1,0:T(8,128)S(1)} %collective-permute-done.23.m2_ref, ...), custom_call_target="tpu_custom_call" | custom-call | tf_op jit(solution)/shard_map/left_factor/pallas_call | solution.py:434
  (49 shorter events, 2.2 us)
Async XLA Ops:
  0.6 8.1 %copy-start = (f32[1,32,64,64]{3,2,1,0:T(8,128)S(1)}, f32[1,32,64,64]{3,2,1,0:T(8,128)}, u32[]{:S(2)}) copy-start(f32[1,32,64,64]{3,2,1,0:T(8,128)} %param.10) | copy-start | bytes 1572868
  0.6 13.9 %all-to-all-start = ((f32[32,16,256]{2,1,0:T(8,128)}), f32[32,16,256]{2,1,0:T(8,128)S(1)}, u32[]{:S(2)}, u32[]{:S(2)}) async-start(f32[32,16,256]{2,1,0:T(8,128)} %bitcast.61), calls=%async_computation | async-start | bytes 1048576 | tf_op jit(solution)/shard_map/all_to_all | solution.py:480
  32.9 21.4 %copy-start.3 = (f32[1,64,64]{2,1,0:T(8,128)S(1)}, f32[1,64,64]{2,1,0:T(8,128)}, u32[]{:S(2)}) copy-start(f32[1,64,64]{2,1,0:T(8,128)} %param.11) | copy-start | bytes 49156
  44.6 1.8 %copy-start.1 = (f32[848,8,128]{2,1,0:T(8,128)}, f32[848,8,128]{2,1,0:T(8,128)S(1)}, u32[]{:S(2)}) copy-start(f32[848,8,128]{2,1,0:T(8,128)S(1)} %get-tuple-element.67.keep) | copy-start | bytes 10420228
  46.3 2.2 %collective-permute-start = (f32[176,8,128]{2,1,0:T(8,128)S(1)}, f32[176,8,128]{2,1,0:T(8,128)S(1)}, u32[]{:S(2)}, u32[]{:S(2)}) collective-permute-start(f32[176,8,128]{2,1,0:T(8,128)S(1)} %get-tuple-element.69), channel_id=1, source_target_pairs={{0,4},{4,0},{1,5},{5,1},{2,6},{6,2},{3,7},{7,3},{8,12},{12,8},{9,1... | collective-permute-start | bytes 2162696 | tf_op jit(solution)/shard_map/ppermute | solution.py:23
  48.5 11.5 %collective-permute-start.5 = (f32[848,8,128]{2,1,0:T(8,128)}, f32[848,8,128]{2,1,0:T(8,128)}, u32[]{:S(2)}, u32[]{:S(2)}) collective-permute-start(f32[848,8,128]{2,1,0:T(8,128)} %get-tuple-element.80), channel_id=1, source_target_pairs={{0,4},{4,0},{1,5},{5,1},{2,6},{6,2},{3,7},{7,3},{8,12},{12,8},{9,1... | collective-permute-start | bytes 10420232 | tf_op jit(solution)/shard_map/ppermute | solution.py:23
  48.7 11.3 %collective-permute-start.1 = (f32[48,8,128]{2,1,0:T(8,128)S(1)}, f32[48,8,128]{2,1,0:T(8,128)S(1)}, u32[]{:S(2)}, u32[]{:S(2)}) collective-permute-start(f32[48,8,128]{2,1,0:T(8,128)S(1)} %get-tuple-element.76), channel_id=1, source_target_pairs={{0,64},{64,128},{128,192},{192,0},{1,65},{65,129},{129,193},{193,1... | collective-permute-start | bytes 589832 | tf_op jit(solution)/shard_map/ppermute | solution.py:19
  50.5 9.6 %collective-permute-start.2 = (f32[48,8,128]{2,1,0:T(8,128)S(1)}, f32[48,8,128]{2,1,0:T(8,128)S(1)}, u32[]{:S(2)}, u32[]{:S(2)}) collective-permute-start(f32[48,8,128]{2,1,0:T(8,128)S(1)} %get-tuple-element.77), channel_id=1, source_target_pairs={{0,192},{64,0},{128,64},{192,128},{1,193},{65,1},{129,65},{193,129... | collective-permute-start | bytes 589832 | tf_op jit(solution)/shard_map/ppermute | solution.py:19
  52.1 6.2 %collective-permute-start.3 = (f32[40,8,128]{2,1,0:T(8,128)S(1)}, f32[40,8,128]{2,1,0:T(8,128)S(1)}, u32[]{:S(2)}, u32[]{:S(2)}) collective-permute-start(f32[40,8,128]{2,1,0:T(8,128)S(1)} %get-tuple-element.78), channel_id=1, source_target_pairs={{0,8},{8,16},{16,24},{24,32},{32,40},{40,48},{48,56},{56,0},{1,9},... | collective-permute-start | bytes 491528 | tf_op jit(solution)/shard_map/ppermute | solution.py:19
  54.2 5.9 %collective-permute-start.4 = (f32[40,8,128]{2,1,0:T(8,128)S(1)}, f32[40,8,128]{2,1,0:T(8,128)S(1)}, u32[]{:S(2)}, u32[]{:S(2)}) collective-permute-start(f32[40,8,128]{2,1,0:T(8,128)S(1)} %get-tuple-element.79), channel_id=1, source_target_pairs={{0,56},{8,0},{16,8},{24,16},{32,24},{40,32},{48,40},{56,48},{1,57}... | collective-permute-start | bytes 491528 | tf_op jit(solution)/shard_map/ppermute | solution.py:19
  58.2 12.5 %collective-permute-start.10 = (f32[64,64]{1,0:T(8,128)S(1)}, f32[64,64]{1,0:T(8,128)S(1)}, u32[]{:S(2)}, u32[]{:S(2)}) collective-permute-start(f32[64,64]{1,0:T(8,128)S(1)} %convolution_bitcast_fusion.2), channel_id=1, source_target_pairs={{0,4},{4,0},{1,5},{5,1},{2,6},{6,2},{3,7},{7,3},{8,12},{12,8},{9,1... | collective-permute-start | bytes 49160 | tf_op jit(solution)/shard_map/ppermute | solution.py:23
  60.1 2.0 %copy-start.2 = (f32[848,8,128]{2,1,0:T(8,128)S(1)}, f32[848,8,128]{2,1,0:T(8,128)}, u32[]{:S(2)}) copy-start(f32[848,8,128]{2,1,0:T(8,128)} %copy-done.1) | copy-start | bytes 10420228
  62.0 8.7 %copy-start.4 = (f32[1,64,64]{2,1,0:T(8,128)S(1)}, f32[1,64,64]{2,1,0:T(8,128)}, u32[]{:S(2)}) copy-start(f32[1,64,64]{2,1,0:T(8,128)} %param.12) | copy-start | bytes 49156
  64.2 15.2 %collective-permute-start.6 = (f32[96,8,128]{2,1,0:T(8,128)S(1)}, f32[96,8,128]{2,1,0:T(8,128)S(1)}, u32[]{:S(2)}, u32[]{:S(2)}) collective-permute-start(f32[96,8,128]{2,1,0:T(8,128)S(1)} %get-tuple-element.92), channel_id=1, source_target_pairs={{0,64},{64,128},{128,192},{192,0},{1,65},{65,129},{129,193},{193,1... | collective-permute-start | bytes 1179656 | tf_op jit(solution)/shard_map/ppermute | solution.py:19
  64.6 14.8 %collective-permute-start.7 = (f32[96,8,128]{2,1,0:T(8,128)S(1)}, f32[96,8,128]{2,1,0:T(8,128)S(1)}, u32[]{:S(2)}, u32[]{:S(2)}) collective-permute-start(f32[96,8,128]{2,1,0:T(8,128)S(1)} %get-tuple-element.93), channel_id=1, source_target_pairs={{0,192},{64,0},{128,64},{192,128},{1,193},{65,1},{129,65},{193,129... | collective-permute-start | bytes 1179656 | tf_op jit(solution)/shard_map/ppermute | solution.py:19
  67.7 10.5 %collective-permute-start.8 = (f32[80,8,128]{2,1,0:T(8,128)S(1)}, f32[80,8,128]{2,1,0:T(8,128)S(1)}, u32[]{:S(2)}, u32[]{:S(2)}) collective-permute-start(f32[80,8,128]{2,1,0:T(8,128)S(1)} %get-tuple-element.94), channel_id=1, source_target_pairs={{0,8},{8,16},{16,24},{24,32},{32,40},{40,48},{48,56},{56,0},{1,9},... | collective-permute-start | bytes 983048 | tf_op jit(solution)/shard_map/ppermute | solution.py:19
  70.7 8.7 %collective-permute-start.9 = (f32[80,8,128]{2,1,0:T(8,128)S(1)}, f32[80,8,128]{2,1,0:T(8,128)S(1)}, u32[]{:S(2)}, u32[]{:S(2)}) collective-permute-start(f32[80,8,128]{2,1,0:T(8,128)S(1)} %get-tuple-element.95), channel_id=1, source_target_pairs={{0,56},{8,0},{16,8},{24,16},{32,24},{40,32},{48,40},{56,48},{1,57}... | collective-permute-start | bytes 983048 | tf_op jit(solution)/shard_map/ppermute | solution.py:19
  71.2 13.0 %collective-permute-start.13 = (f32[64,64]{1,0:T(8,128)S(1)}, f32[64,64]{1,0:T(8,128)S(1)}, u32[]{:S(2)}, u32[]{:S(2)}) collective-permute-start(f32[64,64]{1,0:T(8,128)S(1)} %convolution_bitcast_fusion.1), channel_id=1, source_target_pairs={{0,8},{8,0},{16,24},{24,16},{32,40},{40,32},{48,56},{56,48},{1,9},... | collective-permute-start | bytes 49160 | tf_op jit(solution)/shard_map/ppermute | solution.py:23
  73.8 10.4 %copy-start.5 = (f32[1,64,64]{2,1,0:T(8,128)S(1)}, f32[1,64,64]{2,1,0:T(8,128)}, u32[]{:S(2)}) copy-start(f32[1,64,64]{2,1,0:T(8,128)} %param.13) | copy-start | bytes 49156
  81.6 10.4 %collective-permute-start.11 = (f32[98,8,128]{2,1,0:T(8,128)S(1)}, f32[98,8,128]{2,1,0:T(8,128)S(1)}, u32[]{:S(2)}, u32[]{:S(2)}) collective-permute-start(f32[98,8,128]{2,1,0:T(8,128)S(1)} %get-tuple-element.105), channel_id=1, source_target_pairs={{0,8},{8,16},{16,24},{24,32},{32,40},{40,48},{48,56},{56,0},{1,9},... | collective-permute-start | bytes 1204232 | tf_op jit(solution)/shard_map/ppermute | solution.py:19
  84.2 11.2 %collective-permute-start.12 = (f32[98,8,128]{2,1,0:T(8,128)S(1)}, f32[98,8,128]{2,1,0:T(8,128)S(1)}, u32[]{:S(2)}, u32[]{:S(2)}) collective-permute-start(f32[98,8,128]{2,1,0:T(8,128)S(1)} %get-tuple-element.106), channel_id=1, source_target_pairs={{0,56},{8,0},{16,8},{24,16},{32,24},{40,32},{48,40},{56,48},{1,57}... | collective-permute-start | bytes 1204232 | tf_op jit(solution)/shard_map/ppermute | solution.py:19
  84.6 15.0 %collective-permute-start.16 = (f32[64,64]{1,0:T(8,128)S(1)}, f32[64,64]{1,0:T(8,128)S(1)}, u32[]{:S(2)}, u32[]{:S(2)}) collective-permute-start(f32[64,64]{1,0:T(8,128)S(1)} %convolution_bitcast_fusion), channel_id=1, source_target_pairs={{0,16},{8,24},{16,0},{24,8},{32,48},{40,56},{48,32},{56,40},{1,17}... | collective-permute-start | bytes 49160 | tf_op jit(solution)/shard_map/ppermute | solution.py:23
  97.5 7.9 %collective-permute-start.14 = (f32[92,8,128]{2,1,0:T(8,128)S(1)}, f32[92,8,128]{2,1,0:T(8,128)S(1)}, u32[]{:S(2)}, u32[]{:S(2)}) collective-permute-start(f32[92,8,128]{2,1,0:T(8,128)S(1)} %get-tuple-element.113), channel_id=1, source_target_pairs={{0,8},{8,16},{16,24},{24,32},{32,40},{40,48},{48,56},{56,0},{1,9},... | collective-permute-start | bytes 1130504 | tf_op jit(solution)/shard_map/ppermute | solution.py:19
  99.0 8.0 %collective-permute-start.15 = (f32[92,8,128]{2,1,0:T(8,128)S(1)}, f32[92,8,128]{2,1,0:T(8,128)S(1)}, u32[]{:S(2)}, u32[]{:S(2)}) collective-permute-start(f32[92,8,128]{2,1,0:T(8,128)S(1)} %get-tuple-element.114), channel_id=1, source_target_pairs={{0,56},{8,0},{16,8},{24,16},{32,24},{40,32},{48,40},{56,48},{1,57}... | collective-permute-start | bytes 1130504 | tf_op jit(solution)/shard_map/ppermute | solution.py:19
  109.1 11.8 %collective-permute-start.19 = (f32[20,8,128]{2,1,0:T(8,128)S(1)}, f32[20,8,128]{2,1,0:T(8,128)S(1)}, u32[]{:S(2)}, u32[]{:S(2)}) collective-permute-start(f32[20,8,128]{2,1,0:T(8,128)S(1)} %get-tuple-element.122), channel_id=1, source_target_pairs={{0,64},{64,128},{128,192},{192,0},{1,65},{65,129},{129,193},{193,1... | collective-permute-start | bytes 245768 | tf_op jit(solution)/shard_map/ppermute | solution.py:19
  109.1 11.7 %collective-permute-start.20 = (f32[20,8,128]{2,1,0:T(8,128)S(1)}, f32[20,8,128]{2,1,0:T(8,128)S(1)}, u32[]{:S(2)}, u32[]{:S(2)}) collective-permute-start(f32[20,8,128]{2,1,0:T(8,128)S(1)} %get-tuple-element.123), channel_id=1, source_target_pairs={{0,128},{64,192},{128,0},{192,64},{1,129},{65,193},{129,1},{193,65... | collective-permute-start | bytes 245768 | tf_op jit(solution)/shard_map/ppermute | solution.py:19
  112.9 8.0 %collective-permute-start.21 = (f32[20,8,128]{2,1,0:T(8,128)S(1)}, f32[20,8,128]{2,1,0:T(8,128)S(1)}, u32[]{:S(2)}, u32[]{:S(2)}) collective-permute-start(f32[20,8,128]{2,1,0:T(8,128)S(1)} %get-tuple-element.124), channel_id=1, source_target_pairs={{0,192},{64,0},{128,64},{192,128},{1,193},{65,1},{129,65},{193,129... | collective-permute-start | bytes 245768 | tf_op jit(solution)/shard_map/ppermute | solution.py:19
  112.9 6.2 %collective-permute-start.17 = (f32[12,8,128]{2,1,0:T(8,128)S(1)}, f32[12,8,128]{2,1,0:T(8,128)S(1)}, u32[]{:S(2)}, u32[]{:S(2)}) collective-permute-start(f32[12,8,128]{2,1,0:T(8,128)S(1)} %get-tuple-element.119), channel_id=1, source_target_pairs={{0,16},{8,24},{16,32},{24,40},{32,48},{40,56},{48,0},{56,8},{1,17}... | collective-permute-start | bytes 147464 | tf_op jit(solution)/shard_map/ppermute | solution.py:19
  115.9 5.0 %collective-permute-start.18 = (f32[12,8,128]{2,1,0:T(8,128)S(1)}, f32[12,8,128]{2,1,0:T(8,128)S(1)}, u32[]{:S(2)}, u32[]{:S(2)}) collective-permute-start(f32[12,8,128]{2,1,0:T(8,128)S(1)} %get-tuple-element.120), channel_id=1, source_target_pairs={{0,48},{8,56},{16,0},{24,8},{32,16},{40,24},{48,32},{56,40},{1,49}... | collective-permute-start | bytes 147464 | tf_op jit(solution)/shard_map/ppermute | solution.py:19
  121.2 5.2 %collective-permute-start.22 = (f32[8,8,128]{2,1,0:T(8,128)S(1)}, f32[8,8,128]{2,1,0:T(8,128)S(1)}, u32[]{:S(2)}, u32[]{:S(2)}) collective-permute-start(f32[8,8,128]{2,1,0:T(8,128)S(1)} %get-tuple-element.126), channel_id=1, source_target_pairs={{0,1},{1,2},{2,3},{3,0},{4,5},{5,6},{6,7},{7,4},{8,9},{9,10},{10,1... | collective-permute-start | bytes 98312 | tf_op jit(solution)/shard_map/ppermute | solution.py:19
  121.7 5.4 %collective-permute-start.23 = (f32[8,8,128]{2,1,0:T(8,128)S(1)}, f32[8,8,128]{2,1,0:T(8,128)S(1)}, u32[]{:S(2)}, u32[]{:S(2)}) collective-permute-start(f32[8,8,128]{2,1,0:T(8,128)S(1)} %get-tuple-element.127), channel_id=1, source_target_pairs={{0,2},{1,3},{2,0},{3,1},{4,6},{5,7},{6,4},{7,5},{8,10},{9,11},{10,... | collective-permute-start | bytes 98312 | tf_op jit(solution)/shard_map/ppermute | solution.py:19
  124.4 3.9 %collective-permute-start.24 = (f32[8,8,128]{2,1,0:T(8,128)S(1)}, f32[8,8,128]{2,1,0:T(8,128)S(1)}, u32[]{:S(2)}, u32[]{:S(2)}) collective-permute-start(f32[8,8,128]{2,1,0:T(8,128)S(1)} %get-tuple-element.128), channel_id=1, source_target_pairs={{0,3},{1,0},{2,1},{3,2},{4,7},{5,4},{6,5},{7,6},{8,11},{9,8},{10,9... | collective-permute-start | bytes 98312 | tf_op jit(solution)/shard_map/ppermute | solution.py:19

commit v7 on v6

--- a/solution.py
+++ b/solution.py
@@ -114,7 +114,41 @@
     )(x, moves)
 
 
-def node_kernel(me_ref, g_ref, out_ref, s_ref, l_ref):
+def level_term(level, transfer):
+    moved = jnp.dot(level, transfer, precision=HIGHEST, preferred_element_type=jnp.float32)
+    return jnp.dot(transfer.T, moved, precision=HIGHEST, preferred_element_type=jnp.float32)
+
+
+def first_level_kernel(packed_ref, move_ref, gram_ref, term_ref):
+    leaves = packed_ref.shape[1] - 1
+    gram = unpacked(jnp.sum(packed_ref[:, leaves], axis=0))
+    gram_ref[...] = gram
+    term_ref[...] = level_term(gram, move_ref[...])
+
+
+def next_level_kernel(mine_ref, other_ref, move_ref, gram_ref, term_ref):
+    gram = mine_ref[...] + other_ref[...]
+    gram_ref[...] = gram
+    term_ref[...] = level_term(gram, move_ref[...])
+
+
+def level(kernel, *arrays):
+    vmem = pl.BlockSpec(memory_space=pltpu.VMEM)
+    return pl.pallas_call(
+        kernel,
+        in_specs=[vmem] * len(arrays),
+        out_specs=(vmem, vmem),
+        out_shape=(jax.ShapeDtypeStruct((RANK, RANK), jnp.float32),) * 2,
+        compiler_params=pltpu.CompilerParams(vmem_limit_bytes=4 * 2**20),
+        name=kernel.__name__,
+    )(*arrays)
+
+
+def node_kernel(me_ref, g1_ref, g2_ref, g3_ref, mine_ref, other_ref, out_ref, s_ref, l_ref):
+    g_ref = l_ref
+    for t, ref in enumerate((g1_ref, g2_ref, g3_ref)):
+        g_ref[t] = ref[...]
+    g_ref[3] = mine_ref[...] + other_ref[...]
     to_lanes(g_ref, s_ref)
     factor_in_place(s_ref)
     for c in range(RANK):
@@ -125,18 +159,19 @@
 
 def node_lower(me, grams, width):
     vmem = pl.BlockSpec(memory_space=pltpu.VMEM)
+    count = len(grams) - 1
     return pl.pallas_call(
         node_kernel,
-        out_shape=jax.ShapeDtypeStruct((grams.shape[0], width, RANK), jnp.float32),
-        in_specs=[pl.BlockSpec(memory_space=pltpu.SMEM), vmem],
+        out_shape=jax.ShapeDtypeStruct((count, width, RANK), jnp.float32),
+        in_specs=[pl.BlockSpec(memory_space=pltpu.SMEM)] + [vmem] * len(grams),
         out_specs=vmem,
         scratch_shapes=[
-            pltpu.VMEM((RANK, RANK, grams.shape[0]), jnp.float32),
-            pltpu.VMEM(grams.shape, jnp.float32),
+            pltpu.VMEM((RANK, RANK, count), jnp.float32),
+            pltpu.VMEM((count, RANK, RANK), jnp.float32),
         ],
         compiler_params=pltpu.CompilerParams(vmem_limit_bytes=10 * 2**20),
         name="node_factors",
-    )(me, grams)
+    )(me, *grams)
 
 
 def split(value):
@@ -173,7 +208,7 @@
 
 def product_kernel(
     me_ref, place_ref, c_hbm, l_ref, o0_ref, o1_ref, o2_ref, o3_ref, rows_ref,
-    acc_ref, c_ref, sems, out_sems,
+    acc_ref, c_ref, sems,
 ):
     leaves, listed, width, _ = c_hbm.shape
     slots, group = c_ref.shape[0], c_ref.shape[1]
@@ -217,18 +252,10 @@
         return carry
 
     lax.fori_loop(0, steps, body, 0)
-    near, far = o0_ref.shape[0], o1_ref.shape[0]
-    total = near + far
-    copies = [
-        pltpu.make_async_copy(acc_ref.at[pl.ds(at, far)], ref, sem)
-        for at, ref, sem in ((near, o1_ref, out_sems.at[0]), (total + near, o3_ref, out_sems.at[1]))
-    ]
-    for copy in copies:
-        copy.start()
-    o0_ref[...] = acc_ref[:near]
-    o2_ref[...] = acc_ref[total : total + near]
-    for copy in copies:
-        copy.wait()
+    at = 0
+    for ref in (o0_ref, o1_ref, o2_ref, o3_ref):
+        ref[...] = acc_ref[at : at + ref.shape[0]]
+        at += ref.shape[0]
 
 
 def weighted_sums(me, place, blocks, packed, parts):
@@ -249,12 +276,11 @@
             hbm,
             vmem,
         ],
-        out_specs=(vmem, hbm, vmem, hbm, vmem),
+        out_specs=(vmem,) * (len(parts) + 1),
         scratch_shapes=[
             pltpu.VMEM((sum(parts) + TILE, top, 2 * rank), jnp.float32),
             pltpu.VMEM((slots, group, listed, width, rank), jnp.float32),
             pltpu.SemaphoreType.DMA((slots,)),
-            pltpu.SemaphoreType.DMA((2,)),
         ],
         out_shape=tuple(out(rows) for rows in parts)
         + (jax.ShapeDtypeStruct((leaves, width, rank), jnp.float32),),
@@ -490,10 +516,6 @@
     got_near, away_far = tie(got_near, away_far)
     got_far = swap(away_far, "core", 1)
 
-    def level_term(level, transfer):
-        moved = jnp.dot(level, transfer, precision=HIGHEST)
-        return jnp.dot(transfer.T, moved, precision=HIGHEST)
-
     def along(axis, up, down):
         return shift(up, axis, 1), shift(down, axis, -1)
 
@@ -505,10 +527,9 @@
     sent = run_round(
         round1_kernel, plan, (y_rows // 2,) * 2 + (z_rows // 2,) * 2, keep_near, got_near
     )
-    sent, terms = tie(sent, packed[:, share])
+    sent, shared = tie(sent, packed)
     rz_up, rz_down, ry_up, ry_down = send(sent)
-    grams = [unpacked(jnp.sum(terms, axis=0))]
-    term = level_term(grams[0], node_transfer[0])
+    gram1, term = level(first_level_kernel, shared, node_transfer[0])
     other = swap(term, "core", 1)
     ry_up, ry_down, rz_up, rz_down, got_far, term = tie(
         ry_up, ry_down, rz_up, rz_down, got_far, term
@@ -520,8 +541,7 @@
     )
     sent, term = tie(sent, term)
     rz_up, rz_down, ry_up, ry_down = send(sent)
-    grams.append(term + other)
-    term = level_term(grams[1], pair_transfer[0])
+    gram2, term = level(next_level_kernel, term, other, pair_transfer[0])
     other = swap(term, "z", 1)
     ry_up, ry_down, rz_up, rz_down, term = tie(ry_up, ry_down, rz_up, rz_down, term)
 
@@ -531,8 +551,7 @@
     )
     up, down, term = tie(up, down, term)
     ride_up, ride_down = along("z", up, down)
-    grams.append(term + other)
-    term = level_term(grams[2], quad_transfer[0])
+    gram3, term = level(next_level_kernel, term, other, quad_transfer[0])
     other = swap(term, "z", 2)
     ride_up, ride_down, term = tie(ride_up, ride_down, term)
 
@@ -540,8 +559,7 @@
     up, down = run_round(round4_kernel, plan, (both, both), *sums, ey, ride_up, ride_down)
     up, down, term = tie(up, down, term)
     rz_up, rz_down = along("z", up, down)
-    grams.append(term + other)
-    node_weights = node_lower(me, jnp.stack(grams), width)
+    node_weights = node_lower(me, (gram1, gram2, gram3, term, other), width)
     rz_up, rz_down, node_weights = tie(rz_up, rz_down, node_weights)
 
     ez, y_one, y_two, y_three, z_two, z_six = run_round(

time: 131 us -> 120 us (0.916)
  Pallas kernels: 32.3 us -> 24 us
  waiting for transfers between devices: 35 us -> 38.9 us
  local copies, waits for them, and re-layouts: 5.31 us -> 1.5 us
  starting transfers between devices: 40.2 us -> 37.3 us
    ppermute x5, waiting for transfers between devices: 2.2 us -> 15 us  [swap(): lax.ppermute(value, axis, [(i, i ^ mask) for i in range(lax.axis_size(axi...]
    ppermute x20, waiting for transfers between devices: 27 us -> 18.1 us  [shift(): lax.ppermute(value, axis, [(i, (i + step) % size) for i in range(size)])]
    pallas_call x5, Pallas kernels: 8.6 us -> 0.67 us  [run_round(): pl.pallas_call(functools.partial(kernel, plan), in_specs=[vmem] * len(arr...]
    unnamed x13 -> x9, local copies, waits for them, and re-layouts: 4.27 us -> 0.53 us
    ppermute x5, starting transfers between devices: 6.95 us -> 4.07 us  [swap(): lax.ppermute(value, axis, [(i, i ^ mask) for i in range(lax.axis_size(axi...]
    pallas_call x1, Pallas kernels: 11.7 us -> 10.3 us  [weighted_sums(): pl.pallas_call(product_kernel, in_specs=[pl.BlockSpec(memory_space=pltpu....]
    pallas_call x1 -> x4, Pallas kernels: 4.75 us -> 5.8 us  [the longest x1 4.74 us: node_lower(): pl.pallas_call(node_kernel, out_shape=jax.ShapeDtypeStruct((count, width,...]
  transfers between devices with their start and end apart: 26 -> 26, of which waited for: 15 -> 14; matrix products, arithmetic and copies ran while one was open for 4% -> 3% of each run, Pallas kernels for 9% -> 5%
where the time goes in v7:
time: 120 us; the launch traced here: 118 us
  waiting for transfers between devices  38.9 us (32%)
  starting transfers between devices  37.3 us (31%)
  Pallas kernels  24 us (20%)
  blocking collectives  13.1 us (11%)
  other arithmetic  2.17 us (2%)
  local copies, waits for them, and re-layouts  1.5 us (1%)
    ppermute x20, starting transfers between devices, shift(): lax.ppermute(value, axis, [(i, (i + step) % size) for i in range(size)])  28.8 us
    ppermute x20, waiting for transfers between devices, shift(): lax.ppermute(value, axis, [(i, (i + step) % size) for i in range(size)])  18.1 us
    ppermute x5, waiting for transfers between devices, swap(): lax.ppermute(value, axis, [(i, i ^ mask) for i in range(lax.axis_size(axi...  15 us
    all_gather x1, blocking collectives, shards(): packed = lax.all_gather(mine, 'rk', axis=0, tiled=False)  13.1 us
    pallas_call x1, Pallas kernels, weighted_sums(): pl.pallas_call(product_kernel, in_specs=[pl.BlockSpec(memory_space=pltpu....  10.3 us
    all_to_all x1, waiting for transfers between devices, shards(): lax.all_to_all(local, 'rk', split_axis=0, concat_axis=0, tiled=True)  5.82 us
    pallas_call x1, Pallas kernels, leaf_factors(): pl.pallas_call(leaf_kernel, out_shape=jax.ShapeDtypeStruct((leaves + 1, R...  5.19 us
    pallas_call x1, Pallas kernels, node_lower(): pl.pallas_call(node_kernel, out_shape=jax.ShapeDtypeStruct((count, width,...  4.74 us
  transfers between devices with their start and end apart: 26, of which 14 were waited for; matrix products, arithmetic and copies ran while one was open for 3% of the time, Pallas kernels for 5%

profile of v7, /device:TPU:32, one launch (start us, length us, event | category | flops | bytes accessed | tf_op | source)
XLA Modules:
  0.0 117.8 jit_solution(13069730375772461396)
XLA Ops:
  0.6 4.4 %all-to-all-start = ((f32[32,16,256]{2,1,0:T(8,128)}), f32[32,16,256]{2,1,0:T(8,128)S(1)}, u32[]{:S(2)}, u32[]{:S(2)}) async-start(f32[32,16,256]{2,1,0:T(8,128)} %bitcast.33), calls=%async_computation | async-start | bytes 1048576 | tf_op jit(solution)/shard_map/all_to_all | solution.py:506
  5.1 0.7 iota_compare_fusion
  5.9 0.8 squeeze.22
  6.7 0.5 broadcast.120
  7.2 1.4 %reduce.3 = s32[32,32]{1,0:T(8,128)S(1)} reduce(s32[1,32,32,1]{2,3,1,0:T(1,128)} %param.15, s32[]{:T(128)} %broadcast.120), dimensions={0,3}, to_apply=%param.15.reduce_sub_computation.3 | reduce | bytes 8196 | tf_op args[6]
  8.7 5.8 %all-to-all-done = f32[32,16,256]{2,1,0:T(8,128)S(1)} async-done(((f32[32,16,256]{2,1,0:T(8,128)}), f32[32,16,256]{2,1,0:T(8,128)S(1)}, u32[]{:S(2)}, u32[]{:S(2)}) %all-to-all-start) | async-done | bytes 524320 | tf_op jit(solution)/shard_map/all_to_all | solution.py:506
  14.6 5.2 %leaf_factors.1 = f32[9,32,128]{2,1,0:T(8,128)S(1)} custom-call(f32[4,8,16,256]{3,2,1,0:T(8,128)S(1)} %bitcast.28, f32[8,64,64]{2,1,0:T(8,128)S(1)} %dynamic-slice_bitcast_fusion.move_ref), custom_call_target="tpu_custom_call" | custom-call | tf_op jit(solution)/shard_map/leaf_factors/pallas_call | solution.py:103
  19.8 13.1 %all-gather = f32[36,32,128]{2,1,0:T(8,128)S(1)} all-gather(f32[9,32,128]{2,1,0:T(8,128)S(1)} %leaf_factors.1), channel_id=2, replica_groups=mesh['y'=4,'z'=8,'core'=2,'rk'=4] {'rk'}, dimensions={0}, use_global_device_ids=true | all-gather | bytes 737280 | tf_op jit(solution)/shard_map/all_gather | solution.py:509
  32.9 10.3 %weighted_sums.1 = (f32[176,8,128]{2,1,0:T(8,128)S(1)}, f32[848,8,128]{2,1,0:T(8,128)S(1)}, f32[176,8,128]{2,1,0:T(8,128)S(1)}, f32[848,8,128]{2,1,0:T(8,128)S(1)}, f32[32,16,64]{2,1,0:T(8,128)}) custom-call(s32[1]{0:T(128)} %bitcast.me_ref, s32[1024]{0:T(1024)S(1)} %add_select_fusion.5.place_ref, f32[32,32,16,64]{3,2,1,0:T(8,128)} %bitcast.32, ...), custom_call_target="tpu_custom_call" | custom-call | tf_op jit(solution)/shard_map/weighted_sums/pallas_call | solution.py:271
  43.3 2.2 %collective-permute-done.got = f32[176,8,128]{2,1,0:T(8,128)S(1)} collective-permute-done((f32[176,8,128]{2,1,0:T(8,128)S(1)}, f32[176,8,128]{2,1,0:T(8,128)S(1)}, u32[]{:S(2)}, u32[]{:S(2)}) %collective-permute-start) | collective-permute-done | bytes 720928 | tf_op jit(solution)/shard_map/ppermute | solution.py:23
  45.7 1.7 %collective-permute-start.1 = (f32[48,8,128]{2,1,0:T(8,128)S(1)}, f32[48,8,128]{2,1,0:T(8,128)S(1)}, u32[]{:S(2)}, u32[]{:S(2)}) collective-permute-start(f32[48,8,128]{2,1,0:T(8,128)S(1)} %get-tuple-element.82), channel_id=1, source_target_pairs={{0,64},{64,128},{128,192},{192,0},{1,65},{65,129},{129,193},{193,1... | collective-permute-start | bytes 589832 | tf_op jit(solution)/shard_map/ppermute | solution.py:19
  47.4 1.6 %collective-permute-start.2 = (f32[48,8,128]{2,1,0:T(8,128)S(1)}, f32[48,8,128]{2,1,0:T(8,128)S(1)}, u32[]{:S(2)}, u32[]{:S(2)}) collective-permute-start(f32[48,8,128]{2,1,0:T(8,128)S(1)} %get-tuple-element.83), channel_id=1, source_target_pairs={{0,192},{64,0},{128,64},{192,128},{1,193},{65,1},{129,65},{193,129... | collective-permute-start | bytes 589832 | tf_op jit(solution)/shard_map/ppermute | solution.py:19
  49.0 1.9 %collective-permute-start.3 = (f32[40,8,128]{2,1,0:T(8,128)S(1)}, f32[40,8,128]{2,1,0:T(8,128)S(1)}, u32[]{:S(2)}, u32[]{:S(2)}) collective-permute-start(f32[40,8,128]{2,1,0:T(8,128)S(1)} %get-tuple-element.84), channel_id=1, source_target_pairs={{0,8},{8,16},{16,24},{24,32},{32,40},{40,48},{48,56},{56,0},{1,9},... | collective-permute-start | bytes 491528 | tf_op jit(solution)/shard_map/ppermute | solution.py:19
  51.0 0.4 first_level_kernel.1
  51.4 3.6 %collective-permute-done.3.rz_up = f32[40,8,128]{2,1,0:T(8,128)S(1)} collective-permute-done((f32[40,8,128]{2,1,0:T(8,128)S(1)}, f32[40,8,128]{2,1,0:T(8,128)S(1)}, u32[]{:S(2)}, u32[]{:S(2)}) %collective-permute-start.3) | collective-permute-done | bytes 163872 | tf_op jit(solution)/shard_map/ppermute | solution.py:19
  55.1 1.9 %collective-permute-done.4.rz_down = f32[40,8,128]{2,1,0:T(8,128)S(1)} collective-permute-done((f32[40,8,128]{2,1,0:T(8,128)S(1)}, f32[40,8,128]{2,1,0:T(8,128)S(1)}, u32[]{:S(2)}, u32[]{:S(2)}) %collective-permute-start.4) | collective-permute-done | bytes 163872 | tf_op jit(solution)/shard_map/ppermute | solution.py:19
  57.0 0.2 round2_kernel.1
  57.1 0.4 collective-permute-start.6
  57.5 3.1 %collective-permute-start.7 = (f32[96,8,128]{2,1,0:T(8,128)S(1)}, f32[96,8,128]{2,1,0:T(8,128)S(1)}, u32[]{:S(2)}, u32[]{:S(2)}) collective-permute-start(f32[96,8,128]{2,1,0:T(8,128)S(1)} %get-tuple-element.100), channel_id=1, source_target_pairs={{0,192},{64,0},{128,64},{192,128},{1,193},{65,1},{129,65},{193,129... | collective-permute-start | bytes 1179656 | tf_op jit(solution)/shard_map/ppermute | solution.py:19
  60.6 3.0 %collective-permute-start.8 = (f32[80,8,128]{2,1,0:T(8,128)S(1)}, f32[80,8,128]{2,1,0:T(8,128)S(1)}, u32[]{:S(2)}, u32[]{:S(2)}) collective-permute-start(f32[80,8,128]{2,1,0:T(8,128)S(1)} %get-tuple-element.101), channel_id=1, source_target_pairs={{0,8},{8,16},{16,24},{24,32},{32,40},{40,48},{48,56},{56,0},{1,9},... | collective-permute-start | bytes 983048 | tf_op jit(solution)/shard_map/ppermute | solution.py:19
  63.6 1.2 %collective-permute-done.10.other_ref = f32[64,64]{1,0:T(8,128)S(1)} collective-permute-done((f32[64,64]{1,0:T(8,128)S(1)}, f32[64,64]{1,0:T(8,128)S(1)}, u32[]{:S(2)}, u32[]{:S(2)}) %collective-permute-start.10) | collective-permute-done | bytes 16416 | tf_op jit(solution)/shard_map/ppermute | solution.py:23
  64.8 0.3 next_level_kernel.2
  65.2 4.6 %collective-permute-done.8.rz_up = f32[80,8,128]{2,1,0:T(8,128)S(1)} collective-permute-done((f32[80,8,128]{2,1,0:T(8,128)S(1)}, f32[80,8,128]{2,1,0:T(8,128)S(1)}, u32[]{:S(2)}, u32[]{:S(2)}) %collective-permute-start.8) | collective-permute-done | bytes 327712 | tf_op jit(solution)/shard_map/ppermute | solution.py:19
  69.8 2.5 %collective-permute-done.9.rz_down = f32[80,8,128]{2,1,0:T(8,128)S(1)} collective-permute-done((f32[80,8,128]{2,1,0:T(8,128)S(1)}, f32[80,8,128]{2,1,0:T(8,128)S(1)}, u32[]{:S(2)}, u32[]{:S(2)}) %collective-permute-start.9) | collective-permute-done | bytes 327712 | tf_op jit(solution)/shard_map/ppermute | solution.py:19
  72.3 0.2 round3_kernel.1
  72.6 1.8 %collective-permute-start.11 = (f32[98,8,128]{2,1,0:T(8,128)S(1)}, f32[98,8,128]{2,1,0:T(8,128)S(1)}, u32[]{:S(2)}, u32[]{:S(2)}) collective-permute-start(f32[98,8,128]{2,1,0:T(8,128)S(1)} %get-tuple-element.113), channel_id=1, source_target_pairs={{0,8},{8,16},{16,24},{24,32},{32,40},{40,48},{48,56},{56,0},{1,9},... | collective-permute-start | bytes 1204232 | tf_op jit(solution)/shard_map/ppermute | solution.py:19
  74.4 0.3 collective-permute-start.12
  74.7 1.7 %collective-permute-start.13 = (f32[64,64]{1,0:T(8,128)S(1)}, f32[64,64]{1,0:T(8,128)S(1)}, u32[]{:S(2)}, u32[]{:S(2)}) collective-permute-start(f32[64,64]{1,0:T(8,128)S(1)} %get-tuple-element.115.mine_ref), channel_id=1, source_target_pairs={{0,8},{8,0},{16,24},{24,16},{32,40},{40,32},{48,56},{56,48},{1,9},... | collective-permute-start | bytes 49160 | tf_op jit(solution)/shard_map/ppermute | solution.py:23
  76.3 5.6 %collective-permute-done.13.other_ref = f32[64,64]{1,0:T(8,128)S(1)} collective-permute-done((f32[64,64]{1,0:T(8,128)S(1)}, f32[64,64]{1,0:T(8,128)S(1)}, u32[]{:S(2)}, u32[]{:S(2)}) %collective-permute-start.13) | collective-permute-done | bytes 16416 | tf_op jit(solution)/shard_map/ppermute | solution.py:23
  81.9 0.3 next_level_kernel.3
  82.2 0.4 collective-permute-done.12.rz_down.z_down
  82.7 2.9 %collective-permute-start.14 = (f32[92,8,128]{2,1,0:T(8,128)S(1)}, f32[92,8,128]{2,1,0:T(8,128)S(1)}, u32[]{:S(2)}, u32[]{:S(2)}) collective-permute-start(f32[92,8,128]{2,1,0:T(8,128)S(1)} %get-tuple-element.122), channel_id=1, source_target_pairs={{0,8},{8,16},{16,24},{24,32},{32,40},{40,48},{48,56},{56,0},{1,9},... | collective-permute-start | bytes 1130504 | tf_op jit(solution)/shard_map/ppermute | solution.py:19
  85.6 2.2 %collective-permute-start.16 = (f32[64,64]{1,0:T(8,128)S(1)}, f32[64,64]{1,0:T(8,128)S(1)}, u32[]{:S(2)}, u32[]{:S(2)}) collective-permute-start(f32[64,64]{1,0:T(8,128)S(1)} %get-tuple-element.127.mine_ref), channel_id=1, source_target_pairs={{0,16},{8,24},{16,0},{24,8},{32,48},{40,56},{48,32},{56,40},{1,17}... | collective-permute-start | bytes 49160 | tf_op jit(solution)/shard_map/ppermute | solution.py:23
  87.8 6.0 %collective-permute-done.16.other_ref = f32[64,64]{1,0:T(8,128)S(1)} collective-permute-done((f32[64,64]{1,0:T(8,128)S(1)}, f32[64,64]{1,0:T(8,128)S(1)}, u32[]{:S(2)}, u32[]{:S(2)}) %collective-permute-start.16) | collective-permute-done | bytes 16416 | tf_op jit(solution)/shard_map/ppermute | solution.py:23
  93.8 4.7 %node_factors.1 = f32[4,16,64]{2,1,0:T(8,128)} custom-call(s32[1]{0:T(128)} %bitcast.me_ref, f32[64,64]{1,0:T(8,128)S(1)} %get-tuple-element.124.g1_ref, f32[64,64]{1,0:T(8,128)S(1)} %get-tuple-element.125.g2_ref, f32[64,64]{1,0:T(8,128)S(1)} %get-tuple-element.126.g3_ref, f32[64,64]{1,0:T(8,128)S(1)} %get-tuple-element.127.mine_ref, ...), custom_call_target="tpu_custom_call" | custom-call | tf_op jit(solution)/shard_map/node_factors/pallas_call | solution.py:163
  98.7 0.3 collective-permute-start.19
  99.0 3.4 %collective-permute-start.20 = (f32[20,8,128]{2,1,0:T(8,128)S(1)}, f32[20,8,128]{2,1,0:T(8,128)S(1)}, u32[]{:S(2)}, u32[]{:S(2)}) collective-permute-start(f32[20,8,128]{2,1,0:T(8,128)S(1)} %get-tuple-element.135), channel_id=1, source_target_pairs={{0,128},{64,192},{128,0},{192,64},{1,129},{65,193},{129,1},{193,65... | collective-permute-start | bytes 245768 | tf_op jit(solution)/shard_map/ppermute | solution.py:19
  102.4 0.8 collective-permute-start.17
  103.2 3.3 %collective-permute-start.18 = (f32[12,8,128]{2,1,0:T(8,128)S(1)}, f32[12,8,128]{2,1,0:T(8,128)S(1)}, u32[]{:S(2)}, u32[]{:S(2)}) collective-permute-start(f32[12,8,128]{2,1,0:T(8,128)S(1)} %get-tuple-element.132), channel_id=1, source_target_pairs={{0,48},{8,56},{16,0},{24,8},{32,16},{40,24},{48,32},{56,40},{1,49}... | collective-permute-start | bytes 147464 | tf_op jit(solution)/shard_map/ppermute | solution.py:19
  106.5 2.1 %collective-permute-done.17.z_two = f32[12,8,128]{2,1,0:T(8,128)S(1)} collective-permute-done((f32[12,8,128]{2,1,0:T(8,128)S(1)}, f32[12,8,128]{2,1,0:T(8,128)S(1)}, u32[]{:S(2)}, u32[]{:S(2)}) %collective-permute-start.17) | collective-permute-done | bytes 49184 | tf_op jit(solution)/shard_map/ppermute | solution.py:19
  108.6 0.3 pack.1
  108.9 0.6 collective-permute-start.22
  109.5 2.7 %collective-permute-start.23 = (f32[8,8,128]{2,1,0:T(8,128)S(1)}, f32[8,8,128]{2,1,0:T(8,128)S(1)}, u32[]{:S(2)}, u32[]{:S(2)}) collective-permute-start(f32[8,8,128]{2,1,0:T(8,128)S(1)} %get-tuple-element.139), channel_id=1, source_target_pairs={{0,2},{1,3},{2,0},{3,1},{4,6},{5,7},{6,4},{7,5},{8,10},{9,11},{10,... | collective-permute-start | bytes 98312 | tf_op jit(solution)/shard_map/ppermute | solution.py:19
  112.1 0.9 collective-permute-start.24
  113.1 1.0 collective-permute-done.22.m1_ref
  114.1 0.8 collective-permute-done.23.m2_ref
  114.9 1.2 collective-permute-done.24.m3_ref
  116.1 1.7 %left_factor.1 = f32[32,16,64]{2,1,0:T(8,128)} custom-call(s32[1]{0:T(128)} %bitcast.me_ref, f32[4,9,32,128]{3,2,1,0:T(8,128)S(1)} %bitcast.27, f32[8,8,128]{2,1,0:T(8,128)S(1)} %get-tuple-element.137.m0_ref, f32[8,8,128]{2,1,0:T(8,128)S(1)} %collective-permute-done.22.m1_ref, f32[8,8,128]{2,1,0:T(8,128)S(1)} %collective-permute-done.23.m2_ref, ...), custom_call_target="tpu_custom_call" | custom-call | tf_op jit(solution)/shard_map/left_factor/pallas_call | solution.py:460
  (34 shorter events, 0.9 us)
Async XLA Ops:
  0.6 8.1 %copy-start = (f32[1,32,64,64]{3,2,1,0:T(8,128)S(1)}, f32[1,32,64,64]{3,2,1,0:T(8,128)}, u32[]{:S(2)}) copy-start(f32[1,32,64,64]{3,2,1,0:T(8,128)} %param.10) | copy-start | bytes 1572868
  0.6 13.9 %all-to-all-start = ((f32[32,16,256]{2,1,0:T(8,128)}), f32[32,16,256]{2,1,0:T(8,128)S(1)}, u32[]{:S(2)}, u32[]{:S(2)}) async-start(f32[32,16,256]{2,1,0:T(8,128)} %bitcast.33), calls=%async_computation | async-start | bytes 1048576 | tf_op jit(solution)/shard_map/all_to_all | solution.py:506
  32.9 18.2 %copy-start.1 = (f32[1,64,64]{2,1,0:T(8,128)S(1)}, f32[1,64,64]{2,1,0:T(8,128)}, u32[]{:S(2)}) copy-start(f32[1,64,64]{2,1,0:T(8,128)} %param.11) | copy-start | bytes 49156
  43.2 2.3 %collective-permute-start = (f32[176,8,128]{2,1,0:T(8,128)S(1)}, f32[176,8,128]{2,1,0:T(8,128)S(1)}, u32[]{:S(2)}, u32[]{:S(2)}) collective-permute-start(f32[176,8,128]{2,1,0:T(8,128)S(1)} %get-tuple-element.75), channel_id=1, source_target_pairs={{0,4},{4,0},{1,5},{5,1},{2,6},{6,2},{3,7},{7,3},{8,12},{12,8},{9,1... | collective-permute-start | bytes 2162696 | tf_op jit(solution)/shard_map/ppermute | solution.py:23
  45.5 11.5 %collective-permute-start.5 = (f32[848,8,128]{2,1,0:T(8,128)S(1)}, f32[848,8,128]{2,1,0:T(8,128)S(1)}, u32[]{:S(2)}, u32[]{:S(2)}) collective-permute-start(f32[848,8,128]{2,1,0:T(8,128)S(1)} %get-tuple-element.86), channel_id=1, source_target_pairs={{0,4},{4,0},{1,5},{5,1},{2,6},{6,2},{3,7},{7,3},{8,12},{12,8},{9,1... | collective-permute-start | bytes 10420232 | tf_op jit(solution)/shard_map/ppermute | solution.py:23
  45.7 11.3 %collective-permute-start.1 = (f32[48,8,128]{2,1,0:T(8,128)S(1)}, f32[48,8,128]{2,1,0:T(8,128)S(1)}, u32[]{:S(2)}, u32[]{:S(2)}) collective-permute-start(f32[48,8,128]{2,1,0:T(8,128)S(1)} %get-tuple-element.82), channel_id=1, source_target_pairs={{0,64},{64,128},{128,192},{192,0},{1,65},{65,129},{129,193},{193,1... | collective-permute-start | bytes 589832 | tf_op jit(solution)/shard_map/ppermute | solution.py:19
  47.4 9.6 %collective-permute-start.2 = (f32[48,8,128]{2,1,0:T(8,128)S(1)}, f32[48,8,128]{2,1,0:T(8,128)S(1)}, u32[]{:S(2)}, u32[]{:S(2)}) collective-permute-start(f32[48,8,128]{2,1,0:T(8,128)S(1)} %get-tuple-element.83), channel_id=1, source_target_pairs={{0,192},{64,0},{128,64},{192,128},{1,193},{65,1},{129,65},{193,129... | collective-permute-start | bytes 589832 | tf_op jit(solution)/shard_map/ppermute | solution.py:19
  49.0 6.1 %collective-permute-start.3 = (f32[40,8,128]{2,1,0:T(8,128)S(1)}, f32[40,8,128]{2,1,0:T(8,128)S(1)}, u32[]{:S(2)}, u32[]{:S(2)}) collective-permute-start(f32[40,8,128]{2,1,0:T(8,128)S(1)} %get-tuple-element.84), channel_id=1, source_target_pairs={{0,8},{8,16},{16,24},{24,32},{32,40},{40,48},{48,56},{56,0},{1,9},... | collective-permute-start | bytes 491528 | tf_op jit(solution)/shard_map/ppermute | solution.py:19
  50.9 6.1 %collective-permute-start.4 = (f32[40,8,128]{2,1,0:T(8,128)S(1)}, f32[40,8,128]{2,1,0:T(8,128)S(1)}, u32[]{:S(2)}, u32[]{:S(2)}) collective-permute-start(f32[40,8,128]{2,1,0:T(8,128)S(1)} %get-tuple-element.85), channel_id=1, source_target_pairs={{0,56},{8,0},{16,8},{24,16},{32,24},{40,32},{48,40},{56,48},{1,57}... | collective-permute-start | bytes 491528 | tf_op jit(solution)/shard_map/ppermute | solution.py:19
  56.9 7.9 %copy-start.2 = (f32[1,64,64]{2,1,0:T(8,128)S(1)}, f32[1,64,64]{2,1,0:T(8,128)}, u32[]{:S(2)}) copy-start(f32[1,64,64]{2,1,0:T(8,128)} %param.12) | copy-start | bytes 49156
  57.1 15.2 %collective-permute-start.6 = (f32[96,8,128]{2,1,0:T(8,128)S(1)}, f32[96,8,128]{2,1,0:T(8,128)S(1)}, u32[]{:S(2)}, u32[]{:S(2)}) collective-permute-start(f32[96,8,128]{2,1,0:T(8,128)S(1)} %get-tuple-element.99), channel_id=1, source_target_pairs={{0,64},{64,128},{128,192},{192,0},{1,65},{65,129},{129,193},{193,1... | collective-permute-start | bytes 1179656 | tf_op jit(solution)/shard_map/ppermute | solution.py:19
  57.5 14.8 %collective-permute-start.7 = (f32[96,8,128]{2,1,0:T(8,128)S(1)}, f32[96,8,128]{2,1,0:T(8,128)S(1)}, u32[]{:S(2)}, u32[]{:S(2)}) collective-permute-start(f32[96,8,128]{2,1,0:T(8,128)S(1)} %get-tuple-element.100), channel_id=1, source_target_pairs={{0,192},{64,0},{128,64},{192,128},{1,193},{65,1},{129,65},{193,129... | collective-permute-start | bytes 1179656 | tf_op jit(solution)/shard_map/ppermute | solution.py:19
  60.6 9.1 %collective-permute-start.8 = (f32[80,8,128]{2,1,0:T(8,128)S(1)}, f32[80,8,128]{2,1,0:T(8,128)S(1)}, u32[]{:S(2)}, u32[]{:S(2)}) collective-permute-start(f32[80,8,128]{2,1,0:T(8,128)S(1)} %get-tuple-element.101), channel_id=1, source_target_pairs={{0,8},{8,16},{16,24},{24,32},{32,40},{40,48},{48,56},{56,0},{1,9},... | collective-permute-start | bytes 983048 | tf_op jit(solution)/shard_map/ppermute | solution.py:19
  63.6 8.7 %collective-permute-start.9 = (f32[80,8,128]{2,1,0:T(8,128)S(1)}, f32[80,8,128]{2,1,0:T(8,128)S(1)}, u32[]{:S(2)}, u32[]{:S(2)}) collective-permute-start(f32[80,8,128]{2,1,0:T(8,128)S(1)} %get-tuple-element.102), channel_id=1, source_target_pairs={{0,56},{8,0},{16,8},{24,16},{32,24},{40,32},{48,40},{56,48},{1,57}... | collective-permute-start | bytes 983048 | tf_op jit(solution)/shard_map/ppermute | solution.py:19
  63.6 1.2 %collective-permute-start.10 = (f32[64,64]{1,0:T(8,128)S(1)}, f32[64,64]{1,0:T(8,128)S(1)}, u32[]{:S(2)}, u32[]{:S(2)}) collective-permute-start(f32[64,64]{1,0:T(8,128)S(1)} %get-tuple-element.103.mine_ref), channel_id=1, source_target_pairs={{0,4},{4,0},{1,5},{5,1},{2,6},{6,2},{3,7},{7,3},{8,12},{12,8},{9,1... | collective-permute-start | bytes 49160 | tf_op jit(solution)/shard_map/ppermute | solution.py:23
  72.3 9.6 %copy-start.3 = (f32[1,64,64]{2,1,0:T(8,128)S(1)}, f32[1,64,64]{2,1,0:T(8,128)}, u32[]{:S(2)}) copy-start(f32[1,64,64]{2,1,0:T(8,128)} %param.13) | copy-start | bytes 49156
  72.6 9.7 %collective-permute-start.11 = (f32[98,8,128]{2,1,0:T(8,128)S(1)}, f32[98,8,128]{2,1,0:T(8,128)S(1)}, u32[]{:S(2)}, u32[]{:S(2)}) collective-permute-start(f32[98,8,128]{2,1,0:T(8,128)S(1)} %get-tuple-element.113), channel_id=1, source_target_pairs={{0,8},{8,16},{16,24},{24,32},{32,40},{40,48},{48,56},{56,0},{1,9},... | collective-permute-start | bytes 1204232 | tf_op jit(solution)/shard_map/ppermute | solution.py:19
  74.4 8.2 %collective-permute-start.12 = (f32[98,8,128]{2,1,0:T(8,128)S(1)}, f32[98,8,128]{2,1,0:T(8,128)S(1)}, u32[]{:S(2)}, u32[]{:S(2)}) collective-permute-start(f32[98,8,128]{2,1,0:T(8,128)S(1)} %get-tuple-element.114), channel_id=1, source_target_pairs={{0,56},{8,0},{16,8},{24,16},{32,24},{40,32},{48,40},{56,48},{1,57}... | collective-permute-start | bytes 1204232 | tf_op jit(solution)/shard_map/ppermute | solution.py:19
  74.7 7.2 %collective-permute-start.13 = (f32[64,64]{1,0:T(8,128)S(1)}, f32[64,64]{1,0:T(8,128)S(1)}, u32[]{:S(2)}, u32[]{:S(2)}) collective-permute-start(f32[64,64]{1,0:T(8,128)S(1)} %get-tuple-element.115.mine_ref), channel_id=1, source_target_pairs={{0,8},{8,0},{16,24},{24,16},{32,40},{40,32},{48,56},{56,48},{1,9},... | collective-permute-start | bytes 49160 | tf_op jit(solution)/shard_map/ppermute | solution.py:23
  82.7 15.8 %collective-permute-start.14 = (f32[92,8,128]{2,1,0:T(8,128)S(1)}, f32[92,8,128]{2,1,0:T(8,128)S(1)}, u32[]{:S(2)}, u32[]{:S(2)}) collective-permute-start(f32[92,8,128]{2,1,0:T(8,128)S(1)} %get-tuple-element.122), channel_id=1, source_target_pairs={{0,8},{8,16},{16,24},{24,32},{32,40},{40,48},{48,56},{56,0},{1,9},... | collective-permute-start | bytes 1130504 | tf_op jit(solution)/shard_map/ppermute | solution.py:19
  85.6 13.0 %collective-permute-start.15 = (f32[92,8,128]{2,1,0:T(8,128)S(1)}, f32[92,8,128]{2,1,0:T(8,128)S(1)}, u32[]{:S(2)}, u32[]{:S(2)}) collective-permute-start(f32[92,8,128]{2,1,0:T(8,128)S(1)} %get-tuple-element.123), channel_id=1, source_target_pairs={{0,56},{8,0},{16,8},{24,16},{32,24},{40,32},{48,40},{56,48},{1,57}... | collective-permute-start | bytes 1130504 | tf_op jit(solution)/shard_map/ppermute | solution.py:19
  85.6 8.2 %collective-permute-start.16 = (f32[64,64]{1,0:T(8,128)S(1)}, f32[64,64]{1,0:T(8,128)S(1)}, u32[]{:S(2)}, u32[]{:S(2)}) collective-permute-start(f32[64,64]{1,0:T(8,128)S(1)} %get-tuple-element.127.mine_ref), channel_id=1, source_target_pairs={{0,16},{8,24},{16,0},{24,8},{32,48},{40,56},{48,32},{56,40},{1,17}... | collective-permute-start | bytes 49160 | tf_op jit(solution)/shard_map/ppermute | solution.py:23
  98.7 9.9 %collective-permute-start.19 = (f32[20,8,128]{2,1,0:T(8,128)S(1)}, f32[20,8,128]{2,1,0:T(8,128)S(1)}, u32[]{:S(2)}, u32[]{:S(2)}) collective-permute-start(f32[20,8,128]{2,1,0:T(8,128)S(1)} %get-tuple-element.134), channel_id=1, source_target_pairs={{0,64},{64,128},{128,192},{192,0},{1,65},{65,129},{129,193},{193,1... | collective-permute-start | bytes 245768 | tf_op jit(solution)/shard_map/ppermute | solution.py:19
  99.0 9.6 %collective-permute-start.20 = (f32[20,8,128]{2,1,0:T(8,128)S(1)}, f32[20,8,128]{2,1,0:T(8,128)S(1)}, u32[]{:S(2)}, u32[]{:S(2)}) collective-permute-start(f32[20,8,128]{2,1,0:T(8,128)S(1)} %get-tuple-element.135), channel_id=1, source_target_pairs={{0,128},{64,192},{128,0},{192,64},{1,129},{65,193},{129,1},{193,65... | collective-permute-start | bytes 245768 | tf_op jit(solution)/shard_map/ppermute | solution.py:19
  102.4 6.2 %collective-permute-start.21 = (f32[20,8,128]{2,1,0:T(8,128)S(1)}, f32[20,8,128]{2,1,0:T(8,128)S(1)}, u32[]{:S(2)}, u32[]{:S(2)}) collective-permute-start(f32[20,8,128]{2,1,0:T(8,128)S(1)} %get-tuple-element.136), channel_id=1, source_target_pairs={{0,192},{64,0},{128,64},{192,128},{1,193},{65,1},{129,65},{193,129... | collective-permute-start | bytes 245768 | tf_op jit(solution)/shard_map/ppermute | solution.py:19
  102.4 6.2 %collective-permute-start.17 = (f32[12,8,128]{2,1,0:T(8,128)S(1)}, f32[12,8,128]{2,1,0:T(8,128)S(1)}, u32[]{:S(2)}, u32[]{:S(2)}) collective-permute-start(f32[12,8,128]{2,1,0:T(8,128)S(1)} %get-tuple-element.131), channel_id=1, source_target_pairs={{0,16},{8,24},{16,32},{24,40},{32,48},{40,56},{48,0},{56,8},{1,17}... | collective-permute-start | bytes 147464 | tf_op jit(solution)/shard_map/ppermute | solution.py:19
  103.2 5.4 %collective-permute-start.18 = (f32[12,8,128]{2,1,0:T(8,128)S(1)}, f32[12,8,128]{2,1,0:T(8,128)S(1)}, u32[]{:S(2)}, u32[]{:S(2)}) collective-permute-start(f32[12,8,128]{2,1,0:T(8,128)S(1)} %get-tuple-element.132), channel_id=1, source_target_pairs={{0,48},{8,56},{16,0},{24,8},{32,16},{40,24},{48,32},{56,40},{1,49}... | collective-permute-start | bytes 147464 | tf_op jit(solution)/shard_map/ppermute | solution.py:19
  108.9 5.2 %collective-permute-start.22 = (f32[8,8,128]{2,1,0:T(8,128)S(1)}, f32[8,8,128]{2,1,0:T(8,128)S(1)}, u32[]{:S(2)}, u32[]{:S(2)}) collective-permute-start(f32[8,8,128]{2,1,0:T(8,128)S(1)} %get-tuple-element.138), channel_id=1, source_target_pairs={{0,1},{1,2},{2,3},{3,0},{4,5},{5,6},{6,7},{7,4},{8,9},{9,10},{10,1... | collective-permute-start | bytes 98312 | tf_op jit(solution)/shard_map/ppermute | solution.py:19
  109.5 5.4 %collective-permute-start.23 = (f32[8,8,128]{2,1,0:T(8,128)S(1)}, f32[8,8,128]{2,1,0:T(8,128)S(1)}, u32[]{:S(2)}, u32[]{:S(2)}) collective-permute-start(f32[8,8,128]{2,1,0:T(8,128)S(1)} %get-tuple-element.139), channel_id=1, source_target_pairs={{0,2},{1,3},{2,0},{3,1},{4,6},{5,7},{6,4},{7,5},{8,10},{9,11},{10,... | collective-permute-start | bytes 98312 | tf_op jit(solution)/shard_map/ppermute | solution.py:19
  112.1 3.9 %collective-permute-start.24 = (f32[8,8,128]{2,1,0:T(8,128)S(1)}, f32[8,8,128]{2,1,0:T(8,128)S(1)}, u32[]{:S(2)}, u32[]{:S(2)}) collective-permute-start(f32[8,8,128]{2,1,0:T(8,128)S(1)} %get-tuple-element.140), channel_id=1, source_target_pairs={{0,3},{1,0},{2,1},{3,2},{4,7},{5,4},{6,5},{7,6},{8,11},{9,8},{10,9... | collective-permute-start | bytes 98312 | tf_op jit(solution)/shard_map/ppermute | solution.py:19

commit v8 on v7

--- a/solution.py
+++ b/solution.py
@@ -332,26 +332,23 @@
     return jnp.concatenate([whole[:rows], whole[rows:] + extra], axis=0)
 
 
-def round1_kernel(plan, keep, got, y_up, y_down, z_up, z_down):
-    y = plan.both(keep, got, ("y", 2))
+def round1_kernel(plan, keep, got, y_two, z_up, z_down):
+    y_two[...] = plan.both(keep, got, ("y", 2))
     z = plan.both(keep, got, ("z", 4))
-    half = y.shape[0] // 2
-    y_up[...] = y[:half]
-    y_down[...] = y[half:]
     half = z.shape[0] // 2
     z_up[...] = z[:half]
     z_down[...] = z[half:]
 
 
-def round2_kernel(plan, keep, got, ry_up, ry_down, rz_up, rz_down, y_up, y_down, z_up, z_down):
-    y_up[...] = low_add(plan.both(keep, got, ("y", 1)), ry_up[...])
-    y_down[...] = high_add(plan.both(keep, got, ("y", 3)), ry_down[...])
+def round2_kernel(plan, keep, got, rz_up, rz_down, y_up, y_down, z_up, z_down):
+    y_up[...] = plan.both(keep, got, ("y", 1))
+    y_down[...] = plan.both(keep, got, ("y", 3))
     z_up[...] = low_add(plan.both(keep, got, ("z", 3)), rz_up[...])
     z_down[...] = high_add(plan.both(keep, got, ("z", 5)), rz_down[...])
 
 
-def round3_kernel(plan, keep, got, ry_up, ry_down, rz_up, rz_down, ey, z_up, z_down):
-    ey[...] = plan.both(keep, got, ("y", 0)) + ry_up[...] + ry_down[...]
+def round3_kernel(plan, keep, got, ry_two, ry_up, ry_down, rz_up, rz_down, ey, z_up, z_down):
+    ey[...] = plan.both(keep, got, ("y", 0)) + ry_two[...] + ry_up[...] + ry_down[...]
     rows, cut = plan.rows["z"], plan.cut
     half = cut // 2
     z_up[:rows] = plan.both(keep, got, ("z", 2)) + rz_up[...]
@@ -519,41 +516,39 @@
     def along(axis, up, down):
         return shift(up, axis, 1), shift(down, axis, -1)
 
-    def send(messages):
-        y_up, y_down, z_up, z_down = messages
-        return along("z", z_up, z_down) + along("y", y_up, y_down)
-
     y_rows, z_rows, cut, rest = plan.rows["y"], plan.rows["z"], plan.cut, plan.rest
-    sent = run_round(
-        round1_kernel, plan, (y_rows // 2,) * 2 + (z_rows // 2,) * 2, keep_near, got_near
-    )
-    sent, shared = tie(sent, packed)
-    rz_up, rz_down, ry_up, ry_down = send(sent)
+    y_two, z_up, z_down = run_round(
+        round1_kernel, plan, (y_rows, z_rows // 2, z_rows // 2), keep_near, got_near
+    )
+    y_two, z_up, z_down, shared = tie(y_two, z_up, z_down, packed)
+    rz_up, rz_down = along("z", z_up, z_down)
+    ry_two = shift(y_two, "y", 2)
     gram1, term = level(first_level_kernel, shared, node_transfer[0])
     other = swap(term, "core", 1)
-    ry_up, ry_down, rz_up, rz_down, got_far, term = tie(
-        ry_up, ry_down, rz_up, rz_down, got_far, term
-    )
+    rz_up, rz_down, got_far, other = tie(rz_up, rz_down, got_far, other)
     sums = (keep_far, got_far)
 
-    sent = run_round(
-        round2_kernel, plan, (y_rows,) * 2 + (z_rows,) * 2, *sums, ry_up, ry_down, rz_up, rz_down
-    )
-    sent, term = tie(sent, term)
-    rz_up, rz_down, ry_up, ry_down = send(sent)
+    y_up, y_down, z_up, z_down = run_round(
+        round2_kernel, plan, (y_rows,) * 2 + (z_rows,) * 2, *sums, rz_up, rz_down
+    )
+    y_up, y_down, z_up, z_down, term = tie(y_up, y_down, z_up, z_down, term)
+    rz_up, rz_down = along("z", z_up, z_down)
+    ry_up, ry_down = along("y", y_up, y_down)
     gram2, term = level(next_level_kernel, term, other, pair_transfer[0])
     other = swap(term, "z", 1)
-    ry_up, ry_down, rz_up, rz_down, term = tie(ry_up, ry_down, rz_up, rz_down, term)
+    ry_two, ry_up, ry_down, rz_up, rz_down, other = tie(
+        ry_two, ry_up, ry_down, rz_up, rz_down, other
+    )
 
     ride = z_rows + cut // 2 + cut
     ey, up, down = run_round(
-        round3_kernel, plan, (y_rows, ride, ride), *sums, ry_up, ry_down, rz_up, rz_down
+        round3_kernel, plan, (y_rows, ride, ride), *sums, ry_two, ry_up, ry_down, rz_up, rz_down
     )
     up, down, term = tie(up, down, term)
     ride_up, ride_down = along("z", up, down)
     gram3, term = level(next_level_kernel, term, other, quad_transfer[0])
     other = swap(term, "z", 2)
-    ride_up, ride_down, term = tie(ride_up, ride_down, term)
+    ride_up, ride_down, other = tie(ride_up, ride_down, other)
 
     both = z_rows + cut
     up, down = run_round(round4_kernel, plan, (both, both), *sums, ey, ride_up, ride_down)

time: 120 us -> 122 us (1.017); the launches traced: 118 us -> 121 us
  starting transfers between devices: 37.3 us -> 44.8 us
  waiting for transfers between devices: 38.9 us -> 35.1 us
    ppermute x20 -> x19, starting transfers between devices: 28.8 us -> 32.7 us  [shift(): lax.ppermute(value, axis, [(i, (i + step) % size) for i in range(size)])]
    ppermute x5, starting transfers between devices: 4.07 us -> 7.6 us  [swap(): lax.ppermute(value, axis, [(i, i ^ mask) for i in range(lax.axis_size(axi...]
    ppermute x20 -> x19, waiting for transfers between devices: 18.1 us -> 15.2 us  [shift(): lax.ppermute(value, axis, [(i, (i + step) % size) for i in range(size)])]
  transfers between devices with their start and end apart: 26 -> 25, of which waited for: 14 -> 16; matrix products, arithmetic and copies ran while one was open for 3% -> 3% of each run, Pallas kernels for 5% -> 5%
where the time goes in v8:
time: 122 us; the launch traced here: 121 us
  starting transfers between devices  44.8 us (37%)
  waiting for transfers between devices  35.1 us (29%)
  Pallas kernels  24 us (20%)
  blocking collectives  13.1 us (11%)
  other arithmetic  2.17 us (2%)
  local copies, waits for them, and re-layouts  1.5 us (1%)
    ppermute x19, starting transfers between devices, shift(): lax.ppermute(value, axis, [(i, (i + step) % size) for i in range(size)])  32.7 us
    ppermute x19, waiting for transfers between devices, shift(): lax.ppermute(value, axis, [(i, (i + step) % size) for i in range(size)])  15.2 us
    ppermute x5, waiting for transfers between devices, swap(): lax.ppermute(value, axis, [(i, i ^ mask) for i in range(lax.axis_size(axi...  14.1 us
    all_gather x1, blocking collectives, shards(): packed = lax.all_gather(mine, 'rk', axis=0, tiled=False)  13.1 us
    pallas_call x1, Pallas kernels, weighted_sums(): pl.pallas_call(product_kernel, in_specs=[pl.BlockSpec(memory_space=pltpu....  10.2 us
    ppermute x5, starting transfers between devices, swap(): lax.ppermute(value, axis, [(i, i ^ mask) for i in range(lax.axis_size(axi...  7.6 us
    all_to_all x1, waiting for transfers between devices, shards(): lax.all_to_all(local, 'rk', split_axis=0, concat_axis=0, tiled=True)  5.82 us
    pallas_call x1, Pallas kernels, leaf_factors(): pl.pallas_call(leaf_kernel, out_shape=jax.ShapeDtypeStruct((leaves + 1, R...  5.19 us
  transfers between devices with their start and end apart: 25, of which 16 were waited for; matrix products, arithmetic and copies ran while one was open for 3% of the time, Pallas kernels for 5%

profile of v8, /device:TPU:32, one launch (start us, length us, event | category | flops | bytes accessed | tf_op | source)
XLA Modules:
  0.0 121.4 jit_solution(11067208424048829827)
XLA Ops:
  0.6 4.4 %all-to-all-start = ((f32[32,16,256]{2,1,0:T(8,128)}), f32[32,16,256]{2,1,0:T(8,128)S(1)}, u32[]{:S(2)}, u32[]{:S(2)}) async-start(f32[32,16,256]{2,1,0:T(8,128)} %bitcast.33), calls=%async_computation | async-start | bytes 1048576 | tf_op jit(solution)/shard_map/all_to_all | solution.py:503
  5.1 0.7 iota_compare_fusion
  5.9 0.8 squeeze.22
  6.7 0.5 broadcast.120
  7.2 1.4 %reduce.3 = s32[32,32]{1,0:T(8,128)S(1)} reduce(s32[1,32,32,1]{2,3,1,0:T(1,128)} %param.15, s32[]{:T(128)} %broadcast.120), dimensions={0,3}, to_apply=%param.15.reduce_sub_computation.3 | reduce | bytes 8196 | tf_op args[6]
  8.7 5.8 %all-to-all-done = f32[32,16,256]{2,1,0:T(8,128)S(1)} async-done(((f32[32,16,256]{2,1,0:T(8,128)}), f32[32,16,256]{2,1,0:T(8,128)S(1)}, u32[]{:S(2)}, u32[]{:S(2)}) %all-to-all-start) | async-done | bytes 524320 | tf_op jit(solution)/shard_map/all_to_all | solution.py:503
  14.6 5.2 %leaf_factors.1 = f32[9,32,128]{2,1,0:T(8,128)S(1)} custom-call(f32[4,8,16,256]{3,2,1,0:T(8,128)S(1)} %bitcast.28, f32[8,64,64]{2,1,0:T(8,128)S(1)} %dynamic-slice_bitcast_fusion.move_ref), custom_call_target="tpu_custom_call" | custom-call | tf_op jit(solution)/shard_map/leaf_factors/pallas_call | solution.py:103
  19.8 13.1 %all-gather = f32[36,32,128]{2,1,0:T(8,128)S(1)} all-gather(f32[9,32,128]{2,1,0:T(8,128)S(1)} %leaf_factors.1), channel_id=2, replica_groups=mesh['y'=4,'z'=8,'core'=2,'rk'=4] {'rk'}, dimensions={0}, use_global_device_ids=true | all-gather | bytes 737280 | tf_op jit(solution)/shard_map/all_gather | solution.py:506
  32.9 10.2 %weighted_sums.1 = (f32[176,8,128]{2,1,0:T(8,128)S(1)}, f32[848,8,128]{2,1,0:T(8,128)S(1)}, f32[176,8,128]{2,1,0:T(8,128)S(1)}, f32[848,8,128]{2,1,0:T(8,128)S(1)}, f32[32,16,64]{2,1,0:T(8,128)}) custom-call(s32[1]{0:T(128)} %bitcast.me_ref, s32[1024]{0:T(1024)S(1)} %add_select_fusion.5.place_ref, f32[32,32,16,64]{3,2,1,0:T(8,128)} %bitcast.32, ...), custom_call_target="tpu_custom_call" | custom-call | tf_op jit(solution)/shard_map/weighted_sums/pallas_call | solution.py:271
  43.2 2.2 %collective-permute-done.got = f32[176,8,128]{2,1,0:T(8,128)S(1)} collective-permute-done((f32[176,8,128]{2,1,0:T(8,128)S(1)}, f32[176,8,128]{2,1,0:T(8,128)S(1)}, u32[]{:S(2)}, u32[]{:S(2)}) %collective-permute-start) | collective-permute-done | bytes 720928 | tf_op jit(solution)/shard_map/ppermute | solution.py:23
  45.6 2.2 %collective-permute-start.1 = (f32[40,8,128]{2,1,0:T(8,128)S(1)}, f32[40,8,128]{2,1,0:T(8,128)S(1)}, u32[]{:S(2)}, u32[]{:S(2)}) collective-permute-start(f32[40,8,128]{2,1,0:T(8,128)S(1)} %get-tuple-element.78), channel_id=1, source_target_pairs={{0,8},{8,16},{16,24},{24,32},{32,40},{40,48},{48,56},{56,0},{1,9},... | collective-permute-start | bytes 491528 | tf_op jit(solution)/shard_map/ppermute | solution.py:19
  47.8 0.4 first_level_kernel.1
  48.3 3.2 %collective-permute-start.5 = (f32[96,8,128]{2,1,0:T(8,128)S(1)}, f32[96,8,128]{2,1,0:T(8,128)S(1)}, u32[]{:S(2)}, u32[]{:S(2)}) collective-permute-start(f32[96,8,128]{2,1,0:T(8,128)S(1)} %get-tuple-element.84), channel_id=1, source_target_pairs={{0,128},{64,192},{128,0},{192,64},{1,129},{65,193},{129,1},{193,65... | collective-permute-start | bytes 1179656 | tf_op jit(solution)/shard_map/ppermute | solution.py:19
  51.6 0.6 collective-permute-done.1.rz_up
  52.2 1.8 %collective-permute-done.2.rz_down = f32[40,8,128]{2,1,0:T(8,128)S(1)} collective-permute-done((f32[40,8,128]{2,1,0:T(8,128)S(1)}, f32[40,8,128]{2,1,0:T(8,128)S(1)}, u32[]{:S(2)}, u32[]{:S(2)}) %collective-permute-start.2) | collective-permute-done | bytes 163872 | tf_op jit(solution)/shard_map/ppermute | solution.py:19
  54.2 1.8 %collective-permute-start.6 = (f32[96,8,128]{2,1,0:T(8,128)S(1)}, f32[96,8,128]{2,1,0:T(8,128)S(1)}, u32[]{:S(2)}, u32[]{:S(2)}) collective-permute-start(f32[96,8,128]{2,1,0:T(8,128)S(1)} %get-tuple-element.91), channel_id=1, source_target_pairs={{0,64},{64,128},{128,192},{192,0},{1,65},{65,129},{129,193},{193,1... | collective-permute-start | bytes 1179656 | tf_op jit(solution)/shard_map/ppermute | solution.py:19
  55.9 1.7 %collective-permute-start.7 = (f32[96,8,128]{2,1,0:T(8,128)S(1)}, f32[96,8,128]{2,1,0:T(8,128)S(1)}, u32[]{:S(2)}, u32[]{:S(2)}) collective-permute-start(f32[96,8,128]{2,1,0:T(8,128)S(1)} %get-tuple-element.92), channel_id=1, source_target_pairs={{0,192},{64,0},{128,64},{192,128},{1,193},{65,1},{129,65},{193,129... | collective-permute-start | bytes 1179656 | tf_op jit(solution)/shard_map/ppermute | solution.py:19
  57.6 3.0 %collective-permute-start.8 = (f32[80,8,128]{2,1,0:T(8,128)S(1)}, f32[80,8,128]{2,1,0:T(8,128)S(1)}, u32[]{:S(2)}, u32[]{:S(2)}) collective-permute-start(f32[80,8,128]{2,1,0:T(8,128)S(1)} %get-tuple-element.93), channel_id=1, source_target_pairs={{0,8},{8,16},{16,24},{24,32},{32,40},{40,48},{48,56},{56,0},{1,9},... | collective-permute-start | bytes 983048 | tf_op jit(solution)/shard_map/ppermute | solution.py:19
  60.7 0.3 next_level_kernel.2
  61.0 0.8 collective-permute-done.5.ry_two
  61.7 3.9 %collective-permute-start.10 = (f32[64,64]{1,0:T(8,128)S(1)}, f32[64,64]{1,0:T(8,128)S(1)}, u32[]{:S(2)}, u32[]{:S(2)}) collective-permute-start(f32[64,64]{1,0:T(8,128)S(1)} %get-tuple-element.108.mine_ref), channel_id=1, source_target_pairs={{0,8},{8,0},{16,24},{24,16},{32,40},{40,32},{48,56},{56,48},{1,9},... | collective-permute-start | bytes 49160 | tf_op jit(solution)/shard_map/ppermute | solution.py:23
  65.7 2.5 %collective-permute-done.10.other_ref = f32[64,64]{1,0:T(8,128)S(1)} collective-permute-done((f32[64,64]{1,0:T(8,128)S(1)}, f32[64,64]{1,0:T(8,128)S(1)}, u32[]{:S(2)}, u32[]{:S(2)}) %collective-permute-start.10) | collective-permute-done | bytes 16416 | tf_op jit(solution)/shard_map/ppermute | solution.py:23
  68.2 2.0 %collective-permute-done.9.rz_down = f32[80,8,128]{2,1,0:T(8,128)S(1)} collective-permute-done((f32[80,8,128]{2,1,0:T(8,128)S(1)}, f32[80,8,128]{2,1,0:T(8,128)S(1)}, u32[]{:S(2)}, u32[]{:S(2)}) %collective-permute-start.9) | collective-permute-done | bytes 327712 | tf_op jit(solution)/shard_map/ppermute | solution.py:19
  70.4 2.5 %collective-permute-start.11 = (f32[98,8,128]{2,1,0:T(8,128)S(1)}, f32[98,8,128]{2,1,0:T(8,128)S(1)}, u32[]{:S(2)}, u32[]{:S(2)}) collective-permute-start(f32[98,8,128]{2,1,0:T(8,128)S(1)} %get-tuple-element.106), channel_id=1, source_target_pairs={{0,8},{8,16},{16,24},{24,32},{32,40},{40,48},{48,56},{56,0},{1,9},... | collective-permute-start | bytes 1204232 | tf_op jit(solution)/shard_map/ppermute | solution.py:19
  73.0 1.7 %collective-permute-start.12 = (f32[98,8,128]{2,1,0:T(8,128)S(1)}, f32[98,8,128]{2,1,0:T(8,128)S(1)}, u32[]{:S(2)}, u32[]{:S(2)}) collective-permute-start(f32[98,8,128]{2,1,0:T(8,128)S(1)} %get-tuple-element.107), channel_id=1, source_target_pairs={{0,56},{8,0},{16,8},{24,16},{32,24},{40,32},{48,40},{56,48},{1,57}... | collective-permute-start | bytes 1204232 | tf_op jit(solution)/shard_map/ppermute | solution.py:19
  74.6 0.3 next_level_kernel.3
  74.9 3.3 %collective-permute-start.13 = (f32[64,64]{1,0:T(8,128)S(1)}, f32[64,64]{1,0:T(8,128)S(1)}, u32[]{:S(2)}, u32[]{:S(2)}) collective-permute-start(f32[64,64]{1,0:T(8,128)S(1)} %get-tuple-element.120.mine_ref), channel_id=1, source_target_pairs={{0,16},{8,24},{16,0},{24,8},{32,48},{40,56},{48,32},{56,40},{1,17}... | collective-permute-start | bytes 49160 | tf_op jit(solution)/shard_map/ppermute | solution.py:23
  78.3 9.3 %collective-permute-done.13.other_ref = f32[64,64]{1,0:T(8,128)S(1)} collective-permute-done((f32[64,64]{1,0:T(8,128)S(1)}, f32[64,64]{1,0:T(8,128)S(1)}, u32[]{:S(2)}, u32[]{:S(2)}) %collective-permute-start.13) | collective-permute-done | bytes 16416 | tf_op jit(solution)/shard_map/ppermute | solution.py:23
  87.7 0.3 collective-permute-start.14
  88.0 1.8 %collective-permute-start.15 = (f32[92,8,128]{2,1,0:T(8,128)S(1)}, f32[92,8,128]{2,1,0:T(8,128)S(1)}, u32[]{:S(2)}, u32[]{:S(2)}) collective-permute-start(f32[92,8,128]{2,1,0:T(8,128)S(1)} %get-tuple-element.116), channel_id=1, source_target_pairs={{0,56},{8,0},{16,8},{24,16},{32,24},{40,32},{48,40},{56,48},{1,57}... | collective-permute-start | bytes 1130504 | tf_op jit(solution)/shard_map/ppermute | solution.py:19
  89.8 4.7 %node_factors.1 = f32[4,16,64]{2,1,0:T(8,128)} custom-call(s32[1]{0:T(128)} %bitcast.me_ref, f32[64,64]{1,0:T(8,128)S(1)} %get-tuple-element.117.g1_ref, f32[64,64]{1,0:T(8,128)S(1)} %get-tuple-element.118.g2_ref, f32[64,64]{1,0:T(8,128)S(1)} %get-tuple-element.119.g3_ref, f32[64,64]{1,0:T(8,128)S(1)} %get-tuple-element.120.mine_ref, ...), custom_call_target="tpu_custom_call" | custom-call | tf_op jit(solution)/shard_map/node_factors/pallas_call | solution.py:163
  94.6 2.5 %collective-permute-done.14.rz_up = f32[92,8,128]{2,1,0:T(8,128)S(1)} collective-permute-done((f32[92,8,128]{2,1,0:T(8,128)S(1)}, f32[92,8,128]{2,1,0:T(8,128)S(1)}, u32[]{:S(2)}, u32[]{:S(2)}) %collective-permute-start.14) | collective-permute-done | bytes 376864 | tf_op jit(solution)/shard_map/ppermute | solution.py:19
  97.1 0.8 collective-permute-done.15.rz_down
  97.9 1.5 %collective-permute-start.18 = (f32[20,8,128]{2,1,0:T(8,128)S(1)}, f32[20,8,128]{2,1,0:T(8,128)S(1)}, u32[]{:S(2)}, u32[]{:S(2)}) collective-permute-start(f32[20,8,128]{2,1,0:T(8,128)S(1)} %get-tuple-element.128), channel_id=1, source_target_pairs={{0,64},{64,128},{128,192},{192,0},{1,65},{65,129},{129,193},{193,1... | collective-permute-start | bytes 245768 | tf_op jit(solution)/shard_map/ppermute | solution.py:19
  99.4 3.1 %collective-permute-start.19 = (f32[20,8,128]{2,1,0:T(8,128)S(1)}, f32[20,8,128]{2,1,0:T(8,128)S(1)}, u32[]{:S(2)}, u32[]{:S(2)}) collective-permute-start(f32[20,8,128]{2,1,0:T(8,128)S(1)} %get-tuple-element.129), channel_id=1, source_target_pairs={{0,128},{64,192},{128,0},{192,64},{1,129},{65,193},{129,1},{193,65... | collective-permute-start | bytes 245768 | tf_op jit(solution)/shard_map/ppermute | solution.py:19
  102.6 1.6 %collective-permute-start.20 = (f32[20,8,128]{2,1,0:T(8,128)S(1)}, f32[20,8,128]{2,1,0:T(8,128)S(1)}, u32[]{:S(2)}, u32[]{:S(2)}) collective-permute-start(f32[20,8,128]{2,1,0:T(8,128)S(1)} %get-tuple-element.130), channel_id=1, source_target_pairs={{0,192},{64,0},{128,64},{192,128},{1,193},{65,1},{129,65},{193,129... | collective-permute-start | bytes 245768 | tf_op jit(solution)/shard_map/ppermute | solution.py:19
  104.2 3.0 %collective-permute-start.16 = (f32[12,8,128]{2,1,0:T(8,128)S(1)}, f32[12,8,128]{2,1,0:T(8,128)S(1)}, u32[]{:S(2)}, u32[]{:S(2)}) collective-permute-start(f32[12,8,128]{2,1,0:T(8,128)S(1)} %get-tuple-element.125), channel_id=1, source_target_pairs={{0,16},{8,24},{16,32},{24,40},{32,48},{40,56},{48,0},{56,8},{1,17}... | collective-permute-start | bytes 147464 | tf_op jit(solution)/shard_map/ppermute | solution.py:19
  107.1 1.1 collective-permute-start.17
  108.3 2.1 %collective-permute-done.16.z_two = f32[12,8,128]{2,1,0:T(8,128)S(1)} collective-permute-done((f32[12,8,128]{2,1,0:T(8,128)S(1)}, f32[12,8,128]{2,1,0:T(8,128)S(1)}, u32[]{:S(2)}, u32[]{:S(2)}) %collective-permute-start.16) | collective-permute-done | bytes 49184 | tf_op jit(solution)/shard_map/ppermute | solution.py:19
  110.4 1.8 %collective-permute-done.17.z_six = f32[12,8,128]{2,1,0:T(8,128)S(1)} collective-permute-done((f32[12,8,128]{2,1,0:T(8,128)S(1)}, f32[12,8,128]{2,1,0:T(8,128)S(1)}, u32[]{:S(2)}, u32[]{:S(2)}) %collective-permute-start.17) | collective-permute-done | bytes 49184 | tf_op jit(solution)/shard_map/ppermute | solution.py:19
  112.2 0.3 pack.1
  112.5 0.6 collective-permute-start.21
  113.0 2.7 %collective-permute-start.22 = (f32[8,8,128]{2,1,0:T(8,128)S(1)}, f32[8,8,128]{2,1,0:T(8,128)S(1)}, u32[]{:S(2)}, u32[]{:S(2)}) collective-permute-start(f32[8,8,128]{2,1,0:T(8,128)S(1)} %get-tuple-element.133), channel_id=1, source_target_pairs={{0,2},{1,3},{2,0},{3,1},{4,6},{5,7},{6,4},{7,5},{8,10},{9,11},{10,... | collective-permute-start | bytes 98312 | tf_op jit(solution)/shard_map/ppermute | solution.py:19
  115.7 0.9 collective-permute-start.23
  116.7 1.0 collective-permute-done.21.m1_ref
  117.7 0.8 collective-permute-done.22.m2_ref
  118.5 1.2 collective-permute-done.23.m3_ref
  119.6 1.7 %left_factor.1 = f32[32,16,64]{2,1,0:T(8,128)} custom-call(s32[1]{0:T(128)} %bitcast.me_ref, f32[4,9,32,128]{3,2,1,0:T(8,128)S(1)} %bitcast.27, f32[8,8,128]{2,1,0:T(8,128)S(1)} %get-tuple-element.131.m0_ref, f32[8,8,128]{2,1,0:T(8,128)S(1)} %collective-permute-done.21.m1_ref, f32[8,8,128]{2,1,0:T(8,128)S(1)} %collective-permute-done.22.m2_ref, ...), custom_call_target="tpu_custom_call" | custom-call | tf_op jit(solution)/shard_map/left_factor/pallas_call | solution.py:457
  (32 shorter events, 1.3 us)
Async XLA Ops:
  0.6 8.1 %copy-start = (f32[1,32,64,64]{3,2,1,0:T(8,128)S(1)}, f32[1,32,64,64]{3,2,1,0:T(8,128)}, u32[]{:S(2)}) copy-start(f32[1,32,64,64]{3,2,1,0:T(8,128)} %param.10) | copy-start | bytes 1572868
  0.6 13.9 %all-to-all-start = ((f32[32,16,256]{2,1,0:T(8,128)}), f32[32,16,256]{2,1,0:T(8,128)S(1)}, u32[]{:S(2)}, u32[]{:S(2)}) async-start(f32[32,16,256]{2,1,0:T(8,128)} %bitcast.33), calls=%async_computation | async-start | bytes 1048576 | tf_op jit(solution)/shard_map/all_to_all | solution.py:503
  32.9 14.9 %copy-start.1 = (f32[1,64,64]{2,1,0:T(8,128)S(1)}, f32[1,64,64]{2,1,0:T(8,128)}, u32[]{:S(2)}) copy-start(f32[1,64,64]{2,1,0:T(8,128)} %param.11) | copy-start | bytes 49156
  43.1 2.3 %collective-permute-start = (f32[176,8,128]{2,1,0:T(8,128)S(1)}, f32[176,8,128]{2,1,0:T(8,128)S(1)}, u32[]{:S(2)}, u32[]{:S(2)}) collective-permute-start(f32[176,8,128]{2,1,0:T(8,128)S(1)} %get-tuple-element.72), channel_id=1, source_target_pairs={{0,4},{4,0},{1,5},{5,1},{2,6},{6,2},{3,7},{7,3},{8,12},{12,8},{9,1... | collective-permute-start | bytes 2162696 | tf_op jit(solution)/shard_map/ppermute | solution.py:23
  45.4 8.6 %collective-permute-start.3 = (f32[848,8,128]{2,1,0:T(8,128)S(1)}, f32[848,8,128]{2,1,0:T(8,128)S(1)}, u32[]{:S(2)}, u32[]{:S(2)}) collective-permute-start(f32[848,8,128]{2,1,0:T(8,128)S(1)} %get-tuple-element.80), channel_id=1, source_target_pairs={{0,4},{4,0},{1,5},{5,1},{2,6},{6,2},{3,7},{7,3},{8,12},{12,8},{9,1... | collective-permute-start | bytes 10420232 | tf_op jit(solution)/shard_map/ppermute | solution.py:23
  45.6 6.6 %collective-permute-start.1 = (f32[40,8,128]{2,1,0:T(8,128)S(1)}, f32[40,8,128]{2,1,0:T(8,128)S(1)}, u32[]{:S(2)}, u32[]{:S(2)}) collective-permute-start(f32[40,8,128]{2,1,0:T(8,128)S(1)} %get-tuple-element.78), channel_id=1, source_target_pairs={{0,8},{8,16},{16,24},{24,32},{32,40},{40,48},{48,56},{56,0},{1,9},... | collective-permute-start | bytes 491528 | tf_op jit(solution)/shard_map/ppermute | solution.py:19
  47.8 6.2 %collective-permute-start.2 = (f32[40,8,128]{2,1,0:T(8,128)S(1)}, f32[40,8,128]{2,1,0:T(8,128)S(1)}, u32[]{:S(2)}, u32[]{:S(2)}) collective-permute-start(f32[40,8,128]{2,1,0:T(8,128)S(1)} %get-tuple-element.79), channel_id=1, source_target_pairs={{0,56},{8,0},{16,8},{24,16},{32,24},{40,32},{48,40},{56,48},{1,57}... | collective-permute-start | bytes 491528 | tf_op jit(solution)/shard_map/ppermute | solution.py:19
  48.2 3.4 %collective-permute-start.4 = (f32[64,64]{1,0:T(8,128)S(1)}, f32[64,64]{1,0:T(8,128)S(1)}, u32[]{:S(2)}, u32[]{:S(2)}) collective-permute-start(f32[64,64]{1,0:T(8,128)S(1)} %get-tuple-element.95.mine_ref), channel_id=1, source_target_pairs={{0,4},{4,0},{1,5},{5,1},{2,6},{6,2},{3,7},{7,3},{8,12},{12,8},{9,1... | collective-permute-start | bytes 49160 | tf_op jit(solution)/shard_map/ppermute | solution.py:23
  48.3 13.5 %collective-permute-start.5 = (f32[96,8,128]{2,1,0:T(8,128)S(1)}, f32[96,8,128]{2,1,0:T(8,128)S(1)}, u32[]{:S(2)}, u32[]{:S(2)}) collective-permute-start(f32[96,8,128]{2,1,0:T(8,128)S(1)} %get-tuple-element.84), channel_id=1, source_target_pairs={{0,128},{64,192},{128,0},{192,64},{1,129},{65,193},{129,1},{193,65... | collective-permute-start | bytes 1179656 | tf_op jit(solution)/shard_map/ppermute | solution.py:19
  54.0 6.6 %copy-start.2 = (f32[1,64,64]{2,1,0:T(8,128)S(1)}, f32[1,64,64]{2,1,0:T(8,128)}, u32[]{:S(2)}) copy-start(f32[1,64,64]{2,1,0:T(8,128)} %param.12) | copy-start | bytes 49156
  54.2 16.0 %collective-permute-start.6 = (f32[96,8,128]{2,1,0:T(8,128)S(1)}, f32[96,8,128]{2,1,0:T(8,128)S(1)}, u32[]{:S(2)}, u32[]{:S(2)}) collective-permute-start(f32[96,8,128]{2,1,0:T(8,128)S(1)} %get-tuple-element.91), channel_id=1, source_target_pairs={{0,64},{64,128},{128,192},{192,0},{1,65},{65,129},{129,193},{193,1... | collective-permute-start | bytes 1179656 | tf_op jit(solution)/shard_map/ppermute | solution.py:19
  55.9 14.2 %collective-permute-start.7 = (f32[96,8,128]{2,1,0:T(8,128)S(1)}, f32[96,8,128]{2,1,0:T(8,128)S(1)}, u32[]{:S(2)}, u32[]{:S(2)}) collective-permute-start(f32[96,8,128]{2,1,0:T(8,128)S(1)} %get-tuple-element.92), channel_id=1, source_target_pairs={{0,192},{64,0},{128,64},{192,128},{1,193},{65,1},{129,65},{193,129... | collective-permute-start | bytes 1179656 | tf_op jit(solution)/shard_map/ppermute | solution.py:19
  57.6 10.6 %collective-permute-start.8 = (f32[80,8,128]{2,1,0:T(8,128)S(1)}, f32[80,8,128]{2,1,0:T(8,128)S(1)}, u32[]{:S(2)}, u32[]{:S(2)}) collective-permute-start(f32[80,8,128]{2,1,0:T(8,128)S(1)} %get-tuple-element.93), channel_id=1, source_target_pairs={{0,8},{8,16},{16,24},{24,32},{32,40},{40,48},{48,56},{56,0},{1,9},... | collective-permute-start | bytes 983048 | tf_op jit(solution)/shard_map/ppermute | solution.py:19
  60.7 9.5 %collective-permute-start.9 = (f32[80,8,128]{2,1,0:T(8,128)S(1)}, f32[80,8,128]{2,1,0:T(8,128)S(1)}, u32[]{:S(2)}, u32[]{:S(2)}) collective-permute-start(f32[80,8,128]{2,1,0:T(8,128)S(1)} %get-tuple-element.94), channel_id=1, source_target_pairs={{0,56},{8,0},{16,8},{24,16},{32,24},{40,32},{48,40},{56,48},{1,57}... | collective-permute-start | bytes 983048 | tf_op jit(solution)/shard_map/ppermute | solution.py:19
  61.7 12.9 %copy-start.3 = (f32[1,64,64]{2,1,0:T(8,128)S(1)}, f32[1,64,64]{2,1,0:T(8,128)}, u32[]{:S(2)}) copy-start(f32[1,64,64]{2,1,0:T(8,128)} %param.13) | copy-start | bytes 49156
  61.7 6.5 %collective-permute-start.10 = (f32[64,64]{1,0:T(8,128)S(1)}, f32[64,64]{1,0:T(8,128)S(1)}, u32[]{:S(2)}, u32[]{:S(2)}) collective-permute-start(f32[64,64]{1,0:T(8,128)S(1)} %get-tuple-element.108.mine_ref), channel_id=1, source_target_pairs={{0,8},{8,0},{16,24},{24,16},{32,40},{40,32},{48,56},{56,48},{1,9},... | collective-permute-start | bytes 49160 | tf_op jit(solution)/shard_map/ppermute | solution.py:23
  70.4 17.2 %collective-permute-start.11 = (f32[98,8,128]{2,1,0:T(8,128)S(1)}, f32[98,8,128]{2,1,0:T(8,128)S(1)}, u32[]{:S(2)}, u32[]{:S(2)}) collective-permute-start(f32[98,8,128]{2,1,0:T(8,128)S(1)} %get-tuple-element.106), channel_id=1, source_target_pairs={{0,8},{8,16},{16,24},{24,32},{32,40},{40,48},{48,56},{56,0},{1,9},... | collective-permute-start | bytes 1204232 | tf_op jit(solution)/shard_map/ppermute | solution.py:19
  73.0 14.7 %collective-permute-start.12 = (f32[98,8,128]{2,1,0:T(8,128)S(1)}, f32[98,8,128]{2,1,0:T(8,128)S(1)}, u32[]{:S(2)}, u32[]{:S(2)}) collective-permute-start(f32[98,8,128]{2,1,0:T(8,128)S(1)} %get-tuple-element.107), channel_id=1, source_target_pairs={{0,56},{8,0},{16,8},{24,16},{32,24},{40,32},{48,40},{56,48},{1,57}... | collective-permute-start | bytes 1204232 | tf_op jit(solution)/shard_map/ppermute | solution.py:19
  74.9 12.6 %collective-permute-start.13 = (f32[64,64]{1,0:T(8,128)S(1)}, f32[64,64]{1,0:T(8,128)S(1)}, u32[]{:S(2)}, u32[]{:S(2)}) collective-permute-start(f32[64,64]{1,0:T(8,128)S(1)} %get-tuple-element.120.mine_ref), channel_id=1, source_target_pairs={{0,16},{8,24},{16,0},{24,8},{32,48},{40,56},{48,32},{56,40},{1,17}... | collective-permute-start | bytes 49160 | tf_op jit(solution)/shard_map/ppermute | solution.py:23
  87.7 9.3 %collective-permute-start.14 = (f32[92,8,128]{2,1,0:T(8,128)S(1)}, f32[92,8,128]{2,1,0:T(8,128)S(1)}, u32[]{:S(2)}, u32[]{:S(2)}) collective-permute-start(f32[92,8,128]{2,1,0:T(8,128)S(1)} %get-tuple-element.115), channel_id=1, source_target_pairs={{0,8},{8,16},{16,24},{24,32},{32,40},{40,48},{48,56},{56,0},{1,9},... | collective-permute-start | bytes 1130504 | tf_op jit(solution)/shard_map/ppermute | solution.py:19
  88.0 9.8 %collective-permute-start.15 = (f32[92,8,128]{2,1,0:T(8,128)S(1)}, f32[92,8,128]{2,1,0:T(8,128)S(1)}, u32[]{:S(2)}, u32[]{:S(2)}) collective-permute-start(f32[92,8,128]{2,1,0:T(8,128)S(1)} %get-tuple-element.116), channel_id=1, source_target_pairs={{0,56},{8,0},{16,8},{24,16},{32,24},{40,32},{48,40},{56,48},{1,57}... | collective-permute-start | bytes 1130504 | tf_op jit(solution)/shard_map/ppermute | solution.py:19
  97.9 14.2 %collective-permute-start.18 = (f32[20,8,128]{2,1,0:T(8,128)S(1)}, f32[20,8,128]{2,1,0:T(8,128)S(1)}, u32[]{:S(2)}, u32[]{:S(2)}) collective-permute-start(f32[20,8,128]{2,1,0:T(8,128)S(1)} %get-tuple-element.128), channel_id=1, source_target_pairs={{0,64},{64,128},{128,192},{192,0},{1,65},{65,129},{129,193},{193,1... | collective-permute-start | bytes 245768 | tf_op jit(solution)/shard_map/ppermute | solution.py:19
  99.4 12.7 %collective-permute-start.19 = (f32[20,8,128]{2,1,0:T(8,128)S(1)}, f32[20,8,128]{2,1,0:T(8,128)S(1)}, u32[]{:S(2)}, u32[]{:S(2)}) collective-permute-start(f32[20,8,128]{2,1,0:T(8,128)S(1)} %get-tuple-element.129), channel_id=1, source_target_pairs={{0,128},{64,192},{128,0},{192,64},{1,129},{65,193},{129,1},{193,65... | collective-permute-start | bytes 245768 | tf_op jit(solution)/shard_map/ppermute | solution.py:19
  102.6 9.6 %collective-permute-start.20 = (f32[20,8,128]{2,1,0:T(8,128)S(1)}, f32[20,8,128]{2,1,0:T(8,128)S(1)}, u32[]{:S(2)}, u32[]{:S(2)}) collective-permute-start(f32[20,8,128]{2,1,0:T(8,128)S(1)} %get-tuple-element.130), channel_id=1, source_target_pairs={{0,192},{64,0},{128,64},{192,128},{1,193},{65,1},{129,65},{193,129... | collective-permute-start | bytes 245768 | tf_op jit(solution)/shard_map/ppermute | solution.py:19
  104.2 6.2 %collective-permute-start.16 = (f32[12,8,128]{2,1,0:T(8,128)S(1)}, f32[12,8,128]{2,1,0:T(8,128)S(1)}, u32[]{:S(2)}, u32[]{:S(2)}) collective-permute-start(f32[12,8,128]{2,1,0:T(8,128)S(1)} %get-tuple-element.125), channel_id=1, source_target_pairs={{0,16},{8,24},{16,32},{24,40},{32,48},{40,56},{48,0},{56,8},{1,17}... | collective-permute-start | bytes 147464 | tf_op jit(solution)/shard_map/ppermute | solution.py:19
  107.1 5.0 %collective-permute-start.17 = (f32[12,8,128]{2,1,0:T(8,128)S(1)}, f32[12,8,128]{2,1,0:T(8,128)S(1)}, u32[]{:S(2)}, u32[]{:S(2)}) collective-permute-start(f32[12,8,128]{2,1,0:T(8,128)S(1)} %get-tuple-element.126), channel_id=1, source_target_pairs={{0,48},{8,56},{16,0},{24,8},{32,16},{40,24},{48,32},{56,40},{1,49}... | collective-permute-start | bytes 147464 | tf_op jit(solution)/shard_map/ppermute | solution.py:19
  112.5 5.2 %collective-permute-start.21 = (f32[8,8,128]{2,1,0:T(8,128)S(1)}, f32[8,8,128]{2,1,0:T(8,128)S(1)}, u32[]{:S(2)}, u32[]{:S(2)}) collective-permute-start(f32[8,8,128]{2,1,0:T(8,128)S(1)} %get-tuple-element.132), channel_id=1, source_target_pairs={{0,1},{1,2},{2,3},{3,0},{4,5},{5,6},{6,7},{7,4},{8,9},{9,10},{10,1... | collective-permute-start | bytes 98312 | tf_op jit(solution)/shard_map/ppermute | solution.py:19
  113.0 5.4 %collective-permute-start.22 = (f32[8,8,128]{2,1,0:T(8,128)S(1)}, f32[8,8,128]{2,1,0:T(8,128)S(1)}, u32[]{:S(2)}, u32[]{:S(2)}) collective-permute-start(f32[8,8,128]{2,1,0:T(8,128)S(1)} %get-tuple-element.133), channel_id=1, source_target_pairs={{0,2},{1,3},{2,0},{3,1},{4,6},{5,7},{6,4},{7,5},{8,10},{9,11},{10,... | collective-permute-start | bytes 98312 | tf_op jit(solution)/shard_map/ppermute | solution.py:19
  115.7 3.9 %collective-permute-start.23 = (f32[8,8,128]{2,1,0:T(8,128)S(1)}, f32[8,8,128]{2,1,0:T(8,128)S(1)}, u32[]{:S(2)}, u32[]{:S(2)}) collective-permute-start(f32[8,8,128]{2,1,0:T(8,128)S(1)} %get-tuple-element.134), channel_id=1, source_target_pairs={{0,3},{1,0},{2,1},{3,2},{4,7},{5,4},{6,5},{7,6},{8,11},{9,8},{10,9... | collective-permute-start | bytes 98312 | tf_op jit(solution)/shard_map/ppermute | solution.py:19

commit v9 on v8

--- a/solution.py
+++ b/solution.py
@@ -444,12 +444,11 @@
         turned = jnp.concatenate(rows, axis=0).T
         for q in range(batch):
             j = g * batch + q
-            out_ref[j] = jnp.dot(
-                turned[q * piece : (q + 1) * piece, :],
-                unpacked(l_ref[j // share, j % share]),
-                precision=HIGHEST,
-                preferred_element_type=jnp.float32,
-            )
+            high, low = split(turned[q * piece : (q + 1) * piece, :])
+            w_high, w_low = split(unpacked(l_ref[j // share, j % share]))
+            total = jnp.dot(high, w_high, preferred_element_type=jnp.float32)
+            total = total + jnp.dot(low, w_high, preferred_element_type=jnp.float32)
+            out_ref[j] = total + jnp.dot(high, w_low, preferred_element_type=jnp.float32)
 
 
 def final(me, packed, messages, slots):
@@ -525,7 +524,7 @@
     ry_two = shift(y_two, "y", 2)
     gram1, term = level(first_level_kernel, shared, node_transfer[0])
     other = swap(term, "core", 1)
-    rz_up, rz_down, got_far, other = tie(rz_up, rz_down, got_far, other)
+    ry_two, rz_up, rz_down, got_far, other = tie(ry_two, rz_up, rz_down, got_far, other)
     sums = (keep_far, got_far)
 
     y_up, y_down, z_up, z_down = run_round(
@@ -536,9 +535,7 @@
     ry_up, ry_down = along("y", y_up, y_down)
     gram2, term = level(next_level_kernel, term, other, pair_transfer[0])
     other = swap(term, "z", 1)
-    ry_two, ry_up, ry_down, rz_up, rz_down, other = tie(
-        ry_two, ry_up, ry_down, rz_up, rz_down, other
-    )
+    ry_up, ry_down, rz_up, rz_down, other = tie(ry_up, ry_down, rz_up, rz_down, other)
 
     ride = z_rows + cut // 2 + cut
     ey, up, down = run_round(

time: 122 us -> 119 us (0.975)
  starting transfers between devices: 44.8 us -> 41.8 us
    ppermute x19, starting transfers between devices: 32.7 us -> 29.5 us  [shift(): lax.ppermute(value, axis, [(i, (i + step) % size) for i in range(size)])]
where the time goes in v9:
time: 119 us; the launch traced here: 118 us
  starting transfers between devices  41.8 us (35%)
  waiting for transfers between devices  35.3 us (30%)
  Pallas kernels  23.7 us (20%)
  blocking collectives  13.1 us (11%)
  other arithmetic  2.17 us (2%)
  local copies, waits for them, and re-layouts  1.5 us (1%)
    ppermute x19, starting transfers between devices, shift(): lax.ppermute(value, axis, [(i, (i + step) % size) for i in range(size)])  29.5 us
    ppermute x19, waiting for transfers between devices, shift(): lax.ppermute(value, axis, [(i, (i + step) % size) for i in range(size)])  15.7 us
    ppermute x5, waiting for transfers between devices, swap(): lax.ppermute(value, axis, [(i, i ^ mask) for i in range(lax.axis_size(axi...  13.9 us
    all_gather x1, blocking collectives, shards(): packed = lax.all_gather(mine, 'rk', axis=0, tiled=False)  13.1 us
    pallas_call x1, Pallas kernels, weighted_sums(): pl.pallas_call(product_kernel, in_specs=[pl.BlockSpec(memory_space=pltpu....  10.4 us
    ppermute x5, starting transfers between devices, swap(): lax.ppermute(value, axis, [(i, i ^ mask) for i in range(lax.axis_size(axi...  7.86 us
    all_to_all x1, waiting for transfers between devices, shards(): lax.all_to_all(local, 'rk', split_axis=0, concat_axis=0, tiled=True)  5.82 us
    pallas_call x1, Pallas kernels, leaf_factors(): pl.pallas_call(leaf_kernel, out_shape=jax.ShapeDtypeStruct((leaves + 1, R...  5.19 us
  transfers between devices with their start and end apart: 25, of which 16 were waited for; matrix products, arithmetic and copies ran while one was open for 3% of the time, Pallas kernels for 5%

profile of v9, /device:TPU:32, one launch (start us, length us, event | category | flops | bytes accessed | tf_op | source)
XLA Modules:
  0.0 118.4 jit_solution(7580407549416121818)
XLA Ops:
  0.6 4.4 %all-to-all-start = ((f32[32,16,256]{2,1,0:T(8,128)}), f32[32,16,256]{2,1,0:T(8,128)S(1)}, u32[]{:S(2)}, u32[]{:S(2)}) async-start(f32[32,16,256]{2,1,0:T(8,128)} %bitcast.33), calls=%async_computation | async-start | bytes 1048576 | tf_op jit(solution)/shard_map/all_to_all | solution.py:502
  5.1 0.7 iota_compare_fusion
  5.9 0.8 squeeze.22
  6.7 0.5 broadcast.120
  7.2 1.4 %reduce.3 = s32[32,32]{1,0:T(8,128)S(1)} reduce(s32[1,32,32,1]{2,3,1,0:T(1,128)} %param.15, s32[]{:T(128)} %broadcast.120), dimensions={0,3}, to_apply=%param.15.reduce_sub_computation.3 | reduce | bytes 8196 | tf_op args[6]
  8.7 5.8 %all-to-all-done = f32[32,16,256]{2,1,0:T(8,128)S(1)} async-done(((f32[32,16,256]{2,1,0:T(8,128)}), f32[32,16,256]{2,1,0:T(8,128)S(1)}, u32[]{:S(2)}, u32[]{:S(2)}) %all-to-all-start) | async-done | bytes 524320 | tf_op jit(solution)/shard_map/all_to_all | solution.py:502
  14.6 5.2 %leaf_factors.1 = f32[9,32,128]{2,1,0:T(8,128)S(1)} custom-call(f32[4,8,16,256]{3,2,1,0:T(8,128)S(1)} %bitcast.28, f32[8,64,64]{2,1,0:T(8,128)S(1)} %dynamic-slice_bitcast_fusion.move_ref), custom_call_target="tpu_custom_call" | custom-call | tf_op jit(solution)/shard_map/leaf_factors/pallas_call | solution.py:103
  19.8 13.1 %all-gather = f32[36,32,128]{2,1,0:T(8,128)S(1)} all-gather(f32[9,32,128]{2,1,0:T(8,128)S(1)} %leaf_factors.1), channel_id=2, replica_groups=mesh['y'=4,'z'=8,'core'=2,'rk'=4] {'rk'}, dimensions={0}, use_global_device_ids=true | all-gather | bytes 737280 | tf_op jit(solution)/shard_map/all_gather | solution.py:505
  32.9 10.4 %weighted_sums.1 = (f32[176,8,128]{2,1,0:T(8,128)S(1)}, f32[848,8,128]{2,1,0:T(8,128)S(1)}, f32[176,8,128]{2,1,0:T(8,128)S(1)}, f32[848,8,128]{2,1,0:T(8,128)S(1)}, f32[32,16,64]{2,1,0:T(8,128)}) custom-call(s32[1]{0:T(128)} %bitcast.me_ref, s32[1024]{0:T(1024)S(1)} %add_select_fusion.5.place_ref, f32[32,32,16,64]{3,2,1,0:T(8,128)} %bitcast.32, ...), custom_call_target="tpu_custom_call" | custom-call | tf_op jit(solution)/shard_map/weighted_sums/pallas_call | solution.py:271
  43.4 2.2 %collective-permute-done.got = f32[176,8,128]{2,1,0:T(8,128)S(1)} collective-permute-done((f32[176,8,128]{2,1,0:T(8,128)S(1)}, f32[176,8,128]{2,1,0:T(8,128)S(1)}, u32[]{:S(2)}, u32[]{:S(2)}) %collective-permute-start) | collective-permute-done | bytes 720928 | tf_op jit(solution)/shard_map/ppermute | solution.py:23
  45.8 3.2 %collective-permute-start.1 = (f32[96,8,128]{2,1,0:T(8,128)S(1)}, f32[96,8,128]{2,1,0:T(8,128)S(1)}, u32[]{:S(2)}, u32[]{:S(2)}) collective-permute-start(f32[96,8,128]{2,1,0:T(8,128)S(1)} %get-tuple-element.78), channel_id=1, source_target_pairs={{0,128},{64,192},{128,0},{192,64},{1,129},{65,193},{129,1},{193,65... | collective-permute-start | bytes 1179656 | tf_op jit(solution)/shard_map/ppermute | solution.py:19
  48.9 2.0 %collective-permute-start.2 = (f32[40,8,128]{2,1,0:T(8,128)S(1)}, f32[40,8,128]{2,1,0:T(8,128)S(1)}, u32[]{:S(2)}, u32[]{:S(2)}) collective-permute-start(f32[40,8,128]{2,1,0:T(8,128)S(1)} %get-tuple-element.79), channel_id=1, source_target_pairs={{0,8},{8,16},{16,24},{24,32},{32,40},{40,48},{48,56},{56,0},{1,9},... | collective-permute-start | bytes 491528 | tf_op jit(solution)/shard_map/ppermute | solution.py:19
  50.9 0.4 first_level_kernel.1
  51.3 1.2 %collective-permute-done.5.other_ref = f32[64,64]{1,0:T(8,128)S(1)} collective-permute-done((f32[64,64]{1,0:T(8,128)S(1)}, f32[64,64]{1,0:T(8,128)S(1)}, u32[]{:S(2)}, u32[]{:S(2)}) %collective-permute-start.5) | collective-permute-done | bytes 16416 | tf_op jit(solution)/shard_map/ppermute | solution.py:23
  52.6 2.5 %collective-permute-done.2.rz_up = f32[40,8,128]{2,1,0:T(8,128)S(1)} collective-permute-done((f32[40,8,128]{2,1,0:T(8,128)S(1)}, f32[40,8,128]{2,1,0:T(8,128)S(1)}, u32[]{:S(2)}, u32[]{:S(2)}) %collective-permute-start.2) | collective-permute-done | bytes 163872 | tf_op jit(solution)/shard_map/ppermute | solution.py:19
  55.1 2.0 %collective-permute-done.3.rz_down = f32[40,8,128]{2,1,0:T(8,128)S(1)} collective-permute-done((f32[40,8,128]{2,1,0:T(8,128)S(1)}, f32[40,8,128]{2,1,0:T(8,128)S(1)}, u32[]{:S(2)}, u32[]{:S(2)}) %collective-permute-start.3) | collective-permute-done | bytes 163872 | tf_op jit(solution)/shard_map/ppermute | solution.py:19
  57.1 1.7 %collective-permute-done.1.ry_two = f32[96,8,128]{2,1,0:T(8,128)S(1)} collective-permute-done((f32[96,8,128]{2,1,0:T(8,128)S(1)}, f32[96,8,128]{2,1,0:T(8,128)S(1)}, u32[]{:S(2)}, u32[]{:S(2)}) %collective-permute-start.1) | collective-permute-done | bytes 393248 | tf_op jit(solution)/shard_map/ppermute | solution.py:19
  58.9 1.7 %collective-permute-start.6 = (f32[96,8,128]{2,1,0:T(8,128)S(1)}, f32[96,8,128]{2,1,0:T(8,128)S(1)}, u32[]{:S(2)}, u32[]{:S(2)}) collective-permute-start(f32[96,8,128]{2,1,0:T(8,128)S(1)} %get-tuple-element.92), channel_id=1, source_target_pairs={{0,64},{64,128},{128,192},{192,0},{1,65},{65,129},{129,193},{193,1... | collective-permute-start | bytes 1179656 | tf_op jit(solution)/shard_map/ppermute | solution.py:19
  60.6 1.8 %collective-permute-start.7 = (f32[96,8,128]{2,1,0:T(8,128)S(1)}, f32[96,8,128]{2,1,0:T(8,128)S(1)}, u32[]{:S(2)}, u32[]{:S(2)}) collective-permute-start(f32[96,8,128]{2,1,0:T(8,128)S(1)} %get-tuple-element.93), channel_id=1, source_target_pairs={{0,192},{64,0},{128,64},{192,128},{1,193},{65,1},{129,65},{193,129... | collective-permute-start | bytes 1179656 | tf_op jit(solution)/shard_map/ppermute | solution.py:19
  62.4 1.8 %collective-permute-start.8 = (f32[80,8,128]{2,1,0:T(8,128)S(1)}, f32[80,8,128]{2,1,0:T(8,128)S(1)}, u32[]{:S(2)}, u32[]{:S(2)}) collective-permute-start(f32[80,8,128]{2,1,0:T(8,128)S(1)} %get-tuple-element.94), channel_id=1, source_target_pairs={{0,8},{8,16},{16,24},{24,32},{32,40},{40,48},{48,56},{56,0},{1,9},... | collective-permute-start | bytes 983048 | tf_op jit(solution)/shard_map/ppermute | solution.py:19
  64.2 0.2 collective-permute-start.9
  64.4 0.3 next_level_kernel.2
  64.8 3.9 %collective-permute-start.10 = (f32[64,64]{1,0:T(8,128)S(1)}, f32[64,64]{1,0:T(8,128)S(1)}, u32[]{:S(2)}, u32[]{:S(2)}) collective-permute-start(f32[64,64]{1,0:T(8,128)S(1)} %get-tuple-element.108.mine_ref), channel_id=1, source_target_pairs={{0,8},{8,0},{16,24},{24,16},{32,40},{40,32},{48,56},{56,48},{1,9},... | collective-permute-start | bytes 49160 | tf_op jit(solution)/shard_map/ppermute | solution.py:23
  68.7 3.1 %collective-permute-done.10.other_ref = f32[64,64]{1,0:T(8,128)S(1)} collective-permute-done((f32[64,64]{1,0:T(8,128)S(1)}, f32[64,64]{1,0:T(8,128)S(1)}, u32[]{:S(2)}, u32[]{:S(2)}) %collective-permute-start.10) | collective-permute-done | bytes 16416 | tf_op jit(solution)/shard_map/ppermute | solution.py:23
  71.8 1.1 collective-permute-done.9.rz_down
  72.9 0.3 round3_kernel.1
  73.2 3.9 %collective-permute-start.11 = (f32[98,8,128]{2,1,0:T(8,128)S(1)}, f32[98,8,128]{2,1,0:T(8,128)S(1)}, u32[]{:S(2)}, u32[]{:S(2)}) collective-permute-start(f32[98,8,128]{2,1,0:T(8,128)S(1)} %get-tuple-element.106), channel_id=1, source_target_pairs={{0,8},{8,16},{16,24},{24,32},{32,40},{40,48},{48,56},{56,0},{1,9},... | collective-permute-start | bytes 1204232 | tf_op jit(solution)/shard_map/ppermute | solution.py:19
  77.1 0.3 next_level_kernel.3
  77.5 3.7 %collective-permute-start.13 = (f32[64,64]{1,0:T(8,128)S(1)}, f32[64,64]{1,0:T(8,128)S(1)}, u32[]{:S(2)}, u32[]{:S(2)}) collective-permute-start(f32[64,64]{1,0:T(8,128)S(1)} %get-tuple-element.120.mine_ref), channel_id=1, source_target_pairs={{0,16},{8,24},{16,0},{24,8},{32,48},{40,56},{48,32},{56,40},{1,17}... | collective-permute-start | bytes 49160 | tf_op jit(solution)/shard_map/ppermute | solution.py:23
  81.2 7.4 %collective-permute-done.13.other_ref = f32[64,64]{1,0:T(8,128)S(1)} collective-permute-done((f32[64,64]{1,0:T(8,128)S(1)}, f32[64,64]{1,0:T(8,128)S(1)}, u32[]{:S(2)}, u32[]{:S(2)}) %collective-permute-start.13) | collective-permute-done | bytes 16416 | tf_op jit(solution)/shard_map/ppermute | solution.py:23
  88.7 0.2 collective-permute-start.14
  88.8 1.9 %collective-permute-start.15 = (f32[92,8,128]{2,1,0:T(8,128)S(1)}, f32[92,8,128]{2,1,0:T(8,128)S(1)}, u32[]{:S(2)}, u32[]{:S(2)}) collective-permute-start(f32[92,8,128]{2,1,0:T(8,128)S(1)} %get-tuple-element.116), channel_id=1, source_target_pairs={{0,56},{8,0},{16,8},{24,16},{32,24},{40,32},{48,40},{56,48},{1,57}... | collective-permute-start | bytes 1130504 | tf_op jit(solution)/shard_map/ppermute | solution.py:19
  90.8 4.7 %node_factors.1 = f32[4,16,64]{2,1,0:T(8,128)} custom-call(s32[1]{0:T(128)} %bitcast.me_ref, f32[64,64]{1,0:T(8,128)S(1)} %get-tuple-element.117.g1_ref, f32[64,64]{1,0:T(8,128)S(1)} %get-tuple-element.118.g2_ref, f32[64,64]{1,0:T(8,128)S(1)} %get-tuple-element.119.g3_ref, f32[64,64]{1,0:T(8,128)S(1)} %get-tuple-element.120.mine_ref, ...), custom_call_target="tpu_custom_call" | custom-call | tf_op jit(solution)/shard_map/node_factors/pallas_call | solution.py:163
  95.5 0.8 collective-permute-done.14.rz_up
  96.6 3.2 %collective-permute-start.19 = (f32[20,8,128]{2,1,0:T(8,128)S(1)}, f32[20,8,128]{2,1,0:T(8,128)S(1)}, u32[]{:S(2)}, u32[]{:S(2)}) collective-permute-start(f32[20,8,128]{2,1,0:T(8,128)S(1)} %get-tuple-element.129), channel_id=1, source_target_pairs={{0,128},{64,192},{128,0},{192,64},{1,129},{65,193},{129,1},{193,65... | collective-permute-start | bytes 245768 | tf_op jit(solution)/shard_map/ppermute | solution.py:19
  99.8 1.0 collective-permute-start.20
  100.8 3.8 %collective-permute-start.16 = (f32[12,8,128]{2,1,0:T(8,128)S(1)}, f32[12,8,128]{2,1,0:T(8,128)S(1)}, u32[]{:S(2)}, u32[]{:S(2)}) collective-permute-start(f32[12,8,128]{2,1,0:T(8,128)S(1)} %get-tuple-element.125), channel_id=1, source_target_pairs={{0,16},{8,24},{16,32},{24,40},{32,48},{40,56},{48,0},{56,8},{1,17}... | collective-permute-start | bytes 147464 | tf_op jit(solution)/shard_map/ppermute | solution.py:19
  104.6 0.5 collective-permute-start.17
  105.1 2.1 %collective-permute-done.16.z_two = f32[12,8,128]{2,1,0:T(8,128)S(1)} collective-permute-done((f32[12,8,128]{2,1,0:T(8,128)S(1)}, f32[12,8,128]{2,1,0:T(8,128)S(1)}, u32[]{:S(2)}, u32[]{:S(2)}) %collective-permute-start.16) | collective-permute-done | bytes 49184 | tf_op jit(solution)/shard_map/ppermute | solution.py:19
  107.2 2.4 %collective-permute-done.17.z_six = f32[12,8,128]{2,1,0:T(8,128)S(1)} collective-permute-done((f32[12,8,128]{2,1,0:T(8,128)S(1)}, f32[12,8,128]{2,1,0:T(8,128)S(1)}, u32[]{:S(2)}, u32[]{:S(2)}) %collective-permute-start.17) | collective-permute-done | bytes 49184 | tf_op jit(solution)/shard_map/ppermute | solution.py:19
  109.6 0.3 pack.1
  109.9 0.6 collective-permute-start.21
  110.5 2.7 %collective-permute-start.22 = (f32[8,8,128]{2,1,0:T(8,128)S(1)}, f32[8,8,128]{2,1,0:T(8,128)S(1)}, u32[]{:S(2)}, u32[]{:S(2)}) collective-permute-start(f32[8,8,128]{2,1,0:T(8,128)S(1)} %get-tuple-element.133), channel_id=1, source_target_pairs={{0,2},{1,3},{2,0},{3,1},{4,6},{5,7},{6,4},{7,5},{8,10},{9,11},{10,... | collective-permute-start | bytes 98312 | tf_op jit(solution)/shard_map/ppermute | solution.py:19
  113.1 0.9 collective-permute-start.23
  114.1 1.0 collective-permute-done.21.m1_ref
  115.1 0.8 collective-permute-done.22.m2_ref
  115.9 1.2 collective-permute-done.23.m3_ref
  117.1 1.3 %left_factor.1 = f32[32,16,64]{2,1,0:T(8,128)} custom-call(s32[1]{0:T(128)} %bitcast.me_ref, f32[4,9,32,128]{3,2,1,0:T(8,128)S(1)} %bitcast.27, f32[8,8,128]{2,1,0:T(8,128)S(1)} %get-tuple-element.131.m0_ref, f32[8,8,128]{2,1,0:T(8,128)S(1)} %collective-permute-done.21.m1_ref, f32[8,8,128]{2,1,0:T(8,128)S(1)} %collective-permute-done.22.m2_ref, ...), custom_call_target="tpu_custom_call" | custom-call | tf_op jit(solution)/shard_map/left_factor/pallas_call | solution.py:456
  (32 shorter events, 1.1 us)
Async XLA Ops:
  0.6 8.1 %copy-start = (f32[1,32,64,64]{3,2,1,0:T(8,128)S(1)}, f32[1,32,64,64]{3,2,1,0:T(8,128)}, u32[]{:S(2)}) copy-start(f32[1,32,64,64]{3,2,1,0:T(8,128)} %param.10) | copy-start | bytes 1572868
  0.6 13.9 %all-to-all-start = ((f32[32,16,256]{2,1,0:T(8,128)}), f32[32,16,256]{2,1,0:T(8,128)S(1)}, u32[]{:S(2)}, u32[]{:S(2)}) async-start(f32[32,16,256]{2,1,0:T(8,128)} %bitcast.33), calls=%async_computation | async-start | bytes 1048576 | tf_op jit(solution)/shard_map/all_to_all | solution.py:502
  32.9 18.1 %copy-start.1 = (f32[1,64,64]{2,1,0:T(8,128)S(1)}, f32[1,64,64]{2,1,0:T(8,128)}, u32[]{:S(2)}) copy-start(f32[1,64,64]{2,1,0:T(8,128)} %param.11) | copy-start | bytes 49156
  43.3 2.3 %collective-permute-start = (f32[176,8,128]{2,1,0:T(8,128)S(1)}, f32[176,8,128]{2,1,0:T(8,128)S(1)}, u32[]{:S(2)}, u32[]{:S(2)}) collective-permute-start(f32[176,8,128]{2,1,0:T(8,128)S(1)} %get-tuple-element.72), channel_id=1, source_target_pairs={{0,4},{4,0},{1,5},{5,1},{2,6},{6,2},{3,7},{7,3},{8,12},{12,8},{9,1... | collective-permute-start | bytes 2162696 | tf_op jit(solution)/shard_map/ppermute | solution.py:23
  45.5 13.2 %collective-permute-start.4 = (f32[848,8,128]{2,1,0:T(8,128)S(1)}, f32[848,8,128]{2,1,0:T(8,128)S(1)}, u32[]{:S(2)}, u32[]{:S(2)}) collective-permute-start(f32[848,8,128]{2,1,0:T(8,128)S(1)} %get-tuple-element.81), channel_id=1, source_target_pairs={{0,4},{4,0},{1,5},{5,1},{2,6},{6,2},{3,7},{7,3},{8,12},{12,8},{9,1... | collective-permute-start | bytes 10420232 | tf_op jit(solution)/shard_map/ppermute | solution.py:23
  45.8 13.0 %collective-permute-start.1 = (f32[96,8,128]{2,1,0:T(8,128)S(1)}, f32[96,8,128]{2,1,0:T(8,128)S(1)}, u32[]{:S(2)}, u32[]{:S(2)}) collective-permute-start(f32[96,8,128]{2,1,0:T(8,128)S(1)} %get-tuple-element.78), channel_id=1, source_target_pairs={{0,128},{64,192},{128,0},{192,64},{1,129},{65,193},{129,1},{193,65... | collective-permute-start | bytes 1179656 | tf_op jit(solution)/shard_map/ppermute | solution.py:19
  48.9 6.2 %collective-permute-start.2 = (f32[40,8,128]{2,1,0:T(8,128)S(1)}, f32[40,8,128]{2,1,0:T(8,128)S(1)}, u32[]{:S(2)}, u32[]{:S(2)}) collective-permute-start(f32[40,8,128]{2,1,0:T(8,128)S(1)} %get-tuple-element.79), channel_id=1, source_target_pairs={{0,8},{8,16},{16,24},{24,32},{32,40},{40,48},{48,56},{56,0},{1,9},... | collective-permute-start | bytes 491528 | tf_op jit(solution)/shard_map/ppermute | solution.py:19
  50.9 6.1 %collective-permute-start.3 = (f32[40,8,128]{2,1,0:T(8,128)S(1)}, f32[40,8,128]{2,1,0:T(8,128)S(1)}, u32[]{:S(2)}, u32[]{:S(2)}) collective-permute-start(f32[40,8,128]{2,1,0:T(8,128)S(1)} %get-tuple-element.80), channel_id=1, source_target_pairs={{0,56},{8,0},{16,8},{24,16},{32,24},{40,32},{48,40},{56,48},{1,57}... | collective-permute-start | bytes 491528 | tf_op jit(solution)/shard_map/ppermute | solution.py:19
  51.3 1.2 %collective-permute-start.5 = (f32[64,64]{1,0:T(8,128)S(1)}, f32[64,64]{1,0:T(8,128)S(1)}, u32[]{:S(2)}, u32[]{:S(2)}) collective-permute-start(f32[64,64]{1,0:T(8,128)S(1)} %get-tuple-element.96.mine_ref), channel_id=1, source_target_pairs={{0,4},{4,0},{1,5},{5,1},{2,6},{6,2},{3,7},{7,3},{8,12},{12,8},{9,1... | collective-permute-start | bytes 49160 | tf_op jit(solution)/shard_map/ppermute | solution.py:23
  58.7 5.7 %copy-start.2 = (f32[1,64,64]{2,1,0:T(8,128)S(1)}, f32[1,64,64]{2,1,0:T(8,128)}, u32[]{:S(2)}) copy-start(f32[1,64,64]{2,1,0:T(8,128)} %param.12) | copy-start | bytes 49156
  58.9 14.0 %collective-permute-start.6 = (f32[96,8,128]{2,1,0:T(8,128)S(1)}, f32[96,8,128]{2,1,0:T(8,128)S(1)}, u32[]{:S(2)}, u32[]{:S(2)}) collective-permute-start(f32[96,8,128]{2,1,0:T(8,128)S(1)} %get-tuple-element.92), channel_id=1, source_target_pairs={{0,64},{64,128},{128,192},{192,0},{1,65},{65,129},{129,193},{193,1... | collective-permute-start | bytes 1179656 | tf_op jit(solution)/shard_map/ppermute | solution.py:19
  60.6 12.3 %collective-permute-start.7 = (f32[96,8,128]{2,1,0:T(8,128)S(1)}, f32[96,8,128]{2,1,0:T(8,128)S(1)}, u32[]{:S(2)}, u32[]{:S(2)}) collective-permute-start(f32[96,8,128]{2,1,0:T(8,128)S(1)} %get-tuple-element.93), channel_id=1, source_target_pairs={{0,192},{64,0},{128,64},{192,128},{1,193},{65,1},{129,65},{193,129... | collective-permute-start | bytes 1179656 | tf_op jit(solution)/shard_map/ppermute | solution.py:19
  62.4 9.4 %collective-permute-start.8 = (f32[80,8,128]{2,1,0:T(8,128)S(1)}, f32[80,8,128]{2,1,0:T(8,128)S(1)}, u32[]{:S(2)}, u32[]{:S(2)}) collective-permute-start(f32[80,8,128]{2,1,0:T(8,128)S(1)} %get-tuple-element.94), channel_id=1, source_target_pairs={{0,8},{8,16},{16,24},{24,32},{32,40},{40,48},{48,56},{56,0},{1,9},... | collective-permute-start | bytes 983048 | tf_op jit(solution)/shard_map/ppermute | solution.py:19
  64.2 8.7 %collective-permute-start.9 = (f32[80,8,128]{2,1,0:T(8,128)S(1)}, f32[80,8,128]{2,1,0:T(8,128)S(1)}, u32[]{:S(2)}, u32[]{:S(2)}) collective-permute-start(f32[80,8,128]{2,1,0:T(8,128)S(1)} %get-tuple-element.95), channel_id=1, source_target_pairs={{0,56},{8,0},{16,8},{24,16},{32,24},{40,32},{48,40},{56,48},{1,57}... | collective-permute-start | bytes 983048 | tf_op jit(solution)/shard_map/ppermute | solution.py:19
  64.8 12.4 %copy-start.3 = (f32[1,64,64]{2,1,0:T(8,128)S(1)}, f32[1,64,64]{2,1,0:T(8,128)}, u32[]{:S(2)}) copy-start(f32[1,64,64]{2,1,0:T(8,128)} %param.13) | copy-start | bytes 49156
  64.8 7.0 %collective-permute-start.10 = (f32[64,64]{1,0:T(8,128)S(1)}, f32[64,64]{1,0:T(8,128)S(1)}, u32[]{:S(2)}, u32[]{:S(2)}) collective-permute-start(f32[64,64]{1,0:T(8,128)S(1)} %get-tuple-element.108.mine_ref), channel_id=1, source_target_pairs={{0,8},{8,0},{16,24},{24,16},{32,40},{40,32},{48,56},{56,48},{1,9},... | collective-permute-start | bytes 49160 | tf_op jit(solution)/shard_map/ppermute | solution.py:23
  73.2 15.4 %collective-permute-start.11 = (f32[98,8,128]{2,1,0:T(8,128)S(1)}, f32[98,8,128]{2,1,0:T(8,128)S(1)}, u32[]{:S(2)}, u32[]{:S(2)}) collective-permute-start(f32[98,8,128]{2,1,0:T(8,128)S(1)} %get-tuple-element.106), channel_id=1, source_target_pairs={{0,8},{8,16},{16,24},{24,32},{32,40},{40,48},{48,56},{56,0},{1,9},... | collective-permute-start | bytes 1204232 | tf_op jit(solution)/shard_map/ppermute | solution.py:19
  77.1 11.4 %collective-permute-start.12 = (f32[98,8,128]{2,1,0:T(8,128)S(1)}, f32[98,8,128]{2,1,0:T(8,128)S(1)}, u32[]{:S(2)}, u32[]{:S(2)}) collective-permute-start(f32[98,8,128]{2,1,0:T(8,128)S(1)} %get-tuple-element.107), channel_id=1, source_target_pairs={{0,56},{8,0},{16,8},{24,16},{32,24},{40,32},{48,40},{56,48},{1,57}... | collective-permute-start | bytes 1204232 | tf_op jit(solution)/shard_map/ppermute | solution.py:19
  77.5 11.1 %collective-permute-start.13 = (f32[64,64]{1,0:T(8,128)S(1)}, f32[64,64]{1,0:T(8,128)S(1)}, u32[]{:S(2)}, u32[]{:S(2)}) collective-permute-start(f32[64,64]{1,0:T(8,128)S(1)} %get-tuple-element.120.mine_ref), channel_id=1, source_target_pairs={{0,16},{8,24},{16,0},{24,8},{32,48},{40,56},{48,32},{56,40},{1,17}... | collective-permute-start | bytes 49160 | tf_op jit(solution)/shard_map/ppermute | solution.py:23
  88.7 7.7 %collective-permute-start.14 = (f32[92,8,128]{2,1,0:T(8,128)S(1)}, f32[92,8,128]{2,1,0:T(8,128)S(1)}, u32[]{:S(2)}, u32[]{:S(2)}) collective-permute-start(f32[92,8,128]{2,1,0:T(8,128)S(1)} %get-tuple-element.115), channel_id=1, source_target_pairs={{0,8},{8,16},{16,24},{24,32},{32,40},{40,48},{48,56},{56,0},{1,9},... | collective-permute-start | bytes 1130504 | tf_op jit(solution)/shard_map/ppermute | solution.py:19
  88.8 7.6 %collective-permute-start.15 = (f32[92,8,128]{2,1,0:T(8,128)S(1)}, f32[92,8,128]{2,1,0:T(8,128)S(1)}, u32[]{:S(2)}, u32[]{:S(2)}) collective-permute-start(f32[92,8,128]{2,1,0:T(8,128)S(1)} %get-tuple-element.116), channel_id=1, source_target_pairs={{0,56},{8,0},{16,8},{24,16},{32,24},{40,32},{48,40},{56,48},{1,57}... | collective-permute-start | bytes 1130504 | tf_op jit(solution)/shard_map/ppermute | solution.py:19
  96.5 13.0 %collective-permute-start.18 = (f32[20,8,128]{2,1,0:T(8,128)S(1)}, f32[20,8,128]{2,1,0:T(8,128)S(1)}, u32[]{:S(2)}, u32[]{:S(2)}) collective-permute-start(f32[20,8,128]{2,1,0:T(8,128)S(1)} %get-tuple-element.128), channel_id=1, source_target_pairs={{0,64},{64,128},{128,192},{192,0},{1,65},{65,129},{129,193},{193,1... | collective-permute-start | bytes 245768 | tf_op jit(solution)/shard_map/ppermute | solution.py:19
  96.6 13.0 %collective-permute-start.19 = (f32[20,8,128]{2,1,0:T(8,128)S(1)}, f32[20,8,128]{2,1,0:T(8,128)S(1)}, u32[]{:S(2)}, u32[]{:S(2)}) collective-permute-start(f32[20,8,128]{2,1,0:T(8,128)S(1)} %get-tuple-element.129), channel_id=1, source_target_pairs={{0,128},{64,192},{128,0},{192,64},{1,129},{65,193},{129,1},{193,65... | collective-permute-start | bytes 245768 | tf_op jit(solution)/shard_map/ppermute | solution.py:19
  99.8 9.8 %collective-permute-start.20 = (f32[20,8,128]{2,1,0:T(8,128)S(1)}, f32[20,8,128]{2,1,0:T(8,128)S(1)}, u32[]{:S(2)}, u32[]{:S(2)}) collective-permute-start(f32[20,8,128]{2,1,0:T(8,128)S(1)} %get-tuple-element.130), channel_id=1, source_target_pairs={{0,192},{64,0},{128,64},{192,128},{1,193},{65,1},{129,65},{193,129... | collective-permute-start | bytes 245768 | tf_op jit(solution)/shard_map/ppermute | solution.py:19
  100.8 6.4 %collective-permute-start.16 = (f32[12,8,128]{2,1,0:T(8,128)S(1)}, f32[12,8,128]{2,1,0:T(8,128)S(1)}, u32[]{:S(2)}, u32[]{:S(2)}) collective-permute-start(f32[12,8,128]{2,1,0:T(8,128)S(1)} %get-tuple-element.125), channel_id=1, source_target_pairs={{0,16},{8,24},{16,32},{24,40},{32,48},{40,56},{48,0},{56,8},{1,17}... | collective-permute-start | bytes 147464 | tf_op jit(solution)/shard_map/ppermute | solution.py:19
  104.6 5.0 %collective-permute-start.17 = (f32[12,8,128]{2,1,0:T(8,128)S(1)}, f32[12,8,128]{2,1,0:T(8,128)S(1)}, u32[]{:S(2)}, u32[]{:S(2)}) collective-permute-start(f32[12,8,128]{2,1,0:T(8,128)S(1)} %get-tuple-element.126), channel_id=1, source_target_pairs={{0,48},{8,56},{16,0},{24,8},{32,16},{40,24},{48,32},{56,40},{1,49}... | collective-permute-start | bytes 147464 | tf_op jit(solution)/shard_map/ppermute | solution.py:19
  109.9 5.2 %collective-permute-start.21 = (f32[8,8,128]{2,1,0:T(8,128)S(1)}, f32[8,8,128]{2,1,0:T(8,128)S(1)}, u32[]{:S(2)}, u32[]{:S(2)}) collective-permute-start(f32[8,8,128]{2,1,0:T(8,128)S(1)} %get-tuple-element.132), channel_id=1, source_target_pairs={{0,1},{1,2},{2,3},{3,0},{4,5},{5,6},{6,7},{7,4},{8,9},{9,10},{10,1... | collective-permute-start | bytes 98312 | tf_op jit(solution)/shard_map/ppermute | solution.py:19
  110.5 5.4 %collective-permute-start.22 = (f32[8,8,128]{2,1,0:T(8,128)S(1)}, f32[8,8,128]{2,1,0:T(8,128)S(1)}, u32[]{:S(2)}, u32[]{:S(2)}) collective-permute-start(f32[8,8,128]{2,1,0:T(8,128)S(1)} %get-tuple-element.133), channel_id=1, source_target_pairs={{0,2},{1,3},{2,0},{3,1},{4,6},{5,7},{6,4},{7,5},{8,10},{9,11},{10,... | collective-permute-start | bytes 98312 | tf_op jit(solution)/shard_map/ppermute | solution.py:19
  113.1 3.9 %collective-permute-start.23 = (f32[8,8,128]{2,1,0:T(8,128)S(1)}, f32[8,8,128]{2,1,0:T(8,128)S(1)}, u32[]{:S(2)}, u32[]{:S(2)}) collective-permute-start(f32[8,8,128]{2,1,0:T(8,128)S(1)} %get-tuple-element.134), channel_id=1, source_target_pairs={{0,3},{1,0},{2,1},{3,2},{4,7},{5,4},{6,5},{7,6},{8,11},{9,8},{10,9... | collective-permute-start | bytes 98312 | tf_op jit(solution)/shard_map/ppermute | solution.py:19

commit v10 on v9

--- a/solution.py
+++ b/solution.py
@@ -292,7 +292,7 @@
 class Plan:
     def __init__(self, n_y, n_z, slots):
         self.n_y, self.n_z = n_y, n_z
-        self.cut = 3 * slots // 8
+        self.cut = 7 * slots // 16
         self.rest = slots - self.cut
         self.rows = {"y": n_z * self.cut, "z": n_y * self.rest}
         self.base = {}

time: 119 us -> 121 us (1.017)
  waiting for transfers between devices: 35.3 us -> 37.1 us
    ppermute x19, waiting for transfers between devices: 15.7 us -> 18.6 us  [shift(): lax.ppermute(value, axis, [(i, (i + step) % size) for i in range(size)])]
    ppermute x5, waiting for transfers between devices: 13.9 us -> 12.7 us  [swap(): lax.ppermute(value, axis, [(i, i ^ mask) for i in range(lax.axis_size(axi...]
  transfers between devices with their start and end apart: 25 -> 25, of which waited for: 16 -> 18; matrix products, arithmetic and copies ran while one was open for 3% -> 3% of each run, Pallas kernels for 5% -> 5%
where the time goes in v10:
time: 121 us
  starting transfers between devices  42.4 us (35%)
  waiting for transfers between devices  37.1 us (31%)
  Pallas kernels  23.7 us (20%)
  blocking collectives  13.1 us (11%)
  other arithmetic  2.17 us (2%)
  local copies, waits for them, and re-layouts  1.5 us (1%)
    ppermute x19, starting transfers between devices, shift(): lax.ppermute(value, axis, [(i, (i + step) % size) for i in range(size)])  30 us
    ppermute x19, waiting for transfers between devices, shift(): lax.ppermute(value, axis, [(i, (i + step) % size) for i in range(size)])  18.6 us
    all_gather x1, blocking collectives, shards(): packed = lax.all_gather(mine, 'rk', axis=0, tiled=False)  13.1 us
    ppermute x5, waiting for transfers between devices, swap(): lax.ppermute(value, axis, [(i, i ^ mask) for i in range(lax.axis_size(axi...  12.7 us
    pallas_call x1, Pallas kernels, weighted_sums(): pl.pallas_call(product_kernel, in_specs=[pl.BlockSpec(memory_space=pltpu....  10.4 us
    ppermute x5, starting transfers between devices, swap(): lax.ppermute(value, axis, [(i, i ^ mask) for i in range(lax.axis_size(axi...  8.05 us
    all_to_all x1, waiting for transfers between devices, shards(): lax.all_to_all(local, 'rk', split_axis=0, concat_axis=0, tiled=True)  5.82 us
    pallas_call x1, Pallas kernels, leaf_factors(): pl.pallas_call(leaf_kernel, out_shape=jax.ShapeDtypeStruct((leaves + 1, R...  5.19 us
  transfers between devices with their start and end apart: 25, of which 18 were waited for; matrix products, arithmetic and copies ran while one was open for 3% of the time, Pallas kernels for 5%

profile of v10, /device:TPU:32, one launch (start us, length us, event | category | flops | bytes accessed | tf_op | source)
XLA Modules:
  0.0 120.7 jit_solution(5151638358821169115)
XLA Ops:
  0.6 4.4 %all-to-all-start = ((f32[32,16,256]{2,1,0:T(8,128)}), f32[32,16,256]{2,1,0:T(8,128)S(1)}, u32[]{:S(2)}, u32[]{:S(2)}) async-start(f32[32,16,256]{2,1,0:T(8,128)} %bitcast.33), calls=%async_computation | async-start | bytes 1048576 | tf_op jit(solution)/shard_map/all_to_all | solution.py:502
  5.1 0.7 iota_compare_fusion
  5.9 0.8 squeeze.22
  6.7 0.5 broadcast.120
  7.2 1.4 %reduce.3 = s32[32,32]{1,0:T(8,128)S(1)} reduce(s32[1,32,32,1]{2,3,1,0:T(1,128)} %param.15, s32[]{:T(128)} %broadcast.120), dimensions={0,3}, to_apply=%param.15.reduce_sub_computation.3 | reduce | bytes 8196 | tf_op args[6]
  8.7 5.8 %all-to-all-done = f32[32,16,256]{2,1,0:T(8,128)S(1)} async-done(((f32[32,16,256]{2,1,0:T(8,128)}), f32[32,16,256]{2,1,0:T(8,128)S(1)}, u32[]{:S(2)}, u32[]{:S(2)}) %all-to-all-start) | async-done | bytes 524320 | tf_op jit(solution)/shard_map/all_to_all | solution.py:502
  14.6 5.2 %leaf_factors.1 = f32[9,32,128]{2,1,0:T(8,128)S(1)} custom-call(f32[4,8,16,256]{3,2,1,0:T(8,128)S(1)} %bitcast.28, f32[8,64,64]{2,1,0:T(8,128)S(1)} %dynamic-slice_bitcast_fusion.move_ref), custom_call_target="tpu_custom_call" | custom-call | tf_op jit(solution)/shard_map/leaf_factors/pallas_call | solution.py:103
  19.8 13.1 %all-gather = f32[36,32,128]{2,1,0:T(8,128)S(1)} all-gather(f32[9,32,128]{2,1,0:T(8,128)S(1)} %leaf_factors.1), channel_id=2, replica_groups=mesh['y'=4,'z'=8,'core'=2,'rk'=4] {'rk'}, dimensions={0}, use_global_device_ids=true | all-gather | bytes 737280 | tf_op jit(solution)/shard_map/all_gather | solution.py:505
  32.9 10.4 %weighted_sums.1 = (f32[184,8,128]{2,1,0:T(8,128)S(1)}, f32[840,8,128]{2,1,0:T(8,128)S(1)}, f32[184,8,128]{2,1,0:T(8,128)S(1)}, f32[840,8,128]{2,1,0:T(8,128)S(1)}, f32[32,16,64]{2,1,0:T(8,128)}) custom-call(s32[1]{0:T(128)} %bitcast.me_ref, s32[1024]{0:T(1024)S(1)} %add_select_fusion.5.place_ref, f32[32,32,16,64]{3,2,1,0:T(8,128)} %bitcast.32, ...), custom_call_target="tpu_custom_call" | custom-call | tf_op jit(solution)/shard_map/weighted_sums/pallas_call | solution.py:271
  43.3 2.2 %collective-permute-done.got = f32[184,8,128]{2,1,0:T(8,128)S(1)} collective-permute-done((f32[184,8,128]{2,1,0:T(8,128)S(1)}, f32[184,8,128]{2,1,0:T(8,128)S(1)}, u32[]{:S(2)}, u32[]{:S(2)}) %collective-permute-start) | collective-permute-done | bytes 753696 | tf_op jit(solution)/shard_map/ppermute | solution.py:23
  45.8 3.3 %collective-permute-start.1 = (f32[112,8,128]{2,1,0:T(8,128)S(1)}, f32[112,8,128]{2,1,0:T(8,128)S(1)}, u32[]{:S(2)}, u32[]{:S(2)}) collective-permute-start(f32[112,8,128]{2,1,0:T(8,128)S(1)} %get-tuple-element.78), channel_id=1, source_target_pairs={{0,128},{64,192},{128,0},{192,64},{1,129},{65,193},{129,1},{193,65... | collective-permute-start | bytes 1376264 | tf_op jit(solution)/shard_map/ppermute | solution.py:19
  49.1 1.9 %collective-permute-start.2 = (f32[36,8,128]{2,1,0:T(8,128)S(1)}, f32[36,8,128]{2,1,0:T(8,128)S(1)}, u32[]{:S(2)}, u32[]{:S(2)}) collective-permute-start(f32[36,8,128]{2,1,0:T(8,128)S(1)} %get-tuple-element.79), channel_id=1, source_target_pairs={{0,8},{8,16},{16,24},{24,32},{32,40},{40,48},{48,56},{56,0},{1,9},... | collective-permute-start | bytes 442376 | tf_op jit(solution)/shard_map/ppermute | solution.py:19
  51.2 0.4 first_level_kernel.1
  51.6 1.2 %collective-permute-done.5.other_ref = f32[64,64]{1,0:T(8,128)S(1)} collective-permute-done((f32[64,64]{1,0:T(8,128)S(1)}, f32[64,64]{1,0:T(8,128)S(1)}, u32[]{:S(2)}, u32[]{:S(2)}) %collective-permute-start.5) | collective-permute-done | bytes 16416 | tf_op jit(solution)/shard_map/ppermute | solution.py:23
  52.8 2.2 %collective-permute-done.2.rz_up = f32[36,8,128]{2,1,0:T(8,128)S(1)} collective-permute-done((f32[36,8,128]{2,1,0:T(8,128)S(1)}, f32[36,8,128]{2,1,0:T(8,128)S(1)}, u32[]{:S(2)}, u32[]{:S(2)}) %collective-permute-start.2) | collective-permute-done | bytes 147488 | tf_op jit(solution)/shard_map/ppermute | solution.py:19
  55.0 1.9 %collective-permute-done.3.rz_down = f32[36,8,128]{2,1,0:T(8,128)S(1)} collective-permute-done((f32[36,8,128]{2,1,0:T(8,128)S(1)}, f32[36,8,128]{2,1,0:T(8,128)S(1)}, u32[]{:S(2)}, u32[]{:S(2)}) %collective-permute-start.3) | collective-permute-done | bytes 147488 | tf_op jit(solution)/shard_map/ppermute | solution.py:19
  56.9 3.3 %collective-permute-done.1.ry_two = f32[112,8,128]{2,1,0:T(8,128)S(1)} collective-permute-done((f32[112,8,128]{2,1,0:T(8,128)S(1)}, f32[112,8,128]{2,1,0:T(8,128)S(1)}, u32[]{:S(2)}, u32[]{:S(2)}) %collective-permute-start.1) | collective-permute-done | bytes 458784 | tf_op jit(solution)/shard_map/ppermute | solution.py:19
  60.4 1.9 %collective-permute-start.6 = (f32[112,8,128]{2,1,0:T(8,128)S(1)}, f32[112,8,128]{2,1,0:T(8,128)S(1)}, u32[]{:S(2)}, u32[]{:S(2)}) collective-permute-start(f32[112,8,128]{2,1,0:T(8,128)S(1)} %get-tuple-element.92), channel_id=1, source_target_pairs={{0,64},{64,128},{128,192},{192,0},{1,65},{65,129},{129,193},{193,1... | collective-permute-start | bytes 1376264 | tf_op jit(solution)/shard_map/ppermute | solution.py:19
  62.2 1.6 %collective-permute-start.7 = (f32[112,8,128]{2,1,0:T(8,128)S(1)}, f32[112,8,128]{2,1,0:T(8,128)S(1)}, u32[]{:S(2)}, u32[]{:S(2)}) collective-permute-start(f32[112,8,128]{2,1,0:T(8,128)S(1)} %get-tuple-element.93), channel_id=1, source_target_pairs={{0,192},{64,0},{128,64},{192,128},{1,193},{65,1},{129,65},{193,129... | collective-permute-start | bytes 1376264 | tf_op jit(solution)/shard_map/ppermute | solution.py:19
  63.8 2.0 %collective-permute-start.8 = (f32[72,8,128]{2,1,0:T(8,128)S(1)}, f32[72,8,128]{2,1,0:T(8,128)S(1)}, u32[]{:S(2)}, u32[]{:S(2)}) collective-permute-start(f32[72,8,128]{2,1,0:T(8,128)S(1)} %get-tuple-element.94), channel_id=1, source_target_pairs={{0,8},{8,16},{16,24},{24,32},{32,40},{40,48},{48,56},{56,0},{1,9},... | collective-permute-start | bytes 884744 | tf_op jit(solution)/shard_map/ppermute | solution.py:19
  65.9 0.3 next_level_kernel.2
  66.2 4.1 %collective-permute-start.10 = (f32[64,64]{1,0:T(8,128)S(1)}, f32[64,64]{1,0:T(8,128)S(1)}, u32[]{:S(2)}, u32[]{:S(2)}) collective-permute-start(f32[64,64]{1,0:T(8,128)S(1)} %get-tuple-element.108.mine_ref), channel_id=1, source_target_pairs={{0,8},{8,0},{16,24},{24,16},{32,40},{40,32},{48,56},{56,48},{1,9},... | collective-permute-start | bytes 49160 | tf_op jit(solution)/shard_map/ppermute | solution.py:23
  70.3 2.3 %collective-permute-done.10.other_ref = f32[64,64]{1,0:T(8,128)S(1)} collective-permute-done((f32[64,64]{1,0:T(8,128)S(1)}, f32[64,64]{1,0:T(8,128)S(1)}, u32[]{:S(2)}, u32[]{:S(2)}) %collective-permute-start.10) | collective-permute-done | bytes 16416 | tf_op jit(solution)/shard_map/ppermute | solution.py:23
  72.6 1.2 collective-permute-done.9.rz_down
  73.9 0.3 round3_kernel.1
  74.2 3.9 %collective-permute-start.11 = (f32[93,8,128]{2,1,0:T(8,128)S(1)}, f32[93,8,128]{2,1,0:T(8,128)S(1)}, u32[]{:S(2)}, u32[]{:S(2)}) collective-permute-start(f32[93,8,128]{2,1,0:T(8,128)S(1)} %get-tuple-element.106), channel_id=1, source_target_pairs={{0,8},{8,16},{16,24},{24,32},{32,40},{40,48},{48,56},{56,0},{1,9},... | collective-permute-start | bytes 1142792 | tf_op jit(solution)/shard_map/ppermute | solution.py:19
  78.1 0.3 next_level_kernel.3
  78.4 3.7 %collective-permute-start.13 = (f32[64,64]{1,0:T(8,128)S(1)}, f32[64,64]{1,0:T(8,128)S(1)}, u32[]{:S(2)}, u32[]{:S(2)}) collective-permute-start(f32[64,64]{1,0:T(8,128)S(1)} %get-tuple-element.120.mine_ref), channel_id=1, source_target_pairs={{0,16},{8,24},{16,0},{24,8},{32,48},{40,56},{48,32},{56,40},{1,17}... | collective-permute-start | bytes 49160 | tf_op jit(solution)/shard_map/ppermute | solution.py:23
  82.1 6.9 %collective-permute-done.13.other_ref = f32[64,64]{1,0:T(8,128)S(1)} collective-permute-done((f32[64,64]{1,0:T(8,128)S(1)}, f32[64,64]{1,0:T(8,128)S(1)}, u32[]{:S(2)}, u32[]{:S(2)}) %collective-permute-start.13) | collective-permute-done | bytes 16416 | tf_op jit(solution)/shard_map/ppermute | solution.py:23
  89.2 0.3 collective-permute-start.14
  89.5 1.8 %collective-permute-start.15 = (f32[86,8,128]{2,1,0:T(8,128)S(1)}, f32[86,8,128]{2,1,0:T(8,128)S(1)}, u32[]{:S(2)}, u32[]{:S(2)}) collective-permute-start(f32[86,8,128]{2,1,0:T(8,128)S(1)} %get-tuple-element.116), channel_id=1, source_target_pairs={{0,56},{8,0},{16,8},{24,16},{32,24},{40,32},{48,40},{56,48},{1,57}... | collective-permute-start | bytes 1056776 | tf_op jit(solution)/shard_map/ppermute | solution.py:19
  91.3 4.7 %node_factors.1 = f32[4,16,64]{2,1,0:T(8,128)} custom-call(s32[1]{0:T(128)} %bitcast.me_ref, f32[64,64]{1,0:T(8,128)S(1)} %get-tuple-element.117.g1_ref, f32[64,64]{1,0:T(8,128)S(1)} %get-tuple-element.118.g2_ref, f32[64,64]{1,0:T(8,128)S(1)} %get-tuple-element.119.g3_ref, f32[64,64]{1,0:T(8,128)S(1)} %get-tuple-element.120.mine_ref, ...), custom_call_target="tpu_custom_call" | custom-call | tf_op jit(solution)/shard_map/node_factors/pallas_call | solution.py:163
  96.0 0.6 collective-permute-done.14.rz_up
  96.6 1.2 %collective-permute-done.15.rz_down = f32[86,8,128]{2,1,0:T(8,128)S(1)} collective-permute-done((f32[86,8,128]{2,1,0:T(8,128)S(1)}, f32[86,8,128]{2,1,0:T(8,128)S(1)}, u32[]{:S(2)}, u32[]{:S(2)}) %collective-permute-start.15) | collective-permute-done | bytes 352288 | tf_op jit(solution)/shard_map/ppermute | solution.py:19
  97.9 0.6 collective-permute-start.18
  98.5 3.5 %collective-permute-start.19 = (f32[18,8,128]{2,1,0:T(8,128)S(1)}, f32[18,8,128]{2,1,0:T(8,128)S(1)}, u32[]{:S(2)}, u32[]{:S(2)}) collective-permute-start(f32[18,8,128]{2,1,0:T(8,128)S(1)} %get-tuple-element.129), channel_id=1, source_target_pairs={{0,128},{64,192},{128,0},{192,64},{1,129},{65,193},{129,1},{193,65... | collective-permute-start | bytes 221192 | tf_op jit(solution)/shard_map/ppermute | solution.py:19
  102.1 0.5 collective-permute-start.20
  102.6 4.2 %collective-permute-start.16 = (f32[14,8,128]{2,1,0:T(8,128)S(1)}, f32[14,8,128]{2,1,0:T(8,128)S(1)}, u32[]{:S(2)}, u32[]{:S(2)}) collective-permute-start(f32[14,8,128]{2,1,0:T(8,128)S(1)} %get-tuple-element.125), channel_id=1, source_target_pairs={{0,16},{8,24},{16,32},{24,40},{32,48},{40,56},{48,0},{56,8},{1,17}... | collective-permute-start | bytes 172040 | tf_op jit(solution)/shard_map/ppermute | solution.py:19
  106.8 2.0 %collective-permute-done.16.z_two = f32[14,8,128]{2,1,0:T(8,128)S(1)} collective-permute-done((f32[14,8,128]{2,1,0:T(8,128)S(1)}, f32[14,8,128]{2,1,0:T(8,128)S(1)}, u32[]{:S(2)}, u32[]{:S(2)}) %collective-permute-start.16) | collective-permute-done | bytes 57376 | tf_op jit(solution)/shard_map/ppermute | solution.py:19
  108.9 3.0 %collective-permute-done.17.z_six = f32[14,8,128]{2,1,0:T(8,128)S(1)} collective-permute-done((f32[14,8,128]{2,1,0:T(8,128)S(1)}, f32[14,8,128]{2,1,0:T(8,128)S(1)}, u32[]{:S(2)}, u32[]{:S(2)}) %collective-permute-start.17) | collective-permute-done | bytes 57376 | tf_op jit(solution)/shard_map/ppermute | solution.py:19
  111.9 0.3 pack.1
  112.3 0.5 collective-permute-start.21
  112.8 2.7 %collective-permute-start.22 = (f32[8,8,128]{2,1,0:T(8,128)S(1)}, f32[8,8,128]{2,1,0:T(8,128)S(1)}, u32[]{:S(2)}, u32[]{:S(2)}) collective-permute-start(f32[8,8,128]{2,1,0:T(8,128)S(1)} %get-tuple-element.133), channel_id=1, source_target_pairs={{0,2},{1,3},{2,0},{3,1},{4,6},{5,7},{6,4},{7,5},{8,10},{9,11},{10,... | collective-permute-start | bytes 98312 | tf_op jit(solution)/shard_map/ppermute | solution.py:19
  115.5 0.9 collective-permute-start.23
  116.4 1.0 collective-permute-done.21.m1_ref
  117.5 0.8 collective-permute-done.22.m2_ref
  118.2 1.2 collective-permute-done.23.m3_ref
  119.4 1.3 %left_factor.1 = f32[32,16,64]{2,1,0:T(8,128)} custom-call(s32[1]{0:T(128)} %bitcast.me_ref, f32[4,9,32,128]{3,2,1,0:T(8,128)S(1)} %bitcast.27, f32[8,8,128]{2,1,0:T(8,128)S(1)} %get-tuple-element.131.m0_ref, f32[8,8,128]{2,1,0:T(8,128)S(1)} %collective-permute-done.21.m1_ref, f32[8,8,128]{2,1,0:T(8,128)S(1)} %collective-permute-done.22.m2_ref, ...), custom_call_target="tpu_custom_call" | custom-call | tf_op jit(solution)/shard_map/left_factor/pallas_call | solution.py:456
  (32 shorter events, 1.3 us)
Async XLA Ops:
  0.6 8.1 %copy-start = (f32[1,32,64,64]{3,2,1,0:T(8,128)S(1)}, f32[1,32,64,64]{3,2,1,0:T(8,128)}, u32[]{:S(2)}) copy-start(f32[1,32,64,64]{3,2,1,0:T(8,128)} %param.10) | copy-start | bytes 1572868
  0.6 13.9 %all-to-all-start = ((f32[32,16,256]{2,1,0:T(8,128)}), f32[32,16,256]{2,1,0:T(8,128)S(1)}, u32[]{:S(2)}, u32[]{:S(2)}) async-start(f32[32,16,256]{2,1,0:T(8,128)} %bitcast.33), calls=%async_computation | async-start | bytes 1048576 | tf_op jit(solution)/shard_map/all_to_all | solution.py:502
  32.9 18.3 %copy-start.1 = (f32[1,64,64]{2,1,0:T(8,128)S(1)}, f32[1,64,64]{2,1,0:T(8,128)}, u32[]{:S(2)}) copy-start(f32[1,64,64]{2,1,0:T(8,128)} %param.11) | copy-start | bytes 49156
  43.2 2.3 %collective-permute-start = (f32[184,8,128]{2,1,0:T(8,128)S(1)}, f32[184,8,128]{2,1,0:T(8,128)S(1)}, u32[]{:S(2)}, u32[]{:S(2)}) collective-permute-start(f32[184,8,128]{2,1,0:T(8,128)S(1)} %get-tuple-element.72), channel_id=1, source_target_pairs={{0,4},{4,0},{1,5},{5,1},{2,6},{6,2},{3,7},{7,3},{8,12},{12,8},{9,1... | collective-permute-start | bytes 2261000 | tf_op jit(solution)/shard_map/ppermute | solution.py:23
  45.6 14.6 %collective-permute-start.4 = (f32[840,8,128]{2,1,0:T(8,128)S(1)}, f32[840,8,128]{2,1,0:T(8,128)S(1)}, u32[]{:S(2)}, u32[]{:S(2)}) collective-permute-start(f32[840,8,128]{2,1,0:T(8,128)S(1)} %get-tuple-element.81), channel_id=1, source_target_pairs={{0,4},{4,0},{1,5},{5,1},{2,6},{6,2},{3,7},{7,3},{8,12},{12,8},{9,1... | collective-permute-start | bytes 10321928 | tf_op jit(solution)/shard_map/ppermute | solution.py:23
  45.8 14.4 %collective-permute-start.1 = (f32[112,8,128]{2,1,0:T(8,128)S(1)}, f32[112,8,128]{2,1,0:T(8,128)S(1)}, u32[]{:S(2)}, u32[]{:S(2)}) collective-permute-start(f32[112,8,128]{2,1,0:T(8,128)S(1)} %get-tuple-element.78), channel_id=1, source_target_pairs={{0,128},{64,192},{128,0},{192,64},{1,129},{65,193},{129,1},{193,65... | collective-permute-start | bytes 1376264 | tf_op jit(solution)/shard_map/ppermute | solution.py:19
  49.1 5.8 %collective-permute-start.2 = (f32[36,8,128]{2,1,0:T(8,128)S(1)}, f32[36,8,128]{2,1,0:T(8,128)S(1)}, u32[]{:S(2)}, u32[]{:S(2)}) collective-permute-start(f32[36,8,128]{2,1,0:T(8,128)S(1)} %get-tuple-element.79), channel_id=1, source_target_pairs={{0,8},{8,16},{16,24},{24,32},{32,40},{40,48},{48,56},{56,0},{1,9},... | collective-permute-start | bytes 442376 | tf_op jit(solution)/shard_map/ppermute | solution.py:19
  51.0 5.8 %collective-permute-start.3 = (f32[36,8,128]{2,1,0:T(8,128)S(1)}, f32[36,8,128]{2,1,0:T(8,128)S(1)}, u32[]{:S(2)}, u32[]{:S(2)}) collective-permute-start(f32[36,8,128]{2,1,0:T(8,128)S(1)} %get-tuple-element.80), channel_id=1, source_target_pairs={{0,56},{8,0},{16,8},{24,16},{32,24},{40,32},{48,40},{56,48},{1,57}... | collective-permute-start | bytes 442376 | tf_op jit(solution)/shard_map/ppermute | solution.py:19
  51.6 1.2 %collective-permute-start.5 = (f32[64,64]{1,0:T(8,128)S(1)}, f32[64,64]{1,0:T(8,128)S(1)}, u32[]{:S(2)}, u32[]{:S(2)}) collective-permute-start(f32[64,64]{1,0:T(8,128)S(1)} %get-tuple-element.96.mine_ref), channel_id=1, source_target_pairs={{0,4},{4,0},{1,5},{5,1},{2,6},{6,2},{3,7},{7,3},{8,12},{12,8},{9,1... | collective-permute-start | bytes 49160 | tf_op jit(solution)/shard_map/ppermute | solution.py:23
  60.2 5.7 %copy-start.2 = (f32[1,64,64]{2,1,0:T(8,128)S(1)}, f32[1,64,64]{2,1,0:T(8,128)}, u32[]{:S(2)}) copy-start(f32[1,64,64]{2,1,0:T(8,128)} %param.12) | copy-start | bytes 49156
  60.4 13.5 %collective-permute-start.6 = (f32[112,8,128]{2,1,0:T(8,128)S(1)}, f32[112,8,128]{2,1,0:T(8,128)S(1)}, u32[]{:S(2)}, u32[]{:S(2)}) collective-permute-start(f32[112,8,128]{2,1,0:T(8,128)S(1)} %get-tuple-element.92), channel_id=1, source_target_pairs={{0,64},{64,128},{128,192},{192,0},{1,65},{65,129},{129,193},{193,1... | collective-permute-start | bytes 1376264 | tf_op jit(solution)/shard_map/ppermute | solution.py:19
  62.2 11.7 %collective-permute-start.7 = (f32[112,8,128]{2,1,0:T(8,128)S(1)}, f32[112,8,128]{2,1,0:T(8,128)S(1)}, u32[]{:S(2)}, u32[]{:S(2)}) collective-permute-start(f32[112,8,128]{2,1,0:T(8,128)S(1)} %get-tuple-element.93), channel_id=1, source_target_pairs={{0,192},{64,0},{128,64},{192,128},{1,193},{65,1},{129,65},{193,129... | collective-permute-start | bytes 1376264 | tf_op jit(solution)/shard_map/ppermute | solution.py:19
  63.8 8.8 %collective-permute-start.8 = (f32[72,8,128]{2,1,0:T(8,128)S(1)}, f32[72,8,128]{2,1,0:T(8,128)S(1)}, u32[]{:S(2)}, u32[]{:S(2)}) collective-permute-start(f32[72,8,128]{2,1,0:T(8,128)S(1)} %get-tuple-element.94), channel_id=1, source_target_pairs={{0,8},{8,16},{16,24},{24,32},{32,40},{40,48},{48,56},{56,0},{1,9},... | collective-permute-start | bytes 884744 | tf_op jit(solution)/shard_map/ppermute | solution.py:19
  65.8 8.0 %collective-permute-start.9 = (f32[72,8,128]{2,1,0:T(8,128)S(1)}, f32[72,8,128]{2,1,0:T(8,128)S(1)}, u32[]{:S(2)}, u32[]{:S(2)}) collective-permute-start(f32[72,8,128]{2,1,0:T(8,128)S(1)} %get-tuple-element.95), channel_id=1, source_target_pairs={{0,56},{8,0},{16,8},{24,16},{32,24},{40,32},{48,40},{56,48},{1,57}... | collective-permute-start | bytes 884744 | tf_op jit(solution)/shard_map/ppermute | solution.py:19
  66.2 11.9 %copy-start.3 = (f32[1,64,64]{2,1,0:T(8,128)S(1)}, f32[1,64,64]{2,1,0:T(8,128)}, u32[]{:S(2)}) copy-start(f32[1,64,64]{2,1,0:T(8,128)} %param.13) | copy-start | bytes 49156
  66.2 6.4 %collective-permute-start.10 = (f32[64,64]{1,0:T(8,128)S(1)}, f32[64,64]{1,0:T(8,128)S(1)}, u32[]{:S(2)}, u32[]{:S(2)}) collective-permute-start(f32[64,64]{1,0:T(8,128)S(1)} %get-tuple-element.108.mine_ref), channel_id=1, source_target_pairs={{0,8},{8,0},{16,24},{24,16},{32,40},{40,32},{48,56},{56,48},{1,9},... | collective-permute-start | bytes 49160 | tf_op jit(solution)/shard_map/ppermute | solution.py:23
  74.2 14.9 %collective-permute-start.11 = (f32[93,8,128]{2,1,0:T(8,128)S(1)}, f32[93,8,128]{2,1,0:T(8,128)S(1)}, u32[]{:S(2)}, u32[]{:S(2)}) collective-permute-start(f32[93,8,128]{2,1,0:T(8,128)S(1)} %get-tuple-element.106), channel_id=1, source_target_pairs={{0,8},{8,16},{16,24},{24,32},{32,40},{40,48},{48,56},{56,0},{1,9},... | collective-permute-start | bytes 1142792 | tf_op jit(solution)/shard_map/ppermute | solution.py:19
  78.1 11.0 %collective-permute-start.12 = (f32[93,8,128]{2,1,0:T(8,128)S(1)}, f32[93,8,128]{2,1,0:T(8,128)S(1)}, u32[]{:S(2)}, u32[]{:S(2)}) collective-permute-start(f32[93,8,128]{2,1,0:T(8,128)S(1)} %get-tuple-element.107), channel_id=1, source_target_pairs={{0,56},{8,0},{16,8},{24,16},{32,24},{40,32},{48,40},{56,48},{1,57}... | collective-permute-start | bytes 1142792 | tf_op jit(solution)/shard_map/ppermute | solution.py:19
  78.4 10.6 %collective-permute-start.13 = (f32[64,64]{1,0:T(8,128)S(1)}, f32[64,64]{1,0:T(8,128)S(1)}, u32[]{:S(2)}, u32[]{:S(2)}) collective-permute-start(f32[64,64]{1,0:T(8,128)S(1)} %get-tuple-element.120.mine_ref), channel_id=1, source_target_pairs={{0,16},{8,24},{16,0},{24,8},{32,48},{40,56},{48,32},{56,40},{1,17}... | collective-permute-start | bytes 49160 | tf_op jit(solution)/shard_map/ppermute | solution.py:23
  89.2 7.4 %collective-permute-start.14 = (f32[86,8,128]{2,1,0:T(8,128)S(1)}, f32[86,8,128]{2,1,0:T(8,128)S(1)}, u32[]{:S(2)}, u32[]{:S(2)}) collective-permute-start(f32[86,8,128]{2,1,0:T(8,128)S(1)} %get-tuple-element.115), channel_id=1, source_target_pairs={{0,8},{8,16},{16,24},{24,32},{32,40},{40,48},{48,56},{56,0},{1,9},... | collective-permute-start | bytes 1056776 | tf_op jit(solution)/shard_map/ppermute | solution.py:19
  89.5 8.4 %collective-permute-start.15 = (f32[86,8,128]{2,1,0:T(8,128)S(1)}, f32[86,8,128]{2,1,0:T(8,128)S(1)}, u32[]{:S(2)}, u32[]{:S(2)}) collective-permute-start(f32[86,8,128]{2,1,0:T(8,128)S(1)} %get-tuple-element.116), channel_id=1, source_target_pairs={{0,56},{8,0},{16,8},{24,16},{32,24},{40,32},{48,40},{56,48},{1,57}... | collective-permute-start | bytes 1056776 | tf_op jit(solution)/shard_map/ppermute | solution.py:19
  97.9 14.0 %collective-permute-start.18 = (f32[18,8,128]{2,1,0:T(8,128)S(1)}, f32[18,8,128]{2,1,0:T(8,128)S(1)}, u32[]{:S(2)}, u32[]{:S(2)}) collective-permute-start(f32[18,8,128]{2,1,0:T(8,128)S(1)} %get-tuple-element.128), channel_id=1, source_target_pairs={{0,64},{64,128},{128,192},{192,0},{1,65},{65,129},{129,193},{193,1... | collective-permute-start | bytes 221192 | tf_op jit(solution)/shard_map/ppermute | solution.py:19
  98.5 13.4 %collective-permute-start.19 = (f32[18,8,128]{2,1,0:T(8,128)S(1)}, f32[18,8,128]{2,1,0:T(8,128)S(1)}, u32[]{:S(2)}, u32[]{:S(2)}) collective-permute-start(f32[18,8,128]{2,1,0:T(8,128)S(1)} %get-tuple-element.129), channel_id=1, source_target_pairs={{0,128},{64,192},{128,0},{192,64},{1,129},{65,193},{129,1},{193,65... | collective-permute-start | bytes 221192 | tf_op jit(solution)/shard_map/ppermute | solution.py:19
  102.1 9.9 %collective-permute-start.20 = (f32[18,8,128]{2,1,0:T(8,128)S(1)}, f32[18,8,128]{2,1,0:T(8,128)S(1)}, u32[]{:S(2)}, u32[]{:S(2)}) collective-permute-start(f32[18,8,128]{2,1,0:T(8,128)S(1)} %get-tuple-element.130), channel_id=1, source_target_pairs={{0,192},{64,0},{128,64},{192,128},{1,193},{65,1},{129,65},{193,129... | collective-permute-start | bytes 221192 | tf_op jit(solution)/shard_map/ppermute | solution.py:19
  102.6 6.3 %collective-permute-start.16 = (f32[14,8,128]{2,1,0:T(8,128)S(1)}, f32[14,8,128]{2,1,0:T(8,128)S(1)}, u32[]{:S(2)}, u32[]{:S(2)}) collective-permute-start(f32[14,8,128]{2,1,0:T(8,128)S(1)} %get-tuple-element.125), channel_id=1, source_target_pairs={{0,16},{8,24},{16,32},{24,40},{32,48},{40,56},{48,0},{56,8},{1,17}... | collective-permute-start | bytes 172040 | tf_op jit(solution)/shard_map/ppermute | solution.py:19
  106.8 5.1 %collective-permute-start.17 = (f32[14,8,128]{2,1,0:T(8,128)S(1)}, f32[14,8,128]{2,1,0:T(8,128)S(1)}, u32[]{:S(2)}, u32[]{:S(2)}) collective-permute-start(f32[14,8,128]{2,1,0:T(8,128)S(1)} %get-tuple-element.126), channel_id=1, source_target_pairs={{0,48},{8,56},{16,0},{24,8},{32,16},{40,24},{48,32},{56,40},{1,49}... | collective-permute-start | bytes 172040 | tf_op jit(solution)/shard_map/ppermute | solution.py:19
  112.3 5.2 %collective-permute-start.21 = (f32[8,8,128]{2,1,0:T(8,128)S(1)}, f32[8,8,128]{2,1,0:T(8,128)S(1)}, u32[]{:S(2)}, u32[]{:S(2)}) collective-permute-start(f32[8,8,128]{2,1,0:T(8,128)S(1)} %get-tuple-element.132), channel_id=1, source_target_pairs={{0,1},{1,2},{2,3},{3,0},{4,5},{5,6},{6,7},{7,4},{8,9},{9,10},{10,1... | collective-permute-start | bytes 98312 | tf_op jit(solution)/shard_map/ppermute | solution.py:19
  112.8 5.4 %collective-permute-start.22 = (f32[8,8,128]{2,1,0:T(8,128)S(1)}, f32[8,8,128]{2,1,0:T(8,128)S(1)}, u32[]{:S(2)}, u32[]{:S(2)}) collective-permute-start(f32[8,8,128]{2,1,0:T(8,128)S(1)} %get-tuple-element.133), channel_id=1, source_target_pairs={{0,2},{1,3},{2,0},{3,1},{4,6},{5,7},{6,4},{7,5},{8,10},{9,11},{10,... | collective-permute-start | bytes 98312 | tf_op jit(solution)/shard_map/ppermute | solution.py:19
  115.5 3.9 %collective-permute-start.23 = (f32[8,8,128]{2,1,0:T(8,128)S(1)}, f32[8,8,128]{2,1,0:T(8,128)S(1)}, u32[]{:S(2)}, u32[]{:S(2)}) collective-permute-start(f32[8,8,128]{2,1,0:T(8,128)S(1)} %get-tuple-element.134), channel_id=1, source_target_pairs={{0,3},{1,0},{2,1},{3,2},{4,7},{5,4},{6,5},{7,6},{8,11},{9,8},{10,9... | collective-permute-start | bytes 98312 | tf_op jit(solution)/shard_map/ppermute | solution.py:19

commit v11 on v10

--- a/solution.py
+++ b/solution.py
@@ -292,7 +292,7 @@
 class Plan:
     def __init__(self, n_y, n_z, slots):
         self.n_y, self.n_z = n_y, n_z
-        self.cut = 7 * slots // 16
+        self.cut = 5 * slots // 16
         self.rest = slots - self.cut
         self.rows = {"y": n_z * self.cut, "z": n_y * self.rest}
         self.base = {}

time: 121 us -> 117 us (0.967)
  waiting for transfers between devices: 37.1 us -> 34.1 us
    ppermute x19, waiting for transfers between devices: 18.6 us -> 15 us  [shift(): lax.ppermute(value, axis, [(i, (i + step) % size) for i in range(size)])]
    ppermute x5, starting transfers between devices: 8.05 us -> 6.47 us  [swap(): lax.ppermute(value, axis, [(i, i ^ mask) for i in range(lax.axis_size(axi...]
  transfers between devices with their start and end apart: 25 -> 25, of which waited for: 18 -> 16; matrix products, arithmetic and copies ran while one was open for 3% -> 3% of each run, Pallas kernels for 5% -> 5%
where the time goes in v11:
time: 117 us
  starting transfers between devices  41.4 us (35%)
  waiting for transfers between devices  34.1 us (29%)
  Pallas kernels  23.7 us (20%)
  blocking collectives  13.1 us (11%)
  other arithmetic  2.17 us (2%)
  local copies, waits for them, and re-layouts  1.5 us (1%)
    ppermute x19, starting transfers between devices, shift(): lax.ppermute(value, axis, [(i, (i + step) % size) for i in range(size)])  30.5 us
    ppermute x19, waiting for transfers between devices, shift(): lax.ppermute(value, axis, [(i, (i + step) % size) for i in range(size)])  15 us
    ppermute x5, waiting for transfers between devices, swap(): lax.ppermute(value, axis, [(i, i ^ mask) for i in range(lax.axis_size(axi...  13.3 us
    all_gather x1, blocking collectives, shards(): packed = lax.all_gather(mine, 'rk', axis=0, tiled=False)  13.1 us
    pallas_call x1, Pallas kernels, weighted_sums(): pl.pallas_call(product_kernel, in_specs=[pl.BlockSpec(memory_space=pltpu....  10.3 us
    ppermute x5, starting transfers between devices, swap(): lax.ppermute(value, axis, [(i, i ^ mask) for i in range(lax.axis_size(axi...  6.47 us
    all_to_all x1, waiting for transfers between devices, shards(): lax.all_to_all(local, 'rk', split_axis=0, concat_axis=0, tiled=True)  5.82 us
    pallas_call x1, Pallas kernels, leaf_factors(): pl.pallas_call(leaf_kernel, out_shape=jax.ShapeDtypeStruct((leaves + 1, R...  5.19 us
  transfers between devices with their start and end apart: 25, of which 16 were waited for; matrix products, arithmetic and copies ran while one was open for 3% of the time, Pallas kernels for 5%

profile of v11, /device:TPU:32, one launch (start us, length us, event | category | flops | bytes accessed | tf_op | source)
XLA Modules:
  0.0 116.7 jit_solution(7924838507912405682)
XLA Ops:
  0.6 4.4 %all-to-all-start = ((f32[32,16,256]{2,1,0:T(8,128)}), f32[32,16,256]{2,1,0:T(8,128)S(1)}, u32[]{:S(2)}, u32[]{:S(2)}) async-start(f32[32,16,256]{2,1,0:T(8,128)} %bitcast.33), calls=%async_computation | async-start | bytes 1048576 | tf_op jit(solution)/shard_map/all_to_all | solution.py:502
  5.1 0.7 iota_compare_fusion
  5.9 0.8 squeeze.22
  6.7 0.5 broadcast.120
  7.2 1.4 %reduce.3 = s32[32,32]{1,0:T(8,128)S(1)} reduce(s32[1,32,32,1]{2,3,1,0:T(1,128)} %param.15, s32[]{:T(128)} %broadcast.120), dimensions={0,3}, to_apply=%param.15.reduce_sub_computation.3 | reduce | bytes 8196 | tf_op args[6]
  8.7 5.8 %all-to-all-done = f32[32,16,256]{2,1,0:T(8,128)S(1)} async-done(((f32[32,16,256]{2,1,0:T(8,128)}), f32[32,16,256]{2,1,0:T(8,128)S(1)}, u32[]{:S(2)}, u32[]{:S(2)}) %all-to-all-start) | async-done | bytes 524320 | tf_op jit(solution)/shard_map/all_to_all | solution.py:502
  14.6 5.2 %leaf_factors.1 = f32[9,32,128]{2,1,0:T(8,128)S(1)} custom-call(f32[4,8,16,256]{3,2,1,0:T(8,128)S(1)} %bitcast.28, f32[8,64,64]{2,1,0:T(8,128)S(1)} %dynamic-slice_bitcast_fusion.move_ref), custom_call_target="tpu_custom_call" | custom-call | tf_op jit(solution)/shard_map/leaf_factors/pallas_call | solution.py:103
  19.8 13.1 %all-gather = f32[36,32,128]{2,1,0:T(8,128)S(1)} all-gather(f32[9,32,128]{2,1,0:T(8,128)S(1)} %leaf_factors.1), channel_id=2, replica_groups=mesh['y'=4,'z'=8,'core'=2,'rk'=4] {'rk'}, dimensions={0}, use_global_device_ids=true | all-gather | bytes 737280 | tf_op jit(solution)/shard_map/all_gather | solution.py:505
  32.9 10.3 %weighted_sums.1 = (f32[168,8,128]{2,1,0:T(8,128)S(1)}, f32[856,8,128]{2,1,0:T(8,128)S(1)}, f32[168,8,128]{2,1,0:T(8,128)S(1)}, f32[856,8,128]{2,1,0:T(8,128)S(1)}, f32[32,16,64]{2,1,0:T(8,128)}) custom-call(s32[1]{0:T(128)} %bitcast.me_ref, s32[1024]{0:T(1024)S(1)} %add_select_fusion.5.place_ref, f32[32,32,16,64]{3,2,1,0:T(8,128)} %bitcast.32, ...), custom_call_target="tpu_custom_call" | custom-call | tf_op jit(solution)/shard_map/weighted_sums/pallas_call | solution.py:271
  43.3 2.1 %collective-permute-done.got = f32[168,8,128]{2,1,0:T(8,128)S(1)} collective-permute-done((f32[168,8,128]{2,1,0:T(8,128)S(1)}, f32[168,8,128]{2,1,0:T(8,128)S(1)}, u32[]{:S(2)}, u32[]{:S(2)}) %collective-permute-start) | collective-permute-done | bytes 688160 | tf_op jit(solution)/shard_map/ppermute | solution.py:23
  45.6 3.3 %collective-permute-start.1 = (f32[80,8,128]{2,1,0:T(8,128)S(1)}, f32[80,8,128]{2,1,0:T(8,128)S(1)}, u32[]{:S(2)}, u32[]{:S(2)}) collective-permute-start(f32[80,8,128]{2,1,0:T(8,128)S(1)} %get-tuple-element.78), channel_id=1, source_target_pairs={{0,128},{64,192},{128,0},{192,64},{1,129},{65,193},{129,1},{193,65... | collective-permute-start | bytes 983048 | tf_op jit(solution)/shard_map/ppermute | solution.py:19
  48.9 2.1 %collective-permute-start.2 = (f32[44,8,128]{2,1,0:T(8,128)S(1)}, f32[44,8,128]{2,1,0:T(8,128)S(1)}, u32[]{:S(2)}, u32[]{:S(2)}) collective-permute-start(f32[44,8,128]{2,1,0:T(8,128)S(1)} %get-tuple-element.79), channel_id=1, source_target_pairs={{0,8},{8,16},{16,24},{24,32},{32,40},{40,48},{48,56},{56,0},{1,9},... | collective-permute-start | bytes 540680 | tf_op jit(solution)/shard_map/ppermute | solution.py:19
  51.0 0.4 first_level_kernel.1
  51.4 1.2 %collective-permute-done.5.other_ref = f32[64,64]{1,0:T(8,128)S(1)} collective-permute-done((f32[64,64]{1,0:T(8,128)S(1)}, f32[64,64]{1,0:T(8,128)S(1)}, u32[]{:S(2)}, u32[]{:S(2)}) %collective-permute-start.5) | collective-permute-done | bytes 16416 | tf_op jit(solution)/shard_map/ppermute | solution.py:23
  52.6 2.9 %collective-permute-done.2.rz_up = f32[44,8,128]{2,1,0:T(8,128)S(1)} collective-permute-done((f32[44,8,128]{2,1,0:T(8,128)S(1)}, f32[44,8,128]{2,1,0:T(8,128)S(1)}, u32[]{:S(2)}, u32[]{:S(2)}) %collective-permute-start.2) | collective-permute-done | bytes 180256 | tf_op jit(solution)/shard_map/ppermute | solution.py:19
  55.4 1.9 %collective-permute-done.3.rz_down = f32[44,8,128]{2,1,0:T(8,128)S(1)} collective-permute-done((f32[44,8,128]{2,1,0:T(8,128)S(1)}, f32[44,8,128]{2,1,0:T(8,128)S(1)}, u32[]{:S(2)}, u32[]{:S(2)}) %collective-permute-start.3) | collective-permute-done | bytes 180256 | tf_op jit(solution)/shard_map/ppermute | solution.py:19
  57.5 3.1 %collective-permute-start.8 = (f32[88,8,128]{2,1,0:T(8,128)S(1)}, f32[88,8,128]{2,1,0:T(8,128)S(1)}, u32[]{:S(2)}, u32[]{:S(2)}) collective-permute-start(f32[88,8,128]{2,1,0:T(8,128)S(1)} %get-tuple-element.94), channel_id=1, source_target_pairs={{0,8},{8,16},{16,24},{24,32},{32,40},{40,48},{48,56},{56,0},{1,9},... | collective-permute-start | bytes 1081352 | tf_op jit(solution)/shard_map/ppermute | solution.py:19
  60.6 0.7 collective-permute-start.6
  61.3 2.5 %collective-permute-start.7 = (f32[80,8,128]{2,1,0:T(8,128)S(1)}, f32[80,8,128]{2,1,0:T(8,128)S(1)}, u32[]{:S(2)}, u32[]{:S(2)}) collective-permute-start(f32[80,8,128]{2,1,0:T(8,128)S(1)} %get-tuple-element.93), channel_id=1, source_target_pairs={{0,192},{64,0},{128,64},{192,128},{1,193},{65,1},{129,65},{193,129... | collective-permute-start | bytes 983048 | tf_op jit(solution)/shard_map/ppermute | solution.py:19
  63.9 0.3 next_level_kernel.2
  64.2 3.2 %collective-permute-start.10 = (f32[64,64]{1,0:T(8,128)S(1)}, f32[64,64]{1,0:T(8,128)S(1)}, u32[]{:S(2)}, u32[]{:S(2)}) collective-permute-start(f32[64,64]{1,0:T(8,128)S(1)} %get-tuple-element.108.mine_ref), channel_id=1, source_target_pairs={{0,8},{8,0},{16,24},{24,16},{32,40},{40,32},{48,56},{56,48},{1,9},... | collective-permute-start | bytes 49160 | tf_op jit(solution)/shard_map/ppermute | solution.py:23
  67.4 1.9 %collective-permute-done.10.other_ref = f32[64,64]{1,0:T(8,128)S(1)} collective-permute-done((f32[64,64]{1,0:T(8,128)S(1)}, f32[64,64]{1,0:T(8,128)S(1)}, u32[]{:S(2)}, u32[]{:S(2)}) %collective-permute-start.10) | collective-permute-done | bytes 16416 | tf_op jit(solution)/shard_map/ppermute | solution.py:23
  69.3 1.1 collective-permute-done.6.ry_up
  70.4 0.4 collective-permute-done.9.rz_down
  71.1 2.5 %collective-permute-start.11 = (f32[103,8,128]{2,1,0:T(8,128)S(1)}, f32[103,8,128]{2,1,0:T(8,128)S(1)}, u32[]{:S(2)}, u32[]{:S(2)}) collective-permute-start(f32[103,8,128]{2,1,0:T(8,128)S(1)} %get-tuple-element.106), channel_id=1, source_target_pairs={{0,8},{8,16},{16,24},{24,32},{32,40},{40,48},{48,56},{56,0},{1,9},... | collective-permute-start | bytes 1265672 | tf_op jit(solution)/shard_map/ppermute | solution.py:19
  73.6 0.8 collective-permute-start.12
  74.4 0.3 next_level_kernel.3
  74.7 3.1 %collective-permute-start.13 = (f32[64,64]{1,0:T(8,128)S(1)}, f32[64,64]{1,0:T(8,128)S(1)}, u32[]{:S(2)}, u32[]{:S(2)}) collective-permute-start(f32[64,64]{1,0:T(8,128)S(1)} %get-tuple-element.120.mine_ref), channel_id=1, source_target_pairs={{0,16},{8,24},{16,0},{24,8},{32,48},{40,56},{48,32},{56,40},{1,17}... | collective-permute-start | bytes 49160 | tf_op jit(solution)/shard_map/ppermute | solution.py:23
  77.8 8.0 %collective-permute-done.13.other_ref = f32[64,64]{1,0:T(8,128)S(1)} collective-permute-done((f32[64,64]{1,0:T(8,128)S(1)}, f32[64,64]{1,0:T(8,128)S(1)}, u32[]{:S(2)}, u32[]{:S(2)}) %collective-permute-start.13) | collective-permute-done | bytes 16416 | tf_op jit(solution)/shard_map/ppermute | solution.py:23
  86.2 1.8 %collective-permute-start.15 = (f32[98,8,128]{2,1,0:T(8,128)S(1)}, f32[98,8,128]{2,1,0:T(8,128)S(1)}, u32[]{:S(2)}, u32[]{:S(2)}) collective-permute-start(f32[98,8,128]{2,1,0:T(8,128)S(1)} %get-tuple-element.116), channel_id=1, source_target_pairs={{0,56},{8,0},{16,8},{24,16},{32,24},{40,32},{48,40},{56,48},{1,57}... | collective-permute-start | bytes 1204232 | tf_op jit(solution)/shard_map/ppermute | solution.py:19
  88.0 4.7 %node_factors.1 = f32[4,16,64]{2,1,0:T(8,128)} custom-call(s32[1]{0:T(128)} %bitcast.me_ref, f32[64,64]{1,0:T(8,128)S(1)} %get-tuple-element.117.g1_ref, f32[64,64]{1,0:T(8,128)S(1)} %get-tuple-element.118.g2_ref, f32[64,64]{1,0:T(8,128)S(1)} %get-tuple-element.119.g3_ref, f32[64,64]{1,0:T(8,128)S(1)} %get-tuple-element.120.mine_ref, ...), custom_call_target="tpu_custom_call" | custom-call | tf_op jit(solution)/shard_map/node_factors/pallas_call | solution.py:163
  92.7 1.3 %collective-permute-done.14.rz_up = f32[98,8,128]{2,1,0:T(8,128)S(1)} collective-permute-done((f32[98,8,128]{2,1,0:T(8,128)S(1)}, f32[98,8,128]{2,1,0:T(8,128)S(1)}, u32[]{:S(2)}, u32[]{:S(2)}) %collective-permute-start.14) | collective-permute-done | bytes 401440 | tf_op jit(solution)/shard_map/ppermute | solution.py:19
  94.0 0.8 collective-permute-done.15.rz_down
  94.9 1.1 collective-permute-start.18
  96.0 2.9 %collective-permute-start.19 = (f32[22,8,128]{2,1,0:T(8,128)S(1)}, f32[22,8,128]{2,1,0:T(8,128)S(1)}, u32[]{:S(2)}, u32[]{:S(2)}) collective-permute-start(f32[22,8,128]{2,1,0:T(8,128)S(1)} %get-tuple-element.129), channel_id=1, source_target_pairs={{0,128},{64,192},{128,0},{192,64},{1,129},{65,193},{129,1},{193,65... | collective-permute-start | bytes 270344 | tf_op jit(solution)/shard_map/ppermute | solution.py:19
  98.9 1.1 collective-permute-start.20
  100.0 3.0 %collective-permute-start.16 = (f32[10,8,128]{2,1,0:T(8,128)S(1)}, f32[10,8,128]{2,1,0:T(8,128)S(1)}, u32[]{:S(2)}, u32[]{:S(2)}) collective-permute-start(f32[10,8,128]{2,1,0:T(8,128)S(1)} %get-tuple-element.125), channel_id=1, source_target_pairs={{0,16},{8,24},{16,32},{24,40},{32,48},{40,56},{48,0},{56,8},{1,17}... | collective-permute-start | bytes 122888 | tf_op jit(solution)/shard_map/ppermute | solution.py:19
  103.0 1.1 collective-permute-start.17
  104.1 2.0 %collective-permute-done.16.z_two = f32[10,8,128]{2,1,0:T(8,128)S(1)} collective-permute-done((f32[10,8,128]{2,1,0:T(8,128)S(1)}, f32[10,8,128]{2,1,0:T(8,128)S(1)}, u32[]{:S(2)}, u32[]{:S(2)}) %collective-permute-start.16) | collective-permute-done | bytes 40992 | tf_op jit(solution)/shard_map/ppermute | solution.py:19
  106.1 1.8 %collective-permute-done.17.z_six = f32[10,8,128]{2,1,0:T(8,128)S(1)} collective-permute-done((f32[10,8,128]{2,1,0:T(8,128)S(1)}, f32[10,8,128]{2,1,0:T(8,128)S(1)}, u32[]{:S(2)}, u32[]{:S(2)}) %collective-permute-start.17) | collective-permute-done | bytes 40992 | tf_op jit(solution)/shard_map/ppermute | solution.py:19
  107.9 0.3 pack.1
  108.2 0.6 collective-permute-start.21
  108.8 2.7 %collective-permute-start.22 = (f32[8,8,128]{2,1,0:T(8,128)S(1)}, f32[8,8,128]{2,1,0:T(8,128)S(1)}, u32[]{:S(2)}, u32[]{:S(2)}) collective-permute-start(f32[8,8,128]{2,1,0:T(8,128)S(1)} %get-tuple-element.133), channel_id=1, source_target_pairs={{0,2},{1,3},{2,0},{3,1},{4,6},{5,7},{6,4},{7,5},{8,10},{9,11},{10,... | collective-permute-start | bytes 98312 | tf_op jit(solution)/shard_map/ppermute | solution.py:19
  111.5 0.9 collective-permute-start.23
  112.4 1.0 collective-permute-done.21.m1_ref
  113.4 0.8 collective-permute-done.22.m2_ref
  114.2 1.2 %collective-permute-done.23.m3_ref = f32[8,8,128]{2,1,0:T(8,128)S(1)} collective-permute-done((f32[8,8,128]{2,1,0:T(8,128)S(1)}, f32[8,8,128]{2,1,0:T(8,128)S(1)}, u32[]{:S(2)}, u32[]{:S(2)}) %collective-permute-start.23) | collective-permute-done | bytes 32800 | tf_op jit(solution)/shard_map/ppermute | solution.py:19
  115.4 1.3 %left_factor.1 = f32[32,16,64]{2,1,0:T(8,128)} custom-call(s32[1]{0:T(128)} %bitcast.me_ref, f32[4,9,32,128]{3,2,1,0:T(8,128)S(1)} %bitcast.27, f32[8,8,128]{2,1,0:T(8,128)S(1)} %get-tuple-element.131.m0_ref, f32[8,8,128]{2,1,0:T(8,128)S(1)} %collective-permute-done.21.m1_ref, f32[8,8,128]{2,1,0:T(8,128)S(1)} %collective-permute-done.22.m2_ref, ...), custom_call_target="tpu_custom_call" | custom-call | tf_op jit(solution)/shard_map/left_factor/pallas_call | solution.py:456
  (32 shorter events, 1.5 us)
Async XLA Ops:
  0.6 8.1 %copy-start = (f32[1,32,64,64]{3,2,1,0:T(8,128)S(1)}, f32[1,32,64,64]{3,2,1,0:T(8,128)}, u32[]{:S(2)}) copy-start(f32[1,32,64,64]{3,2,1,0:T(8,128)} %param.10) | copy-start | bytes 1572868
  0.6 13.9 %all-to-all-start = ((f32[32,16,256]{2,1,0:T(8,128)}), f32[32,16,256]{2,1,0:T(8,128)S(1)}, u32[]{:S(2)}, u32[]{:S(2)}) async-start(f32[32,16,256]{2,1,0:T(8,128)} %bitcast.33), calls=%async_computation | async-start | bytes 1048576 | tf_op jit(solution)/shard_map/all_to_all | solution.py:502
  32.9 18.1 %copy-start.1 = (f32[1,64,64]{2,1,0:T(8,128)S(1)}, f32[1,64,64]{2,1,0:T(8,128)}, u32[]{:S(2)}) copy-start(f32[1,64,64]{2,1,0:T(8,128)} %param.11) | copy-start | bytes 49156
  43.2 2.2 %collective-permute-start = (f32[168,8,128]{2,1,0:T(8,128)S(1)}, f32[168,8,128]{2,1,0:T(8,128)S(1)}, u32[]{:S(2)}, u32[]{:S(2)}) collective-permute-start(f32[168,8,128]{2,1,0:T(8,128)S(1)} %get-tuple-element.72), channel_id=1, source_target_pairs={{0,4},{4,0},{1,5},{5,1},{2,6},{6,2},{3,7},{7,3},{8,12},{12,8},{9,1... | collective-permute-start | bytes 2064392 | tf_op jit(solution)/shard_map/ppermute | solution.py:23
  45.4 11.9 %collective-permute-start.4 = (f32[856,8,128]{2,1,0:T(8,128)S(1)}, f32[856,8,128]{2,1,0:T(8,128)S(1)}, u32[]{:S(2)}, u32[]{:S(2)}) collective-permute-start(f32[856,8,128]{2,1,0:T(8,128)S(1)} %get-tuple-element.81), channel_id=1, source_target_pairs={{0,4},{4,0},{1,5},{5,1},{2,6},{6,2},{3,7},{7,3},{8,12},{12,8},{9,1... | collective-permute-start | bytes 10518536 | tf_op jit(solution)/shard_map/ppermute | solution.py:23
  45.6 11.7 %collective-permute-start.1 = (f32[80,8,128]{2,1,0:T(8,128)S(1)}, f32[80,8,128]{2,1,0:T(8,128)S(1)}, u32[]{:S(2)}, u32[]{:S(2)}) collective-permute-start(f32[80,8,128]{2,1,0:T(8,128)S(1)} %get-tuple-element.78), channel_id=1, source_target_pairs={{0,128},{64,192},{128,0},{192,64},{1,129},{65,193},{129,1},{193,65... | collective-permute-start | bytes 983048 | tf_op jit(solution)/shard_map/ppermute | solution.py:19
  48.9 6.5 %collective-permute-start.2 = (f32[44,8,128]{2,1,0:T(8,128)S(1)}, f32[44,8,128]{2,1,0:T(8,128)S(1)}, u32[]{:S(2)}, u32[]{:S(2)}) collective-permute-start(f32[44,8,128]{2,1,0:T(8,128)S(1)} %get-tuple-element.79), channel_id=1, source_target_pairs={{0,8},{8,16},{16,24},{24,32},{32,40},{40,48},{48,56},{56,0},{1,9},... | collective-permute-start | bytes 540680 | tf_op jit(solution)/shard_map/ppermute | solution.py:19
  51.0 6.3 %collective-permute-start.3 = (f32[44,8,128]{2,1,0:T(8,128)S(1)}, f32[44,8,128]{2,1,0:T(8,128)S(1)}, u32[]{:S(2)}, u32[]{:S(2)}) collective-permute-start(f32[44,8,128]{2,1,0:T(8,128)S(1)} %get-tuple-element.80), channel_id=1, source_target_pairs={{0,56},{8,0},{16,8},{24,16},{32,24},{40,32},{48,40},{56,48},{1,57}... | collective-permute-start | bytes 540680 | tf_op jit(solution)/shard_map/ppermute | solution.py:19
  51.4 1.2 %collective-permute-start.5 = (f32[64,64]{1,0:T(8,128)S(1)}, f32[64,64]{1,0:T(8,128)S(1)}, u32[]{:S(2)}, u32[]{:S(2)}) collective-permute-start(f32[64,64]{1,0:T(8,128)S(1)} %get-tuple-element.96.mine_ref), channel_id=1, source_target_pairs={{0,4},{4,0},{1,5},{5,1},{2,6},{6,2},{3,7},{7,3},{8,12},{12,8},{9,1... | collective-permute-start | bytes 49160 | tf_op jit(solution)/shard_map/ppermute | solution.py:23
  57.3 6.6 %copy-start.2 = (f32[1,64,64]{2,1,0:T(8,128)S(1)}, f32[1,64,64]{2,1,0:T(8,128)}, u32[]{:S(2)}) copy-start(f32[1,64,64]{2,1,0:T(8,128)} %param.12) | copy-start | bytes 49156
  57.5 12.9 %collective-permute-start.8 = (f32[88,8,128]{2,1,0:T(8,128)S(1)}, f32[88,8,128]{2,1,0:T(8,128)S(1)}, u32[]{:S(2)}, u32[]{:S(2)}) collective-permute-start(f32[88,8,128]{2,1,0:T(8,128)S(1)} %get-tuple-element.94), channel_id=1, source_target_pairs={{0,8},{8,16},{16,24},{24,32},{32,40},{40,48},{48,56},{56,0},{1,9},... | collective-permute-start | bytes 1081352 | tf_op jit(solution)/shard_map/ppermute | solution.py:19
  60.6 10.2 %collective-permute-start.9 = (f32[88,8,128]{2,1,0:T(8,128)S(1)}, f32[88,8,128]{2,1,0:T(8,128)S(1)}, u32[]{:S(2)}, u32[]{:S(2)}) collective-permute-start(f32[88,8,128]{2,1,0:T(8,128)S(1)} %get-tuple-element.95), channel_id=1, source_target_pairs={{0,56},{8,0},{16,8},{24,16},{32,24},{40,32},{48,40},{56,48},{1,57}... | collective-permute-start | bytes 1081352 | tf_op jit(solution)/shard_map/ppermute | solution.py:19
  60.6 9.8 %collective-permute-start.6 = (f32[80,8,128]{2,1,0:T(8,128)S(1)}, f32[80,8,128]{2,1,0:T(8,128)S(1)}, u32[]{:S(2)}, u32[]{:S(2)}) collective-permute-start(f32[80,8,128]{2,1,0:T(8,128)S(1)} %get-tuple-element.92), channel_id=1, source_target_pairs={{0,64},{64,128},{128,192},{192,0},{1,65},{65,129},{129,193},{193,1... | collective-permute-start | bytes 983048 | tf_op jit(solution)/shard_map/ppermute | solution.py:19
  61.3 9.1 %collective-permute-start.7 = (f32[80,8,128]{2,1,0:T(8,128)S(1)}, f32[80,8,128]{2,1,0:T(8,128)S(1)}, u32[]{:S(2)}, u32[]{:S(2)}) collective-permute-start(f32[80,8,128]{2,1,0:T(8,128)S(1)} %get-tuple-element.93), channel_id=1, source_target_pairs={{0,192},{64,0},{128,64},{192,128},{1,193},{65,1},{129,65},{193,129... | collective-permute-start | bytes 983048 | tf_op jit(solution)/shard_map/ppermute | solution.py:19
  64.2 10.2 %copy-start.3 = (f32[1,64,64]{2,1,0:T(8,128)S(1)}, f32[1,64,64]{2,1,0:T(8,128)}, u32[]{:S(2)}) copy-start(f32[1,64,64]{2,1,0:T(8,128)} %param.13) | copy-start | bytes 49156
  64.2 5.1 %collective-permute-start.10 = (f32[64,64]{1,0:T(8,128)S(1)}, f32[64,64]{1,0:T(8,128)S(1)}, u32[]{:S(2)}, u32[]{:S(2)}) collective-permute-start(f32[64,64]{1,0:T(8,128)S(1)} %get-tuple-element.108.mine_ref), channel_id=1, source_target_pairs={{0,8},{8,0},{16,24},{24,16},{32,40},{40,32},{48,56},{56,48},{1,9},... | collective-permute-start | bytes 49160 | tf_op jit(solution)/shard_map/ppermute | solution.py:23
  71.1 14.7 %collective-permute-start.11 = (f32[103,8,128]{2,1,0:T(8,128)S(1)}, f32[103,8,128]{2,1,0:T(8,128)S(1)}, u32[]{:S(2)}, u32[]{:S(2)}) collective-permute-start(f32[103,8,128]{2,1,0:T(8,128)S(1)} %get-tuple-element.106), channel_id=1, source_target_pairs={{0,8},{8,16},{16,24},{24,32},{32,40},{40,48},{48,56},{56,0},{1,9},... | collective-permute-start | bytes 1265672 | tf_op jit(solution)/shard_map/ppermute | solution.py:19
  73.6 12.2 %collective-permute-start.12 = (f32[103,8,128]{2,1,0:T(8,128)S(1)}, f32[103,8,128]{2,1,0:T(8,128)S(1)}, u32[]{:S(2)}, u32[]{:S(2)}) collective-permute-start(f32[103,8,128]{2,1,0:T(8,128)S(1)} %get-tuple-element.107), channel_id=1, source_target_pairs={{0,56},{8,0},{16,8},{24,16},{32,24},{40,32},{48,40},{56,48},{1,57}... | collective-permute-start | bytes 1265672 | tf_op jit(solution)/shard_map/ppermute | solution.py:19
  74.7 11.1 %collective-permute-start.13 = (f32[64,64]{1,0:T(8,128)S(1)}, f32[64,64]{1,0:T(8,128)S(1)}, u32[]{:S(2)}, u32[]{:S(2)}) collective-permute-start(f32[64,64]{1,0:T(8,128)S(1)} %get-tuple-element.120.mine_ref), channel_id=1, source_target_pairs={{0,16},{8,24},{16,0},{24,8},{32,48},{40,56},{48,32},{56,40},{1,17}... | collective-permute-start | bytes 49160 | tf_op jit(solution)/shard_map/ppermute | solution.py:23
  85.9 8.1 %collective-permute-start.14 = (f32[98,8,128]{2,1,0:T(8,128)S(1)}, f32[98,8,128]{2,1,0:T(8,128)S(1)}, u32[]{:S(2)}, u32[]{:S(2)}) collective-permute-start(f32[98,8,128]{2,1,0:T(8,128)S(1)} %get-tuple-element.115), channel_id=1, source_target_pairs={{0,8},{8,16},{16,24},{24,32},{32,40},{40,48},{48,56},{56,0},{1,9},... | collective-permute-start | bytes 1204232 | tf_op jit(solution)/shard_map/ppermute | solution.py:19
  86.2 8.6 %collective-permute-start.15 = (f32[98,8,128]{2,1,0:T(8,128)S(1)}, f32[98,8,128]{2,1,0:T(8,128)S(1)}, u32[]{:S(2)}, u32[]{:S(2)}) collective-permute-start(f32[98,8,128]{2,1,0:T(8,128)S(1)} %get-tuple-element.116), channel_id=1, source_target_pairs={{0,56},{8,0},{16,8},{24,16},{32,24},{40,32},{48,40},{56,48},{1,57}... | collective-permute-start | bytes 1204232 | tf_op jit(solution)/shard_map/ppermute | solution.py:19
  94.9 13.0 %collective-permute-start.18 = (f32[22,8,128]{2,1,0:T(8,128)S(1)}, f32[22,8,128]{2,1,0:T(8,128)S(1)}, u32[]{:S(2)}, u32[]{:S(2)}) collective-permute-start(f32[22,8,128]{2,1,0:T(8,128)S(1)} %get-tuple-element.128), channel_id=1, source_target_pairs={{0,64},{64,128},{128,192},{192,0},{1,65},{65,129},{129,193},{193,1... | collective-permute-start | bytes 270344 | tf_op jit(solution)/shard_map/ppermute | solution.py:19
  96.0 11.9 %collective-permute-start.19 = (f32[22,8,128]{2,1,0:T(8,128)S(1)}, f32[22,8,128]{2,1,0:T(8,128)S(1)}, u32[]{:S(2)}, u32[]{:S(2)}) collective-permute-start(f32[22,8,128]{2,1,0:T(8,128)S(1)} %get-tuple-element.129), channel_id=1, source_target_pairs={{0,128},{64,192},{128,0},{192,64},{1,129},{65,193},{129,1},{193,65... | collective-permute-start | bytes 270344 | tf_op jit(solution)/shard_map/ppermute | solution.py:19
  98.9 9.0 %collective-permute-start.20 = (f32[22,8,128]{2,1,0:T(8,128)S(1)}, f32[22,8,128]{2,1,0:T(8,128)S(1)}, u32[]{:S(2)}, u32[]{:S(2)}) collective-permute-start(f32[22,8,128]{2,1,0:T(8,128)S(1)} %get-tuple-element.130), channel_id=1, source_target_pairs={{0,192},{64,0},{128,64},{192,128},{1,193},{65,1},{129,65},{193,129... | collective-permute-start | bytes 270344 | tf_op jit(solution)/shard_map/ppermute | solution.py:19
  100.0 6.1 %collective-permute-start.16 = (f32[10,8,128]{2,1,0:T(8,128)S(1)}, f32[10,8,128]{2,1,0:T(8,128)S(1)}, u32[]{:S(2)}, u32[]{:S(2)}) collective-permute-start(f32[10,8,128]{2,1,0:T(8,128)S(1)} %get-tuple-element.125), channel_id=1, source_target_pairs={{0,16},{8,24},{16,32},{24,40},{32,48},{40,56},{48,0},{56,8},{1,17}... | collective-permute-start | bytes 122888 | tf_op jit(solution)/shard_map/ppermute | solution.py:19
  103.0 4.9 %collective-permute-start.17 = (f32[10,8,128]{2,1,0:T(8,128)S(1)}, f32[10,8,128]{2,1,0:T(8,128)S(1)}, u32[]{:S(2)}, u32[]{:S(2)}) collective-permute-start(f32[10,8,128]{2,1,0:T(8,128)S(1)} %get-tuple-element.126), channel_id=1, source_target_pairs={{0,48},{8,56},{16,0},{24,8},{32,16},{40,24},{48,32},{56,40},{1,49}... | collective-permute-start | bytes 122888 | tf_op jit(solution)/shard_map/ppermute | solution.py:19
  108.2 5.2 %collective-permute-start.21 = (f32[8,8,128]{2,1,0:T(8,128)S(1)}, f32[8,8,128]{2,1,0:T(8,128)S(1)}, u32[]{:S(2)}, u32[]{:S(2)}) collective-permute-start(f32[8,8,128]{2,1,0:T(8,128)S(1)} %get-tuple-element.132), channel_id=1, source_target_pairs={{0,1},{1,2},{2,3},{3,0},{4,5},{5,6},{6,7},{7,4},{8,9},{9,10},{10,1... | collective-permute-start | bytes 98312 | tf_op jit(solution)/shard_map/ppermute | solution.py:19
  108.8 5.4 %collective-permute-start.22 = (f32[8,8,128]{2,1,0:T(8,128)S(1)}, f32[8,8,128]{2,1,0:T(8,128)S(1)}, u32[]{:S(2)}, u32[]{:S(2)}) collective-permute-start(f32[8,8,128]{2,1,0:T(8,128)S(1)} %get-tuple-element.133), channel_id=1, source_target_pairs={{0,2},{1,3},{2,0},{3,1},{4,6},{5,7},{6,4},{7,5},{8,10},{9,11},{10,... | collective-permute-start | bytes 98312 | tf_op jit(solution)/shard_map/ppermute | solution.py:19
  111.5 3.9 %collective-permute-start.23 = (f32[8,8,128]{2,1,0:T(8,128)S(1)}, f32[8,8,128]{2,1,0:T(8,128)S(1)}, u32[]{:S(2)}, u32[]{:S(2)}) collective-permute-start(f32[8,8,128]{2,1,0:T(8,128)S(1)} %get-tuple-element.134), channel_id=1, source_target_pairs={{0,3},{1,0},{2,1},{3,2},{4,7},{5,4},{6,5},{7,6},{8,11},{9,8},{10,9... | collective-permute-start | bytes 98312 | tf_op jit(solution)/shard_map/ppermute | solution.py:19
